TPU v7x, 32 devices: a whole 2x2x4 slice. The times are simulated.
32 devices in a mesh: leaf: 8 (over z, x), sub: 4 (over y, core).
Axes of the slice: x: 2, y: 2, z: 4, core: 2. Of those that a mesh axis runs over, the one named last changes fastest.
Arguments:
- points: bfloat16 [131072, 64], P(('leaf', 'sub')), may hold values from -6 to 6
- probes: bfloat16 [131072, 128], P(('leaf', 'sub')), may hold values from -6 to 6
- order: int32 [131072], P(('leaf', 'sub')), may hold values from 0 to 511, as said below
- near_lists: int32 [256, 12], P(('leaf', 'sub')), may hold values from 0 to 255, as said below
- near_counts: int32 [256], P(('leaf', 'sub')), may hold values from 1 to 12, as said below
- leaf_sets: int32 [256, 128], P(('leaf', 'sub')), may hold values from 0 to 511, as said below
- merge_sets: int32 [255, 128], replicated, may hold values from 0 to 255, as said below
Outputs:
- near_samples: float32 [131072, 128], P(('leaf', 'sub'))
- root_samples: float32 [16384], P(('leaf', 'sub'))
Inputs may be any that keep to these rules, and one draw needn't show every extreme that they name: `order`: the 512 entries of each leaf block are a permutation of 0 to 511. `near_lists`: for block g of shard i = g // 32: entry 0 is g; entries 1 to near_counts[g] - 1 are distinct blocks other than g within i * 32 - 8 to (i + 1) * 32 + 7; entries from near_counts[g] on equal g. `near_counts`: some block among the first sixteen of the aligned sixteens of blocks has 12 entries. `leaf_sets`: each row holds distinct values. `merge_sets`: each row holds distinct values; row m - 1 belongs to the node whose two children meet at block m.
All inputs are finite; a program needn't handle non-finite values.
Results may differ from a plain program's by a relative error of at most 0.0029.
Values may be sent and summed in bfloat16 or wider, within the bound.
No kernel may reach another device: no remote copies, remote signals or barrier semaphores. Data moves between devices by JAX's collectives and lax.ppermute only.
A program may use at most 128 MiB of HBM per device.

v0:
```python
import functools

import jax
import jax.numpy as jnp
from jax import lax
from jax.experimental import pallas as pl
from jax.experimental.pallas import tpu as pltpu
from jax.sharding import PartitionSpec as P

LANES = 128
PARTS = 3
VMEM_BYTES = 20 * 1024 * 1024
NEAR_BYTES = 24 * 1024 * 1024
F32 = jnp.float32
BF16 = jnp.bfloat16


def dot(a, b):
    return jnp.dot(a, b, preferred_element_type=F32)


def dot_t(a, b):
    return lax.dot_general(a, b, (((0,), (0,)), ((), ())), preferred_element_type=F32)


def split(x):
    hi = x.astype(BF16)
    return hi, (x - hi.astype(F32)).astype(BF16)


def square_rows(pts):
    x = pts.astype(F32)
    total = jnp.sum(x * x, axis=0, keepdims=True)
    hi = total.astype(BF16).astype(F32)
    mid = (total - hi).astype(BF16).astype(F32)
    low = total - hi - mid
    row = lax.broadcasted_iota(jnp.int32, (16, pts.shape[1]), 0)
    ones = jnp.where(row < 2 * PARTS, 1.0, 0.0)
    return jnp.where(row == 0, hi, jnp.where(row == 1, mid, jnp.where(row == 2, low, ones))).astype(BF16)


def form_map(dim, size):
    k = lax.broadcasted_iota(jnp.int32, (size, size), 0)
    j = lax.broadcasted_iota(jnp.int32, (size, size), 1)
    r = jnp.where((k == j) & (j < dim), 2.0 / dim, 0.0)
    r = jnp.where((j >= dim) & (j < dim + PARTS) & (k == j + PARTS), -1.0 / dim, r)
    r = jnp.where((j >= dim + PARTS) & (j < dim + 2 * PARTS) & (k == j - PARTS), -1.0 / dim, r)
    return r.astype(BF16)


def onehot_in(row, size):
    index = lax.broadcasted_iota(jnp.int32, (size, row.shape[1]), 0)
    return jnp.where(index == row, 1.0, 0.0).astype(BF16)


def column_of(row):
    return jnp.broadcast_to(row.astype(F32), (LANES, row.shape[1])).T


def onehot_out(column, size):
    lane = lax.broadcasted_iota(jnp.int32, column.shape, 1).astype(F32)
    return jnp.concatenate(
        [jnp.where(column == lane + float(i), 1.0, 0.0) for i in range(0, size, LANES)], axis=1
    )


def mix3(m, s):
    m_hi, m_lo = split(m)
    s_hi, s_lo = split(s)
    return dot(m_hi, s_hi) + (dot(m_hi, s_lo) + dot(m_lo, s_hi))


def order_kernel(points_t, order, probes, pack, rows):
    dim = points_t.shape[0]
    many, leaf = rows.shape[:2]
    held = dim + 16
    to_rows = form_map(dim, LANES)
    for b in range(many):
        picks = onehot_in(order[b], leaf)
        tree_t = dot(points_t[:, b * leaf : (b + 1) * leaf], picks).astype(BF16)
        pack[b, :leaf, :] = probes[b * leaf : (b + 1) * leaf, :]
        form = jnp.concatenate([tree_t, square_rows(tree_t)], axis=0)
        for i in range(leaf // LANES):
            pack[b, leaf + i * held : leaf + (i + 1) * held, :] = form[:, i * LANES : (i + 1) * LANES]
        form = jnp.concatenate([form, jnp.zeros((LANES - held, leaf), BF16)], axis=0)
        rows[b] = dot_t(form, to_rows).astype(BF16)


def order_call(points_t, order, probes, blocks):
    dim, npts = points_t.shape
    leaf = npts // blocks
    packed = leaf + leaf // LANES * (dim + 16)
    many = 4 if blocks % 4 == 0 else 1
    return pl.pallas_call(
        order_kernel,
        grid=(blocks // many,),
        in_specs=[
            pl.BlockSpec((dim, many * leaf), lambda b: (0, b)),
            pl.BlockSpec((many, 1, leaf), lambda b: (b, 0, 0)),
            pl.BlockSpec((many * leaf, LANES), lambda b: (b, 0)),
        ],
        out_specs=[
            pl.BlockSpec((many, packed, LANES), lambda b: (b, 0, 0)),
            pl.BlockSpec((many, leaf, LANES), lambda b: (b, 0, 0)),
        ],
        out_shape=[
            jax.ShapeDtypeStruct((blocks, packed, LANES), BF16),
            jax.ShapeDtypeStruct((blocks, leaf, LANES), BF16),
        ],
        compiler_params=pltpu.CompilerParams(vmem_limit_bytes=VMEM_BYTES),
        cost_estimate=pl.CostEstimate(
            flops=blocks * 2 * leaf * leaf * dim, bytes_accessed=10 * npts * LANES, transcendentals=0
        ),
        name="tree_order",
    )(points_t, order, probes)


def form_of(pack_block, leaf, dim):
    held = dim + 16
    columns = [
        pack_block[leaf + i * held : leaf + (i + 1) * held, :] for i in range(leaf // LANES)
    ]
    form = jnp.concatenate(columns, axis=1)
    return jnp.concatenate([form, jnp.zeros((LANES - held, leaf), BF16)], axis=0)


def condense(form, a_rows, chosen):
    size = form.shape[1]
    picks_out = onehot_out(column_of(chosen), size)
    new_rows = dot(picks_out.astype(BF16), a_rows).astype(BF16)
    new_form = dot(form, onehot_in(chosen, size)).astype(BF16)
    weights = jnp.exp(dot(new_rows, form))
    mixing = picks_out + weights / jnp.sum(weights, axis=1, keepdims=True)
    return new_form, new_rows, mixing


def local_tree_kernel(pack, rows, leaf_sets_in, merge_sets_in, out, leaf_sets, merge_sets, sems, *, dim):
    blocks, leaf = rows.shape[:2]
    leaf_copy = pltpu.make_async_copy(leaf_sets_in, leaf_sets, sems.at[0])
    merge_copy = pltpu.make_async_copy(merge_sets_in, merge_sets, sems.at[1])
    leaf_copy.start()
    merge_copy.start()
    leaf_copy.wait()
    first_block = (lax.axis_index("leaf") * lax.axis_size("sub") + lax.axis_index("sub")) * blocks

    nodes = []
    for b in range(blocks):
        form = form_of(pack.at[b], leaf, dim)
        new_form, new_rows, mixing = condense(form, rows[b], leaf_sets[b : b + 1, :])
        m_hi, m_lo = split(mixing)
        probes = pack[b, :leaf, :]
        nodes.append((new_form, new_rows, dot(m_hi, probes) + dot(m_lo, probes)))
    span = 1
    merge_copy.wait()
    while len(nodes) > 1:
        merged = []
        for k in range(len(nodes) // 2):
            left, right = nodes[2 * k], nodes[2 * k + 1]
            chosen = merge_sets[pl.ds(first_block + (2 * k + 1) * span - 1, 1), :]
            new_form, new_rows, mixing = condense(
                jnp.concatenate([left[0], right[0]], axis=1),
                jnp.concatenate([left[1], right[1]], axis=0),
                chosen,
            )
            samples = mix3(mixing, jnp.concatenate([left[2], right[2]], axis=0))
            merged.append((new_form, new_rows, samples))
        nodes = merged
        span *= 2
    held = dim + 16
    out[:held, :] = nodes[0][0][:held, :].astype(F32)
    out[held:, :] = nodes[0][2]


def local_tree_call(pack, rows, leaf_sets, merge_sets, dim):
    blocks, leaf = rows.shape[:2]
    skel = leaf_sets.shape[1]
    return pl.pallas_call(
        functools.partial(local_tree_kernel, dim=dim),
        in_specs=[pl.BlockSpec(memory_space=pltpu.VMEM)] * 2
        + [pl.BlockSpec(memory_space=pltpu.HBM)] * 2,
        out_shape=jax.ShapeDtypeStruct((dim + 16 + skel, LANES), F32),
        scratch_shapes=[
            pltpu.VMEM(leaf_sets.shape, jnp.int32),
            pltpu.VMEM(merge_sets.shape, jnp.int32),
            pltpu.SemaphoreType.DMA((2,)),
        ],
        compiler_params=pltpu.CompilerParams(vmem_limit_bytes=VMEM_BYTES),
        cost_estimate=pl.CostEstimate(
            flops=blocks * 8 * skel * leaf * LANES,
            bytes_accessed=6 * blocks * leaf * LANES,
            transcendentals=blocks * skel * leaf,
        ),
        name="local_tree",
    )(pack, rows, leaf_sets, merge_sets)


def merge_kernel(*refs, dim, blocks, shift, piece):
    merge_sets_in, out, group, merge_sets, sem = refs[-5:]
    parts = refs[:-5]
    count, size = group.shape[:2]
    copy = pltpu.make_async_copy(merge_sets_in, merge_sets, sem)
    copy.start()
    held = dim + 16
    skel = size - held
    rank = lax.axis_index("leaf") * lax.axis_size("sub") + lax.axis_index("sub")
    unit = lax.shift_right_logical(rank, shift)
    place = unit & (count - 1)
    first = unit - place
    span = blocks << shift
    for d, part in enumerate(parts):
        group[place ^ d] = part[...]
    to_rows = form_map(dim, LANES)
    forms = [group[i, :held, :].astype(BF16) for i in range(count)]
    samples = [group[i, held:, :] for i in range(count)]
    copy.wait()
    while len(forms) > 1:
        first = first // 2
        new_forms, new_samples = [], []
        for k in range(len(forms) // 2):
            chosen = merge_sets[pl.ds((2 * (first + k) + 1) * span - 1, 1), :]
            form = jnp.concatenate(forms[2 * k : 2 * k + 2], axis=1)
            form = jnp.concatenate([form, jnp.zeros((LANES - held, 2 * skel), BF16)], axis=0)
            new_form = dot(form, onehot_in(chosen, 2 * skel)).astype(BF16)
            new_rows = dot_t(new_form, to_rows).astype(BF16)
            weights = jnp.exp(dot(new_rows, form))
            picks = onehot_out(column_of(chosen), 2 * skel)
            mixing = picks + weights / jnp.sum(weights, axis=1, keepdims=True)
            new_forms.append(new_form[:held])
            new_samples.append(mix3(mixing, jnp.concatenate(samples[2 * k : 2 * k + 2], axis=0)))
        forms, samples = new_forms, new_samples
        span *= 2
    if piece is None:
        out[:held, :] = forms[0].astype(F32)
        out[held:, :] = samples[0]
    elif piece == 0:
        out[...] = samples[0]
    else:
        column = lax.broadcasted_iota(jnp.int32, (piece, skel), 1)
        row = lax.broadcasted_iota(jnp.int32, (piece, skel), 0) + rank * piece
        take = jnp.where(column == row, 1.0, 0.0).astype(BF16)
        hi, lo = split(samples[0])
        low = (samples[0] - hi.astype(F32) - lo.astype(F32)).astype(BF16)
        out[...] = dot(take, hi) + dot(take, lo) + dot(take, low)


def merge_call(parts, merge_sets, dim, blocks, shift, piece=None):
    count = len(parts)
    size = parts[0].shape[0]
    skel = size - dim - 16
    rows = size if piece is None else (piece or skel)
    return pl.pallas_call(
        functools.partial(merge_kernel, dim=dim, blocks=blocks, shift=shift, piece=piece),
        in_specs=[pl.BlockSpec(memory_space=pltpu.VMEM)] * count
        + [pl.BlockSpec(memory_space=pltpu.HBM)],
        out_shape=jax.ShapeDtypeStruct((rows, LANES), F32),
        scratch_shapes=[
            pltpu.VMEM((count, size, LANES), F32),
            pltpu.VMEM(merge_sets.shape, jnp.int32),
            pltpu.SemaphoreType.DMA(()),
        ],
        compiler_params=pltpu.CompilerParams(vmem_limit_bytes=16 * 1024 * 1024),
        cost_estimate=pl.CostEstimate(
            flops=count * 16 * LANES**3,
            bytes_accessed=4 * count * size * LANES,
            transcendentals=2 * count * LANES**2,
        ),
        name="tree_merge",
    )(*parts, merge_sets)


def near_kernel(*refs, slots, dim, has_acc, last):
    lists, counts, rows = refs[:3]
    refs = refs[3:]
    if has_acc:
        acc_in, refs = refs[0], refs[1:]
    buffers = []
    for _, which in slots:
        number = max(which) + 1
        buffers.append(refs[:number])
        refs = refs[number:]
    out, pair_list = refs
    blocks, leaf = rows.shape[:2]
    near = lists.shape[1]
    window = blocks * lax.axis_size("sub")
    start = lax.axis_index("leaf") * window - blocks
    sub = lax.axis_index("sub")

    def place(table):
        value = jnp.int32(table[0])
        for i in range(1, len(table)):
            value = jnp.where(sub == i, jnp.int32(table[i]), value)
        return value

    starts = [start + place(bases) for bases, _ in slots]
    stride = blocks * near + 8

    def list_block(g, found):
        used = counts[g]

        def list_slot(s, found):
            source = lists[g, s]
            after = []
            for slot, first in enumerate(starts):
                pair_list[slot * stride + found[slot]] = g * blocks + source - first
                inside = (source >= first) & (source < first + blocks) & (s < used)
                after.append(found[slot] + jnp.where(inside, 1, 0))
            return tuple(after)

        return lax.fori_loop(0, near, list_slot, found, unroll=True)

    found = lax.fori_loop(0, blocks, list_block, (jnp.int32(0),) * len(slots))
    if has_acc:
        out[...] = acc_in[...]
    else:
        out[...] = jnp.zeros(out.shape, F32)

    half = leaf // 2

    def add_all(buffer, first, pairs):
        def add_pair(i):
            code = pair_list[first + i]
            g = code // blocks
            local = code - g * blocks
            form = form_of(buffer.at[local], leaf, dim)
            probes = buffer[local, :leaf, :]
            total = None
            for c in range(0, leaf, half):
                weights = jnp.exp(dot(rows[g], form[:, c : c + half])).astype(BF16)
                term = dot(weights, probes[c : c + half])
                total = term if total is None else total + term
            return g, total

        def add_pairs(i, carry):
            for g, total in [add_pair(2 * i), add_pair(2 * i + 1)]:
                out[g] += total
            return carry

        lax.fori_loop(0, pairs // 2, add_pairs, 0)

        @pl.when(pairs % 2 == 1)
        def _():
            g, total = add_pair(pairs - 1)
            out[g] += total

    for slot, (_, which) in enumerate(slots):
        if len(buffers[slot]) == 1:
            add_all(buffers[slot][0], slot * stride, found[slot])
        else:
            held = place(which)
            for number, buffer in enumerate(buffers[slot]):
                add_all(buffer, slot * stride, jnp.where(held == number, found[slot], 0))
    if last:
        out[...] = out[...] * (leaf ** -0.5)


def near_call(lists, counts, rows, acc, sets, dim, last, name):
    blocks, leaf = rows.shape[:2]
    buffers = [b for _, _, bufs in sets for b in bufs]
    slots = tuple((bases, which) for bases, which, _ in sets)
    packed = buffers[0].shape[1]
    smem = pl.BlockSpec(memory_space=pltpu.SMEM)
    vmem = pl.BlockSpec(memory_space=pltpu.VMEM)
    args = [lists, counts, rows] + ([acc] if acc is not None else []) + buffers
    total = len(slots) * blocks
    near = lists.shape[1]
    pairs = total * blocks // 8
    return pl.pallas_call(
        functools.partial(
            near_kernel, slots=slots, dim=dim, has_acc=acc is not None, last=last
        ),
        in_specs=[smem, smem] + [vmem] * (len(args) - 2),
        out_specs=vmem,
        out_shape=jax.ShapeDtypeStruct((blocks, leaf, LANES), F32),
        scratch_shapes=[pltpu.SMEM((len(slots) * (blocks * near + 8),), jnp.int32)],
        compiler_params=pltpu.CompilerParams(vmem_limit_bytes=NEAR_BYTES),
        cost_estimate=pl.CostEstimate(
            flops=1000, bytes_accessed=1000, transcendentals=0
        ),
        name=name,
    )(*args)


def on_device(points, probes, order, near_lists, near_counts, leaf_sets, merge_sets):
    leaf_count = lax.axis_size("leaf")
    sub_count = lax.axis_size("sub")
    blocks, skel = leaf_sets.shape
    npts, dim = points.shape
    leaf = npts // blocks
    axes = ("leaf", "sub")

    def send(x, routes):
        pairs = []
        for place in range(leaf_count):
            for from_sub, step, to_sub in routes:
                if 0 <= place + step < leaf_count:
                    pairs.append((place * sub_count + from_sub, (place + step) * sub_count + to_sub))
        return lax.ppermute(x, axes, pairs)

    swap = [(0, 0, 1), (1, 0, 0), (2, 0, 3), (3, 0, 2)]
    pack, rows = order_call(points.T, order.reshape(blocks, 1, leaf), probes, blocks)
    outer_across = send(pack, [(3, 0, 1), (0, 0, 2)])
    outer_next = send(pack, [(3, 1, 3), (0, -1, 0)])
    beside = send(pack, swap)

    node = local_tree_call(pack, rows, leaf_sets, merge_sets, dim)

    count = leaf_count * sub_count
    bits = count.bit_length() - 1
    sub_bits = sub_count.bit_length() - 1

    def exchange(x, shift, stage_bits):
        parts = [x]
        for d in range(1, 1 << stage_bits):
            parts.append(lax.ppermute(x, axes, [(i, i ^ (d << shift)) for i in range(count)]))
        return parts

    b = blocks
    own_base, beside_base = (b, 2 * b, 3 * b, 4 * b), (2 * b, b, 4 * b, 3 * b)
    early_base, early_beside_base = (5 * b, 4 * b, b, 0), (4 * b, 5 * b, 0, b)
    late_base, late_beside_base = (3 * b, 0, 5 * b, 2 * b), (0, 3 * b, 2 * b, 5 * b)
    single, edge_first, edge_second = (0, 0, 0, 0), (0, 1, 1, 0), (1, 0, 0, 1)
    from_edge, from_inner = [(0, 0, 1), (3, 0, 2)], [(1, 0, 0), (2, 0, 3)]

    def tie(*values):
        return lax.optimization_barrier(values)

    node = merge_call(exchange(node, 0, 1), merge_sets, dim, blocks, 0)
    own_pack, node = tie(pack, node)
    parts = exchange(node, 1, sub_bits - 1)
    acc = near_call(
        near_lists, near_counts, rows, None,
        [(own_base, single, [own_pack])],
        dim, False, "near_first",
    )

    *parts, outer_across, outer_next, own_pack, acc = tie(
        *parts, outer_across, outer_next, own_pack, acc
    )
    forwarded = send(outer_across, [(1, 1, 1), (2, -1, 2)])
    inner_across = send(own_pack, [(2, 0, 0), (1, 0, 3)])
    acc = near_call(
        near_lists, near_counts, rows, acc,
        [
            (beside_base, single, [beside]),
            (early_base, edge_first, [outer_next, outer_across]),
        ],
        dim, False, "near_second",
    )

    *parts, acc = tie(*parts, acc)
    node = merge_call(parts, merge_sets, dim, blocks, 1)
    outer_next, outer_across, node = tie(outer_next, outer_across, node)
    next_beside = send(outer_next, from_edge)
    across_beside = send(outer_across, from_inner)
    shift, stage_bits = sub_bits, min(2, bits - sub_bits)
    parts = exchange(node, shift, stage_bits)
    next_beside, across_beside, node = tie(next_beside, across_beside, node)
    acc = near_call(
        near_lists, near_counts, rows, acc,
        [(early_beside_base, edge_second, [next_beside, across_beside])],
        dim, False, "near_third",
    )

    *parts, inner_across, forwarded, acc = tie(*parts, inner_across, forwarded, acc)
    inner_beside = send(inner_across, from_edge)
    forwarded_beside = send(forwarded, from_inner)
    node = merge_call(parts, merge_sets, dim, blocks, shift)
    shift += stage_bits
    inner_across, forwarded, node = tie(inner_across, forwarded, node)
    parts = exchange(node, shift, bits - shift)
    near = near_call(
        near_lists, near_counts, rows, acc,
        [
            (late_base, edge_first, [inner_across, forwarded]),
            (late_beside_base, edge_second, [inner_beside, forwarded_beside]),
        ],
        dim, True, "near_last",
    )

    *parts, near = tie(*parts, near)
    piece = skel // count
    node = merge_call(parts, merge_sets, dim, blocks, shift, piece)
    if piece:
        root = node.reshape(-1)
    else:
        size = skel * LANES // count
        rank = lax.axis_index("leaf") * sub_count + lax.axis_index("sub")
        root = lax.dynamic_slice_in_dim(node.reshape(-1), rank * size, size, 0)
    return near.reshape(npts, LANES), root


def solution(mesh):
    in_specs = (
        P(("leaf", "sub"), None),
        P(("leaf", "sub"), None),
        P(("leaf", "sub")),
        P(("leaf", "sub"), None),
        P(("leaf", "sub")),
        P(("leaf", "sub"), None),
        P(),
    )
    out_specs = (P(("leaf", "sub"), None), P(("leaf", "sub")))
    return jax.shard_map(
        on_device, mesh=mesh, in_specs=in_specs, out_specs=out_specs, check_vma=False
    )
```

profile of v0, /device:TPU:4, one launch (start us, length us, event | category | flops | bytes accessed | tf_op | source)
XLA Modules:
  0.0 94.1 jit_solution(12899240318171559350)
XLA Ops:
  0.6 1.2 %copy-done.2 = bf16[4096,128]{1,0:T(8,128)(2,1)S(1)} copy-done((bf16[4096,128]{1,0:T(8,128)(2,1)S(1)}, bf16[4096,128]{1,0:T(8,128)(2,1)}, u32[]{:S(2)}) %copy-start.2) | copy-done | bytes 1048600
  1.9 1.0 %copy-done.3 = bf16[4096,64]{0,1:T(8,128)(2,1)S(1)} copy-done((bf16[4096,64]{0,1:T(8,128)(2,1)S(1)}, bf16[4096,64]{0,1:T(8,128)(2,1)}, u32[]{:S(2)}) %copy-start.3) | copy-done | bytes 524312
  3.6 2.6 %tree_order.1 = (bf16[8,832,128]{2,1,0:T(8,128)(2,1)S(1)}, bf16[8,512,128]{2,1,0:T(8,128)(2,1)S(1)}) custom-call(bf16[64,4096]{1,0:T(8,128)(2,1)S(1)} %bitcast.4, s32[8,1,512]{2,1,0:T(1,128)S(1)} %bitcast.5, bf16[4096,128]{1,0:T(8,128)(2,1)S(1)} %copy-done.2), custom_call_target="tpu_custom_call" | custom-call | flops 268435456 | bytes 5242880 | tf_op jit(solution)/shard_map/tree_order/pallas_call | solution.py:94
  6.3 1.3 %collective-permute-start.2 = (bf16[8,832,128]{2,1,0:T(8,128)(2,1)S(1)}, bf16[8,832,128]{2,1,0:T(8,128)(2,1)S(1)}, u32[]{:S(2)}, u32[]{:S(2)}) collective-permute-start(bf16[8,832,128]{2,1,0:T(8,128)(2,1)S(1)} %get-tuple-element.45.pack.refs_3_), channel_id=1, source_target_pairs={{3,1},{0,2},{7,5},{4,6},{11,9},{8,10},{15,13},{12,14},{19,17},{16,... | collective-permute-start | bytes 5111816 | tf_op jit(solution)/shard_map/ppermute | solution.py:397
  8.3 3.3 %collective-permute-start.4 = (bf16[8,832,128]{2,1,0:T(8,128)(2,1)S(1)}, bf16[8,832,128]{2,1,0:T(8,128)(2,1)S(1)}, u32[]{:S(2)}, u32[]{:S(2)}) collective-permute-start(bf16[8,832,128]{2,1,0:T(8,128)(2,1)S(1)} %get-tuple-element.45.pack.refs_3_), channel_id=1, source_target_pairs={{0,1},{1,0},{2,3},{3,2},{4,5},{5,4},{6,7},{7,6},{8,9},{9,8},{10,11... | collective-permute-start | bytes 5111816 | tf_op jit(solution)/shard_map/ppermute | solution.py:397
  13.2 6.9 %local_tree.1.refs_0_ = f32[208,128]{1,0:T(8,128)S(1)} custom-call(bf16[8,832,128]{2,1,0:T(8,128)(2,1)S(1)} %get-tuple-element.45.pack.refs_3_, bf16[8,512,128]{2,1,0:T(8,128)(2,1)S(1)} %get-tuple-element.34.rows.refs_2_, s32[8,128]{1,0:T(8,128)S(1)} %copy-done.7, s32[255,128]{1,0:T(8,128)S(1)} %copy-done), custom_call_target="tpu_custom_call" | custom-call | flops 536870912 | bytes 3145728 | tf_op jit(solution)/shard_map/local_tree/pallas_call | solution.py:177
  20.2 1.3 %collective-permute-done.refs_1_ = f32[208,128]{1,0:T(8,128)S(1)} collective-permute-done((f32[208,128]{1,0:T(8,128)S(1)}, f32[208,128]{1,0:T(8,128)S(1)}, u32[]{:S(2)}, u32[]{:S(2)}) %collective-permute-start) | collective-permute-done | bytes 106528 | tf_op jit(solution)/shard_map/ppermute | solution.py:414
  22.7 6.0 %near_first.1.refs_3_ = f32[8,512,128]{2,1,0:T(8,128)S(1)} custom-call(s32[8,12]{1,0:T(8,128)S(1)} %copy-done.4, s32[8]{0:T(128)S(1)} %copy-done.6, bf16[8,512,128]{2,1,0:T(8,128)(2,1)S(1)} %get-tuple-element.34.rows.refs_2_, bf16[8,832,128]{2,1,0:T(8,128)(2,1)S(1)} %get-tuple-element.45.pack.refs_3_), custom_call_target="tpu_custom_call" | custom-call | flops 1000 | bytes 1000 | tf_op jit(solution)/shard_map/near_first/pallas_call | solution.py:367
  28.8 3.5 %collective-permute-done.1.refs_1_ = f32[208,128]{1,0:T(8,128)S(1)} collective-permute-done((f32[208,128]{1,0:T(8,128)S(1)}, f32[208,128]{1,0:T(8,128)S(1)}, u32[]{:S(2)}, u32[]{:S(2)}) %collective-permute-start.1) | collective-permute-done | bytes 106528 | tf_op jit(solution)/shard_map/ppermute | solution.py:414
  32.3 5.1 %near_second.1.refs_3_ = f32[8,512,128]{2,1,0:T(8,128)S(1)} custom-call(s32[8,12]{1,0:T(8,128)S(1)} %copy-done.4, s32[8]{0:T(128)S(1)} %copy-done.6, bf16[8,512,128]{2,1,0:T(8,128)(2,1)S(1)} %get-tuple-element.34.rows.refs_2_, f32[8,512,128]{2,1,0:T(8,128)S(1)} %near_first.1.refs_3_, bf16[8,832,128]{2,1,0:T(8,128)(2,1)S(1)} %collective-permute-done.4.refs_4_, ...), custom_call_target="tpu_custom_call" | custom-call | flops 1000 | bytes 1000 | tf_op jit(solution)/shard_map/near_second/pallas_call | solution.py:367
  38.4 1.3 %collective-permute-start.10 = (bf16[8,832,128]{2,1,0:T(8,128)(2,1)S(1)}, bf16[8,832,128]{2,1,0:T(8,128)(2,1)S(1)}, u32[]{:S(2)}, u32[]{:S(2)}) collective-permute-start(bf16[8,832,128]{2,1,0:T(8,128)(2,1)S(1)} %collective-permute-done.3.refs_5_), channel_id=1, source_target_pairs={{0,1},{3,2},{4,5},{7,6},{8,9},{11,10},{12,13},{15,14},{16,17},{19,... | collective-permute-start | bytes 5111816 | tf_op jit(solution)/shard_map/ppermute | solution.py:397
  39.7 3.2 %collective-permute-start.11 = (bf16[8,832,128]{2,1,0:T(8,128)(2,1)S(1)}, bf16[8,832,128]{2,1,0:T(8,128)(2,1)S(1)}, u32[]{:S(2)}, u32[]{:S(2)}) collective-permute-start(bf16[8,832,128]{2,1,0:T(8,128)(2,1)S(1)} %collective-permute-done.2.refs_6_), channel_id=1, source_target_pairs={{1,0},{2,3},{5,4},{6,7},{9,8},{10,11},{13,12},{14,15},{17,16},{18,... | collective-permute-start | bytes 5111816 | tf_op jit(solution)/shard_map/ppermute | solution.py:397
  43.0 2.4 %collective-permute-start.8 = (bf16[8,832,128]{2,1,0:T(8,128)(2,1)S(1)}, bf16[8,832,128]{2,1,0:T(8,128)(2,1)S(1)}, u32[]{:S(2)}, u32[]{:S(2)}) collective-permute-start(bf16[8,832,128]{2,1,0:T(8,128)(2,1)S(1)} %get-tuple-element.45.pack.refs_3_), channel_id=1, source_target_pairs={{2,0},{1,3},{6,4},{5,7},{10,8},{9,11},{14,12},{13,15},{18,16},{17,... | collective-permute-start | bytes 5111816 | tf_op jit(solution)/shard_map/ppermute | solution.py:397
  45.4 1.3 %collective-permute-start.9 = (bf16[8,832,128]{2,1,0:T(8,128)(2,1)S(1)}, bf16[8,832,128]{2,1,0:T(8,128)(2,1)S(1)}, u32[]{:S(2)}, u32[]{:S(2)}) collective-permute-start(bf16[8,832,128]{2,1,0:T(8,128)(2,1)S(1)} %collective-permute-done.2.refs_6_), channel_id=1, source_target_pairs={{1,5},{5,9},{6,2},{9,13},{10,6},{13,17},{14,10},{17,21},{18,14},{2... | collective-permute-start | bytes 5111816 | tf_op jit(solution)/shard_map/ppermute | solution.py:397
  46.7 4.9 %collective-permute-start.5 = (f32[208,128]{1,0:T(8,128)S(1)}, f32[208,128]{1,0:T(8,128)S(1)}, u32[]{:S(2)}, u32[]{:S(2)}) collective-permute-start(f32[208,128]{1,0:T(8,128)S(1)} %tree_merge.5.refs_0_), channel_id=1, source_target_pairs={{0,4},{1,5},{2,6},{3,7},{4,0},{5,1},{6,2},{7,3},{8,12},{9,13},{10,... | collective-permute-start | bytes 319496 | tf_op jit(solution)/shard_map/ppermute | solution.py:414
  51.5 2.2 %collective-permute-start.6 = (f32[208,128]{1,0:T(8,128)S(1)}, f32[208,128]{1,0:T(8,128)S(1)}, u32[]{:S(2)}, u32[]{:S(2)}) collective-permute-start(f32[208,128]{1,0:T(8,128)S(1)} %tree_merge.5.refs_0_), channel_id=1, source_target_pairs={{0,8},{1,9},{2,10},{3,11},{4,12},{5,13},{6,14},{7,15},{8,0},{9,1},... | collective-permute-start | bytes 319496 | tf_op jit(solution)/shard_map/ppermute | solution.py:414
  54.5 1.2 %near_third.1.refs_3_ = f32[8,512,128]{2,1,0:T(8,128)S(1)} custom-call(s32[8,12]{1,0:T(8,128)S(1)} %copy-done.4, s32[8]{0:T(128)S(1)} %copy-done.6, bf16[8,512,128]{2,1,0:T(8,128)(2,1)S(1)} %get-tuple-element.34.rows.refs_2_, f32[8,512,128]{2,1,0:T(8,128)S(1)} %near_second.1.refs_3_, bf16[8,832,128]{2,1,0:T(8,128)(2,1)S(1)} %collective-permute-done.10.refs_4_, ...), custom_call_target="tpu_custom_call" | custom-call | flops 1000 | bytes 1000 | tf_op jit(solution)/shard_map/near_third/pallas_call | solution.py:367
  55.7 17.8 %collective-permute-done.5.refs_1_ = f32[208,128]{1,0:T(8,128)S(1)} collective-permute-done((f32[208,128]{1,0:T(8,128)S(1)}, f32[208,128]{1,0:T(8,128)S(1)}, u32[]{:S(2)}, u32[]{:S(2)}) %collective-permute-start.5) | collective-permute-done | bytes 106528 | tf_op jit(solution)/shard_map/ppermute | solution.py:414
  73.9 1.3 %collective-permute-start.13 = (bf16[8,832,128]{2,1,0:T(8,128)(2,1)S(1)}, bf16[8,832,128]{2,1,0:T(8,128)(2,1)S(1)}, u32[]{:S(2)}, u32[]{:S(2)}) collective-permute-start(bf16[8,832,128]{2,1,0:T(8,128)(2,1)S(1)} %collective-permute-done.8.refs_4_), channel_id=1, source_target_pairs={{0,1},{3,2},{4,5},{7,6},{8,9},{11,10},{12,13},{15,14},{16,17},{19,... | collective-permute-start | bytes 5111816 | tf_op jit(solution)/shard_map/ppermute | solution.py:397
  75.2 3.2 %collective-permute-start.14 = (bf16[8,832,128]{2,1,0:T(8,128)(2,1)S(1)}, bf16[8,832,128]{2,1,0:T(8,128)(2,1)S(1)}, u32[]{:S(2)}, u32[]{:S(2)}) collective-permute-start(bf16[8,832,128]{2,1,0:T(8,128)(2,1)S(1)} %collective-permute-done.9.refs_5_), channel_id=1, source_target_pairs={{1,0},{2,3},{5,4},{6,7},{9,8},{10,11},{13,12},{14,15},{17,16},{18,... | collective-permute-start | bytes 5111816 | tf_op jit(solution)/shard_map/ppermute | solution.py:397
  78.4 2.2 %tree_merge.6.refs_0_ = f32[208,128]{1,0:T(8,128)S(1)} custom-call(f32[208,128]{1,0:T(8,128)S(1)} %tree_merge.5.refs_0_, f32[208,128]{1,0:T(8,128)S(1)} %collective-permute-done.5.refs_1_, f32[208,128]{1,0:T(8,128)S(1)} %collective-permute-done.6.refs_2_, f32[208,128]{1,0:T(8,128)S(1)} %collective-permute-done.7.refs_3_, s32[255,128]{1,0:T(8,128)S(1)} %copy-done.1), custom_call_target="tpu_custom_call" | custom-call | flops 134217728 | bytes 425984 | tf_op jit(solution)/shard_map/tree_merge/pallas_call | solution.py:251
  80.7 2.2 %collective-permute-start.12 = (f32[208,128]{1,0:T(8,128)S(1)}, f32[208,128]{1,0:T(8,128)S(1)}, u32[]{:S(2)}, u32[]{:S(2)}) collective-permute-start(f32[208,128]{1,0:T(8,128)S(1)} %tree_merge.6.refs_0_), channel_id=1, source_target_pairs={{0,16},{1,17},{2,18},{3,19},{4,20},{5,21},{6,22},{7,23},{8,24},{9,... | collective-permute-start | bytes 319496 | tf_op jit(solution)/shard_map/ppermute | solution.py:414
  82.9 9.3 %near_last.1 = f32[8,512,128]{2,1,0:T(8,128)} custom-call(s32[8,12]{1,0:T(8,128)S(1)} %copy-done.4, s32[8]{0:T(128)S(1)} %copy-done.6, bf16[8,512,128]{2,1,0:T(8,128)(2,1)S(1)} %get-tuple-element.34.rows.refs_2_, f32[8,512,128]{2,1,0:T(8,128)S(1)} %near_third.1.refs_3_, bf16[8,832,128]{2,1,0:T(8,128)(2,1)S(1)} %collective-permute-done.8.refs_4_, ...), custom_call_target="tpu_custom_call" | custom-call | flops 1000 | bytes 1000 | tf_op jit(solution)/shard_map/near_last/pallas_call | solution.py:367
  92.2 1.7 %tree_merge.7 = f32[4,128]{1,0:T(4,128)} custom-call(f32[208,128]{1,0:T(8,128)S(1)} %tree_merge.6.refs_0_, f32[208,128]{1,0:T(8,128)S(1)} %collective-permute-done.12.refs_1_, s32[255,128]{1,0:T(8,128)S(1)} %copy-done.1), custom_call_target="tpu_custom_call" | custom-call | flops 67108864 | bytes 212992 | tf_op jit(solution)/shard_map/tree_merge/pallas_call | solution.py:251
  (32 shorter events, 6.6 us)
Async XLA Ops:
  0.6 1.2 %copy-start.2 = (bf16[4096,128]{1,0:T(8,128)(2,1)S(1)}, bf16[4096,128]{1,0:T(8,128)(2,1)}, u32[]{:S(2)}) copy-start(bf16[4096,128]{1,0:T(8,128)(2,1)} %probes.1) | copy-start | bytes 3145732
  1.9 1.0 %copy-start.3 = (bf16[4096,64]{0,1:T(8,128)(2,1)S(1)}, bf16[4096,64]{0,1:T(8,128)(2,1)}, u32[]{:S(2)}) copy-start(bf16[4096,64]{0,1:T(8,128)(2,1)} %param.7) | copy-start | bytes 1572868
  2.9 0.7 copy-start.5
  6.3 26.0 %collective-permute-start.2 = (bf16[8,832,128]{2,1,0:T(8,128)(2,1)S(1)}, bf16[8,832,128]{2,1,0:T(8,128)(2,1)S(1)}, u32[]{:S(2)}, u32[]{:S(2)}) collective-permute-start(bf16[8,832,128]{2,1,0:T(8,128)(2,1)S(1)} %get-tuple-element.45.pack.refs_3_), channel_id=1, source_target_pairs={{3,1},{0,2},{7,5},{4,6},{11,9},{8,10},{15,13},{12,14},{19,17},{16,... | collective-permute-start | bytes 5111816 | tf_op jit(solution)/shard_map/ppermute | solution.py:397
  7.6 24.7 %collective-permute-start.3 = (bf16[8,832,128]{2,1,0:T(8,128)(2,1)S(1)}, bf16[8,832,128]{2,1,0:T(8,128)(2,1)S(1)}, u32[]{:S(2)}, u32[]{:S(2)}) collective-permute-start(bf16[8,832,128]{2,1,0:T(8,128)(2,1)S(1)} %get-tuple-element.45.pack.refs_3_), channel_id=1, source_target_pairs={{3,7},{7,11},{4,0},{11,15},{8,4},{15,19},{12,8},{19,23},{16,12},{2... | collective-permute-start | bytes 5111816 | tf_op jit(solution)/shard_map/ppermute | solution.py:397
  8.3 23.9 %collective-permute-start.4 = (bf16[8,832,128]{2,1,0:T(8,128)(2,1)S(1)}, bf16[8,832,128]{2,1,0:T(8,128)(2,1)S(1)}, u32[]{:S(2)}, u32[]{:S(2)}) collective-permute-start(bf16[8,832,128]{2,1,0:T(8,128)(2,1)S(1)} %get-tuple-element.45.pack.refs_3_), channel_id=1, source_target_pairs={{0,1},{1,0},{2,3},{3,2},{4,5},{5,4},{6,7},{7,6},{8,9},{9,8},{10,11... | collective-permute-start | bytes 5111816 | tf_op jit(solution)/shard_map/ppermute | solution.py:397
  11.6 0.9 copy-start
  12.6 0.7 copy-start.7
  13.2 9.5 %copy-start.4 = (s32[8,12]{1,0:T(8,128)S(1)}, s32[8,12]{1,0:T(8,128)}, u32[]{:S(2)}) copy-start(s32[8,12]{1,0:T(8,128)} %refs_0_.7) | copy-start | bytes 1156
  13.2 9.5 %copy-start.6 = (s32[8]{0:T(128)S(1)}, s32[8]{0:T(128)}, u32[]{:S(2)}) copy-start(s32[8]{0:T(128)} %refs_1_.7) | copy-start | bytes 100
  20.1 1.4 %collective-permute-start = (f32[208,128]{1,0:T(8,128)S(1)}, f32[208,128]{1,0:T(8,128)S(1)}, u32[]{:S(2)}, u32[]{:S(2)}) collective-permute-start(f32[208,128]{1,0:T(8,128)S(1)} %local_tree.1.refs_0_), channel_id=1, source_target_pairs={{0,1},{1,0},{2,3},{3,2},{4,5},{5,4},{6,7},{7,6},{8,9},{9,8},{10,11... | collective-permute-start | bytes 319496 | tf_op jit(solution)/shard_map/ppermute | solution.py:414
  22.5 9.8 %collective-permute-start.1 = (f32[208,128]{1,0:T(8,128)S(1)}, f32[208,128]{1,0:T(8,128)S(1)}, u32[]{:S(2)}, u32[]{:S(2)}) collective-permute-start(f32[208,128]{1,0:T(8,128)S(1)} %tree_merge.4.refs_0_), channel_id=1, source_target_pairs={{0,2},{1,3},{2,0},{3,1},{4,6},{5,7},{6,4},{7,5},{8,10},{9,11},{10,... | collective-permute-start | bytes 319496 | tf_op jit(solution)/shard_map/ppermute | solution.py:414
  28.8 8.6 %copy-start.1 = (s32[255,128]{1,0:T(8,128)S(1)}, s32[255,128]{1,0:T(8,128)}, u32[]{:S(2)}) copy-start(s32[255,128]{1,0:T(8,128)} %refs_2_.5) | copy-start | bytes 391684
  38.4 13.1 %collective-permute-start.10 = (bf16[8,832,128]{2,1,0:T(8,128)(2,1)S(1)}, bf16[8,832,128]{2,1,0:T(8,128)(2,1)S(1)}, u32[]{:S(2)}, u32[]{:S(2)}) collective-permute-start(bf16[8,832,128]{2,1,0:T(8,128)(2,1)S(1)} %collective-permute-done.3.refs_5_), channel_id=1, source_target_pairs={{0,1},{3,2},{4,5},{7,6},{8,9},{11,10},{12,13},{15,14},{16,17},{19,... | collective-permute-start | bytes 5111816 | tf_op jit(solution)/shard_map/ppermute | solution.py:397
  39.7 14.0 %collective-permute-start.11 = (bf16[8,832,128]{2,1,0:T(8,128)(2,1)S(1)}, bf16[8,832,128]{2,1,0:T(8,128)(2,1)S(1)}, u32[]{:S(2)}, u32[]{:S(2)}) collective-permute-start(bf16[8,832,128]{2,1,0:T(8,128)(2,1)S(1)} %collective-permute-done.2.refs_6_), channel_id=1, source_target_pairs={{1,0},{2,3},{5,4},{6,7},{9,8},{10,11},{13,12},{14,15},{17,16},{18,... | collective-permute-start | bytes 5111816 | tf_op jit(solution)/shard_map/ppermute | solution.py:397
  43.0 30.9 %collective-permute-start.8 = (bf16[8,832,128]{2,1,0:T(8,128)(2,1)S(1)}, bf16[8,832,128]{2,1,0:T(8,128)(2,1)S(1)}, u32[]{:S(2)}, u32[]{:S(2)}) collective-permute-start(bf16[8,832,128]{2,1,0:T(8,128)(2,1)S(1)} %get-tuple-element.45.pack.refs_3_), channel_id=1, source_target_pairs={{2,0},{1,3},{6,4},{5,7},{10,8},{9,11},{14,12},{13,15},{18,16},{17,... | collective-permute-start | bytes 5111816 | tf_op jit(solution)/shard_map/ppermute | solution.py:397
  45.4 28.5 %collective-permute-start.9 = (bf16[8,832,128]{2,1,0:T(8,128)(2,1)S(1)}, bf16[8,832,128]{2,1,0:T(8,128)(2,1)S(1)}, u32[]{:S(2)}, u32[]{:S(2)}) collective-permute-start(bf16[8,832,128]{2,1,0:T(8,128)(2,1)S(1)} %collective-permute-done.2.refs_6_), channel_id=1, source_target_pairs={{1,5},{5,9},{6,2},{9,13},{10,6},{13,17},{14,10},{17,21},{18,14},{2... | collective-permute-start | bytes 5111816 | tf_op jit(solution)/shard_map/ppermute | solution.py:397
  46.7 26.9 %collective-permute-start.5 = (f32[208,128]{1,0:T(8,128)S(1)}, f32[208,128]{1,0:T(8,128)S(1)}, u32[]{:S(2)}, u32[]{:S(2)}) collective-permute-start(f32[208,128]{1,0:T(8,128)S(1)} %tree_merge.5.refs_0_), channel_id=1, source_target_pairs={{0,4},{1,5},{2,6},{3,7},{4,0},{5,1},{6,2},{7,3},{8,12},{9,13},{10,... | collective-permute-start | bytes 319496 | tf_op jit(solution)/shard_map/ppermute | solution.py:414
  51.5 22.3 %collective-permute-start.6 = (f32[208,128]{1,0:T(8,128)S(1)}, f32[208,128]{1,0:T(8,128)S(1)}, u32[]{:S(2)}, u32[]{:S(2)}) collective-permute-start(f32[208,128]{1,0:T(8,128)S(1)} %tree_merge.5.refs_0_), channel_id=1, source_target_pairs={{0,8},{1,9},{2,10},{3,11},{4,12},{5,13},{6,14},{7,15},{8,0},{9,1},... | collective-permute-start | bytes 319496 | tf_op jit(solution)/shard_map/ppermute | solution.py:414
  53.7 20.2 %collective-permute-start.7 = (f32[208,128]{1,0:T(8,128)S(1)}, f32[208,128]{1,0:T(8,128)S(1)}, u32[]{:S(2)}, u32[]{:S(2)}) collective-permute-start(f32[208,128]{1,0:T(8,128)S(1)} %tree_merge.5.refs_0_), channel_id=1, source_target_pairs={{0,12},{1,13},{2,14},{3,15},{4,8},{5,9},{6,10},{7,11},{8,4},{9,5},... | collective-permute-start | bytes 319496 | tf_op jit(solution)/shard_map/ppermute | solution.py:414
  73.9 9.0 %collective-permute-start.13 = (bf16[8,832,128]{2,1,0:T(8,128)(2,1)S(1)}, bf16[8,832,128]{2,1,0:T(8,128)(2,1)S(1)}, u32[]{:S(2)}, u32[]{:S(2)}) collective-permute-start(bf16[8,832,128]{2,1,0:T(8,128)(2,1)S(1)} %collective-permute-done.8.refs_4_), channel_id=1, source_target_pairs={{0,1},{3,2},{4,5},{7,6},{8,9},{11,10},{12,13},{15,14},{16,17},{19,... | collective-permute-start | bytes 5111816 | tf_op jit(solution)/shard_map/ppermute | solution.py:397
  75.2 7.7 %collective-permute-start.14 = (bf16[8,832,128]{2,1,0:T(8,128)(2,1)S(1)}, bf16[8,832,128]{2,1,0:T(8,128)(2,1)S(1)}, u32[]{:S(2)}, u32[]{:S(2)}) collective-permute-start(bf16[8,832,128]{2,1,0:T(8,128)(2,1)S(1)} %collective-permute-done.9.refs_5_), channel_id=1, source_target_pairs={{1,0},{2,3},{5,4},{6,7},{9,8},{10,11},{13,12},{14,15},{17,16},{18,... | collective-permute-start | bytes 5111816 | tf_op jit(solution)/shard_map/ppermute | solution.py:397
  80.7 11.5 %collective-permute-start.12 = (f32[208,128]{1,0:T(8,128)S(1)}, f32[208,128]{1,0:T(8,128)S(1)}, u32[]{:S(2)}, u32[]{:S(2)}) collective-permute-start(f32[208,128]{1,0:T(8,128)S(1)} %tree_merge.6.refs_0_), channel_id=1, source_target_pairs={{0,16},{1,17},{2,18},{3,19},{4,20},{5,21},{6,22},{7,23},{8,24},{9,... | collective-permute-start | bytes 319496 | tf_op jit(solution)/shard_map/ppermute | solution.py:414
where the time goes:
time: 95.1 us; the launch traced here: 94.1 us
  Pallas kernels  37 us (39%)
  starting transfers between devices  28.5 us (30%)
  waiting for transfers between devices  23 us (24%)
  local copies, waits for them, and re-layouts  4.58 us (5%)
  between operations  0.96 us (1%)
    ppermute x6, waiting for transfers between devices, exchange(): lax.ppermute(x, axes, [(i, i ^ d << shift) for i in range(count)])  22.9 us
    pallas_call x4, Pallas kernels, near_call(): pl.pallas_call(functools.partial(near_kernel, slots=slots, dim=dim, has_a...  21.6 us
    ppermute x9, starting transfers between devices, send(): return lax.ppermute(x, axes, pairs)  18.1 us
    ppermute x6, starting transfers between devices, exchange(): lax.ppermute(x, axes, [(i, i ^ d << shift) for i in range(count)])  10.4 us
    pallas_call x1, Pallas kernels, local_tree_call(): pl.pallas_call(functools.partial(local_tree_kernel, dim=dim), in_specs=[p...  6.87 us
    pallas_call x4, Pallas kernels, merge_call(): pl.pallas_call(functools.partial(merge_kernel, dim=dim, blocks=blocks, sh...  5.88 us
    unnamed x16, local copies, waits for them, and re-layouts  4.58 us
    pallas_call x1, Pallas kernels, order_call(): pl.pallas_call(order_kernel, grid=(blocks // many,), in_specs=[pl.BlockSp...  2.65 us
  transfers between devices with their start and end apart: 15, of which 4 were waited for; matrix products, arithmetic and copies ran while one was open for 0% of the time, Pallas kernels for 28%

commit v1 on v0

--- a/solution.py
+++ b/solution.py
@@ -268,21 +268,15 @@
     )(*parts, merge_sets)
 
 
-def near_kernel(*refs, slots, dim, has_acc, last):
-    lists, counts, rows = refs[:3]
-    refs = refs[3:]
+def near_kernel(*refs, flips, bases, which, dim, has_acc):
+    groups = len(flips)
+    lists, rows, refs = refs[:groups], refs[groups : 2 * groups], refs[2 * groups :]
     if has_acc:
-        acc_in, refs = refs[0], refs[1:]
-    buffers = []
-    for _, which in slots:
-        number = max(which) + 1
-        buffers.append(refs[:number])
-        refs = refs[number:]
-    out, pair_list = refs
-    blocks, leaf = rows.shape[:2]
-    near = lists.shape[1]
+        accs, refs = refs[:groups], refs[groups:]
+    buffers, outs, pair_list = refs[: max(which) + 1], refs[max(which) + 1 : -1], refs[-1]
+    blocks, leaf = rows[0].shape[:2]
+    near = lists[0].shape[1]
     window = blocks * lax.axis_size("sub")
-    start = lax.axis_index("leaf") * window - blocks
     sub = lax.axis_index("sub")
 
     def place(table):
@@ -291,48 +285,45 @@
             value = jnp.where(sub == i, jnp.int32(table[i]), value)
         return value
 
-    starts = [start + place(bases) for bases, _ in slots]
+    source_first = lax.axis_index("leaf") * window - blocks + place(bases)
     stride = blocks * near + 8
-
-    def list_block(g, found):
-        used = counts[g]
-
-        def list_slot(s, found):
-            source = lists[g, s]
-            after = []
-            for slot, first in enumerate(starts):
-                pair_list[slot * stride + found[slot]] = g * blocks + source - first
-                inside = (source >= first) & (source < first + blocks) & (s < used)
-                after.append(found[slot] + jnp.where(inside, 1, 0))
-            return tuple(after)
-
-        return lax.fori_loop(0, near, list_slot, found, unroll=True)
-
-    found = lax.fori_loop(0, blocks, list_block, (jnp.int32(0),) * len(slots))
-    if has_acc:
-        out[...] = acc_in[...]
-    else:
-        out[...] = jnp.zeros(out.shape, F32)
+    found = []
+    for j, flip in enumerate(flips):
+        target_first = lax.axis_index("leaf") * window + (sub ^ flip) * blocks
+
+        def list_block(g, count, j=j, target_first=target_first):
+            for s in range(near):
+                source = lists[j][g, s]
+                local = source - source_first
+                pair_list[j * stride + count] = g * blocks + local
+                inside = (local >= 0) & (local < blocks)
+                if s:
+                    inside = inside & (source != target_first + g)
+                count = count + jnp.where(inside, 1, 0)
+            return count
+
+        found.append(lax.fori_loop(0, blocks, list_block, jnp.int32(0)))
+        outs[j][...] = accs[j][...] if has_acc else jnp.zeros(outs[j].shape, F32)
 
     half = leaf // 2
 
-    def add_all(buffer, first, pairs):
+    def add_all(buffer, j, pairs):
         def add_pair(i):
-            code = pair_list[first + i]
+            code = pair_list[j * stride + i]
             g = code // blocks
             local = code - g * blocks
             form = form_of(buffer.at[local], leaf, dim)
             probes = buffer[local, :leaf, :]
             total = None
             for c in range(0, leaf, half):
-                weights = jnp.exp(dot(rows[g], form[:, c : c + half])).astype(BF16)
+                weights = jnp.exp(dot(rows[j][g], form[:, c : c + half])).astype(BF16)
                 term = dot(weights, probes[c : c + half])
                 total = term if total is None else total + term
             return g, total
 
         def add_pairs(i, carry):
             for g, total in [add_pair(2 * i), add_pair(2 * i + 1)]:
-                out[g] += total
+                outs[j][g] += total
             return carry
 
         lax.fori_loop(0, pairs // 2, add_pairs, 0)
@@ -340,42 +331,34 @@
         @pl.when(pairs % 2 == 1)
         def _():
             g, total = add_pair(pairs - 1)
-            out[g] += total
-
-    for slot, (_, which) in enumerate(slots):
-        if len(buffers[slot]) == 1:
-            add_all(buffers[slot][0], slot * stride, found[slot])
-        else:
-            held = place(which)
-            for number, buffer in enumerate(buffers[slot]):
-                add_all(buffer, slot * stride, jnp.where(held == number, found[slot], 0))
-    if last:
-        out[...] = out[...] * (leaf ** -0.5)
-
-
-def near_call(lists, counts, rows, acc, sets, dim, last, name):
-    blocks, leaf = rows.shape[:2]
-    buffers = [b for _, _, bufs in sets for b in bufs]
-    slots = tuple((bases, which) for bases, which, _ in sets)
-    packed = buffers[0].shape[1]
+            outs[j][g] += total
+
+    held = place(which)
+    for number, buffer in enumerate(buffers):
+        for j in range(groups):
+            pairs = found[j] if len(buffers) == 1 else jnp.where(held == number, found[j], 0)
+            add_all(buffer, j, pairs)
+
+
+def near_call(groups, source, dim, name):
+    flips, lists, rows, accs = zip(*groups)
+    bases, which, buffers = source
+    blocks, leaf = rows[0].shape[:2]
+    has_acc = accs[0] is not None
+    args = [*lists, *rows, *(accs if has_acc else ()), *buffers]
     smem = pl.BlockSpec(memory_space=pltpu.SMEM)
     vmem = pl.BlockSpec(memory_space=pltpu.VMEM)
-    args = [lists, counts, rows] + ([acc] if acc is not None else []) + buffers
-    total = len(slots) * blocks
-    near = lists.shape[1]
-    pairs = total * blocks // 8
+    near = lists[0].shape[1]
     return pl.pallas_call(
         functools.partial(
-            near_kernel, slots=slots, dim=dim, has_acc=acc is not None, last=last
+            near_kernel, flips=flips, bases=bases, which=which, dim=dim, has_acc=has_acc
         ),
-        in_specs=[smem, smem] + [vmem] * (len(args) - 2),
-        out_specs=vmem,
-        out_shape=jax.ShapeDtypeStruct((blocks, leaf, LANES), F32),
-        scratch_shapes=[pltpu.SMEM((len(slots) * (blocks * near + 8),), jnp.int32)],
+        in_specs=[smem] * len(lists) + [vmem] * (len(args) - len(lists)),
+        out_specs=[vmem] * len(groups),
+        out_shape=[jax.ShapeDtypeStruct((blocks, leaf, LANES), F32)] * len(groups),
+        scratch_shapes=[pltpu.SMEM((len(groups) * (blocks * near + 8),), jnp.int32)],
         compiler_params=pltpu.CompilerParams(vmem_limit_bytes=NEAR_BYTES),
-        cost_estimate=pl.CostEstimate(
-            flops=1000, bytes_accessed=1000, transcendentals=0
-        ),
+        cost_estimate=pl.CostEstimate(flops=1000, bytes_accessed=1000, transcendentals=0),
         name=name,
     )(*args)
 
@@ -396,14 +379,6 @@
                     pairs.append((place * sub_count + from_sub, (place + step) * sub_count + to_sub))
         return lax.ppermute(x, axes, pairs)
 
-    swap = [(0, 0, 1), (1, 0, 0), (2, 0, 3), (3, 0, 2)]
-    pack, rows = order_call(points.T, order.reshape(blocks, 1, leaf), probes, blocks)
-    outer_across = send(pack, [(3, 0, 1), (0, 0, 2)])
-    outer_next = send(pack, [(3, 1, 3), (0, -1, 0)])
-    beside = send(pack, swap)
-
-    node = local_tree_call(pack, rows, leaf_sets, merge_sets, dim)
-
     count = leaf_count * sub_count
     bits = count.bit_length() - 1
     sub_bits = sub_count.bit_length() - 1
@@ -414,70 +389,56 @@
             parts.append(lax.ppermute(x, axes, [(i, i ^ (d << shift)) for i in range(count)]))
         return parts
 
-    b = blocks
-    own_base, beside_base = (b, 2 * b, 3 * b, 4 * b), (2 * b, b, 4 * b, 3 * b)
-    early_base, early_beside_base = (5 * b, 4 * b, b, 0), (4 * b, 5 * b, 0, b)
-    late_base, late_beside_base = (3 * b, 0, 5 * b, 2 * b), (0, 3 * b, 2 * b, 5 * b)
-    single, edge_first, edge_second = (0, 0, 0, 0), (0, 1, 1, 0), (1, 0, 0, 1)
-    from_edge, from_inner = [(0, 0, 1), (3, 0, 2)], [(1, 0, 0), (2, 0, 3)]
-
     def tie(*values):
         return lax.optimization_barrier(values)
 
+    b = blocks
+    own_base = (b, 2 * b, 3 * b, 4 * b)
+    early_base, late_base = (5 * b, 4 * b, b, 0), (3 * b, 0, 5 * b, 2 * b)
+    single, by_edge = (0, 0, 0, 0), (0, 1, 1, 0)
+
+    pack, rows = order_call(points.T, order.reshape(blocks, 1, leaf), probes, blocks)
+    outer_across = send(pack, [(3, 0, 1), (0, 0, 2)])
+    outer_next = send(pack, [(3, 1, 3), (0, -1, 0)])
+    beside_rows = exchange(rows, 0, 1)[1]
+    beside_lists = exchange(near_lists, 0, 1)[1]
+
+    rows, beside_lists = tie(rows, beside_lists)
+    node = local_tree_call(pack, rows, leaf_sets, merge_sets, dim)
     node = merge_call(exchange(node, 0, 1), merge_sets, dim, blocks, 0)
     own_pack, node = tie(pack, node)
     parts = exchange(node, 1, sub_bits - 1)
-    acc = near_call(
-        near_lists, near_counts, rows, None,
-        [(own_base, single, [own_pack])],
-        dim, False, "near_first",
-    )
-
-    *parts, outer_across, outer_next, own_pack, acc = tie(
-        *parts, outer_across, outer_next, own_pack, acc
+    own, beside = near_call(
+        [(0, near_lists, rows, None), (1, beside_lists, beside_rows, None)],
+        (own_base, single, [own_pack]), dim, "near_own",
+    )
+
+    *parts, outer_across, outer_next, own_pack, own, beside = tie(
+        *parts, outer_across, outer_next, own_pack, own, beside
     )
     forwarded = send(outer_across, [(1, 1, 1), (2, -1, 2)])
     inner_across = send(own_pack, [(2, 0, 0), (1, 0, 3)])
-    acc = near_call(
-        near_lists, near_counts, rows, acc,
-        [
-            (beside_base, single, [beside]),
-            (early_base, edge_first, [outer_next, outer_across]),
-        ],
-        dim, False, "near_second",
-    )
-
-    *parts, acc = tie(*parts, acc)
+    own, beside = near_call(
+        [(0, near_lists, rows, own), (1, beside_lists, beside_rows, beside)],
+        (early_base, by_edge, [outer_next, outer_across]), dim, "near_early",
+    )
+
+    *parts, beside = tie(*parts, beside)
     node = merge_call(parts, merge_sets, dim, blocks, 1)
-    outer_next, outer_across, node = tie(outer_next, outer_across, node)
-    next_beside = send(outer_next, from_edge)
-    across_beside = send(outer_across, from_inner)
     shift, stage_bits = sub_bits, min(2, bits - sub_bits)
     parts = exchange(node, shift, stage_bits)
-    next_beside, across_beside, node = tie(next_beside, across_beside, node)
-    acc = near_call(
-        near_lists, near_counts, rows, acc,
-        [(early_beside_base, edge_second, [next_beside, across_beside])],
-        dim, False, "near_third",
-    )
-
-    *parts, inner_across, forwarded, acc = tie(*parts, inner_across, forwarded, acc)
-    inner_beside = send(inner_across, from_edge)
-    forwarded_beside = send(forwarded, from_inner)
+
+    *parts, inner_across, forwarded, beside = tie(*parts, inner_across, forwarded, beside)
+    late = (late_base, by_edge, [inner_across, forwarded])
+    (beside,) = near_call([(1, beside_lists, beside_rows, beside)], late, dim, "near_beside")
+    given = exchange(beside, 0, 1)[1]
+    *parts, beside = tie(*parts, beside)
     node = merge_call(parts, merge_sets, dim, blocks, shift)
     shift += stage_bits
-    inner_across, forwarded, node = tie(inner_across, forwarded, node)
+    own, node = tie(own, node)
     parts = exchange(node, shift, bits - shift)
-    near = near_call(
-        near_lists, near_counts, rows, acc,
-        [
-            (late_base, edge_first, [inner_across, forwarded]),
-            (late_beside_base, edge_second, [inner_beside, forwarded_beside]),
-        ],
-        dim, True, "near_last",
-    )
-
-    *parts, near = tie(*parts, near)
+    (own,) = near_call([(0, near_lists, rows, own)], late, dim, "near_last")
+    *parts, own = tie(*parts, own)
     piece = skel // count
     node = merge_call(parts, merge_sets, dim, blocks, shift, piece)
     if piece:
@@ -486,6 +447,7 @@
         size = skel * LANES // count
         rank = lax.axis_index("leaf") * sub_count + lax.axis_index("sub")
         root = lax.dynamic_slice_in_dim(node.reshape(-1), rank * size, size, 0)
+    near = (own + given) * (leaf ** -0.5)
     return near.reshape(npts, LANES), root
 
 

time: 95.1 us -> 85.5 us (0.90)
  the two profiles are of different devices: /device:TPU:4 before, /device:TPU:5 now
where the time goes in v1:
time: 85.5 us; the launch traced here: 84.7 us
  Pallas kernels  32.8 us (38%)
  starting transfers between devices  26.4 us (31%)
  waiting for transfers between devices  18.4 us (22%)
  local copies, waits for them, and re-layouts  4.58 us (5%)
  other arithmetic  1.65 us (2%)
    ppermute x9, starting transfers between devices, exchange(): lax.ppermute(x, axes, [(i, i ^ d << shift) for i in range(count)])  19.6 us
    pallas_call x4, Pallas kernels, near_call(): pl.pallas_call(functools.partial(near_kernel, flips=flips, bases=bases, w...  17.5 us
    ppermute x9, waiting for transfers between devices, exchange(): lax.ppermute(x, axes, [(i, i ^ d << shift) for i in range(count)])  10.9 us
    ppermute x4, waiting for transfers between devices, send(): return lax.ppermute(x, axes, pairs)  7.5 us
    pallas_call x1, Pallas kernels, local_tree_call(): pl.pallas_call(functools.partial(local_tree_kernel, dim=dim), in_specs=[p...  6.85 us
    ppermute x4, starting transfers between devices, send(): return lax.ppermute(x, axes, pairs)  6.82 us
    pallas_call x4, Pallas kernels, merge_call(): pl.pallas_call(functools.partial(merge_kernel, dim=dim, blocks=blocks, sh...  5.82 us
    unnamed x14, local copies, waits for them, and re-layouts  4.58 us
  transfers between devices with their start and end apart: 13, of which 5 were waited for; matrix products, arithmetic and copies ran while one was open for 0% of the time, Pallas kernels for 31%

profile of v1, /device:TPU:5, one launch (start us, length us, event | category | flops | bytes accessed | tf_op | source)
XLA Modules:
  0.0 84.7 jit_solution(2590833672236603586)
XLA Ops:
  0.6 1.2 %copy-done.2 = bf16[4096,128]{1,0:T(8,128)(2,1)S(1)} copy-done((bf16[4096,128]{1,0:T(8,128)(2,1)S(1)}, bf16[4096,128]{1,0:T(8,128)(2,1)}, u32[]{:S(2)}) %copy-start.2) | copy-done | bytes 1048600
  1.9 1.0 %copy-done.3 = bf16[4096,64]{0,1:T(8,128)(2,1)S(1)} copy-done((bf16[4096,64]{0,1:T(8,128)(2,1)S(1)}, bf16[4096,64]{0,1:T(8,128)(2,1)}, u32[]{:S(2)}) %copy-start.3) | copy-done | bytes 524312
  3.6 2.6 %tree_order.1 = (bf16[8,832,128]{2,1,0:T(8,128)(2,1)S(1)}, bf16[8,512,128]{2,1,0:T(8,128)(2,1)S(1)}) custom-call(bf16[64,4096]{1,0:T(8,128)(2,1)S(1)} %bitcast.4, s32[8,1,512]{2,1,0:T(1,128)S(1)} %bitcast.5, bf16[4096,128]{1,0:T(8,128)(2,1)S(1)} %copy-done.2), custom_call_target="tpu_custom_call" | custom-call | flops 268435456 | bytes 5242880 | tf_op jit(solution)/shard_map/tree_order/pallas_call | solution.py:94
  6.3 3.2 %collective-permute-start.5 = (bf16[8,832,128]{2,1,0:T(8,128)(2,1)S(1)}, bf16[8,832,128]{2,1,0:T(8,128)(2,1)S(1)}, u32[]{:S(2)}, u32[]{:S(2)}) collective-permute-start(bf16[8,832,128]{2,1,0:T(8,128)(2,1)S(1)} %get-tuple-element.56.pack.refs_4_), channel_id=1, source_target_pairs={{3,7},{7,11},{4,0},{11,15},{8,4},{15,19},{12,8},{19,23},{16,12},{2... | collective-permute-start | bytes 5111816 | tf_op jit(solution)/shard_map/ppermute | solution.py:380
  9.5 1.4 %collective-permute-start.4 = (bf16[8,832,128]{2,1,0:T(8,128)(2,1)S(1)}, bf16[8,832,128]{2,1,0:T(8,128)(2,1)S(1)}, u32[]{:S(2)}, u32[]{:S(2)}) collective-permute-start(bf16[8,832,128]{2,1,0:T(8,128)(2,1)S(1)} %get-tuple-element.56.pack.refs_4_), channel_id=1, source_target_pairs={{3,1},{0,2},{7,5},{4,6},{11,9},{8,10},{15,13},{12,14},{19,17},{16,... | collective-permute-start | bytes 5111816 | tf_op jit(solution)/shard_map/ppermute | solution.py:380
  11.5 2.0 %collective-permute-done.refs_1_.refs_0_ = s32[8,12]{1,0:T(8,128)S(1)} collective-permute-done((s32[8,12]{1,0:T(8,128)}, s32[8,12]{1,0:T(8,128)S(1)}, u32[]{:S(2)}, u32[]{:S(2)}) %collective-permute-start) | collective-permute-done | bytes 416 | tf_op jit(solution)/shard_map/ppermute | solution.py:389
  15.1 6.9 %local_tree.1.refs_0_ = f32[208,128]{1,0:T(8,128)S(1)} custom-call(bf16[8,832,128]{2,1,0:T(8,128)(2,1)S(1)} %get-tuple-element.56.pack.refs_4_, bf16[8,512,128]{2,1,0:T(8,128)(2,1)S(1)} %get-tuple-element.40.rows.refs_2_.refs_1_, s32[8,128]{1,0:T(8,128)S(1)} %copy-done.6, s32[255,128]{1,0:T(8,128)S(1)} %copy-done), custom_call_target="tpu_custom_call" | custom-call | flops 536870912 | bytes 3145728 | tf_op jit(solution)/shard_map/local_tree/pallas_call | solution.py:177
  24.8 8.5 %near_own.1 = (f32[8,512,128]{2,1,0:T(8,128)S(1)}, f32[8,512,128]{2,1,0:T(8,128)S(1)}) custom-call(s32[8,12]{1,0:T(8,128)S(1)} %copy-done.4, s32[8,12]{1,0:T(8,128)S(1)} %collective-permute-done.refs_1_.refs_0_, bf16[8,512,128]{2,1,0:T(8,128)(2,1)S(1)} %get-tuple-element.40.rows.refs_2_.refs_1_, ...), custom_call_target="tpu_custom_call" | custom-call | flops 1000 | bytes 1000 | tf_op jit(solution)/shard_map/near_own/pallas_call | solution.py:352
  33.3 1.4 %collective-permute-start.9 = (bf16[8,832,128]{2,1,0:T(8,128)(2,1)S(1)}, bf16[8,832,128]{2,1,0:T(8,128)(2,1)S(1)}, u32[]{:S(2)}, u32[]{:S(2)}) collective-permute-start(bf16[8,832,128]{2,1,0:T(8,128)(2,1)S(1)} %get-tuple-element.56.pack.refs_4_), channel_id=1, source_target_pairs={{2,0},{1,3},{6,4},{5,7},{10,8},{9,11},{14,12},{13,15},{18,16},{17,... | collective-permute-start | bytes 5111816 | tf_op jit(solution)/shard_map/ppermute | solution.py:380
  35.5 2.0 %near_early.1 = (f32[8,512,128]{2,1,0:T(8,128)S(1)}, f32[8,512,128]{2,1,0:T(8,128)S(1)}) custom-call(s32[8,12]{1,0:T(8,128)S(1)} %copy-done.4, s32[8,12]{1,0:T(8,128)S(1)} %collective-permute-done.refs_1_.refs_0_, bf16[8,512,128]{2,1,0:T(8,128)(2,1)S(1)} %get-tuple-element.40.rows.refs_2_.refs_1_, ...), custom_call_target="tpu_custom_call" | custom-call | flops 1000 | bytes 1000 | tf_op jit(solution)/shard_map/near_early/pallas_call | solution.py:352
  37.6 1.0 %tree_merge.5.refs_0_ = f32[208,128]{1,0:T(8,128)S(1)} custom-call(f32[208,128]{1,0:T(8,128)S(1)} %tree_merge.4.refs_0_, f32[208,128]{1,0:T(8,128)S(1)} %collective-permute-done.3.refs_1_, s32[255,128]{1,0:T(8,128)S(1)} %copy-done.1), custom_call_target="tpu_custom_call" | custom-call | flops 67108864 | bytes 212992 | tf_op jit(solution)/shard_map/tree_merge/pallas_call | solution.py:251
  38.6 3.7 %collective-permute-start.8 = (f32[208,128]{1,0:T(8,128)S(1)}, f32[208,128]{1,0:T(8,128)S(1)}, u32[]{:S(2)}, u32[]{:S(2)}) collective-permute-start(f32[208,128]{1,0:T(8,128)S(1)} %tree_merge.5.refs_0_), channel_id=1, source_target_pairs={{0,12},{1,13},{2,14},{3,15},{4,8},{5,9},{6,10},{7,11},{8,4},{9,5},... | collective-permute-start | bytes 319496 | tf_op jit(solution)/shard_map/ppermute | solution.py:389
  42.3 1.2 %collective-permute-start.7 = (f32[208,128]{1,0:T(8,128)S(1)}, f32[208,128]{1,0:T(8,128)S(1)}, u32[]{:S(2)}, u32[]{:S(2)}) collective-permute-start(f32[208,128]{1,0:T(8,128)S(1)} %tree_merge.5.refs_0_), channel_id=1, source_target_pairs={{0,8},{1,9},{2,10},{3,11},{4,12},{5,13},{6,14},{7,15},{8,0},{9,1},... | collective-permute-start | bytes 319496 | tf_op jit(solution)/shard_map/ppermute | solution.py:389
  43.5 1.1 %collective-permute-start.6 = (f32[208,128]{1,0:T(8,128)S(1)}, f32[208,128]{1,0:T(8,128)S(1)}, u32[]{:S(2)}, u32[]{:S(2)}) collective-permute-start(f32[208,128]{1,0:T(8,128)S(1)} %tree_merge.5.refs_0_), channel_id=1, source_target_pairs={{0,4},{1,5},{2,6},{3,7},{4,0},{5,1},{6,2},{7,3},{8,12},{9,13},{10,... | collective-permute-start | bytes 319496 | tf_op jit(solution)/shard_map/ppermute | solution.py:389
  44.6 4.6 %collective-permute-done.7.refs_2_ = f32[208,128]{1,0:T(8,128)S(1)} collective-permute-done((f32[208,128]{1,0:T(8,128)S(1)}, f32[208,128]{1,0:T(8,128)S(1)}, u32[]{:S(2)}, u32[]{:S(2)}) %collective-permute-start.7) | collective-permute-done | bytes 106528 | tf_op jit(solution)/shard_map/ppermute | solution.py:389
  49.2 7.5 %collective-permute-done.9.refs_3_ = bf16[8,832,128]{2,1,0:T(8,128)(2,1)S(1)} collective-permute-done((bf16[8,832,128]{2,1,0:T(8,128)(2,1)S(1)}, bf16[8,832,128]{2,1,0:T(8,128)(2,1)S(1)}, u32[]{:S(2)}, u32[]{:S(2)}) %collective-permute-start.9) | collective-permute-done | bytes 1703968 | tf_op jit(solution)/shard_map/ppermute | solution.py:380
  56.7 3.7 %near_beside.1 = f32[8,512,128]{2,1,0:T(8,128)S(1)} custom-call(s32[8,12]{1,0:T(8,128)S(1)} %collective-permute-done.refs_1_.refs_0_, bf16[8,512,128]{2,1,0:T(8,128)(2,1)S(1)} %collective-permute-done.1.refs_3_.refs_1_, f32[8,512,128]{2,1,0:T(8,128)S(1)} %get-tuple-element.62.refs_2_, bf16[8,832,128]{2,1,0:T(8,128)(2,1)S(1)} %collective-permute-done.9.refs_3_, ...), custom_call_target="tpu_custom_call" | custom-call | flops 1000 | bytes 1000 | tf_op jit(solution)/shard_map/near_beside/pallas_call | solution.py:352
  60.4 11.1 %collective-permute-start.12 = (f32[8,512,128]{2,1,0:T(8,128)S(1)}, f32[8,512,128]{2,1,0:T(8,128)S(1)}, u32[]{:S(2)}, u32[]{:S(2)}) collective-permute-start(f32[8,512,128]{2,1,0:T(8,128)S(1)} %near_beside.1), channel_id=1, source_target_pairs={{0,1},{1,0},{2,3},{3,2},{4,5},{5,4},{6,7},{7,6},{8,9},{9,8},{10,11... | collective-permute-start | bytes 6291464 | tf_op jit(solution)/shard_map/ppermute | solution.py:389
  71.5 2.2 %tree_merge.6.refs_0_ = f32[208,128]{1,0:T(8,128)S(1)} custom-call(f32[208,128]{1,0:T(8,128)S(1)} %tree_merge.5.refs_0_, f32[208,128]{1,0:T(8,128)S(1)} %collective-permute-done.6.refs_1_, f32[208,128]{1,0:T(8,128)S(1)} %collective-permute-done.7.refs_2_, f32[208,128]{1,0:T(8,128)S(1)} %collective-permute-done.8.refs_3_, s32[255,128]{1,0:T(8,128)S(1)} %copy-done.1), custom_call_target="tpu_custom_call" | custom-call | flops 134217728 | bytes 425984 | tf_op jit(solution)/shard_map/tree_merge/pallas_call | solution.py:251
  73.7 1.0 %collective-permute-start.11 = (f32[208,128]{1,0:T(8,128)S(1)}, f32[208,128]{1,0:T(8,128)S(1)}, u32[]{:S(2)}, u32[]{:S(2)}) collective-permute-start(f32[208,128]{1,0:T(8,128)S(1)} %tree_merge.6.refs_0_), channel_id=1, source_target_pairs={{0,16},{1,17},{2,18},{3,19},{4,20},{5,21},{6,22},{7,23},{8,24},{9,... | collective-permute-start | bytes 319496 | tf_op jit(solution)/shard_map/ppermute | solution.py:389
  74.7 3.3 %near_last.1 = f32[8,512,128]{2,1,0:T(8,128)S(1)} custom-call(s32[8,12]{1,0:T(8,128)S(1)} %copy-done.4, bf16[8,512,128]{2,1,0:T(8,128)(2,1)S(1)} %get-tuple-element.40.rows.refs_2_.refs_1_, f32[8,512,128]{2,1,0:T(8,128)S(1)} %get-tuple-element.70.refs_2_, bf16[8,832,128]{2,1,0:T(8,128)(2,1)S(1)} %collective-permute-done.9.refs_3_, ...), custom_call_target="tpu_custom_call" | custom-call | flops 1000 | bytes 1000 | tf_op jit(solution)/shard_map/near_last/pallas_call | solution.py:352
  78.0 3.4 %collective-permute-done.11.refs_1_ = f32[208,128]{1,0:T(8,128)S(1)} collective-permute-done((f32[208,128]{1,0:T(8,128)S(1)}, f32[208,128]{1,0:T(8,128)S(1)}, u32[]{:S(2)}, u32[]{:S(2)}) %collective-permute-start.11) | collective-permute-done | bytes 106528 | tf_op jit(solution)/shard_map/ppermute | solution.py:389
  81.3 1.7 %tree_merge.7 = f32[4,128]{1,0:T(4,128)} custom-call(f32[208,128]{1,0:T(8,128)S(1)} %tree_merge.6.refs_0_, f32[208,128]{1,0:T(8,128)S(1)} %collective-permute-done.11.refs_1_, s32[255,128]{1,0:T(8,128)S(1)} %copy-done.1), custom_call_target="tpu_custom_call" | custom-call | flops 67108864 | bytes 212992 | tf_op jit(solution)/shard_map/tree_merge/pallas_call | solution.py:251
  83.0 1.6 %add_multiply_fusion = f32[8,512,128]{2,1,0:T(8,128)} fusion(f32[8,512,128]{2,1,0:T(8,128)S(1)} %near_last.1, f32[8,512,128]{2,1,0:T(8,128)S(1)} %collective-permute-done.12), kind=kLoop, calls=%fused_computation | loop fusion | flops 1048576 | bytes 6291456 | tf_op jit(solution)/shard_map/mul | solution.py:450
  (27 shorter events, 6.5 us)
Async XLA Ops:
  0.6 1.2 %copy-start.2 = (bf16[4096,128]{1,0:T(8,128)(2,1)S(1)}, bf16[4096,128]{1,0:T(8,128)(2,1)}, u32[]{:S(2)}) copy-start(bf16[4096,128]{1,0:T(8,128)(2,1)} %probes.1) | copy-start | bytes 3145732
  1.9 1.0 %copy-start.3 = (bf16[4096,64]{0,1:T(8,128)(2,1)S(1)}, bf16[4096,64]{0,1:T(8,128)(2,1)}, u32[]{:S(2)}) copy-start(bf16[4096,64]{0,1:T(8,128)(2,1)} %param.7) | copy-start | bytes 1572868
  2.9 0.7 copy-start.5
  3.6 21.2 %copy-start.4 = (s32[8,12]{1,0:T(8,128)S(1)}, s32[8,12]{1,0:T(8,128)}, u32[]{:S(2)}) copy-start(s32[8,12]{1,0:T(8,128)} %refs_0_.5) | copy-start | bytes 1156
  6.3 27.0 %collective-permute-start.5 = (bf16[8,832,128]{2,1,0:T(8,128)(2,1)S(1)}, bf16[8,832,128]{2,1,0:T(8,128)(2,1)S(1)}, u32[]{:S(2)}, u32[]{:S(2)}) collective-permute-start(bf16[8,832,128]{2,1,0:T(8,128)(2,1)S(1)} %get-tuple-element.56.pack.refs_4_), channel_id=1, source_target_pairs={{3,7},{7,11},{4,0},{11,15},{8,4},{15,19},{12,8},{19,23},{16,12},{2... | collective-permute-start | bytes 5111816 | tf_op jit(solution)/shard_map/ppermute | solution.py:380
  9.5 23.8 %collective-permute-start.4 = (bf16[8,832,128]{2,1,0:T(8,128)(2,1)S(1)}, bf16[8,832,128]{2,1,0:T(8,128)(2,1)S(1)}, u32[]{:S(2)}, u32[]{:S(2)}) collective-permute-start(bf16[8,832,128]{2,1,0:T(8,128)(2,1)S(1)} %get-tuple-element.56.pack.refs_4_), channel_id=1, source_target_pairs={{3,1},{0,2},{7,5},{4,6},{11,9},{8,10},{15,13},{12,14},{19,17},{16,... | collective-permute-start | bytes 5111816 | tf_op jit(solution)/shard_map/ppermute | solution.py:380
  10.9 13.9 %collective-permute-start.1 = (bf16[8,512,128]{2,1,0:T(8,128)(2,1)S(1)}, bf16[8,512,128]{2,1,0:T(8,128)(2,1)S(1)}, u32[]{:S(2)}, u32[]{:S(2)}) collective-permute-start(bf16[8,512,128]{2,1,0:T(8,128)(2,1)S(1)} %get-tuple-element.40.rows.refs_2_.refs_1_), channel_id=1, source_target_pairs={{0,1},{1,0},{2,3},{3,2},{4,5},{5,4},{6,7},{7,6},{8,9},{9,8},{10,11... | collective-permute-start | bytes 3145736 | tf_op jit(solution)/shard_map/ppermute | solution.py:389
  11.0 2.5 %collective-permute-start = (s32[8,12]{1,0:T(8,128)}, s32[8,12]{1,0:T(8,128)S(1)}, u32[]{:S(2)}, u32[]{:S(2)}) collective-permute-start(s32[8,12]{1,0:T(8,128)} %refs_0_.5), channel_id=1, source_target_pairs={{0,1},{1,0},{2,3},{3,2},{4,5},{5,4},{6,7},{7,6},{8,9},{9,8},{10,11... | collective-permute-start | bytes 1160 | tf_op jit(solution)/shard_map/ppermute | solution.py:389
  13.5 0.9 %copy-start = (s32[255,128]{1,0:T(8,128)S(1)}, s32[255,128]{1,0:T(8,128)}, u32[]{:S(2)}) copy-start(s32[255,128]{1,0:T(8,128)} %refs_2_.5) | copy-start | bytes 391684
  14.4 0.7 copy-start.6
  21.9 1.4 %collective-permute-start.2 = (f32[208,128]{1,0:T(8,128)S(1)}, f32[208,128]{1,0:T(8,128)S(1)}, u32[]{:S(2)}, u32[]{:S(2)}) collective-permute-start(f32[208,128]{1,0:T(8,128)S(1)} %local_tree.1.refs_0_), channel_id=1, source_target_pairs={{0,1},{1,0},{2,3},{3,2},{4,5},{5,4},{6,7},{7,6},{8,9},{9,8},{10,11... | collective-permute-start | bytes 319496 | tf_op jit(solution)/shard_map/ppermute | solution.py:389
  24.3 9.0 %collective-permute-start.3 = (f32[208,128]{1,0:T(8,128)S(1)}, f32[208,128]{1,0:T(8,128)S(1)}, u32[]{:S(2)}, u32[]{:S(2)}) collective-permute-start(f32[208,128]{1,0:T(8,128)S(1)} %tree_merge.4.refs_0_), channel_id=1, source_target_pairs={{0,2},{1,3},{2,0},{3,1},{4,6},{5,7},{6,4},{7,5},{8,10},{9,11},{10,... | collective-permute-start | bytes 319496 | tf_op jit(solution)/shard_map/ppermute | solution.py:389
  33.3 4.3 %copy-start.1 = (s32[255,128]{1,0:T(8,128)S(1)}, s32[255,128]{1,0:T(8,128)}, u32[]{:S(2)}) copy-start(s32[255,128]{1,0:T(8,128)} %refs_2_.5) | copy-start | bytes 391684
  33.3 23.3 %collective-permute-start.9 = (bf16[8,832,128]{2,1,0:T(8,128)(2,1)S(1)}, bf16[8,832,128]{2,1,0:T(8,128)(2,1)S(1)}, u32[]{:S(2)}, u32[]{:S(2)}) collective-permute-start(bf16[8,832,128]{2,1,0:T(8,128)(2,1)S(1)} %get-tuple-element.56.pack.refs_4_), channel_id=1, source_target_pairs={{2,0},{1,3},{6,4},{5,7},{10,8},{9,11},{14,12},{13,15},{18,16},{17,... | collective-permute-start | bytes 5111816 | tf_op jit(solution)/shard_map/ppermute | solution.py:380
  34.8 21.9 %collective-permute-start.10 = (bf16[8,832,128]{2,1,0:T(8,128)(2,1)S(1)}, bf16[8,832,128]{2,1,0:T(8,128)(2,1)S(1)}, u32[]{:S(2)}, u32[]{:S(2)}) collective-permute-start(bf16[8,832,128]{2,1,0:T(8,128)(2,1)S(1)} %collective-permute-done.4.refs_7_), channel_id=1, source_target_pairs={{1,5},{5,9},{6,2},{9,13},{10,6},{13,17},{14,10},{17,21},{18,14},{2... | collective-permute-start | bytes 5111816 | tf_op jit(solution)/shard_map/ppermute | solution.py:380
  38.6 6.0 %collective-permute-start.8 = (f32[208,128]{1,0:T(8,128)S(1)}, f32[208,128]{1,0:T(8,128)S(1)}, u32[]{:S(2)}, u32[]{:S(2)}) collective-permute-start(f32[208,128]{1,0:T(8,128)S(1)} %tree_merge.5.refs_0_), channel_id=1, source_target_pairs={{0,12},{1,13},{2,14},{3,15},{4,8},{5,9},{6,10},{7,11},{8,4},{9,5},... | collective-permute-start | bytes 319496 | tf_op jit(solution)/shard_map/ppermute | solution.py:389
  42.3 6.9 %collective-permute-start.7 = (f32[208,128]{1,0:T(8,128)S(1)}, f32[208,128]{1,0:T(8,128)S(1)}, u32[]{:S(2)}, u32[]{:S(2)}) collective-permute-start(f32[208,128]{1,0:T(8,128)S(1)} %tree_merge.5.refs_0_), channel_id=1, source_target_pairs={{0,8},{1,9},{2,10},{3,11},{4,12},{5,13},{6,14},{7,15},{8,0},{9,1},... | collective-permute-start | bytes 319496 | tf_op jit(solution)/shard_map/ppermute | solution.py:389
  43.5 5.7 %collective-permute-start.6 = (f32[208,128]{1,0:T(8,128)S(1)}, f32[208,128]{1,0:T(8,128)S(1)}, u32[]{:S(2)}, u32[]{:S(2)}) collective-permute-start(f32[208,128]{1,0:T(8,128)S(1)} %tree_merge.5.refs_0_), channel_id=1, source_target_pairs={{0,4},{1,5},{2,6},{3,7},{4,0},{5,1},{6,2},{7,3},{8,12},{9,13},{10,... | collective-permute-start | bytes 319496 | tf_op jit(solution)/shard_map/ppermute | solution.py:389
  60.4 22.7 %collective-permute-start.12 = (f32[8,512,128]{2,1,0:T(8,128)S(1)}, f32[8,512,128]{2,1,0:T(8,128)S(1)}, u32[]{:S(2)}, u32[]{:S(2)}) collective-permute-start(f32[8,512,128]{2,1,0:T(8,128)S(1)} %near_beside.1), channel_id=1, source_target_pairs={{0,1},{1,0},{2,3},{3,2},{4,5},{5,4},{6,7},{7,6},{8,9},{9,8},{10,11... | collective-permute-start | bytes 6291464 | tf_op jit(solution)/shard_map/ppermute | solution.py:389
  73.7 7.7 %collective-permute-start.11 = (f32[208,128]{1,0:T(8,128)S(1)}, f32[208,128]{1,0:T(8,128)S(1)}, u32[]{:S(2)}, u32[]{:S(2)}) collective-permute-start(f32[208,128]{1,0:T(8,128)S(1)} %tree_merge.6.refs_0_), channel_id=1, source_target_pairs={{0,16},{1,17},{2,18},{3,19},{4,20},{5,21},{6,22},{7,23},{8,24},{9,... | collective-permute-start | bytes 319496 | tf_op jit(solution)/shard_map/ppermute | solution.py:389

commit v2 on v1

--- a/solution.py
+++ b/solution.py
@@ -268,12 +268,18 @@
     )(*parts, merge_sets)
 
 
-def near_kernel(*refs, flips, bases, which, dim, has_acc):
-    groups = len(flips)
-    lists, rows, refs = refs[:groups], refs[groups : 2 * groups], refs[2 * groups :]
-    if has_acc:
-        accs, refs = refs[:groups], refs[groups:]
-    buffers, outs, pair_list = refs[: max(which) + 1], refs[max(which) + 1 : -1], refs[-1]
+def near_kernel(*refs, flips, has_acc, sets, tasks, dim):
+    refs = list(refs)
+
+    def take(number):
+        taken = refs[:number]
+        del refs[:number]
+        return taken
+
+    lists, rows = take(len(flips)), take(len(flips))
+    accs = [take(1)[0] if has else None for has in has_acc]
+    buffers = [take(max(which) + 1) for _, which in sets]
+    outs, (pair_list,) = take(len(flips)), refs
     blocks, leaf = rows[0].shape[:2]
     near = lists[0].shape[1]
     window = blocks * lax.axis_size("sub")
@@ -285,31 +291,39 @@
             value = jnp.where(sub == i, jnp.int32(table[i]), value)
         return value
 
-    source_first = lax.axis_index("leaf") * window - blocks + place(bases)
+    window_first = lax.axis_index("leaf") * window - blocks
     stride = blocks * near + 8
-    found = []
+    found = [jnp.int32(0)] * len(tasks)
     for j, flip in enumerate(flips):
+        mine = [t for t, (_, group) in enumerate(tasks) if group == j]
+        firsts = [window_first + place(sets[tasks[t][0]][0]) for t in mine]
         target_first = lax.axis_index("leaf") * window + (sub ^ flip) * blocks
 
-        def list_block(g, count, j=j, target_first=target_first):
+        def list_block(g, counts, j=j, mine=mine, firsts=firsts, target_first=target_first):
             for s in range(near):
                 source = lists[j][g, s]
-                local = source - source_first
-                pair_list[j * stride + count] = g * blocks + local
-                inside = (local >= 0) & (local < blocks)
-                if s:
-                    inside = inside & (source != target_first + g)
-                count = count + jnp.where(inside, 1, 0)
-            return count
-
-        found.append(lax.fori_loop(0, blocks, list_block, jnp.int32(0)))
-        outs[j][...] = accs[j][...] if has_acc else jnp.zeros(outs[j].shape, F32)
+                used = (source != target_first + g) if s else True
+                after = []
+                for t, first, count in zip(mine, firsts, counts):
+                    local = source - first
+                    pair_list[t * stride + count] = g * blocks + local
+                    inside = (local >= 0) & (local < blocks) & used
+                    after.append(count + jnp.where(inside, 1, 0))
+                counts = tuple(after)
+            return counts
+
+        counts = lax.fori_loop(0, blocks, list_block, (jnp.int32(0),) * len(mine))
+        for t, count in zip(mine, counts):
+            found[t] = count
+        outs[j][...] = jnp.zeros(outs[j].shape, F32) if accs[j] is None else accs[j][...]
 
     half = leaf // 2
 
-    def add_all(buffer, j, pairs):
+    def add_all(buffer, t, pairs):
+        j = tasks[t][1]
+
         def add_pair(i):
-            code = pair_list[j * stride + i]
+            code = pair_list[t * stride + i]
             g = code // blocks
             local = code - g * blocks
             form = form_of(buffer.at[local], leaf, dim)
@@ -333,30 +347,34 @@
             g, total = add_pair(pairs - 1)
             outs[j][g] += total
 
-    held = place(which)
-    for number, buffer in enumerate(buffers):
-        for j in range(groups):
-            pairs = found[j] if len(buffers) == 1 else jnp.where(held == number, found[j], 0)
-            add_all(buffer, j, pairs)
-
-
-def near_call(groups, source, dim, name):
+    for t, (number, _) in enumerate(tasks):
+        held = place(sets[number][1])
+        for k, buffer in enumerate(buffers[number]):
+            pairs = found[t] if len(buffers[number]) == 1 else jnp.where(held == k, found[t], 0)
+            add_all(buffer, t, pairs)
+
+
+def near_call(groups, sources, tasks, dim, name):
     flips, lists, rows, accs = zip(*groups)
-    bases, which, buffers = source
     blocks, leaf = rows[0].shape[:2]
-    has_acc = accs[0] is not None
-    args = [*lists, *rows, *(accs if has_acc else ()), *buffers]
+    held = [acc for acc in accs if acc is not None]
+    args = [*lists, *rows, *held, *(b for _, _, buffers in sources for b in buffers)]
     smem = pl.BlockSpec(memory_space=pltpu.SMEM)
     vmem = pl.BlockSpec(memory_space=pltpu.VMEM)
     near = lists[0].shape[1]
     return pl.pallas_call(
         functools.partial(
-            near_kernel, flips=flips, bases=bases, which=which, dim=dim, has_acc=has_acc
+            near_kernel,
+            flips=flips,
+            has_acc=tuple(acc is not None for acc in accs),
+            sets=tuple((bases, which) for bases, which, _ in sources),
+            tasks=tasks,
+            dim=dim,
         ),
         in_specs=[smem] * len(lists) + [vmem] * (len(args) - len(lists)),
         out_specs=[vmem] * len(groups),
         out_shape=[jax.ShapeDtypeStruct((blocks, leaf, LANES), F32)] * len(groups),
-        scratch_shapes=[pltpu.SMEM((len(groups) * (blocks * near + 8),), jnp.int32)],
+        scratch_shapes=[pltpu.SMEM((len(tasks) * (blocks * near + 8),), jnp.int32)],
         compiler_params=pltpu.CompilerParams(vmem_limit_bytes=NEAR_BYTES),
         cost_estimate=pl.CostEstimate(flops=1000, bytes_accessed=1000, transcendentals=0),
         name=name,
@@ -403,44 +421,49 @@
     beside_rows = exchange(rows, 0, 1)[1]
     beside_lists = exchange(near_lists, 0, 1)[1]
 
-    rows, beside_lists = tie(rows, beside_lists)
     node = local_tree_call(pack, rows, leaf_sets, merge_sets, dim)
-    node = merge_call(exchange(node, 0, 1), merge_sets, dim, blocks, 0)
+    node, beside_lists = tie(node, beside_lists)
+
+    def level(parts, bit, piece=None):
+        return merge_call(parts, merge_sets, dim, blocks, bit, piece)
+
+    node = level(exchange(node, 0, 1), 0)
     own_pack, node = tie(pack, node)
-    parts = exchange(node, 1, sub_bits - 1)
-    own, beside = near_call(
-        [(0, near_lists, rows, None), (1, beside_lists, beside_rows, None)],
-        (own_base, single, [own_pack]), dim, "near_own",
-    )
-
-    *parts, outer_across, outer_next, own_pack, own, beside = tie(
-        *parts, outer_across, outer_next, own_pack, own, beside
+    parts = exchange(node, 1, 1)
+    own_set = (own_base, single, [own_pack])
+    (beside,) = near_call(
+        [(1, beside_lists, beside_rows, None)], [own_set], ((0, 0),), dim, "near_own"
+    )
+
+    *parts, outer_across, outer_next, own_pack, beside = tie(
+        *parts, outer_across, outer_next, own_pack, beside
     )
     forwarded = send(outer_across, [(1, 1, 1), (2, -1, 2)])
     inner_across = send(own_pack, [(2, 0, 0), (1, 0, 3)])
+    node = level(parts, 1)
+    parts = exchange(node, 2, 1)
+    own_set = (own_base, single, [own_pack])
+    early_set = (early_base, by_edge, [outer_next, outer_across])
     own, beside = near_call(
-        [(0, near_lists, rows, own), (1, beside_lists, beside_rows, beside)],
-        (early_base, by_edge, [outer_next, outer_across]), dim, "near_early",
+        [(0, near_lists, rows, None), (1, beside_lists, beside_rows, beside)],
+        [own_set, early_set], ((0, 0), (1, 0), (1, 1)), dim, "near_early",
     )
 
     *parts, beside = tie(*parts, beside)
-    node = merge_call(parts, merge_sets, dim, blocks, 1)
-    shift, stage_bits = sub_bits, min(2, bits - sub_bits)
-    parts = exchange(node, shift, stage_bits)
-
-    *parts, inner_across, forwarded, beside = tie(*parts, inner_across, forwarded, beside)
-    late = (late_base, by_edge, [inner_across, forwarded])
-    (beside,) = near_call([(1, beside_lists, beside_rows, beside)], late, dim, "near_beside")
+    node = level(parts, 2)
+    for bit in range(3, bits - 1):
+        node = level(exchange(node, bit, 1), bit)
+    parts = exchange(node, bits - 1, 1)
+    inner_across, forwarded, beside, node = tie(inner_across, forwarded, beside, node)
+    late_set = (late_base, by_edge, [inner_across, forwarded])
+    (beside,) = near_call(
+        [(1, beside_lists, beside_rows, beside)], [late_set], ((0, 0),), dim, "near_beside"
+    )
     given = exchange(beside, 0, 1)[1]
-    *parts, beside = tie(*parts, beside)
-    node = merge_call(parts, merge_sets, dim, blocks, shift)
-    shift += stage_bits
-    own, node = tie(own, node)
-    parts = exchange(node, shift, bits - shift)
-    (own,) = near_call([(0, near_lists, rows, own)], late, dim, "near_last")
+    (own,) = near_call([(0, near_lists, rows, own)], [late_set], ((0, 0),), dim, "near_last")
     *parts, own = tie(*parts, own)
     piece = skel // count
-    node = merge_call(parts, merge_sets, dim, blocks, shift, piece)
+    node = level(parts, bits - 1, piece)
     if piece:
         root = node.reshape(-1)
     else:

time: 85.5 us -> 84.8 us (level)
  the two profiles are of different devices: /device:TPU:5 before, /device:TPU:0 now
where the time goes in v2:
time: 84.8 us; the launch traced here: 83.5 us
  Pallas kernels  37.2 us (44%)
  starting transfers between devices  28.6 us (34%)
  waiting for transfers between devices  10.7 us (13%)
  local copies, waits for them, and re-layouts  4.58 us (5%)
  other arithmetic  1.56 us (2%)
    pallas_call x4, Pallas kernels, near_call(): pl.pallas_call(functools.partial(near_kernel, flips=flips, has_acc=tuple(...  22.2 us
    ppermute x8, starting transfers between devices, exchange(): lax.ppermute(x, axes, [(i, i ^ d << shift) for i in range(count)])  20.2 us
    ppermute x8, waiting for transfers between devices, exchange(): lax.ppermute(x, axes, [(i, i ^ d << shift) for i in range(count)])  8.49 us
    ppermute x4, starting transfers between devices, send(): return lax.ppermute(x, axes, pairs)  8.32 us
    pallas_call x1, Pallas kernels, local_tree_call(): pl.pallas_call(functools.partial(local_tree_kernel, dim=dim), in_specs=[p...  6.86 us
    pallas_call x5, Pallas kernels, merge_call(): pl.pallas_call(functools.partial(merge_kernel, dim=dim, blocks=blocks, sh...  5.57 us
    unnamed x14, local copies, waits for them, and re-layouts  4.58 us
    pallas_call x1, Pallas kernels, order_call(): pl.pallas_call(order_kernel, grid=(blocks // many,), in_specs=[pl.BlockSp...  2.65 us
  transfers between devices with their start and end apart: 12, of which 5 were waited for; matrix products, arithmetic and copies ran while one was open for 0% of the time, Pallas kernels for 39%

profile of v2, /device:TPU:0, one launch (start us, length us, event | category | flops | bytes accessed | tf_op | source)
XLA Modules:
  0.0 83.5 jit_solution(11624842804710918579)
XLA Ops:
  0.6 1.2 %copy-done.2 = bf16[4096,128]{1,0:T(8,128)(2,1)S(1)} copy-done((bf16[4096,128]{1,0:T(8,128)(2,1)S(1)}, bf16[4096,128]{1,0:T(8,128)(2,1)}, u32[]{:S(2)}) %copy-start.2) | copy-done | bytes 1048600
  1.9 1.0 %copy-done.3 = bf16[4096,64]{0,1:T(8,128)(2,1)S(1)} copy-done((bf16[4096,64]{0,1:T(8,128)(2,1)S(1)}, bf16[4096,64]{0,1:T(8,128)(2,1)}, u32[]{:S(2)}) %copy-start.3) | copy-done | bytes 524312
  3.6 2.6 %tree_order.1 = (bf16[8,832,128]{2,1,0:T(8,128)(2,1)S(1)}, bf16[8,512,128]{2,1,0:T(8,128)(2,1)S(1)}) custom-call(bf16[64,4096]{1,0:T(8,128)(2,1)S(1)} %bitcast.4, s32[8,1,512]{2,1,0:T(1,128)S(1)} %bitcast.5, bf16[4096,128]{1,0:T(8,128)(2,1)S(1)} %copy-done.2), custom_call_target="tpu_custom_call" | custom-call | flops 268435456 | bytes 5242880 | tf_op jit(solution)/shard_map/tree_order/pallas_call | solution.py:94
  6.3 5.0 %collective-permute-start.3 = (bf16[8,832,128]{2,1,0:T(8,128)(2,1)S(1)}, bf16[8,832,128]{2,1,0:T(8,128)(2,1)S(1)}, u32[]{:S(2)}, u32[]{:S(2)}) collective-permute-start(bf16[8,832,128]{2,1,0:T(8,128)(2,1)S(1)} %get-tuple-element.34.pack.refs_2_.refs_5_), channel_id=1, source_target_pairs={{3,1},{0,2},{7,5},{4,6},{11,9},{8,10},{15,13},{12,14},{19,17},{16,... | collective-permute-start | bytes 5111816 | tf_op jit(solution)/shard_map/ppermute | solution.py:398
  11.3 1.3 %collective-permute-start.4 = (bf16[8,832,128]{2,1,0:T(8,128)(2,1)S(1)}, bf16[8,832,128]{2,1,0:T(8,128)(2,1)S(1)}, u32[]{:S(2)}, u32[]{:S(2)}) collective-permute-start(bf16[8,832,128]{2,1,0:T(8,128)(2,1)S(1)} %get-tuple-element.34.pack.refs_2_.refs_5_), channel_id=1, source_target_pairs={{3,7},{7,11},{4,0},{11,15},{8,4},{15,19},{12,8},{19,23},{16,12},{2... | collective-permute-start | bytes 5111816 | tf_op jit(solution)/shard_map/ppermute | solution.py:398
  14.7 6.9 %local_tree.1.refs_0_ = f32[208,128]{1,0:T(8,128)S(1)} custom-call(bf16[8,832,128]{2,1,0:T(8,128)(2,1)S(1)} %get-tuple-element.34.pack.refs_2_.refs_5_, bf16[8,512,128]{2,1,0:T(8,128)(2,1)S(1)} %get-tuple-element.26.rows.refs_2_.refs_1_, s32[8,128]{1,0:T(8,128)S(1)} %copy-done.6, s32[255,128]{1,0:T(8,128)S(1)} %copy-done), custom_call_target="tpu_custom_call" | custom-call | flops 536870912 | bytes 3145728 | tf_op jit(solution)/shard_map/local_tree/pallas_call | solution.py:177
  21.7 1.2 %collective-permute-done.1.refs_1_ = f32[208,128]{1,0:T(8,128)S(1)} collective-permute-done((f32[208,128]{1,0:T(8,128)S(1)}, f32[208,128]{1,0:T(8,128)S(1)}, u32[]{:S(2)}, u32[]{:S(2)}) %collective-permute-start.1) | collective-permute-done | bytes 106528 | tf_op jit(solution)/shard_map/ppermute | solution.py:407
  24.0 1.7 %collective-permute-start.2 = (f32[208,128]{1,0:T(8,128)S(1)}, f32[208,128]{1,0:T(8,128)S(1)}, u32[]{:S(2)}, u32[]{:S(2)}) collective-permute-start(f32[208,128]{1,0:T(8,128)S(1)} %tree_merge.5.refs_0_), channel_id=1, source_target_pairs={{0,2},{1,3},{2,0},{3,1},{4,6},{5,7},{6,4},{7,5},{8,10},{9,11},{10,... | collective-permute-start | bytes 319496 | tf_op jit(solution)/shard_map/ppermute | solution.py:407
  25.7 3.7 %near_own.1.refs_4_ = f32[8,512,128]{2,1,0:T(8,128)S(1)} custom-call(s32[8,12]{1,0:T(8,128)S(1)} %collective-permute-done.refs_0_.refs_1_, bf16[8,512,128]{2,1,0:T(8,128)(2,1)S(1)} %collective-permute-done.5.refs_1_.refs_3_, bf16[8,832,128]{2,1,0:T(8,128)(2,1)S(1)} %get-tuple-element.34.pack.refs_2_.refs_5_), custom_call_target="tpu_custom_call" | custom-call | flops 1000 | bytes 1000 | tf_op jit(solution)/shard_map/near_own/pallas_call | solution.py:365
  29.4 3.4 %collective-permute-done.2.refs_1_ = f32[208,128]{1,0:T(8,128)S(1)} collective-permute-done((f32[208,128]{1,0:T(8,128)S(1)}, f32[208,128]{1,0:T(8,128)S(1)}, u32[]{:S(2)}, u32[]{:S(2)}) %collective-permute-start.2) | collective-permute-done | bytes 106528 | tf_op jit(solution)/shard_map/ppermute | solution.py:407
  32.8 2.2 %collective-permute-done.4.refs_6_ = bf16[8,832,128]{2,1,0:T(8,128)(2,1)S(1)} collective-permute-done((bf16[8,832,128]{2,1,0:T(8,128)(2,1)S(1)}, bf16[8,832,128]{2,1,0:T(8,128)(2,1)S(1)}, u32[]{:S(2)}, u32[]{:S(2)}) %collective-permute-start.4) | collective-permute-done | bytes 1703968 | tf_op jit(solution)/shard_map/ppermute | solution.py:398
  35.0 1.3 %collective-permute-start.9 = (bf16[8,832,128]{2,1,0:T(8,128)(2,1)S(1)}, bf16[8,832,128]{2,1,0:T(8,128)(2,1)S(1)}, u32[]{:S(2)}, u32[]{:S(2)}) collective-permute-start(bf16[8,832,128]{2,1,0:T(8,128)(2,1)S(1)} %get-tuple-element.34.pack.refs_2_.refs_5_), channel_id=1, source_target_pairs={{2,0},{1,3},{6,4},{5,7},{10,8},{9,11},{14,12},{13,15},{18,16},{17,... | collective-permute-start | bytes 5111816 | tf_op jit(solution)/shard_map/ppermute | solution.py:398
  37.0 1.0 %tree_merge.6.refs_0_ = f32[208,128]{1,0:T(8,128)S(1)} custom-call(f32[208,128]{1,0:T(8,128)S(1)} %tree_merge.5.refs_0_, f32[208,128]{1,0:T(8,128)S(1)} %collective-permute-done.2.refs_1_, s32[255,128]{1,0:T(8,128)S(1)} %copy-done.1), custom_call_target="tpu_custom_call" | custom-call | flops 67108864 | bytes 212992 | tf_op jit(solution)/shard_map/tree_merge/pallas_call | solution.py:251
  38.0 2.5 %collective-permute-start.6 = (f32[208,128]{1,0:T(8,128)S(1)}, f32[208,128]{1,0:T(8,128)S(1)}, u32[]{:S(2)}, u32[]{:S(2)}) collective-permute-start(f32[208,128]{1,0:T(8,128)S(1)} %tree_merge.6.refs_0_), channel_id=1, source_target_pairs={{0,4},{1,5},{2,6},{3,7},{4,0},{5,1},{6,2},{7,3},{8,12},{9,13},{10,... | collective-permute-start | bytes 319496 | tf_op jit(solution)/shard_map/ppermute | solution.py:407
  40.5 11.5 %near_early.1 = (f32[8,512,128]{2,1,0:T(8,128)S(1)}, f32[8,512,128]{2,1,0:T(8,128)S(1)}) custom-call(s32[8,12]{1,0:T(8,128)S(1)} %copy-done.5, s32[8,12]{1,0:T(8,128)S(1)} %collective-permute-done.refs_0_.refs_1_, bf16[8,512,128]{2,1,0:T(8,128)(2,1)S(1)} %get-tuple-element.26.rows.refs_2_.refs_1_, ...), custom_call_target="tpu_custom_call" | custom-call | flops 1000 | bytes 1000 | tf_op jit(solution)/shard_map/near_early/pallas_call | solution.py:365
  52.1 1.0 %tree_merge.7.refs_0_ = f32[208,128]{1,0:T(8,128)S(1)} custom-call(f32[208,128]{1,0:T(8,128)S(1)} %tree_merge.6.refs_0_, f32[208,128]{1,0:T(8,128)S(1)} %collective-permute-done.6.refs_1_, s32[255,128]{1,0:T(8,128)S(1)} %copy-done.1), custom_call_target="tpu_custom_call" | custom-call | flops 67108864 | bytes 212992 | tf_op jit(solution)/shard_map/tree_merge/pallas_call | solution.py:251
  53.0 11.9 %collective-permute-start.7 = (f32[208,128]{1,0:T(8,128)S(1)}, f32[208,128]{1,0:T(8,128)S(1)}, u32[]{:S(2)}, u32[]{:S(2)}) collective-permute-start(f32[208,128]{1,0:T(8,128)S(1)} %tree_merge.7.refs_0_), channel_id=1, source_target_pairs={{0,8},{1,9},{2,10},{3,11},{4,12},{5,13},{6,14},{7,15},{8,0},{9,1},... | collective-permute-start | bytes 319496 | tf_op jit(solution)/shard_map/ppermute | solution.py:407
  64.9 3.2 %collective-permute-done.7.refs_1_ = f32[208,128]{1,0:T(8,128)S(1)} collective-permute-done((f32[208,128]{1,0:T(8,128)S(1)}, f32[208,128]{1,0:T(8,128)S(1)}, u32[]{:S(2)}, u32[]{:S(2)}) %collective-permute-start.7) | collective-permute-done | bytes 106528 | tf_op jit(solution)/shard_map/ppermute | solution.py:407
  68.2 1.0 %tree_merge.8.refs_0_ = f32[208,128]{1,0:T(8,128)S(1)} custom-call(f32[208,128]{1,0:T(8,128)S(1)} %tree_merge.7.refs_0_, f32[208,128]{1,0:T(8,128)S(1)} %collective-permute-done.7.refs_1_, s32[255,128]{1,0:T(8,128)S(1)} %copy-done.1), custom_call_target="tpu_custom_call" | custom-call | flops 67108864 | bytes 212992 | tf_op jit(solution)/shard_map/tree_merge/pallas_call | solution.py:251
  69.2 1.9 %near_beside.1 = f32[8,512,128]{2,1,0:T(8,128)S(1)} custom-call(s32[8,12]{1,0:T(8,128)S(1)} %collective-permute-done.refs_0_.refs_1_, bf16[8,512,128]{2,1,0:T(8,128)(2,1)S(1)} %collective-permute-done.5.refs_1_.refs_3_, f32[8,512,128]{2,1,0:T(8,128)S(1)} %get-tuple-element.45.refs_2_, bf16[8,832,128]{2,1,0:T(8,128)(2,1)S(1)} %collective-permute-done.9.refs_3_, ...), custom_call_target="tpu_custom_call" | custom-call | flops 1000 | bytes 1000 | tf_op jit(solution)/shard_map/near_beside/pallas_call | solution.py:365
  71.2 3.4 %collective-permute-start.8 = (f32[208,128]{1,0:T(8,128)S(1)}, f32[208,128]{1,0:T(8,128)S(1)}, u32[]{:S(2)}, u32[]{:S(2)}) collective-permute-start(f32[208,128]{1,0:T(8,128)S(1)} %tree_merge.8.refs_0_), channel_id=1, source_target_pairs={{0,16},{1,17},{2,18},{3,19},{4,20},{5,21},{6,22},{7,23},{8,24},{9,... | collective-permute-start | bytes 319496 | tf_op jit(solution)/shard_map/ppermute | solution.py:407
  74.6 5.1 %near_last.1 = f32[8,512,128]{2,1,0:T(8,128)S(1)} custom-call(s32[8,12]{1,0:T(8,128)S(1)} %copy-done.5, bf16[8,512,128]{2,1,0:T(8,128)(2,1)S(1)} %get-tuple-element.26.rows.refs_2_.refs_1_, f32[8,512,128]{2,1,0:T(8,128)S(1)} %get-tuple-element.40.refs_2_, bf16[8,832,128]{2,1,0:T(8,128)(2,1)S(1)} %collective-permute-done.9.refs_3_, ...), custom_call_target="tpu_custom_call" | custom-call | flops 1000 | bytes 1000 | tf_op jit(solution)/shard_map/near_last/pallas_call | solution.py:365
  80.2 1.7 %tree_merge.9 = f32[4,128]{1,0:T(4,128)} custom-call(f32[208,128]{1,0:T(8,128)S(1)} %tree_merge.8.refs_0_, f32[208,128]{1,0:T(8,128)S(1)} %collective-permute-done.8.refs_1_, s32[255,128]{1,0:T(8,128)S(1)} %copy-done.1), custom_call_target="tpu_custom_call" | custom-call | flops 67108864 | bytes 212992 | tf_op jit(solution)/shard_map/tree_merge/pallas_call | solution.py:251
  81.9 1.6 %add_multiply_fusion = f32[8,512,128]{2,1,0:T(8,128)} fusion(f32[8,512,128]{2,1,0:T(8,128)S(1)} %near_last.1, f32[8,512,128]{2,1,0:T(8,128)S(1)} %collective-permute-done.11), kind=kLoop, calls=%fused_computation | loop fusion | flops 1048576 | bytes 6291456 | tf_op jit(solution)/shard_map/mul | solution.py:473
  (26 shorter events, 5.4 us)
Async XLA Ops:
  0.6 1.2 %copy-start.2 = (bf16[4096,128]{1,0:T(8,128)(2,1)S(1)}, bf16[4096,128]{1,0:T(8,128)(2,1)}, u32[]{:S(2)}) copy-start(bf16[4096,128]{1,0:T(8,128)(2,1)} %probes.1) | copy-start | bytes 3145732
  1.9 1.0 %copy-start.3 = (bf16[4096,64]{0,1:T(8,128)(2,1)S(1)}, bf16[4096,64]{0,1:T(8,128)(2,1)}, u32[]{:S(2)}) copy-start(bf16[4096,64]{0,1:T(8,128)(2,1)} %param.7) | copy-start | bytes 1572868
  2.9 0.7 copy-start.4
  6.3 26.5 %collective-permute-start.3 = (bf16[8,832,128]{2,1,0:T(8,128)(2,1)S(1)}, bf16[8,832,128]{2,1,0:T(8,128)(2,1)S(1)}, u32[]{:S(2)}, u32[]{:S(2)}) collective-permute-start(bf16[8,832,128]{2,1,0:T(8,128)(2,1)S(1)} %get-tuple-element.34.pack.refs_2_.refs_5_), channel_id=1, source_target_pairs={{3,1},{0,2},{7,5},{4,6},{11,9},{8,10},{15,13},{12,14},{19,17},{16,... | collective-permute-start | bytes 5111816 | tf_op jit(solution)/shard_map/ppermute | solution.py:398
  11.3 23.7 %collective-permute-start.4 = (bf16[8,832,128]{2,1,0:T(8,128)(2,1)S(1)}, bf16[8,832,128]{2,1,0:T(8,128)(2,1)S(1)}, u32[]{:S(2)}, u32[]{:S(2)}) collective-permute-start(bf16[8,832,128]{2,1,0:T(8,128)(2,1)S(1)} %get-tuple-element.34.pack.refs_2_.refs_5_), channel_id=1, source_target_pairs={{3,7},{7,11},{4,0},{11,15},{8,4},{15,19},{12,8},{19,23},{16,12},{2... | collective-permute-start | bytes 5111816 | tf_op jit(solution)/shard_map/ppermute | solution.py:398
  12.6 13.1 %collective-permute-start.5 = (bf16[8,512,128]{2,1,0:T(8,128)(2,1)S(1)}, bf16[8,512,128]{2,1,0:T(8,128)(2,1)S(1)}, u32[]{:S(2)}, u32[]{:S(2)}) collective-permute-start(bf16[8,512,128]{2,1,0:T(8,128)(2,1)S(1)} %get-tuple-element.26.rows.refs_2_.refs_1_), channel_id=1, source_target_pairs={{0,1},{1,0},{2,3},{3,2},{4,5},{5,4},{6,7},{7,6},{8,9},{9,8},{10,11... | collective-permute-start | bytes 3145736 | tf_op jit(solution)/shard_map/ppermute | solution.py:407
  12.6 9.0 %collective-permute-start = (s32[8,12]{1,0:T(8,128)}, s32[8,12]{1,0:T(8,128)S(1)}, u32[]{:S(2)}, u32[]{:S(2)}) collective-permute-start(s32[8,12]{1,0:T(8,128)} %refs_0_.3), channel_id=1, source_target_pairs={{0,1},{1,0},{2,3},{3,2},{4,5},{5,4},{6,7},{7,6},{8,9},{9,8},{10,11... | collective-permute-start | bytes 1160 | tf_op jit(solution)/shard_map/ppermute | solution.py:407
  13.1 0.9 %copy-start = (s32[255,128]{1,0:T(8,128)S(1)}, s32[255,128]{1,0:T(8,128)}, u32[]{:S(2)}) copy-start(s32[255,128]{1,0:T(8,128)} %refs_2_.9) | copy-start | bytes 391684
  14.0 0.7 copy-start.6
  21.6 1.4 %collective-permute-start.1 = (f32[208,128]{1,0:T(8,128)S(1)}, f32[208,128]{1,0:T(8,128)S(1)}, u32[]{:S(2)}, u32[]{:S(2)}) collective-permute-start(f32[208,128]{1,0:T(8,128)S(1)} %local_tree.1.refs_0_), channel_id=1, source_target_pairs={{0,1},{1,0},{2,3},{3,2},{4,5},{5,4},{6,7},{7,6},{8,9},{9,8},{10,11... | collective-permute-start | bytes 319496 | tf_op jit(solution)/shard_map/ppermute | solution.py:407
  23.9 13.1 %copy-start.1 = (s32[255,128]{1,0:T(8,128)S(1)}, s32[255,128]{1,0:T(8,128)}, u32[]{:S(2)}) copy-start(s32[255,128]{1,0:T(8,128)} %refs_2_.9) | copy-start | bytes 391684
  24.0 16.5 %copy-start.5 = (s32[8,12]{1,0:T(8,128)S(1)}, s32[8,12]{1,0:T(8,128)}, u32[]{:S(2)}) copy-start(s32[8,12]{1,0:T(8,128)} %refs_0_.3) | copy-start | bytes 1156
  24.0 8.8 %collective-permute-start.2 = (f32[208,128]{1,0:T(8,128)S(1)}, f32[208,128]{1,0:T(8,128)S(1)}, u32[]{:S(2)}, u32[]{:S(2)}) collective-permute-start(f32[208,128]{1,0:T(8,128)S(1)} %tree_merge.5.refs_0_), channel_id=1, source_target_pairs={{0,2},{1,3},{2,0},{3,1},{4,6},{5,7},{6,4},{7,5},{8,10},{9,11},{10,... | collective-permute-start | bytes 319496 | tf_op jit(solution)/shard_map/ppermute | solution.py:407
  35.0 34.2 %collective-permute-start.9 = (bf16[8,832,128]{2,1,0:T(8,128)(2,1)S(1)}, bf16[8,832,128]{2,1,0:T(8,128)(2,1)S(1)}, u32[]{:S(2)}, u32[]{:S(2)}) collective-permute-start(bf16[8,832,128]{2,1,0:T(8,128)(2,1)S(1)} %get-tuple-element.34.pack.refs_2_.refs_5_), channel_id=1, source_target_pairs={{2,0},{1,3},{6,4},{5,7},{10,8},{9,11},{14,12},{13,15},{18,16},{17,... | collective-permute-start | bytes 5111816 | tf_op jit(solution)/shard_map/ppermute | solution.py:398
  36.3 32.9 %collective-permute-start.10 = (bf16[8,832,128]{2,1,0:T(8,128)(2,1)S(1)}, bf16[8,832,128]{2,1,0:T(8,128)(2,1)S(1)}, u32[]{:S(2)}, u32[]{:S(2)}) collective-permute-start(bf16[8,832,128]{2,1,0:T(8,128)(2,1)S(1)} %collective-permute-done.3.refs_7_), channel_id=1, source_target_pairs={{1,5},{5,9},{6,2},{9,13},{10,6},{13,17},{14,10},{17,21},{18,14},{2... | collective-permute-start | bytes 5111816 | tf_op jit(solution)/shard_map/ppermute | solution.py:398
  38.0 14.0 %collective-permute-start.6 = (f32[208,128]{1,0:T(8,128)S(1)}, f32[208,128]{1,0:T(8,128)S(1)}, u32[]{:S(2)}, u32[]{:S(2)}) collective-permute-start(f32[208,128]{1,0:T(8,128)S(1)} %tree_merge.6.refs_0_), channel_id=1, source_target_pairs={{0,4},{1,5},{2,6},{3,7},{4,0},{5,1},{6,2},{7,3},{8,12},{9,13},{10,... | collective-permute-start | bytes 319496 | tf_op jit(solution)/shard_map/ppermute | solution.py:407
  53.0 15.1 %collective-permute-start.7 = (f32[208,128]{1,0:T(8,128)S(1)}, f32[208,128]{1,0:T(8,128)S(1)}, u32[]{:S(2)}, u32[]{:S(2)}) collective-permute-start(f32[208,128]{1,0:T(8,128)S(1)} %tree_merge.7.refs_0_), channel_id=1, source_target_pairs={{0,8},{1,9},{2,10},{3,11},{4,12},{5,13},{6,14},{7,15},{8,0},{9,1},... | collective-permute-start | bytes 319496 | tf_op jit(solution)/shard_map/ppermute | solution.py:407
  71.1 10.8 %collective-permute-start.11 = (f32[8,512,128]{2,1,0:T(8,128)S(1)}, f32[8,512,128]{2,1,0:T(8,128)S(1)}, u32[]{:S(2)}, u32[]{:S(2)}) collective-permute-start(f32[8,512,128]{2,1,0:T(8,128)S(1)} %near_beside.1), channel_id=1, source_target_pairs={{0,1},{1,0},{2,3},{3,2},{4,5},{5,4},{6,7},{7,6},{8,9},{9,8},{10,11... | collective-permute-start | bytes 6291464 | tf_op jit(solution)/shard_map/ppermute | solution.py:407
  71.2 9.1 %collective-permute-start.8 = (f32[208,128]{1,0:T(8,128)S(1)}, f32[208,128]{1,0:T(8,128)S(1)}, u32[]{:S(2)}, u32[]{:S(2)}) collective-permute-start(f32[208,128]{1,0:T(8,128)S(1)} %tree_merge.8.refs_0_), channel_id=1, source_target_pairs={{0,16},{1,17},{2,18},{3,19},{4,20},{5,21},{6,22},{7,23},{8,24},{9,... | collective-permute-start | bytes 319496 | tf_op jit(solution)/shard_map/ppermute | solution.py:407

commit v3 on v2

--- a/solution.py
+++ b/solution.py
@@ -70,7 +70,7 @@
     return dot(m_hi, s_hi) + (dot(m_hi, s_lo) + dot(m_lo, s_hi))
 
 
-def order_kernel(points_t, order, probes, pack, rows):
+def order_kernel(points_t, order, probes, pack, rows, *halves):
     dim = points_t.shape[0]
     many, leaf = rows.shape[:2]
     held = dim + 16
@@ -84,13 +84,18 @@
             pack[b, leaf + i * held : leaf + (i + 1) * held, :] = form[:, i * LANES : (i + 1) * LANES]
         form = jnp.concatenate([form, jnp.zeros((LANES - held, leaf), BF16)], axis=0)
         rows[b] = dot_t(form, to_rows).astype(BF16)
+    for step, half in enumerate(halves):
+
+        @pl.when(pl.program_id(0) == step)
+        def _(half=half):
+            half[...] = pack[...]
 
 
 def order_call(points_t, order, probes, blocks):
     dim, npts = points_t.shape
     leaf = npts // blocks
     packed = leaf + leaf // LANES * (dim + 16)
-    many = 4 if blocks % 4 == 0 else 1
+    many = blocks // 2
     return pl.pallas_call(
         order_kernel,
         grid=(blocks // many,),
@@ -102,10 +107,14 @@
         out_specs=[
             pl.BlockSpec((many, packed, LANES), lambda b: (b, 0, 0)),
             pl.BlockSpec((many, leaf, LANES), lambda b: (b, 0, 0)),
+            pl.BlockSpec((many, packed, LANES), lambda b: (0, 0, 0)),
+            pl.BlockSpec((many, packed, LANES), lambda b: (0, 0, 0)),
         ],
         out_shape=[
             jax.ShapeDtypeStruct((blocks, packed, LANES), BF16),
             jax.ShapeDtypeStruct((blocks, leaf, LANES), BF16),
+            jax.ShapeDtypeStruct((many, packed, LANES), BF16),
+            jax.ShapeDtypeStruct((many, packed, LANES), BF16),
         ],
         compiler_params=pltpu.CompilerParams(vmem_limit_bytes=VMEM_BYTES),
         cost_estimate=pl.CostEstimate(
@@ -278,7 +287,7 @@
 
     lists, rows = take(len(flips)), take(len(flips))
     accs = [take(1)[0] if has else None for has in has_acc]
-    buffers = [take(max(which) + 1) for _, which in sets]
+    buffers = [take(max(which) + 1) for _, _, which in sets]
     outs, (pair_list,) = take(len(flips)), refs
     blocks, leaf = rows[0].shape[:2]
     near = lists[0].shape[1]
@@ -297,17 +306,18 @@
     for j, flip in enumerate(flips):
         mine = [t for t, (_, group) in enumerate(tasks) if group == j]
         firsts = [window_first + place(sets[tasks[t][0]][0]) for t in mine]
+        sizes = [place(sets[tasks[t][0]][1]) for t in mine]
         target_first = lax.axis_index("leaf") * window + (sub ^ flip) * blocks
 
-        def list_block(g, counts, j=j, mine=mine, firsts=firsts, target_first=target_first):
+        def list_block(g, counts, j=j, mine=mine, firsts=firsts, sizes=sizes, target_first=target_first):
             for s in range(near):
                 source = lists[j][g, s]
                 used = (source != target_first + g) if s else True
                 after = []
-                for t, first, count in zip(mine, firsts, counts):
+                for t, first, size, count in zip(mine, firsts, sizes, counts):
                     local = source - first
                     pair_list[t * stride + count] = g * blocks + local
-                    inside = (local >= 0) & (local < blocks) & used
+                    inside = (local >= 0) & (local < size) & used
                     after.append(count + jnp.where(inside, 1, 0))
                 counts = tuple(after)
             return counts
@@ -348,7 +358,7 @@
             outs[j][g] += total
 
     for t, (number, _) in enumerate(tasks):
-        held = place(sets[number][1])
+        held = place(sets[number][2])
         for k, buffer in enumerate(buffers[number]):
             pairs = found[t] if len(buffers[number]) == 1 else jnp.where(held == k, found[t], 0)
             add_all(buffer, t, pairs)
@@ -358,7 +368,7 @@
     flips, lists, rows, accs = zip(*groups)
     blocks, leaf = rows[0].shape[:2]
     held = [acc for acc in accs if acc is not None]
-    args = [*lists, *rows, *held, *(b for _, _, buffers in sources for b in buffers)]
+    args = [*lists, *rows, *held, *(b for *_, buffers in sources for b in buffers)]
     smem = pl.BlockSpec(memory_space=pltpu.SMEM)
     vmem = pl.BlockSpec(memory_space=pltpu.VMEM)
     near = lists[0].shape[1]
@@ -367,7 +377,7 @@
             near_kernel,
             flips=flips,
             has_acc=tuple(acc is not None for acc in accs),
-            sets=tuple((bases, which) for bases, which, _ in sources),
+            sets=tuple(source[:3] for source in sources),
             tasks=tasks,
             dim=dim,
         ),
@@ -410,43 +420,50 @@
     def tie(*values):
         return lax.optimization_barrier(values)
 
-    b = blocks
+    b, h = blocks, blocks // 2
     own_base = (b, 2 * b, 3 * b, 4 * b)
-    early_base, late_base = (5 * b, 4 * b, b, 0), (3 * b, 0, 5 * b, 2 * b)
+    early_base, late_base = (5 * b, 4 * b, b, 0), (3 * b, h, 5 * b + h, 2 * b)
+    second_base, forwarded_base = (0, 4 * b + h, b + h, 0), (0, 0, 5 * b, 0)
+    whole, mixed, inner = (b, b, b, b), (b, h, h, b), (0, h, h, 0)
     single, by_edge = (0, 0, 0, 0), (0, 1, 1, 0)
 
-    pack, rows = order_call(points.T, order.reshape(blocks, 1, leaf), probes, blocks)
-    outer_across = send(pack, [(3, 0, 1), (0, 0, 2)])
+    def level(parts, bit, piece=None):
+        return merge_call(parts, merge_sets, dim, blocks, bit, piece)
+
+    pack, rows, *halves = order_call(points.T, order.reshape(blocks, 1, leaf), probes, blocks)
+    across = [send(half, [(3, 0, 1), (0, 0, 2)]) for half in halves]
     outer_next = send(pack, [(3, 1, 3), (0, -1, 0)])
     beside_rows = exchange(rows, 0, 1)[1]
     beside_lists = exchange(near_lists, 0, 1)[1]
 
     node = local_tree_call(pack, rows, leaf_sets, merge_sets, dim)
-    node, beside_lists = tie(node, beside_lists)
-
-    def level(parts, bit, piece=None):
-        return merge_call(parts, merge_sets, dim, blocks, bit, piece)
-
+    node, beside_lists, across[0] = tie(node, beside_lists, across[0])
+    forward = [(1, 1, 1), (2, -1, 2)]
+    forwarded = send(across[0], forward)
     node = level(exchange(node, 0, 1), 0)
     own_pack, node = tie(pack, node)
     parts = exchange(node, 1, 1)
-    own_set = (own_base, single, [own_pack])
+    own_set = (own_base, whole, single, [own_pack])
     (beside,) = near_call(
         [(1, beside_lists, beside_rows, None)], [own_set], ((0, 0),), dim, "near_own"
     )
 
-    *parts, outer_across, outer_next, own_pack, beside = tie(
-        *parts, outer_across, outer_next, own_pack, beside
-    )
-    forwarded = send(outer_across, [(1, 1, 1), (2, -1, 2)])
+    *parts, across[1], outer_next, forwarded, own_pack, beside = tie(
+        *parts, across[1], outer_next, forwarded, own_pack, beside
+    )
+    late_forwarded = send(across[1], forward)
     inner_across = send(own_pack, [(2, 0, 0), (1, 0, 3)])
     node = level(parts, 1)
     parts = exchange(node, 2, 1)
-    own_set = (own_base, single, [own_pack])
-    early_set = (early_base, by_edge, [outer_next, outer_across])
     own, beside = near_call(
         [(0, near_lists, rows, None), (1, beside_lists, beside_rows, beside)],
-        [own_set, early_set], ((0, 0), (1, 0), (1, 1)), dim, "near_early",
+        [
+            (own_base, whole, single, [own_pack]),
+            (early_base, mixed, by_edge, [outer_next, across[0]]),
+            (second_base, inner, single, [across[1]]),
+            (forwarded_base, inner, single, [forwarded]),
+        ],
+        ((0, 0), (1, 0), (2, 0), (3, 0), (1, 1), (2, 1), (3, 1)), dim, "near_early",
     )
 
     *parts, beside = tie(*parts, beside)
@@ -454,8 +471,8 @@
     for bit in range(3, bits - 1):
         node = level(exchange(node, bit, 1), bit)
     parts = exchange(node, bits - 1, 1)
-    inner_across, forwarded, beside, node = tie(inner_across, forwarded, beside, node)
-    late_set = (late_base, by_edge, [inner_across, forwarded])
+    inner_across, late_forwarded, beside, node = tie(inner_across, late_forwarded, beside, node)
+    late_set = (late_base, mixed, by_edge, [inner_across, late_forwarded])
     (beside,) = near_call(
         [(1, beside_lists, beside_rows, beside)], [late_set], ((0, 0),), dim, "near_beside"
     )

time: 84.8 us -> 87.3 us (1.029)
  the two profiles are of different devices: /device:TPU:0 before, /device:TPU:5 now
where the time goes in v3:
time: 87.3 us; the launch traced here: 88.4 us
  starting transfers between devices  34.2 us (39%)
  Pallas kernels  33.9 us (39%)
  waiting for transfers between devices  13.3 us (15%)
  local copies, waits for them, and re-layouts  4.57 us (5%)
  other arithmetic  1.65 us (2%)
  between operations  0.88 us (1%)
    ppermute x8, starting transfers between devices, exchange(): lax.ppermute(x, axes, [(i, i ^ d << shift) for i in range(count)])  24.3 us
    pallas_call x4, Pallas kernels, near_call(): pl.pallas_call(functools.partial(near_kernel, flips=flips, has_acc=tuple(...  18.7 us
    ppermute x6, starting transfers between devices, send(): return lax.ppermute(x, axes, pairs)  9.9 us
    ppermute x6, waiting for transfers between devices, send(): return lax.ppermute(x, axes, pairs)  8.52 us
    pallas_call x1, Pallas kernels, local_tree_call(): pl.pallas_call(functools.partial(local_tree_kernel, dim=dim), in_specs=[p...  6.86 us
    pallas_call x5, Pallas kernels, merge_call(): pl.pallas_call(functools.partial(merge_kernel, dim=dim, blocks=blocks, sh...  5.57 us
    ppermute x8, waiting for transfers between devices, exchange(): lax.ppermute(x, axes, [(i, i ^ d << shift) for i in range(count)])  4.79 us
    unnamed x14, local copies, waits for them, and re-layouts  4.57 us
  transfers between devices with their start and end apart: 14, of which 5 were waited for; matrix products, arithmetic and copies ran while one was open for 0% of the time, Pallas kernels for 32%

profile of v3, /device:TPU:5, one launch (start us, length us, event | category | flops | bytes accessed | tf_op | source)
XLA Modules:
  0.0 88.4 jit_solution(18128959198881536906)
XLA Ops:
  0.6 1.2 %copy-done.2 = bf16[4096,128]{1,0:T(8,128)(2,1)S(1)} copy-done((bf16[4096,128]{1,0:T(8,128)(2,1)S(1)}, bf16[4096,128]{1,0:T(8,128)(2,1)}, u32[]{:S(2)}) %copy-start.2) | copy-done | bytes 1048600
  1.9 1.0 %copy-done.3 = bf16[4096,64]{0,1:T(8,128)(2,1)S(1)} copy-done((bf16[4096,64]{0,1:T(8,128)(2,1)S(1)}, bf16[4096,64]{0,1:T(8,128)(2,1)}, u32[]{:S(2)}) %copy-start.3) | copy-done | bytes 524312
  3.6 2.7 %tree_order.1 = (bf16[8,832,128]{2,1,0:T(8,128)(2,1)S(1)}, bf16[8,512,128]{2,1,0:T(8,128)(2,1)S(1)}, bf16[4,832,128]{2,1,0:T(8,128)(2,1)S(1)}, bf16[4,832,128]{2,1,0:T(8,128)(2,1)S(1)}) custom-call(bf16[64,4096]{1,0:T(8,128)(2,1)S(1)} %bitcast.4, s32[8,1,512]{2,1,0:T(1,128)S(1)} %bitcast.5, bf16[4096,128]{1,0:T(8,128)(2,1)S(1)} %copy-done.2), custom_call_target="tpu_custom_call" | custom-call | flops 268435456 | bytes 5242880 | tf_op jit(solution)/shard_map/tree_order/pallas_call | solution.py:99
  6.3 1.4 %collective-permute-start.1 = (bf16[4,832,128]{2,1,0:T(8,128)(2,1)S(1)}, bf16[4,832,128]{2,1,0:T(8,128)(2,1)S(1)}, u32[]{:S(2)}, u32[]{:S(2)}) collective-permute-start(bf16[4,832,128]{2,1,0:T(8,128)(2,1)S(1)} %get-tuple-element.31), channel_id=1, source_target_pairs={{3,1},{0,2},{7,5},{4,6},{11,9},{8,10},{15,13},{12,14},{19,17},{16,... | collective-permute-start | bytes 2555912 | tf_op jit(solution)/shard_map/ppermute | solution.py:408
  7.7 4.1 %collective-permute-start.5 = (bf16[8,832,128]{2,1,0:T(8,128)(2,1)S(1)}, bf16[8,832,128]{2,1,0:T(8,128)(2,1)S(1)}, u32[]{:S(2)}, u32[]{:S(2)}) collective-permute-start(bf16[8,832,128]{2,1,0:T(8,128)(2,1)S(1)} %get-tuple-element.41.pack.refs_2_.refs_5_), channel_id=1, source_target_pairs={{3,7},{7,11},{4,0},{11,15},{8,4},{15,19},{12,8},{19,23},{16,12},{2... | collective-permute-start | bytes 5111816 | tf_op jit(solution)/shard_map/ppermute | solution.py:408
  12.3 1.8 %collective-permute-start.4 = (bf16[4,832,128]{2,1,0:T(8,128)(2,1)S(1)}, bf16[4,832,128]{2,1,0:T(8,128)(2,1)S(1)}, u32[]{:S(2)}, u32[]{:S(2)}) collective-permute-start(bf16[4,832,128]{2,1,0:T(8,128)(2,1)S(1)} %get-tuple-element.34), channel_id=1, source_target_pairs={{3,1},{0,2},{7,5},{4,6},{11,9},{8,10},{15,13},{12,14},{19,17},{16,... | collective-permute-start | bytes 2555912 | tf_op jit(solution)/shard_map/ppermute | solution.py:408
  15.7 6.9 %local_tree.1.refs_0_ = f32[208,128]{1,0:T(8,128)S(1)} custom-call(bf16[8,832,128]{2,1,0:T(8,128)(2,1)S(1)} %get-tuple-element.41.pack.refs_2_.refs_5_, bf16[8,512,128]{2,1,0:T(8,128)(2,1)S(1)} %get-tuple-element.30.rows.refs_2_.refs_1_, s32[8,128]{1,0:T(8,128)S(1)} %copy-done.6, s32[255,128]{1,0:T(8,128)S(1)} %copy-done), custom_call_target="tpu_custom_call" | custom-call | flops 536870912 | bytes 3145728 | tf_op jit(solution)/shard_map/local_tree/pallas_call | solution.py:186
  23.6 1.2 %collective-permute-done.2.refs_1_ = f32[208,128]{1,0:T(8,128)S(1)} collective-permute-done((f32[208,128]{1,0:T(8,128)S(1)}, f32[208,128]{1,0:T(8,128)S(1)}, u32[]{:S(2)}, u32[]{:S(2)}) %collective-permute-start.2) | collective-permute-done | bytes 106528 | tf_op jit(solution)/shard_map/ppermute | solution.py:417
  25.7 3.0 %collective-permute-start.3 = (f32[208,128]{1,0:T(8,128)S(1)}, f32[208,128]{1,0:T(8,128)S(1)}, u32[]{:S(2)}, u32[]{:S(2)}) collective-permute-start(f32[208,128]{1,0:T(8,128)S(1)} %tree_merge.5.refs_0_), channel_id=1, source_target_pairs={{0,2},{1,3},{2,0},{3,1},{4,6},{5,7},{6,4},{7,5},{8,10},{9,11},{10,... | collective-permute-start | bytes 319496 | tf_op jit(solution)/shard_map/ppermute | solution.py:417
  28.7 5.1 %near_own.1.refs_4_ = f32[8,512,128]{2,1,0:T(8,128)S(1)} custom-call(s32[8,12]{1,0:T(8,128)S(1)} %collective-permute-done.refs_0_.refs_1_, bf16[8,512,128]{2,1,0:T(8,128)(2,1)S(1)} %collective-permute-done.7.refs_1_.refs_3_, bf16[8,832,128]{2,1,0:T(8,128)(2,1)S(1)} %get-tuple-element.41.pack.refs_2_.refs_5_), custom_call_target="tpu_custom_call" | custom-call | flops 1000 | bytes 1000 | tf_op jit(solution)/shard_map/near_own/pallas_call | solution.py:375
  33.8 5.7 %collective-permute-done.5.refs_6_ = bf16[8,832,128]{2,1,0:T(8,128)(2,1)S(1)} collective-permute-done((bf16[8,832,128]{2,1,0:T(8,128)(2,1)S(1)}, bf16[8,832,128]{2,1,0:T(8,128)(2,1)S(1)}, u32[]{:S(2)}, u32[]{:S(2)}) %collective-permute-start.5) | collective-permute-done | bytes 1703968 | tf_op jit(solution)/shard_map/ppermute | solution.py:408
  39.5 1.3 %collective-permute-start.11 = (bf16[8,832,128]{2,1,0:T(8,128)(2,1)S(1)}, bf16[8,832,128]{2,1,0:T(8,128)(2,1)S(1)}, u32[]{:S(2)}, u32[]{:S(2)}) collective-permute-start(bf16[8,832,128]{2,1,0:T(8,128)(2,1)S(1)} %get-tuple-element.41.pack.refs_2_.refs_5_), channel_id=1, source_target_pairs={{2,0},{1,3},{6,4},{5,7},{10,8},{9,11},{14,12},{13,15},{18,16},{17,... | collective-permute-start | bytes 5111816 | tf_op jit(solution)/shard_map/ppermute | solution.py:408
  42.6 2.0 %collective-permute-start.8 = (f32[208,128]{1,0:T(8,128)S(1)}, f32[208,128]{1,0:T(8,128)S(1)}, u32[]{:S(2)}, u32[]{:S(2)}) collective-permute-start(f32[208,128]{1,0:T(8,128)S(1)} %tree_merge.6.refs_0_), channel_id=1, source_target_pairs={{0,4},{1,5},{2,6},{3,7},{4,0},{5,1},{6,2},{7,3},{8,12},{9,13},{10,... | collective-permute-start | bytes 319496 | tf_op jit(solution)/shard_map/ppermute | solution.py:417
  44.5 7.7 %near_early.1 = (f32[8,512,128]{2,1,0:T(8,128)S(1)}, f32[8,512,128]{2,1,0:T(8,128)S(1)}) custom-call(s32[8,12]{1,0:T(8,128)S(1)} %copy-done.4, s32[8,12]{1,0:T(8,128)S(1)} %collective-permute-done.refs_0_.refs_1_, bf16[8,512,128]{2,1,0:T(8,128)(2,1)S(1)} %get-tuple-element.30.rows.refs_2_.refs_1_, ...), custom_call_target="tpu_custom_call" | custom-call | flops 1000 | bytes 1000 | tf_op jit(solution)/shard_map/near_early/pallas_call | solution.py:375
  53.2 5.7 %collective-permute-start.9 = (f32[208,128]{1,0:T(8,128)S(1)}, f32[208,128]{1,0:T(8,128)S(1)}, u32[]{:S(2)}, u32[]{:S(2)}) collective-permute-start(f32[208,128]{1,0:T(8,128)S(1)} %tree_merge.7.refs_0_), channel_id=1, source_target_pairs={{0,8},{1,9},{2,10},{3,11},{4,12},{5,13},{6,14},{7,15},{8,0},{9,1},... | collective-permute-start | bytes 319496 | tf_op jit(solution)/shard_map/ppermute | solution.py:417
  58.9 2.1 %collective-permute-done.9.refs_1_ = f32[208,128]{1,0:T(8,128)S(1)} collective-permute-done((f32[208,128]{1,0:T(8,128)S(1)}, f32[208,128]{1,0:T(8,128)S(1)}, u32[]{:S(2)}, u32[]{:S(2)}) %collective-permute-start.9) | collective-permute-done | bytes 106528 | tf_op jit(solution)/shard_map/ppermute | solution.py:417
  61.9 2.8 %collective-permute-done.11.refs_3_ = bf16[8,832,128]{2,1,0:T(8,128)(2,1)S(1)} collective-permute-done((bf16[8,832,128]{2,1,0:T(8,128)(2,1)S(1)}, bf16[8,832,128]{2,1,0:T(8,128)(2,1)S(1)}, u32[]{:S(2)}, u32[]{:S(2)}) %collective-permute-start.11) | collective-permute-done | bytes 1703968 | tf_op jit(solution)/shard_map/ppermute | solution.py:408
  64.7 3.0 %near_beside.1 = f32[8,512,128]{2,1,0:T(8,128)S(1)} custom-call(s32[8,12]{1,0:T(8,128)S(1)} %collective-permute-done.refs_0_.refs_1_, bf16[8,512,128]{2,1,0:T(8,128)(2,1)S(1)} %collective-permute-done.7.refs_1_.refs_3_, f32[8,512,128]{2,1,0:T(8,128)S(1)} %get-tuple-element.53.refs_2_, bf16[8,832,128]{2,1,0:T(8,128)(2,1)S(1)} %collective-permute-done.11.refs_3_, ...), custom_call_target="tpu_custom_call" | custom-call | flops 1000 | bytes 1000 | tf_op jit(solution)/shard_map/near_beside/pallas_call | solution.py:375
  67.7 5.6 %collective-permute-start.13 = (f32[8,512,128]{2,1,0:T(8,128)S(1)}, f32[8,512,128]{2,1,0:T(8,128)S(1)}, u32[]{:S(2)}, u32[]{:S(2)}) collective-permute-start(f32[8,512,128]{2,1,0:T(8,128)S(1)} %near_beside.1), channel_id=1, source_target_pairs={{0,1},{1,0},{2,3},{3,2},{4,5},{5,4},{6,7},{7,6},{8,9},{9,8},{10,11... | collective-permute-start | bytes 6291464 | tf_op jit(solution)/shard_map/ppermute | solution.py:417
  73.3 7.2 %collective-permute-start.10 = (f32[208,128]{1,0:T(8,128)S(1)}, f32[208,128]{1,0:T(8,128)S(1)}, u32[]{:S(2)}, u32[]{:S(2)}) collective-permute-start(f32[208,128]{1,0:T(8,128)S(1)} %tree_merge.8.refs_0_), channel_id=1, source_target_pairs={{0,16},{1,17},{2,18},{3,19},{4,20},{5,21},{6,22},{7,23},{8,24},{9,... | collective-permute-start | bytes 319496 | tf_op jit(solution)/shard_map/ppermute | solution.py:417
  80.6 3.0 %near_last.1 = f32[8,512,128]{2,1,0:T(8,128)S(1)} custom-call(s32[8,12]{1,0:T(8,128)S(1)} %copy-done.4, bf16[8,512,128]{2,1,0:T(8,128)(2,1)S(1)} %get-tuple-element.30.rows.refs_2_.refs_1_, f32[8,512,128]{2,1,0:T(8,128)S(1)} %get-tuple-element.48.refs_2_, bf16[8,832,128]{2,1,0:T(8,128)(2,1)S(1)} %collective-permute-done.11.refs_3_, ...), custom_call_target="tpu_custom_call" | custom-call | flops 1000 | bytes 1000 | tf_op jit(solution)/shard_map/near_last/pallas_call | solution.py:375
  83.6 1.5 %collective-permute-done.10.refs_1_ = f32[208,128]{1,0:T(8,128)S(1)} collective-permute-done((f32[208,128]{1,0:T(8,128)S(1)}, f32[208,128]{1,0:T(8,128)S(1)}, u32[]{:S(2)}, u32[]{:S(2)}) %collective-permute-start.10) | collective-permute-done | bytes 106528 | tf_op jit(solution)/shard_map/ppermute | solution.py:417
  85.1 1.7 %tree_merge.9 = f32[4,128]{1,0:T(4,128)} custom-call(f32[208,128]{1,0:T(8,128)S(1)} %tree_merge.8.refs_0_, f32[208,128]{1,0:T(8,128)S(1)} %collective-permute-done.10.refs_1_, s32[255,128]{1,0:T(8,128)S(1)} %copy-done.1), custom_call_target="tpu_custom_call" | custom-call | flops 67108864 | bytes 212992 | tf_op jit(solution)/shard_map/tree_merge/pallas_call | solution.py:260
  86.8 1.6 %add_multiply_fusion = f32[8,512,128]{2,1,0:T(8,128)} fusion(f32[8,512,128]{2,1,0:T(8,128)S(1)} %near_last.1, f32[8,512,128]{2,1,0:T(8,128)S(1)} %collective-permute-done.13), kind=kLoop, calls=%fused_computation | loop fusion | flops 1048576 | bytes 6291456 | tf_op jit(solution)/shard_map/mul | solution.py:490
  (30 shorter events, 8.5 us)
Async XLA Ops:
  0.6 1.2 %copy-start.2 = (bf16[4096,128]{1,0:T(8,128)(2,1)S(1)}, bf16[4096,128]{1,0:T(8,128)(2,1)}, u32[]{:S(2)}) copy-start(bf16[4096,128]{1,0:T(8,128)(2,1)} %probes.1) | copy-start | bytes 3145732
  1.9 1.0 %copy-start.3 = (bf16[4096,64]{0,1:T(8,128)(2,1)S(1)}, bf16[4096,64]{0,1:T(8,128)(2,1)}, u32[]{:S(2)}) copy-start(bf16[4096,64]{0,1:T(8,128)(2,1)} %param.7) | copy-start | bytes 1572868
  2.9 0.7 copy-start.5
  6.3 16.3 %collective-permute-start.1 = (bf16[4,832,128]{2,1,0:T(8,128)(2,1)S(1)}, bf16[4,832,128]{2,1,0:T(8,128)(2,1)S(1)}, u32[]{:S(2)}, u32[]{:S(2)}) collective-permute-start(bf16[4,832,128]{2,1,0:T(8,128)(2,1)S(1)} %get-tuple-element.31), channel_id=1, source_target_pairs={{3,1},{0,2},{7,5},{4,6},{11,9},{8,10},{15,13},{12,14},{19,17},{16,... | collective-permute-start | bytes 2555912 | tf_op jit(solution)/shard_map/ppermute | solution.py:408
  7.7 31.8 %collective-permute-start.5 = (bf16[8,832,128]{2,1,0:T(8,128)(2,1)S(1)}, bf16[8,832,128]{2,1,0:T(8,128)(2,1)S(1)}, u32[]{:S(2)}, u32[]{:S(2)}) collective-permute-start(bf16[8,832,128]{2,1,0:T(8,128)(2,1)S(1)} %get-tuple-element.41.pack.refs_2_.refs_5_), channel_id=1, source_target_pairs={{3,7},{7,11},{4,0},{11,15},{8,4},{15,19},{12,8},{19,23},{16,12},{2... | collective-permute-start | bytes 5111816 | tf_op jit(solution)/shard_map/ppermute | solution.py:408
  11.8 16.9 %collective-permute-start.7 = (bf16[8,512,128]{2,1,0:T(8,128)(2,1)S(1)}, bf16[8,512,128]{2,1,0:T(8,128)(2,1)S(1)}, u32[]{:S(2)}, u32[]{:S(2)}) collective-permute-start(bf16[8,512,128]{2,1,0:T(8,128)(2,1)S(1)} %get-tuple-element.30.rows.refs_2_.refs_1_), channel_id=1, source_target_pairs={{0,1},{1,0},{2,3},{3,2},{4,5},{5,4},{6,7},{7,6},{8,9},{9,8},{10,11... | collective-permute-start | bytes 3145736 | tf_op jit(solution)/shard_map/ppermute | solution.py:417
  11.8 10.7 %collective-permute-start = (s32[8,12]{1,0:T(8,128)}, s32[8,12]{1,0:T(8,128)S(1)}, u32[]{:S(2)}, u32[]{:S(2)}) collective-permute-start(s32[8,12]{1,0:T(8,128)} %refs_0_.3), channel_id=1, source_target_pairs={{0,1},{1,0},{2,3},{3,2},{4,5},{5,4},{6,7},{7,6},{8,9},{9,8},{10,11... | collective-permute-start | bytes 1160 | tf_op jit(solution)/shard_map/ppermute | solution.py:417
  12.3 21.4 %collective-permute-start.4 = (bf16[4,832,128]{2,1,0:T(8,128)(2,1)S(1)}, bf16[4,832,128]{2,1,0:T(8,128)(2,1)S(1)}, u32[]{:S(2)}, u32[]{:S(2)}) collective-permute-start(bf16[4,832,128]{2,1,0:T(8,128)(2,1)S(1)} %get-tuple-element.34), channel_id=1, source_target_pairs={{3,1},{0,2},{7,5},{4,6},{11,9},{8,10},{15,13},{12,14},{19,17},{16,... | collective-permute-start | bytes 2555912 | tf_op jit(solution)/shard_map/ppermute | solution.py:408
  14.1 0.9 %copy-start = (s32[255,128]{1,0:T(8,128)S(1)}, s32[255,128]{1,0:T(8,128)}, u32[]{:S(2)}) copy-start(s32[255,128]{1,0:T(8,128)} %refs_2_.9) | copy-start | bytes 391684
  15.0 0.7 copy-start.6
  22.6 16.9 %collective-permute-start.6 = (bf16[4,832,128]{2,1,0:T(8,128)(2,1)S(1)}, bf16[4,832,128]{2,1,0:T(8,128)(2,1)S(1)}, u32[]{:S(2)}, u32[]{:S(2)}) collective-permute-start(bf16[4,832,128]{2,1,0:T(8,128)(2,1)S(1)} %collective-permute-done.1.refs_7_), channel_id=1, source_target_pairs={{1,5},{5,9},{6,2},{9,13},{10,6},{13,17},{14,10},{17,21},{18,14},{2... | collective-permute-start | bytes 2555912 | tf_op jit(solution)/shard_map/ppermute | solution.py:408
  23.3 1.4 %collective-permute-start.2 = (f32[208,128]{1,0:T(8,128)S(1)}, f32[208,128]{1,0:T(8,128)S(1)}, u32[]{:S(2)}, u32[]{:S(2)}) collective-permute-start(f32[208,128]{1,0:T(8,128)S(1)} %local_tree.1.refs_0_), channel_id=1, source_target_pairs={{0,1},{1,0},{2,3},{3,2},{4,5},{5,4},{6,7},{7,6},{8,9},{9,8},{10,11... | collective-permute-start | bytes 319496 | tf_op jit(solution)/shard_map/ppermute | solution.py:417
  25.7 15.9 %copy-start.1 = (s32[255,128]{1,0:T(8,128)S(1)}, s32[255,128]{1,0:T(8,128)}, u32[]{:S(2)}) copy-start(s32[255,128]{1,0:T(8,128)} %refs_2_.9) | copy-start | bytes 391684
  25.7 18.8 %copy-start.4 = (s32[8,12]{1,0:T(8,128)S(1)}, s32[8,12]{1,0:T(8,128)}, u32[]{:S(2)}) copy-start(s32[8,12]{1,0:T(8,128)} %refs_0_.3) | copy-start | bytes 1156
  25.7 8.1 %collective-permute-start.3 = (f32[208,128]{1,0:T(8,128)S(1)}, f32[208,128]{1,0:T(8,128)S(1)}, u32[]{:S(2)}, u32[]{:S(2)}) collective-permute-start(f32[208,128]{1,0:T(8,128)S(1)} %tree_merge.5.refs_0_), channel_id=1, source_target_pairs={{0,2},{1,3},{2,0},{3,1},{4,6},{5,7},{6,4},{7,5},{8,10},{9,11},{10,... | collective-permute-start | bytes 319496 | tf_op jit(solution)/shard_map/ppermute | solution.py:417
  39.5 25.2 %collective-permute-start.11 = (bf16[8,832,128]{2,1,0:T(8,128)(2,1)S(1)}, bf16[8,832,128]{2,1,0:T(8,128)(2,1)S(1)}, u32[]{:S(2)}, u32[]{:S(2)}) collective-permute-start(bf16[8,832,128]{2,1,0:T(8,128)(2,1)S(1)} %get-tuple-element.41.pack.refs_2_.refs_5_), channel_id=1, source_target_pairs={{2,0},{1,3},{6,4},{5,7},{10,8},{9,11},{14,12},{13,15},{18,16},{17,... | collective-permute-start | bytes 5111816 | tf_op jit(solution)/shard_map/ppermute | solution.py:408
  40.8 21.1 %collective-permute-start.12 = (bf16[4,832,128]{2,1,0:T(8,128)(2,1)S(1)}, bf16[4,832,128]{2,1,0:T(8,128)(2,1)S(1)}, u32[]{:S(2)}, u32[]{:S(2)}) collective-permute-start(bf16[4,832,128]{2,1,0:T(8,128)(2,1)S(1)} %collective-permute-done.4.refs_8_), channel_id=1, source_target_pairs={{1,5},{5,9},{6,2},{9,13},{10,6},{13,17},{14,10},{17,21},{18,14},{2... | collective-permute-start | bytes 2555912 | tf_op jit(solution)/shard_map/ppermute | solution.py:408
  42.6 9.6 %collective-permute-start.8 = (f32[208,128]{1,0:T(8,128)S(1)}, f32[208,128]{1,0:T(8,128)S(1)}, u32[]{:S(2)}, u32[]{:S(2)}) collective-permute-start(f32[208,128]{1,0:T(8,128)S(1)} %tree_merge.6.refs_0_), channel_id=1, source_target_pairs={{0,4},{1,5},{2,6},{3,7},{4,0},{5,1},{6,2},{7,3},{8,12},{9,13},{10,... | collective-permute-start | bytes 319496 | tf_op jit(solution)/shard_map/ppermute | solution.py:417
  53.2 7.8 %collective-permute-start.9 = (f32[208,128]{1,0:T(8,128)S(1)}, f32[208,128]{1,0:T(8,128)S(1)}, u32[]{:S(2)}, u32[]{:S(2)}) collective-permute-start(f32[208,128]{1,0:T(8,128)S(1)} %tree_merge.7.refs_0_), channel_id=1, source_target_pairs={{0,8},{1,9},{2,10},{3,11},{4,12},{5,13},{6,14},{7,15},{8,0},{9,1},... | collective-permute-start | bytes 319496 | tf_op jit(solution)/shard_map/ppermute | solution.py:417
  67.7 19.1 %collective-permute-start.13 = (f32[8,512,128]{2,1,0:T(8,128)S(1)}, f32[8,512,128]{2,1,0:T(8,128)S(1)}, u32[]{:S(2)}, u32[]{:S(2)}) collective-permute-start(f32[8,512,128]{2,1,0:T(8,128)S(1)} %near_beside.1), channel_id=1, source_target_pairs={{0,1},{1,0},{2,3},{3,2},{4,5},{5,4},{6,7},{7,6},{8,9},{9,8},{10,11... | collective-permute-start | bytes 6291464 | tf_op jit(solution)/shard_map/ppermute | solution.py:417
  73.3 11.7 %collective-permute-start.10 = (f32[208,128]{1,0:T(8,128)S(1)}, f32[208,128]{1,0:T(8,128)S(1)}, u32[]{:S(2)}, u32[]{:S(2)}) collective-permute-start(f32[208,128]{1,0:T(8,128)S(1)} %tree_merge.8.refs_0_), channel_id=1, source_target_pairs={{0,16},{1,17},{2,18},{3,19},{4,20},{5,21},{6,22},{7,23},{8,24},{9,... | collective-permute-start | bytes 319496 | tf_op jit(solution)/shard_map/ppermute | solution.py:417

commit v4 on v2

--- a/solution.py
+++ b/solution.py
@@ -81,7 +81,7 @@
         pack[b, :leaf, :] = probes[b * leaf : (b + 1) * leaf, :]
         form = jnp.concatenate([tree_t, square_rows(tree_t)], axis=0)
         for i in range(leaf // LANES):
-            pack[b, leaf + i * held : leaf + (i + 1) * held, :] = form[:, i * LANES : (i + 1) * LANES]
+            pack[b, leaf + i * dim : leaf + (i + 1) * dim, :] = tree_t[:, i * LANES : (i + 1) * LANES]
         form = jnp.concatenate([form, jnp.zeros((LANES - held, leaf), BF16)], axis=0)
         rows[b] = dot_t(form, to_rows).astype(BF16)
 
@@ -89,7 +89,7 @@
 def order_call(points_t, order, probes, blocks):
     dim, npts = points_t.shape
     leaf = npts // blocks
-    packed = leaf + leaf // LANES * (dim + 16)
+    packed = leaf + leaf // LANES * dim
     many = 4 if blocks % 4 == 0 else 1
     return pl.pallas_call(
         order_kernel,
@@ -116,12 +116,12 @@
 
 
 def form_of(pack_block, leaf, dim):
-    held = dim + 16
-    columns = [
-        pack_block[leaf + i * held : leaf + (i + 1) * held, :] for i in range(leaf // LANES)
-    ]
+    columns = []
+    for i in range(leaf // LANES):
+        pts = pack_block[leaf + i * dim : leaf + (i + 1) * dim, :]
+        columns.append(jnp.concatenate([pts, square_rows(pts)], axis=0))
     form = jnp.concatenate(columns, axis=1)
-    return jnp.concatenate([form, jnp.zeros((LANES - held, leaf), BF16)], axis=0)
+    return jnp.concatenate([form, jnp.zeros((LANES - dim - 16, leaf), BF16)], axis=0)
 
 
 def condense(form, a_rows, chosen):
@@ -438,10 +438,13 @@
     *parts, outer_across, outer_next, own_pack, beside = tie(
         *parts, outer_across, outer_next, own_pack, beside
     )
+    inner_across = send(own_pack, [(2, 0, 0), (1, 0, 3)])
+    for bit in range(1, bits - 1):
+        node = level(parts, bit)
+        parts = exchange(node, bit + 1, 1)
+    node = level(parts, bits - 1, skel // count)
+    outer_across, node = tie(outer_across, node)
     forwarded = send(outer_across, [(1, 1, 1), (2, -1, 2)])
-    inner_across = send(own_pack, [(2, 0, 0), (1, 0, 3)])
-    node = level(parts, 1)
-    parts = exchange(node, 2, 1)
     own_set = (own_base, single, [own_pack])
     early_set = (early_base, by_edge, [outer_next, outer_across])
     own, beside = near_call(
@@ -449,22 +452,14 @@
         [own_set, early_set], ((0, 0), (1, 0), (1, 1)), dim, "near_early",
     )
 
-    *parts, beside = tie(*parts, beside)
-    node = level(parts, 2)
-    for bit in range(3, bits - 1):
-        node = level(exchange(node, bit, 1), bit)
-    parts = exchange(node, bits - 1, 1)
-    inner_across, forwarded, beside, node = tie(inner_across, forwarded, beside, node)
+    inner_across, forwarded, beside = tie(inner_across, forwarded, beside)
     late_set = (late_base, by_edge, [inner_across, forwarded])
     (beside,) = near_call(
         [(1, beside_lists, beside_rows, beside)], [late_set], ((0, 0),), dim, "near_beside"
     )
     given = exchange(beside, 0, 1)[1]
     (own,) = near_call([(0, near_lists, rows, own)], [late_set], ((0, 0),), dim, "near_last")
-    *parts, own = tie(*parts, own)
-    piece = skel // count
-    node = level(parts, bits - 1, piece)
-    if piece:
+    if skel // count:
         root = node.reshape(-1)
     else:
         size = skel * LANES // count

time: 84.8 us -> 86.2 us (1.017)
  the two profiles are of different devices: /device:TPU:0 before, /device:TPU:29 now
where the time goes in v4:
time: 86.2 us; the launch traced here: 84.9 us
  Pallas kernels  33.9 us (39%)
  waiting for transfers between devices  22.6 us (26%)
  starting transfers between devices  21.3 us (25%)
  local copies, waits for them, and re-layouts  4.58 us (5%)
  other arithmetic  1.65 us (2%)
    pallas_call x4, Pallas kernels, near_call(): pl.pallas_call(functools.partial(near_kernel, flips=flips, has_acc=tuple(...  18.7 us
    ppermute x8, waiting for transfers between devices, exchange(): lax.ppermute(x, axes, [(i, i ^ d << shift) for i in range(count)])  17.1 us
    ppermute x8, starting transfers between devices, exchange(): lax.ppermute(x, axes, [(i, i ^ d << shift) for i in range(count)])  14.7 us
    pallas_call x1, Pallas kernels, local_tree_call(): pl.pallas_call(functools.partial(local_tree_kernel, dim=dim), in_specs=[p...  7.01 us
    ppermute x4, starting transfers between devices, send(): return lax.ppermute(x, axes, pairs)  6.55 us
    pallas_call x5, Pallas kernels, merge_call(): pl.pallas_call(functools.partial(merge_kernel, dim=dim, blocks=blocks, sh...  5.54 us
    ppermute x4, waiting for transfers between devices, send(): return lax.ppermute(x, axes, pairs)  5.53 us
    unnamed x14, local copies, waits for them, and re-layouts  4.58 us
  transfers between devices with their start and end apart: 12, of which 7 were waited for; matrix products, arithmetic and copies ran while one was open for 0% of the time, Pallas kernels for 30%

profile of v4, /device:TPU:29, one launch (start us, length us, event | category | flops | bytes accessed | tf_op | source)
XLA Modules:
  0.0 84.9 jit_solution(1840842907867562645)
XLA Ops:
  0.6 1.2 %copy-done.2 = bf16[4096,128]{1,0:T(8,128)(2,1)S(1)} copy-done((bf16[4096,128]{1,0:T(8,128)(2,1)S(1)}, bf16[4096,128]{1,0:T(8,128)(2,1)}, u32[]{:S(2)}) %copy-start.2) | copy-done | bytes 1048600
  1.9 1.0 %copy-done.3 = bf16[4096,64]{0,1:T(8,128)(2,1)S(1)} copy-done((bf16[4096,64]{0,1:T(8,128)(2,1)S(1)}, bf16[4096,64]{0,1:T(8,128)(2,1)}, u32[]{:S(2)}) %copy-start.3) | copy-done | bytes 524312
  3.6 2.6 %tree_order.1 = (bf16[8,768,128]{2,1,0:T(8,128)(2,1)S(1)}, bf16[8,512,128]{2,1,0:T(8,128)(2,1)S(1)}) custom-call(bf16[64,4096]{1,0:T(8,128)(2,1)S(1)} %bitcast.4, s32[8,1,512]{2,1,0:T(1,128)S(1)} %bitcast.5, bf16[4096,128]{1,0:T(8,128)(2,1)S(1)} %copy-done.2), custom_call_target="tpu_custom_call" | custom-call | flops 268435456 | bytes 5242880 | tf_op jit(solution)/shard_map/tree_order/pallas_call | solution.py:94
  6.3 3.1 %collective-permute-start.5 = (bf16[8,768,128]{2,1,0:T(8,128)(2,1)S(1)}, bf16[8,768,128]{2,1,0:T(8,128)(2,1)S(1)}, u32[]{:S(2)}, u32[]{:S(2)}) collective-permute-start(bf16[8,768,128]{2,1,0:T(8,128)(2,1)S(1)} %get-tuple-element.28.pack.refs_2_.refs_5_), channel_id=1, source_target_pairs={{3,7},{7,11},{4,0},{11,15},{8,4},{15,19},{12,8},{19,23},{16,12},{2... | collective-permute-start | bytes 4718600 | tf_op jit(solution)/shard_map/ppermute | solution.py:398
  9.4 1.4 %collective-permute-start.4 = (bf16[8,768,128]{2,1,0:T(8,128)(2,1)S(1)}, bf16[8,768,128]{2,1,0:T(8,128)(2,1)S(1)}, u32[]{:S(2)}, u32[]{:S(2)}) collective-permute-start(bf16[8,768,128]{2,1,0:T(8,128)(2,1)S(1)} %get-tuple-element.28.pack.refs_2_.refs_5_), channel_id=1, source_target_pairs={{3,1},{0,2},{7,5},{4,6},{11,9},{8,10},{15,13},{12,14},{19,17},{16,... | collective-permute-start | bytes 4718600 | tf_op jit(solution)/shard_map/ppermute | solution.py:398
  13.0 7.0 %local_tree.1.refs_0_ = f32[208,128]{1,0:T(8,128)S(1)} custom-call(bf16[8,768,128]{2,1,0:T(8,128)(2,1)S(1)} %get-tuple-element.28.pack.refs_2_.refs_5_, bf16[8,512,128]{2,1,0:T(8,128)(2,1)S(1)} %get-tuple-element.21.rows.refs_2_.refs_1_, s32[8,128]{1,0:T(8,128)S(1)} %copy-done.6, s32[255,128]{1,0:T(8,128)S(1)} %copy-done), custom_call_target="tpu_custom_call" | custom-call | flops 536870912 | bytes 3145728 | tf_op jit(solution)/shard_map/local_tree/pallas_call | solution.py:177
  20.1 1.2 %collective-permute-done.2.refs_1_ = f32[208,128]{1,0:T(8,128)S(1)} collective-permute-done((f32[208,128]{1,0:T(8,128)S(1)}, f32[208,128]{1,0:T(8,128)S(1)}, u32[]{:S(2)}, u32[]{:S(2)}) %collective-permute-start.2) | collective-permute-done | bytes 106528 | tf_op jit(solution)/shard_map/ppermute | solution.py:407
  21.4 1.0 %tree_merge.5.refs_0_ = f32[208,128]{1,0:T(8,128)S(1)} custom-call(f32[208,128]{1,0:T(8,128)S(1)} %local_tree.1.refs_0_, f32[208,128]{1,0:T(8,128)S(1)} %collective-permute-done.2.refs_1_, s32[255,128]{1,0:T(8,128)S(1)} %copy-done), custom_call_target="tpu_custom_call" | custom-call | flops 67108864 | bytes 212992 | tf_op jit(solution)/shard_map/tree_merge/pallas_call | solution.py:251
  23.1 3.1 %near_own.1.refs_4_ = f32[8,512,128]{2,1,0:T(8,128)S(1)} custom-call(s32[8,12]{1,0:T(8,128)S(1)} %collective-permute-done.refs_0_.refs_1_, bf16[8,512,128]{2,1,0:T(8,128)(2,1)S(1)} %collective-permute-done.1.refs_1_.refs_3_, bf16[8,768,128]{2,1,0:T(8,128)(2,1)S(1)} %get-tuple-element.28.pack.refs_2_.refs_5_), custom_call_target="tpu_custom_call" | custom-call | flops 1000 | bytes 1000 | tf_op jit(solution)/shard_map/near_own/pallas_call | solution.py:365
  26.2 4.1 %collective-permute-done.3.refs_1_ = f32[208,128]{1,0:T(8,128)S(1)} collective-permute-done((f32[208,128]{1,0:T(8,128)S(1)}, f32[208,128]{1,0:T(8,128)S(1)}, u32[]{:S(2)}, u32[]{:S(2)}) %collective-permute-start.3) | collective-permute-done | bytes 106528 | tf_op jit(solution)/shard_map/ppermute | solution.py:407
  30.3 1.0 %tree_merge.6.refs_0_ = f32[208,128]{1,0:T(8,128)S(1)} custom-call(f32[208,128]{1,0:T(8,128)S(1)} %tree_merge.5.refs_0_, f32[208,128]{1,0:T(8,128)S(1)} %collective-permute-done.3.refs_1_, s32[255,128]{1,0:T(8,128)S(1)} %copy-done.1), custom_call_target="tpu_custom_call" | custom-call | flops 67108864 | bytes 212992 | tf_op jit(solution)/shard_map/tree_merge/pallas_call | solution.py:251
  31.4 3.5 %collective-permute-done.6.refs_1_ = f32[208,128]{1,0:T(8,128)S(1)} collective-permute-done((f32[208,128]{1,0:T(8,128)S(1)}, f32[208,128]{1,0:T(8,128)S(1)}, u32[]{:S(2)}, u32[]{:S(2)}) %collective-permute-start.6) | collective-permute-done | bytes 106528 | tf_op jit(solution)/shard_map/ppermute | solution.py:407
  34.9 1.0 %tree_merge.7.refs_0_ = f32[208,128]{1,0:T(8,128)S(1)} custom-call(f32[208,128]{1,0:T(8,128)S(1)} %tree_merge.6.refs_0_, f32[208,128]{1,0:T(8,128)S(1)} %collective-permute-done.6.refs_1_, s32[255,128]{1,0:T(8,128)S(1)} %copy-done.1), custom_call_target="tpu_custom_call" | custom-call | flops 67108864 | bytes 212992 | tf_op jit(solution)/shard_map/tree_merge/pallas_call | solution.py:251
  36.2 3.4 %collective-permute-done.7.refs_1_ = f32[208,128]{1,0:T(8,128)S(1)} collective-permute-done((f32[208,128]{1,0:T(8,128)S(1)}, f32[208,128]{1,0:T(8,128)S(1)}, u32[]{:S(2)}, u32[]{:S(2)}) %collective-permute-start.7) | collective-permute-done | bytes 106528 | tf_op jit(solution)/shard_map/ppermute | solution.py:407
  39.5 1.0 %tree_merge.8.refs_0_ = f32[208,128]{1,0:T(8,128)S(1)} custom-call(f32[208,128]{1,0:T(8,128)S(1)} %tree_merge.7.refs_0_, f32[208,128]{1,0:T(8,128)S(1)} %collective-permute-done.7.refs_1_, s32[255,128]{1,0:T(8,128)S(1)} %copy-done.1), custom_call_target="tpu_custom_call" | custom-call | flops 67108864 | bytes 212992 | tf_op jit(solution)/shard_map/tree_merge/pallas_call | solution.py:251
  40.6 1.3 %collective-permute-start.9 = (bf16[8,768,128]{2,1,0:T(8,128)(2,1)S(1)}, bf16[8,768,128]{2,1,0:T(8,128)(2,1)S(1)}, u32[]{:S(2)}, u32[]{:S(2)}) collective-permute-start(bf16[8,768,128]{2,1,0:T(8,128)(2,1)S(1)} %get-tuple-element.28.pack.refs_2_.refs_5_), channel_id=1, source_target_pairs={{2,0},{1,3},{6,4},{5,7},{10,8},{9,11},{14,12},{13,15},{18,16},{17,... | collective-permute-start | bytes 4718600 | tf_op jit(solution)/shard_map/ppermute | solution.py:398
  41.9 4.1 %collective-permute-done.8.refs_1_ = f32[208,128]{1,0:T(8,128)S(1)} collective-permute-done((f32[208,128]{1,0:T(8,128)S(1)}, f32[208,128]{1,0:T(8,128)S(1)}, u32[]{:S(2)}, u32[]{:S(2)}) %collective-permute-start.8) | collective-permute-done | bytes 106528 | tf_op jit(solution)/shard_map/ppermute | solution.py:407
  46.1 1.7 %tree_merge.9 = f32[4,128]{1,0:T(4,128)} custom-call(f32[208,128]{1,0:T(8,128)S(1)} %tree_merge.8.refs_0_, f32[208,128]{1,0:T(8,128)S(1)} %collective-permute-done.8.refs_1_, s32[255,128]{1,0:T(8,128)S(1)} %copy-done.1), custom_call_target="tpu_custom_call" | custom-call | flops 67108864 | bytes 212992 | tf_op jit(solution)/shard_map/tree_merge/pallas_call | solution.py:251
  48.5 9.5 %near_early.1 = (f32[8,512,128]{2,1,0:T(8,128)S(1)}, f32[8,512,128]{2,1,0:T(8,128)S(1)}) custom-call(s32[8,12]{1,0:T(8,128)S(1)} %copy-done.4, s32[8,12]{1,0:T(8,128)S(1)} %collective-permute-done.refs_0_.refs_1_, bf16[8,512,128]{2,1,0:T(8,128)(2,1)S(1)} %get-tuple-element.21.rows.refs_2_.refs_1_, ...), custom_call_target="tpu_custom_call" | custom-call | flops 1000 | bytes 1000 | tf_op jit(solution)/shard_map/near_early/pallas_call | solution.py:365
  58.0 5.5 %collective-permute-done.9.refs_3_ = bf16[8,768,128]{2,1,0:T(8,128)(2,1)S(1)} collective-permute-done((bf16[8,768,128]{2,1,0:T(8,128)(2,1)S(1)}, bf16[8,768,128]{2,1,0:T(8,128)(2,1)S(1)}, u32[]{:S(2)}, u32[]{:S(2)}) %collective-permute-start.9) | collective-permute-done | bytes 1572896 | tf_op jit(solution)/shard_map/ppermute | solution.py:398
  63.5 3.1 %near_beside.1 = f32[8,512,128]{2,1,0:T(8,128)S(1)} custom-call(s32[8,12]{1,0:T(8,128)S(1)} %collective-permute-done.refs_0_.refs_1_, bf16[8,512,128]{2,1,0:T(8,128)(2,1)S(1)} %collective-permute-done.1.refs_1_.refs_3_, f32[8,512,128]{2,1,0:T(8,128)S(1)} %get-tuple-element.38.refs_2_, bf16[8,768,128]{2,1,0:T(8,128)(2,1)S(1)} %collective-permute-done.9.refs_3_, ...), custom_call_target="tpu_custom_call" | custom-call | flops 1000 | bytes 1000 | tf_op jit(solution)/shard_map/near_beside/pallas_call | solution.py:365
  66.6 12.8 %collective-permute-start.11 = (f32[8,512,128]{2,1,0:T(8,128)S(1)}, f32[8,512,128]{2,1,0:T(8,128)S(1)}, u32[]{:S(2)}, u32[]{:S(2)}) collective-permute-start(f32[8,512,128]{2,1,0:T(8,128)S(1)} %near_beside.1), channel_id=1, source_target_pairs={{0,1},{1,0},{2,3},{3,2},{4,5},{5,4},{6,7},{7,6},{8,9},{9,8},{10,11... | collective-permute-start | bytes 6291464 | tf_op jit(solution)/shard_map/ppermute | solution.py:407
  79.4 3.1 %near_last.1 = f32[8,512,128]{2,1,0:T(8,128)S(1)} custom-call(s32[8,12]{1,0:T(8,128)S(1)} %copy-done.4, bf16[8,512,128]{2,1,0:T(8,128)(2,1)S(1)} %get-tuple-element.21.rows.refs_2_.refs_1_, f32[8,512,128]{2,1,0:T(8,128)S(1)} %get-tuple-element.34.refs_2_, bf16[8,768,128]{2,1,0:T(8,128)(2,1)S(1)} %collective-permute-done.9.refs_3_, ...), custom_call_target="tpu_custom_call" | custom-call | flops 1000 | bytes 1000 | tf_op jit(solution)/shard_map/near_last/pallas_call | solution.py:365
  83.2 1.6 %add_multiply_fusion = f32[8,512,128]{2,1,0:T(8,128)} fusion(f32[8,512,128]{2,1,0:T(8,128)S(1)} %near_last.1, f32[8,512,128]{2,1,0:T(8,128)S(1)} %collective-permute-done.11), kind=kLoop, calls=%fused_computation | loop fusion | flops 1048576 | bytes 6291456 | tf_op jit(solution)/shard_map/mul | solution.py:468
  (26 shorter events, 5.7 us)
Async XLA Ops:
  0.6 1.2 %copy-start.2 = (bf16[4096,128]{1,0:T(8,128)(2,1)S(1)}, bf16[4096,128]{1,0:T(8,128)(2,1)}, u32[]{:S(2)}) copy-start(bf16[4096,128]{1,0:T(8,128)(2,1)} %probes.1) | copy-start | bytes 3145732
  1.9 1.0 %copy-start.3 = (bf16[4096,64]{0,1:T(8,128)(2,1)S(1)}, bf16[4096,64]{0,1:T(8,128)(2,1)}, u32[]{:S(2)}) copy-start(bf16[4096,64]{0,1:T(8,128)(2,1)} %param.7) | copy-start | bytes 1572868
  2.9 0.7 copy-start.5
  6.3 24.1 %collective-permute-start.5 = (bf16[8,768,128]{2,1,0:T(8,128)(2,1)S(1)}, bf16[8,768,128]{2,1,0:T(8,128)(2,1)S(1)}, u32[]{:S(2)}, u32[]{:S(2)}) collective-permute-start(bf16[8,768,128]{2,1,0:T(8,128)(2,1)S(1)} %get-tuple-element.28.pack.refs_2_.refs_5_), channel_id=1, source_target_pairs={{3,7},{7,11},{4,0},{11,15},{8,4},{15,19},{12,8},{19,23},{16,12},{2... | collective-permute-start | bytes 4718600 | tf_op jit(solution)/shard_map/ppermute | solution.py:398
  9.4 20.9 %collective-permute-start.4 = (bf16[8,768,128]{2,1,0:T(8,128)(2,1)S(1)}, bf16[8,768,128]{2,1,0:T(8,128)(2,1)S(1)}, u32[]{:S(2)}, u32[]{:S(2)}) collective-permute-start(bf16[8,768,128]{2,1,0:T(8,128)(2,1)S(1)} %get-tuple-element.28.pack.refs_2_.refs_5_), channel_id=1, source_target_pairs={{3,1},{0,2},{7,5},{4,6},{11,9},{8,10},{15,13},{12,14},{19,17},{16,... | collective-permute-start | bytes 4718600 | tf_op jit(solution)/shard_map/ppermute | solution.py:398
  10.8 12.3 %collective-permute-start.1 = (bf16[8,512,128]{2,1,0:T(8,128)(2,1)S(1)}, bf16[8,512,128]{2,1,0:T(8,128)(2,1)S(1)}, u32[]{:S(2)}, u32[]{:S(2)}) collective-permute-start(bf16[8,512,128]{2,1,0:T(8,128)(2,1)S(1)} %get-tuple-element.21.rows.refs_2_.refs_1_), channel_id=1, source_target_pairs={{0,1},{1,0},{2,3},{3,2},{4,5},{5,4},{6,7},{7,6},{8,9},{9,8},{10,11... | collective-permute-start | bytes 3145736 | tf_op jit(solution)/shard_map/ppermute | solution.py:407
  10.9 9.1 %collective-permute-start = (s32[8,12]{1,0:T(8,128)}, s32[8,12]{1,0:T(8,128)S(1)}, u32[]{:S(2)}, u32[]{:S(2)}) collective-permute-start(s32[8,12]{1,0:T(8,128)} %refs_0_.3), channel_id=1, source_target_pairs={{0,1},{1,0},{2,3},{3,2},{4,5},{5,4},{6,7},{7,6},{8,9},{9,8},{10,11... | collective-permute-start | bytes 1160 | tf_op jit(solution)/shard_map/ppermute | solution.py:407
  11.4 0.9 %copy-start = (s32[255,128]{1,0:T(8,128)S(1)}, s32[255,128]{1,0:T(8,128)}, u32[]{:S(2)}) copy-start(s32[255,128]{1,0:T(8,128)} %refs_2_.9) | copy-start | bytes 391684
  12.3 0.7 copy-start.6
  20.0 1.4 %collective-permute-start.2 = (f32[208,128]{1,0:T(8,128)S(1)}, f32[208,128]{1,0:T(8,128)S(1)}, u32[]{:S(2)}, u32[]{:S(2)}) collective-permute-start(f32[208,128]{1,0:T(8,128)S(1)} %local_tree.1.refs_0_), channel_id=1, source_target_pairs={{0,1},{1,0},{2,3},{3,2},{4,5},{5,4},{6,7},{7,6},{8,9},{9,8},{10,11... | collective-permute-start | bytes 319496 | tf_op jit(solution)/shard_map/ppermute | solution.py:407
  22.3 8.0 %copy-start.1 = (s32[255,128]{1,0:T(8,128)S(1)}, s32[255,128]{1,0:T(8,128)}, u32[]{:S(2)}) copy-start(s32[255,128]{1,0:T(8,128)} %refs_2_.9) | copy-start | bytes 391684
  22.3 26.2 %copy-start.4 = (s32[8,12]{1,0:T(8,128)S(1)}, s32[8,12]{1,0:T(8,128)}, u32[]{:S(2)}) copy-start(s32[8,12]{1,0:T(8,128)} %refs_0_.3) | copy-start | bytes 1156
  22.4 8.0 %collective-permute-start.3 = (f32[208,128]{1,0:T(8,128)S(1)}, f32[208,128]{1,0:T(8,128)S(1)}, u32[]{:S(2)}, u32[]{:S(2)}) collective-permute-start(f32[208,128]{1,0:T(8,128)S(1)} %tree_merge.5.refs_0_), channel_id=1, source_target_pairs={{0,2},{1,3},{2,0},{3,1},{4,6},{5,7},{6,4},{7,5},{8,10},{9,11},{10,... | collective-permute-start | bytes 319496 | tf_op jit(solution)/shard_map/ppermute | solution.py:407
  31.3 3.6 %collective-permute-start.6 = (f32[208,128]{1,0:T(8,128)S(1)}, f32[208,128]{1,0:T(8,128)S(1)}, u32[]{:S(2)}, u32[]{:S(2)}) collective-permute-start(f32[208,128]{1,0:T(8,128)S(1)} %tree_merge.6.refs_0_), channel_id=1, source_target_pairs={{0,4},{1,5},{2,6},{3,7},{4,0},{5,1},{6,2},{7,3},{8,12},{9,13},{10,... | collective-permute-start | bytes 319496 | tf_op jit(solution)/shard_map/ppermute | solution.py:407
  35.9 3.6 %collective-permute-start.7 = (f32[208,128]{1,0:T(8,128)S(1)}, f32[208,128]{1,0:T(8,128)S(1)}, u32[]{:S(2)}, u32[]{:S(2)}) collective-permute-start(f32[208,128]{1,0:T(8,128)S(1)} %tree_merge.7.refs_0_), channel_id=1, source_target_pairs={{0,8},{1,9},{2,10},{3,11},{4,12},{5,13},{6,14},{7,15},{8,0},{9,1},... | collective-permute-start | bytes 319496 | tf_op jit(solution)/shard_map/ppermute | solution.py:407
  40.5 5.6 %collective-permute-start.8 = (f32[208,128]{1,0:T(8,128)S(1)}, f32[208,128]{1,0:T(8,128)S(1)}, u32[]{:S(2)}, u32[]{:S(2)}) collective-permute-start(f32[208,128]{1,0:T(8,128)S(1)} %tree_merge.8.refs_0_), channel_id=1, source_target_pairs={{0,16},{1,17},{2,18},{3,19},{4,20},{5,21},{6,22},{7,23},{8,24},{9,... | collective-permute-start | bytes 319496 | tf_op jit(solution)/shard_map/ppermute | solution.py:407
  40.6 22.9 %collective-permute-start.9 = (bf16[8,768,128]{2,1,0:T(8,128)(2,1)S(1)}, bf16[8,768,128]{2,1,0:T(8,128)(2,1)S(1)}, u32[]{:S(2)}, u32[]{:S(2)}) collective-permute-start(bf16[8,768,128]{2,1,0:T(8,128)(2,1)S(1)} %get-tuple-element.28.pack.refs_2_.refs_5_), channel_id=1, source_target_pairs={{2,0},{1,3},{6,4},{5,7},{10,8},{9,11},{14,12},{13,15},{18,16},{17,... | collective-permute-start | bytes 4718600 | tf_op jit(solution)/shard_map/ppermute | solution.py:398
  47.7 15.8 %collective-permute-start.10 = (bf16[8,768,128]{2,1,0:T(8,128)(2,1)S(1)}, bf16[8,768,128]{2,1,0:T(8,128)(2,1)S(1)}, u32[]{:S(2)}, u32[]{:S(2)}) collective-permute-start(bf16[8,768,128]{2,1,0:T(8,128)(2,1)S(1)} %collective-permute-done.4.refs_7_), channel_id=1, source_target_pairs={{1,5},{5,9},{6,2},{9,13},{10,6},{13,17},{14,10},{17,21},{18,14},{2... | collective-permute-start | bytes 4718600 | tf_op jit(solution)/shard_map/ppermute | solution.py:398
  66.6 16.6 %collective-permute-start.11 = (f32[8,512,128]{2,1,0:T(8,128)S(1)}, f32[8,512,128]{2,1,0:T(8,128)S(1)}, u32[]{:S(2)}, u32[]{:S(2)}) collective-permute-start(f32[8,512,128]{2,1,0:T(8,128)S(1)} %near_beside.1), channel_id=1, source_target_pairs={{0,1},{1,0},{2,3},{3,2},{4,5},{5,4},{6,7},{7,6},{8,9},{9,8},{10,11... | collective-permute-start | bytes 6291464 | tf_op jit(solution)/shard_map/ppermute | solution.py:407

commit v5 on v4

--- a/solution.py
+++ b/solution.py
@@ -260,7 +260,7 @@
         ],
         compiler_params=pltpu.CompilerParams(vmem_limit_bytes=16 * 1024 * 1024),
         cost_estimate=pl.CostEstimate(
-            flops=count * 16 * LANES**3,
+            flops=count * 10**9,
             bytes_accessed=4 * count * size * LANES,
             transcendentals=2 * count * LANES**2,
         ),
@@ -427,9 +427,8 @@
     def level(parts, bit, piece=None):
         return merge_call(parts, merge_sets, dim, blocks, bit, piece)
 
-    node = level(exchange(node, 0, 1), 0)
     own_pack, node = tie(pack, node)
-    parts = exchange(node, 1, 1)
+    parts = exchange(node, 0, sub_bits)
     own_set = (own_base, single, [own_pack])
     (beside,) = near_call(
         [(1, beside_lists, beside_rows, None)], [own_set], ((0, 0),), dim, "near_own"
@@ -439,11 +438,12 @@
         *parts, outer_across, outer_next, own_pack, beside
     )
     inner_across = send(own_pack, [(2, 0, 0), (1, 0, 3)])
-    for bit in range(1, bits - 1):
-        node = level(parts, bit)
-        parts = exchange(node, bit + 1, 1)
-    node = level(parts, bits - 1, skel // count)
-    outer_across, node = tie(outer_across, node)
+    shift, stage = 0, sub_bits
+    while shift + stage < bits:
+        node = level(parts, shift)
+        shift, stage = shift + stage, min(3, bits - shift - stage)
+        parts = exchange(node, shift, stage)
+    outer_across, *parts = tie(outer_across, *parts)
     forwarded = send(outer_across, [(1, 1, 1), (2, -1, 2)])
     own_set = (own_base, single, [own_pack])
     early_set = (early_base, by_edge, [outer_next, outer_across])
@@ -452,7 +452,9 @@
         [own_set, early_set], ((0, 0), (1, 0), (1, 1)), dim, "near_early",
     )
 
-    inner_across, forwarded, beside = tie(inner_across, forwarded, beside)
+    inner_across, beside, *parts = tie(inner_across, beside, *parts)
+    node = level(parts, shift, skel // count)
+    forwarded, beside, node = tie(forwarded, beside, node)
     late_set = (late_base, by_edge, [inner_across, forwarded])
     (beside,) = near_call(
         [(1, beside_lists, beside_rows, beside)], [late_set], ((0, 0),), dim, "near_beside"

time: 86.2 us -> 96.4 us (1.12)
  the two profiles are of different devices: /device:TPU:29 before, /device:TPU:0 now
where the time goes in v5:
time: 96.4 us; the launch traced here: 96.7 us
  Pallas kernels  43.6 us (45%)
  starting transfers between devices  30.9 us (32%)
  waiting for transfers between devices  15.1 us (16%)
  local copies, waits for them, and re-layouts  4.58 us (5%)
  other arithmetic  1.65 us (2%)
    pallas_call x4, Pallas kernels, near_call(): pl.pallas_call(functools.partial(near_kernel, flips=flips, has_acc=tuple(...  26.3 us
    ppermute x13, starting transfers between devices, exchange(): lax.ppermute(x, axes, [(i, i ^ d << shift) for i in range(count)])  23.1 us
    ppermute x13, waiting for transfers between devices, exchange(): lax.ppermute(x, axes, [(i, i ^ d << shift) for i in range(count)])  15.1 us
    ppermute x4, starting transfers between devices, send(): return lax.ppermute(x, axes, pairs)  7.77 us
    pallas_call x2, Pallas kernels, merge_call(): pl.pallas_call(functools.partial(merge_kernel, dim=dim, blocks=blocks, sh...  7.67 us
    pallas_call x1, Pallas kernels, local_tree_call(): pl.pallas_call(functools.partial(local_tree_kernel, dim=dim), in_specs=[p...  7.01 us
    unnamed x14, local copies, waits for them, and re-layouts  4.58 us
    pallas_call x1, Pallas kernels, order_call(): pl.pallas_call(order_kernel, grid=(blocks // many,), in_specs=[pl.BlockSp...  2.64 us
  transfers between devices with their start and end apart: 17, of which 7 were waited for; matrix products, arithmetic and copies ran while one was open for 0% of the time, Pallas kernels for 39%

profile of v5, /device:TPU:0, one launch (start us, length us, event | category | flops | bytes accessed | tf_op | source)
XLA Modules:
  0.0 96.7 jit_solution(4528785653195202447)
XLA Ops:
  0.6 1.2 %copy-done = bf16[4096,128]{1,0:T(8,128)(2,1)S(1)} copy-done((bf16[4096,128]{1,0:T(8,128)(2,1)S(1)}, bf16[4096,128]{1,0:T(8,128)(2,1)}, u32[]{:S(2)}) %copy-start) | copy-done | bytes 1048600
  1.9 1.0 %copy-done.1 = bf16[4096,64]{0,1:T(8,128)(2,1)S(1)} copy-done((bf16[4096,64]{0,1:T(8,128)(2,1)S(1)}, bf16[4096,64]{0,1:T(8,128)(2,1)}, u32[]{:S(2)}) %copy-start.1) | copy-done | bytes 524312
  3.6 2.6 %tree_order.1 = (bf16[8,768,128]{2,1,0:T(8,128)(2,1)S(1)}, bf16[8,512,128]{2,1,0:T(8,128)(2,1)S(1)}) custom-call(bf16[64,4096]{1,0:T(8,128)(2,1)S(1)} %bitcast.4, s32[8,1,512]{2,1,0:T(1,128)S(1)} %bitcast.5, bf16[4096,128]{1,0:T(8,128)(2,1)S(1)} %copy-done), custom_call_target="tpu_custom_call" | custom-call | flops 268435456 | bytes 5242880 | tf_op jit(solution)/shard_map/tree_order/pallas_call | solution.py:94
  6.3 1.3 %collective-permute-start.6 = (bf16[8,768,128]{2,1,0:T(8,128)(2,1)S(1)}, bf16[8,768,128]{2,1,0:T(8,128)(2,1)S(1)}, u32[]{:S(2)}, u32[]{:S(2)}) collective-permute-start(bf16[8,768,128]{2,1,0:T(8,128)(2,1)S(1)} %get-tuple-element.47.pack.refs_2_.refs_5_), channel_id=1, source_target_pairs={{3,7},{7,11},{4,0},{11,15},{8,4},{15,19},{12,8},{19,23},{16,12},{2... | collective-permute-start | bytes 4718600 | tf_op jit(solution)/shard_map/ppermute | solution.py:398
  7.6 4.4 %collective-permute-start.5 = (bf16[8,768,128]{2,1,0:T(8,128)(2,1)S(1)}, bf16[8,768,128]{2,1,0:T(8,128)(2,1)S(1)}, u32[]{:S(2)}, u32[]{:S(2)}) collective-permute-start(bf16[8,768,128]{2,1,0:T(8,128)(2,1)S(1)} %get-tuple-element.47.pack.refs_2_.refs_5_), channel_id=1, source_target_pairs={{3,1},{0,2},{7,5},{4,6},{11,9},{8,10},{15,13},{12,14},{19,17},{16,... | collective-permute-start | bytes 4718600 | tf_op jit(solution)/shard_map/ppermute | solution.py:398
  14.2 7.0 %local_tree.1.refs_0_ = f32[208,128]{1,0:T(8,128)S(1)} custom-call(bf16[8,768,128]{2,1,0:T(8,128)(2,1)S(1)} %get-tuple-element.47.pack.refs_2_.refs_5_, bf16[8,512,128]{2,1,0:T(8,128)(2,1)S(1)} %get-tuple-element.40.rows.refs_2_.refs_1_, s32[8,128]{1,0:T(8,128)S(1)} %copy-done.6, s32[255,128]{1,0:T(8,128)S(1)} %copy-done.2), custom_call_target="tpu_custom_call" | custom-call | flops 536870912 | bytes 3145728 | tf_op jit(solution)/shard_map/local_tree/pallas_call | solution.py:177
  21.2 1.4 %collective-permute-start.4 = (f32[208,128]{1,0:T(8,128)S(1)}, f32[208,128]{1,0:T(8,128)S(1)}, u32[]{:S(2)}, u32[]{:S(2)}) collective-permute-start(f32[208,128]{1,0:T(8,128)S(1)} %local_tree.1.refs_0_), channel_id=1, source_target_pairs={{0,3},{1,2},{2,1},{3,0},{4,7},{5,6},{6,5},{7,4},{8,11},{9,10},{10,... | collective-permute-start | bytes 319496 | tf_op jit(solution)/shard_map/ppermute | solution.py:407
  23.2 4.1 %near_own.1.refs_4_ = f32[8,512,128]{2,1,0:T(8,128)S(1)} custom-call(s32[8,12]{1,0:T(8,128)S(1)} %collective-permute-done.refs_0_.refs_1_, bf16[8,512,128]{2,1,0:T(8,128)(2,1)S(1)} %collective-permute-done.1.refs_1_.refs_3_, bf16[8,768,128]{2,1,0:T(8,128)(2,1)S(1)} %get-tuple-element.47.pack.refs_2_.refs_5_), custom_call_target="tpu_custom_call" | custom-call | flops 1000 | bytes 1000 | tf_op jit(solution)/shard_map/near_own/pallas_call | solution.py:365
  27.3 7.4 %collective-permute-done.4.refs_3_ = f32[208,128]{1,0:T(8,128)S(1)} collective-permute-done((f32[208,128]{1,0:T(8,128)S(1)}, f32[208,128]{1,0:T(8,128)S(1)}, u32[]{:S(2)}, u32[]{:S(2)}) %collective-permute-start.4) | collective-permute-done | bytes 106528 | tf_op jit(solution)/shard_map/ppermute | solution.py:407
  34.7 1.3 %collective-permute-start.14 = (bf16[8,768,128]{2,1,0:T(8,128)(2,1)S(1)}, bf16[8,768,128]{2,1,0:T(8,128)(2,1)S(1)}, u32[]{:S(2)}, u32[]{:S(2)}) collective-permute-start(bf16[8,768,128]{2,1,0:T(8,128)(2,1)S(1)} %get-tuple-element.47.pack.refs_2_.refs_5_), channel_id=1, source_target_pairs={{2,0},{1,3},{6,4},{5,7},{10,8},{9,11},{14,12},{13,15},{18,16},{17,... | collective-permute-start | bytes 4718600 | tf_op jit(solution)/shard_map/ppermute | solution.py:398
  36.0 2.2 %tree_merge.2.refs_0_ = f32[208,128]{1,0:T(8,128)S(1)} custom-call(f32[208,128]{1,0:T(8,128)S(1)} %local_tree.1.refs_0_, f32[208,128]{1,0:T(8,128)S(1)} %collective-permute-done.2.refs_1_, f32[208,128]{1,0:T(8,128)S(1)} %collective-permute-done.3.refs_2_, f32[208,128]{1,0:T(8,128)S(1)} %collective-permute-done.4.refs_3_, s32[255,128]{1,0:T(8,128)S(1)} %copy-done.3), custom_call_target="tpu_custom_call" | custom-call | flops 4000000000 | bytes 425984 | tf_op jit(solution)/shard_map/tree_merge/pallas_call | solution.py:251
  38.3 4.3 %collective-permute-start.13 = (f32[208,128]{1,0:T(8,128)S(1)}, f32[208,128]{1,0:T(8,128)S(1)}, u32[]{:S(2)}, u32[]{:S(2)}) collective-permute-start(f32[208,128]{1,0:T(8,128)S(1)} %tree_merge.2.refs_0_), channel_id=1, source_target_pairs={{0,28},{1,29},{2,30},{3,31},{4,24},{5,25},{6,26},{7,27},{8,20},{9,... | collective-permute-start | bytes 319496 | tf_op jit(solution)/shard_map/ppermute | solution.py:407
  43.9 2.1 %collective-permute-start.10 = (f32[208,128]{1,0:T(8,128)S(1)}, f32[208,128]{1,0:T(8,128)S(1)}, u32[]{:S(2)}, u32[]{:S(2)}) collective-permute-start(f32[208,128]{1,0:T(8,128)S(1)} %tree_merge.2.refs_0_), channel_id=1, source_target_pairs={{0,16},{1,17},{2,18},{3,19},{4,20},{5,21},{6,22},{7,23},{8,24},{9,... | collective-permute-start | bytes 319496 | tf_op jit(solution)/shard_map/ppermute | solution.py:407
  46.7 9.8 %collective-permute-start.9 = (f32[208,128]{1,0:T(8,128)S(1)}, f32[208,128]{1,0:T(8,128)S(1)}, u32[]{:S(2)}, u32[]{:S(2)}) collective-permute-start(f32[208,128]{1,0:T(8,128)S(1)} %tree_merge.2.refs_0_), channel_id=1, source_target_pairs={{0,12},{1,13},{2,14},{3,15},{4,8},{5,9},{6,10},{7,11},{8,4},{9,5},... | collective-permute-start | bytes 319496 | tf_op jit(solution)/shard_map/ppermute | solution.py:407
  56.4 1.4 %collective-permute-start.8 = (f32[208,128]{1,0:T(8,128)S(1)}, f32[208,128]{1,0:T(8,128)S(1)}, u32[]{:S(2)}, u32[]{:S(2)}) collective-permute-start(f32[208,128]{1,0:T(8,128)S(1)} %tree_merge.2.refs_0_), channel_id=1, source_target_pairs={{0,8},{1,9},{2,10},{3,11},{4,12},{5,13},{6,14},{7,15},{8,0},{9,1},... | collective-permute-start | bytes 319496 | tf_op jit(solution)/shard_map/ppermute | solution.py:407
  57.8 1.6 %collective-permute-done.11.refs_5_ = f32[208,128]{1,0:T(8,128)S(1)} collective-permute-done((f32[208,128]{1,0:T(8,128)S(1)}, f32[208,128]{1,0:T(8,128)S(1)}, u32[]{:S(2)}, u32[]{:S(2)}) %collective-permute-start.11) | collective-permute-done | bytes 106528 | tf_op jit(solution)/shard_map/ppermute | solution.py:407
  59.4 1.7 %collective-permute-start.7 = (f32[208,128]{1,0:T(8,128)S(1)}, f32[208,128]{1,0:T(8,128)S(1)}, u32[]{:S(2)}, u32[]{:S(2)}) collective-permute-start(f32[208,128]{1,0:T(8,128)S(1)} %tree_merge.2.refs_0_), channel_id=1, source_target_pairs={{0,4},{1,5},{2,6},{3,7},{4,0},{5,1},{6,2},{7,3},{8,12},{9,13},{10,... | collective-permute-start | bytes 319496 | tf_op jit(solution)/shard_map/ppermute | solution.py:407
  61.9 2.4 %collective-permute-done.9.refs_3_ = f32[208,128]{1,0:T(8,128)S(1)} collective-permute-done((f32[208,128]{1,0:T(8,128)S(1)}, f32[208,128]{1,0:T(8,128)S(1)}, u32[]{:S(2)}, u32[]{:S(2)}) %collective-permute-start.9) | collective-permute-done | bytes 106528 | tf_op jit(solution)/shard_map/ppermute | solution.py:407
  64.4 2.0 %collective-permute-done.7.refs_1_ = f32[208,128]{1,0:T(8,128)S(1)} collective-permute-done((f32[208,128]{1,0:T(8,128)S(1)}, f32[208,128]{1,0:T(8,128)S(1)}, u32[]{:S(2)}, u32[]{:S(2)}) %collective-permute-start.7) | collective-permute-done | bytes 106528 | tf_op jit(solution)/shard_map/ppermute | solution.py:407
  67.2 12.9 %near_early.1 = (f32[8,512,128]{2,1,0:T(8,128)S(1)}, f32[8,512,128]{2,1,0:T(8,128)S(1)}) custom-call(s32[8,12]{1,0:T(8,128)S(1)} %copy-done.4, s32[8,12]{1,0:T(8,128)S(1)} %collective-permute-done.refs_0_.refs_1_, bf16[8,512,128]{2,1,0:T(8,128)(2,1)S(1)} %get-tuple-element.40.rows.refs_2_.refs_1_, ...), custom_call_target="tpu_custom_call" | custom-call | flops 1000 | bytes 1000 | tf_op jit(solution)/shard_map/near_early/pallas_call | solution.py:365
  80.1 5.4 %tree_merge.3 = f32[4,128]{1,0:T(4,128)} custom-call(f32[208,128]{1,0:T(8,128)S(1)} %tree_merge.2.refs_0_, f32[208,128]{1,0:T(8,128)S(1)} %collective-permute-done.7.refs_1_, f32[208,128]{1,0:T(8,128)S(1)} %collective-permute-done.8.refs_2_, f32[208,128]{1,0:T(8,128)S(1)} %collective-permute-done.9.refs_3_, f32[208,128]{1,0:T(8,128)S(1)} %collective-permute-done.10.refs_4_, ...), custom_call_target="tpu_custom_call" | custom-call | flops 8000000000 | bytes 851968 | tf_op jit(solution)/shard_map/tree_merge/pallas_call | solution.py:251
  85.6 3.4 %near_beside.1 = f32[8,512,128]{2,1,0:T(8,128)S(1)} custom-call(s32[8,12]{1,0:T(8,128)S(1)} %collective-permute-done.refs_0_.refs_1_, bf16[8,512,128]{2,1,0:T(8,128)(2,1)S(1)} %collective-permute-done.1.refs_1_.refs_3_, f32[8,512,128]{2,1,0:T(8,128)S(1)} %get-tuple-element.76.refs_2_, bf16[8,768,128]{2,1,0:T(8,128)(2,1)S(1)} %collective-permute-done.14.refs_3_, ...), custom_call_target="tpu_custom_call" | custom-call | flops 1000 | bytes 1000 | tf_op jit(solution)/shard_map/near_beside/pallas_call | solution.py:365
  89.0 6.0 %near_last.1 = f32[8,512,128]{2,1,0:T(8,128)S(1)} custom-call(s32[8,12]{1,0:T(8,128)S(1)} %copy-done.4, bf16[8,512,128]{2,1,0:T(8,128)(2,1)S(1)} %get-tuple-element.40.rows.refs_2_.refs_1_, f32[8,512,128]{2,1,0:T(8,128)S(1)} %get-tuple-element.55.refs_2_, bf16[8,768,128]{2,1,0:T(8,128)(2,1)S(1)} %collective-permute-done.14.refs_3_, ...), custom_call_target="tpu_custom_call" | custom-call | flops 1000 | bytes 1000 | tf_op jit(solution)/shard_map/near_last/pallas_call | solution.py:365
  95.0 1.6 %add_multiply_fusion = f32[8,512,128]{2,1,0:T(8,128)} fusion(f32[8,512,128]{2,1,0:T(8,128)S(1)} %near_last.1, f32[8,512,128]{2,1,0:T(8,128)S(1)} %collective-permute-done.16), kind=kLoop, calls=%fused_computation | loop fusion | flops 1048576 | bytes 6291456 | tf_op jit(solution)/shard_map/mul | solution.py:470
  (33 shorter events, 7.3 us)
Async XLA Ops:
  0.6 1.2 %copy-start = (bf16[4096,128]{1,0:T(8,128)(2,1)S(1)}, bf16[4096,128]{1,0:T(8,128)(2,1)}, u32[]{:S(2)}) copy-start(bf16[4096,128]{1,0:T(8,128)(2,1)} %probes.1) | copy-start | bytes 3145732
  1.9 1.0 %copy-start.1 = (bf16[4096,64]{0,1:T(8,128)(2,1)S(1)}, bf16[4096,64]{0,1:T(8,128)(2,1)}, u32[]{:S(2)}) copy-start(bf16[4096,64]{0,1:T(8,128)(2,1)} %param.7) | copy-start | bytes 1572868
  2.9 0.7 copy-start.5
  6.3 28.4 %collective-permute-start.6 = (bf16[8,768,128]{2,1,0:T(8,128)(2,1)S(1)}, bf16[8,768,128]{2,1,0:T(8,128)(2,1)S(1)}, u32[]{:S(2)}, u32[]{:S(2)}) collective-permute-start(bf16[8,768,128]{2,1,0:T(8,128)(2,1)S(1)} %get-tuple-element.47.pack.refs_2_.refs_5_), channel_id=1, source_target_pairs={{3,7},{7,11},{4,0},{11,15},{8,4},{15,19},{12,8},{19,23},{16,12},{2... | collective-permute-start | bytes 4718600 | tf_op jit(solution)/shard_map/ppermute | solution.py:398
  7.6 27.1 %collective-permute-start.5 = (bf16[8,768,128]{2,1,0:T(8,128)(2,1)S(1)}, bf16[8,768,128]{2,1,0:T(8,128)(2,1)S(1)}, u32[]{:S(2)}, u32[]{:S(2)}) collective-permute-start(bf16[8,768,128]{2,1,0:T(8,128)(2,1)S(1)} %get-tuple-element.47.pack.refs_2_.refs_5_), channel_id=1, source_target_pairs={{3,1},{0,2},{7,5},{4,6},{11,9},{8,10},{15,13},{12,14},{19,17},{16,... | collective-permute-start | bytes 4718600 | tf_op jit(solution)/shard_map/ppermute | solution.py:398
  12.0 11.0 %collective-permute-start.1 = (bf16[8,512,128]{2,1,0:T(8,128)(2,1)S(1)}, bf16[8,512,128]{2,1,0:T(8,128)(2,1)S(1)}, u32[]{:S(2)}, u32[]{:S(2)}) collective-permute-start(bf16[8,512,128]{2,1,0:T(8,128)(2,1)S(1)} %get-tuple-element.40.rows.refs_2_.refs_1_), channel_id=1, source_target_pairs={{0,1},{1,0},{2,3},{3,2},{4,5},{5,4},{6,7},{7,6},{8,9},{9,8},{10,11... | collective-permute-start | bytes 3145736 | tf_op jit(solution)/shard_map/ppermute | solution.py:407
  12.1 9.1 %collective-permute-start = (s32[8,12]{1,0:T(8,128)}, s32[8,12]{1,0:T(8,128)S(1)}, u32[]{:S(2)}, u32[]{:S(2)}) collective-permute-start(s32[8,12]{1,0:T(8,128)} %refs_0_.3), channel_id=1, source_target_pairs={{0,1},{1,0},{2,3},{3,2},{4,5},{5,4},{6,7},{7,6},{8,9},{9,8},{10,11... | collective-permute-start | bytes 1160 | tf_op jit(solution)/shard_map/ppermute | solution.py:407
  12.6 0.9 copy-start.2
  13.5 0.7 copy-start.6
  21.2 14.8 %copy-start.3 = (s32[255,128]{1,0:T(8,128)S(1)}, s32[255,128]{1,0:T(8,128)}, u32[]{:S(2)}) copy-start(s32[255,128]{1,0:T(8,128)} %refs_8_.1) | copy-start | bytes 391684
  21.2 13.5 %collective-permute-start.4 = (f32[208,128]{1,0:T(8,128)S(1)}, f32[208,128]{1,0:T(8,128)S(1)}, u32[]{:S(2)}, u32[]{:S(2)}) collective-permute-start(f32[208,128]{1,0:T(8,128)S(1)} %local_tree.1.refs_0_), channel_id=1, source_target_pairs={{0,3},{1,2},{2,1},{3,0},{4,7},{5,6},{6,5},{7,4},{8,11},{9,10},{10,... | collective-permute-start | bytes 319496 | tf_op jit(solution)/shard_map/ppermute | solution.py:407
  22.6 12.1 %collective-permute-start.3 = (f32[208,128]{1,0:T(8,128)S(1)}, f32[208,128]{1,0:T(8,128)S(1)}, u32[]{:S(2)}, u32[]{:S(2)}) collective-permute-start(f32[208,128]{1,0:T(8,128)S(1)} %local_tree.1.refs_0_), channel_id=1, source_target_pairs={{0,2},{1,3},{2,0},{3,1},{4,6},{5,7},{6,4},{7,5},{8,10},{9,11},{10,... | collective-permute-start | bytes 319496 | tf_op jit(solution)/shard_map/ppermute | solution.py:407
  23.0 11.7 %collective-permute-start.2 = (f32[208,128]{1,0:T(8,128)S(1)}, f32[208,128]{1,0:T(8,128)S(1)}, u32[]{:S(2)}, u32[]{:S(2)}) collective-permute-start(f32[208,128]{1,0:T(8,128)S(1)} %local_tree.1.refs_0_), channel_id=1, source_target_pairs={{0,1},{1,0},{2,3},{3,2},{4,5},{5,4},{6,7},{7,6},{8,9},{9,8},{10,11... | collective-permute-start | bytes 319496 | tf_op jit(solution)/shard_map/ppermute | solution.py:407
  27.2 40.0 %copy-start.4 = (s32[8,12]{1,0:T(8,128)S(1)}, s32[8,12]{1,0:T(8,128)}, u32[]{:S(2)}) copy-start(s32[8,12]{1,0:T(8,128)} %refs_0_.3) | copy-start | bytes 1156
  34.7 45.4 %collective-permute-start.14 = (bf16[8,768,128]{2,1,0:T(8,128)(2,1)S(1)}, bf16[8,768,128]{2,1,0:T(8,128)(2,1)S(1)}, u32[]{:S(2)}, u32[]{:S(2)}) collective-permute-start(bf16[8,768,128]{2,1,0:T(8,128)(2,1)S(1)} %get-tuple-element.47.pack.refs_2_.refs_5_), channel_id=1, source_target_pairs={{2,0},{1,3},{6,4},{5,7},{10,8},{9,11},{14,12},{13,15},{18,16},{17,... | collective-permute-start | bytes 4718600 | tf_op jit(solution)/shard_map/ppermute | solution.py:398
  38.3 8.4 %collective-permute-start.13 = (f32[208,128]{1,0:T(8,128)S(1)}, f32[208,128]{1,0:T(8,128)S(1)}, u32[]{:S(2)}, u32[]{:S(2)}) collective-permute-start(f32[208,128]{1,0:T(8,128)S(1)} %tree_merge.2.refs_0_), channel_id=1, source_target_pairs={{0,28},{1,29},{2,30},{3,31},{4,24},{5,25},{6,26},{7,27},{8,20},{9,... | collective-permute-start | bytes 319496 | tf_op jit(solution)/shard_map/ppermute | solution.py:407
  42.6 13.9 %collective-permute-start.12 = (f32[208,128]{1,0:T(8,128)S(1)}, f32[208,128]{1,0:T(8,128)S(1)}, u32[]{:S(2)}, u32[]{:S(2)}) collective-permute-start(f32[208,128]{1,0:T(8,128)S(1)} %tree_merge.2.refs_0_), channel_id=1, source_target_pairs={{0,24},{1,25},{2,26},{3,27},{4,28},{5,29},{6,30},{7,31},{8,16},{9,... | collective-permute-start | bytes 319496 | tf_op jit(solution)/shard_map/ppermute | solution.py:407
  43.1 16.3 %collective-permute-start.11 = (f32[208,128]{1,0:T(8,128)S(1)}, f32[208,128]{1,0:T(8,128)S(1)}, u32[]{:S(2)}, u32[]{:S(2)}) collective-permute-start(f32[208,128]{1,0:T(8,128)S(1)} %tree_merge.2.refs_0_), channel_id=1, source_target_pairs={{0,20},{1,21},{2,22},{3,23},{4,16},{5,17},{6,18},{7,19},{8,28},{9,... | collective-permute-start | bytes 319496 | tf_op jit(solution)/shard_map/ppermute | solution.py:407
  43.9 18.0 %collective-permute-start.10 = (f32[208,128]{1,0:T(8,128)S(1)}, f32[208,128]{1,0:T(8,128)S(1)}, u32[]{:S(2)}, u32[]{:S(2)}) collective-permute-start(f32[208,128]{1,0:T(8,128)S(1)} %tree_merge.2.refs_0_), channel_id=1, source_target_pairs={{0,16},{1,17},{2,18},{3,19},{4,20},{5,21},{6,22},{7,23},{8,24},{9,... | collective-permute-start | bytes 319496 | tf_op jit(solution)/shard_map/ppermute | solution.py:407
  46.7 17.7 %collective-permute-start.9 = (f32[208,128]{1,0:T(8,128)S(1)}, f32[208,128]{1,0:T(8,128)S(1)}, u32[]{:S(2)}, u32[]{:S(2)}) collective-permute-start(f32[208,128]{1,0:T(8,128)S(1)} %tree_merge.2.refs_0_), channel_id=1, source_target_pairs={{0,12},{1,13},{2,14},{3,15},{4,8},{5,9},{6,10},{7,11},{8,4},{9,5},... | collective-permute-start | bytes 319496 | tf_op jit(solution)/shard_map/ppermute | solution.py:407
  56.4 8.0 %collective-permute-start.8 = (f32[208,128]{1,0:T(8,128)S(1)}, f32[208,128]{1,0:T(8,128)S(1)}, u32[]{:S(2)}, u32[]{:S(2)}) collective-permute-start(f32[208,128]{1,0:T(8,128)S(1)} %tree_merge.2.refs_0_), channel_id=1, source_target_pairs={{0,8},{1,9},{2,10},{3,11},{4,12},{5,13},{6,14},{7,15},{8,0},{9,1},... | collective-permute-start | bytes 319496 | tf_op jit(solution)/shard_map/ppermute | solution.py:407
  59.4 7.0 %collective-permute-start.7 = (f32[208,128]{1,0:T(8,128)S(1)}, f32[208,128]{1,0:T(8,128)S(1)}, u32[]{:S(2)}, u32[]{:S(2)}) collective-permute-start(f32[208,128]{1,0:T(8,128)S(1)} %tree_merge.2.refs_0_), channel_id=1, source_target_pairs={{0,4},{1,5},{2,6},{3,7},{4,0},{5,1},{6,2},{7,3},{8,12},{9,13},{10,... | collective-permute-start | bytes 319496 | tf_op jit(solution)/shard_map/ppermute | solution.py:407
  66.4 19.1 %collective-permute-start.15 = (bf16[8,768,128]{2,1,0:T(8,128)(2,1)S(1)}, bf16[8,768,128]{2,1,0:T(8,128)(2,1)S(1)}, u32[]{:S(2)}, u32[]{:S(2)}) collective-permute-start(bf16[8,768,128]{2,1,0:T(8,128)(2,1)S(1)} %collective-permute-done.5.refs_7_), channel_id=1, source_target_pairs={{1,5},{5,9},{6,2},{9,13},{10,6},{13,17},{14,10},{17,21},{18,14},{2... | collective-permute-start | bytes 4718600 | tf_op jit(solution)/shard_map/ppermute | solution.py:398
  89.0 6.1 %collective-permute-start.16 = (f32[8,512,128]{2,1,0:T(8,128)S(1)}, f32[8,512,128]{2,1,0:T(8,128)S(1)}, u32[]{:S(2)}, u32[]{:S(2)}) collective-permute-start(f32[8,512,128]{2,1,0:T(8,128)S(1)} %near_beside.1), channel_id=1, source_target_pairs={{0,1},{1,0},{2,3},{3,2},{4,5},{5,4},{6,7},{7,6},{8,9},{9,8},{10,11... | collective-permute-start | bytes 6291464 | tf_op jit(solution)/shard_map/ppermute | solution.py:407

commit v6 on v4

--- a/solution.py
+++ b/solution.py
@@ -439,12 +439,10 @@
         *parts, outer_across, outer_next, own_pack, beside
     )
     inner_across = send(own_pack, [(2, 0, 0), (1, 0, 3)])
-    for bit in range(1, bits - 1):
-        node = level(parts, bit)
-        parts = exchange(node, bit + 1, 1)
-    node = level(parts, bits - 1, skel // count)
-    outer_across, node = tie(outer_across, node)
     forwarded = send(outer_across, [(1, 1, 1), (2, -1, 2)])
+    node = level(parts, 1)
+    own_pack, node = tie(own_pack, node)
+    parts = exchange(node, 2, 1)
     own_set = (own_base, single, [own_pack])
     early_set = (early_base, by_edge, [outer_next, outer_across])
     own, beside = near_call(
@@ -452,20 +450,28 @@
         [own_set, early_set], ((0, 0), (1, 0), (1, 1)), dim, "near_early",
     )
 
-    inner_across, forwarded, beside = tie(inner_across, forwarded, beside)
+    *parts, inner_across, forwarded, beside = tie(*parts, inner_across, forwarded, beside)
     late_set = (late_base, by_edge, [inner_across, forwarded])
     (beside,) = near_call(
         [(1, beside_lists, beside_rows, beside)], [late_set], ((0, 0),), dim, "near_beside"
     )
     given = exchange(beside, 0, 1)[1]
+    *parts, beside = tie(*parts, beside)
+    shift, stage = 2, 1
+    while shift + stage < bits:
+        node = level(parts, shift)
+        shift, stage = shift + stage, min(2, bits - shift - stage)
+        parts = exchange(node, shift, stage)
     (own,) = near_call([(0, near_lists, rows, own)], [late_set], ((0, 0),), dim, "near_last")
+    *parts, own = tie(*parts, own)
+    node = level(parts, shift, skel // count)
+    near = (own + given) * (leaf ** -0.5)
     if skel // count:
         root = node.reshape(-1)
     else:
         size = skel * LANES // count
         rank = lax.axis_index("leaf") * sub_count + lax.axis_index("sub")
         root = lax.dynamic_slice_in_dim(node.reshape(-1), rank * size, size, 0)
-    near = (own + given) * (leaf ** -0.5)
     return near.reshape(npts, LANES), root
 
 

time: 86.2 us -> 81.8 us (0.949)
  the two profiles are of different devices: /device:TPU:29 before, /device:TPU:0 now
where the time goes in v6:
time: 81.8 us; the launch traced here: 81.1 us
  Pallas kernels  37.8 us (46%)
  starting transfers between devices  20.4 us (25%)
  waiting for transfers between devices  16 us (20%)
  local copies, waits for them, and re-layouts  4.58 us (6%)
  other arithmetic  1.56 us (2%)
  between operations  0.82 us (1%)
    pallas_call x4, Pallas kernels, near_call(): pl.pallas_call(functools.partial(near_kernel, flips=flips, has_acc=tuple(...  22.3 us
    ppermute x9, starting transfers between devices, exchange(): lax.ppermute(x, axes, [(i, i ^ d << shift) for i in range(count)])  12.1 us
    ppermute x9, waiting for transfers between devices, exchange(): lax.ppermute(x, axes, [(i, i ^ d << shift) for i in range(count)])  9.39 us
    ppermute x4, starting transfers between devices, send(): return lax.ppermute(x, axes, pairs)  8.31 us
    pallas_call x1, Pallas kernels, local_tree_call(): pl.pallas_call(functools.partial(local_tree_kernel, dim=dim), in_specs=[p...  7.01 us
    ppermute x4, waiting for transfers between devices, send(): return lax.ppermute(x, axes, pairs)  6.62 us
    pallas_call x4, Pallas kernels, merge_call(): pl.pallas_call(functools.partial(merge_kernel, dim=dim, blocks=blocks, sh...  5.86 us
    unnamed x14, local copies, waits for them, and re-layouts  4.58 us
  transfers between devices with their start and end apart: 13, of which 6 were waited for; matrix products, arithmetic and copies ran while one was open for 0% of the time, Pallas kernels for 38%

profile of v6, /device:TPU:0, one launch (start us, length us, event | category | flops | bytes accessed | tf_op | source)
XLA Modules:
  0.0 81.1 jit_solution(5545883316077413017)
XLA Ops:
  0.6 1.2 %copy-done.2 = bf16[4096,128]{1,0:T(8,128)(2,1)S(1)} copy-done((bf16[4096,128]{1,0:T(8,128)(2,1)S(1)}, bf16[4096,128]{1,0:T(8,128)(2,1)}, u32[]{:S(2)}) %copy-start.2) | copy-done | bytes 1048600
  1.9 1.0 %copy-done.3 = bf16[4096,64]{0,1:T(8,128)(2,1)S(1)} copy-done((bf16[4096,64]{0,1:T(8,128)(2,1)S(1)}, bf16[4096,64]{0,1:T(8,128)(2,1)}, u32[]{:S(2)}) %copy-start.3) | copy-done | bytes 524312
  3.6 2.6 %tree_order.1 = (bf16[8,768,128]{2,1,0:T(8,128)(2,1)S(1)}, bf16[8,512,128]{2,1,0:T(8,128)(2,1)S(1)}) custom-call(bf16[64,4096]{1,0:T(8,128)(2,1)S(1)} %bitcast.4, s32[8,1,512]{2,1,0:T(1,128)S(1)} %bitcast.5, bf16[4096,128]{1,0:T(8,128)(2,1)S(1)} %copy-done.2), custom_call_target="tpu_custom_call" | custom-call | flops 268435456 | bytes 5242880 | tf_op jit(solution)/shard_map/tree_order/pallas_call | solution.py:94
  6.3 5.0 %collective-permute-start.3 = (bf16[8,768,128]{2,1,0:T(8,128)(2,1)S(1)}, bf16[8,768,128]{2,1,0:T(8,128)(2,1)S(1)}, u32[]{:S(2)}, u32[]{:S(2)}) collective-permute-start(bf16[8,768,128]{2,1,0:T(8,128)(2,1)S(1)} %get-tuple-element.42.pack.refs_2_.refs_5_), channel_id=1, source_target_pairs={{3,1},{0,2},{7,5},{4,6},{11,9},{8,10},{15,13},{12,14},{19,17},{16,... | collective-permute-start | bytes 4718600 | tf_op jit(solution)/shard_map/ppermute | solution.py:398
  11.2 1.3 %collective-permute-start.4 = (bf16[8,768,128]{2,1,0:T(8,128)(2,1)S(1)}, bf16[8,768,128]{2,1,0:T(8,128)(2,1)S(1)}, u32[]{:S(2)}, u32[]{:S(2)}) collective-permute-start(bf16[8,768,128]{2,1,0:T(8,128)(2,1)S(1)} %get-tuple-element.42.pack.refs_2_.refs_5_), channel_id=1, source_target_pairs={{3,7},{7,11},{4,0},{11,15},{8,4},{15,19},{12,8},{19,23},{16,12},{2... | collective-permute-start | bytes 4718600 | tf_op jit(solution)/shard_map/ppermute | solution.py:398
  14.7 7.0 %local_tree.1.refs_0_ = f32[208,128]{1,0:T(8,128)S(1)} custom-call(bf16[8,768,128]{2,1,0:T(8,128)(2,1)S(1)} %get-tuple-element.42.pack.refs_2_.refs_5_, bf16[8,512,128]{2,1,0:T(8,128)(2,1)S(1)} %get-tuple-element.31.rows.refs_2_.refs_1_, s32[8,128]{1,0:T(8,128)S(1)} %copy-done.6, s32[255,128]{1,0:T(8,128)S(1)} %copy-done), custom_call_target="tpu_custom_call" | custom-call | flops 536870912 | bytes 3145728 | tf_op jit(solution)/shard_map/local_tree/pallas_call | solution.py:177
  21.9 1.2 %collective-permute-done.1.refs_1_ = f32[208,128]{1,0:T(8,128)S(1)} collective-permute-done((f32[208,128]{1,0:T(8,128)S(1)}, f32[208,128]{1,0:T(8,128)S(1)}, u32[]{:S(2)}, u32[]{:S(2)}) %collective-permute-start.1) | collective-permute-done | bytes 106528 | tf_op jit(solution)/shard_map/ppermute | solution.py:407
  24.1 1.7 %collective-permute-start.2 = (f32[208,128]{1,0:T(8,128)S(1)}, f32[208,128]{1,0:T(8,128)S(1)}, u32[]{:S(2)}, u32[]{:S(2)}) collective-permute-start(f32[208,128]{1,0:T(8,128)S(1)} %tree_merge.4.refs_0_), channel_id=1, source_target_pairs={{0,2},{1,3},{2,0},{3,1},{4,6},{5,7},{6,4},{7,5},{8,10},{9,11},{10,... | collective-permute-start | bytes 319496 | tf_op jit(solution)/shard_map/ppermute | solution.py:407
  25.8 2.3 %near_own.1.refs_4_ = f32[8,512,128]{2,1,0:T(8,128)S(1)} custom-call(s32[8,12]{1,0:T(8,128)S(1)} %collective-permute-done.refs_0_.refs_1_, bf16[8,512,128]{2,1,0:T(8,128)(2,1)S(1)} %collective-permute-done.5.refs_1_.refs_3_, bf16[8,768,128]{2,1,0:T(8,128)(2,1)S(1)} %get-tuple-element.42.pack.refs_2_.refs_5_), custom_call_target="tpu_custom_call" | custom-call | flops 1000 | bytes 1000 | tf_op jit(solution)/shard_map/near_own/pallas_call | solution.py:365
  28.2 3.2 %collective-permute-done.2.refs_1_ = f32[208,128]{1,0:T(8,128)S(1)} collective-permute-done((f32[208,128]{1,0:T(8,128)S(1)}, f32[208,128]{1,0:T(8,128)S(1)}, u32[]{:S(2)}, u32[]{:S(2)}) %collective-permute-start.2) | collective-permute-done | bytes 106528 | tf_op jit(solution)/shard_map/ppermute | solution.py:407
  31.4 2.2 %collective-permute-done.4.refs_6_ = bf16[8,768,128]{2,1,0:T(8,128)(2,1)S(1)} collective-permute-done((bf16[8,768,128]{2,1,0:T(8,128)(2,1)S(1)}, bf16[8,768,128]{2,1,0:T(8,128)(2,1)S(1)}, u32[]{:S(2)}, u32[]{:S(2)}) %collective-permute-start.4) | collective-permute-done | bytes 1572896 | tf_op jit(solution)/shard_map/ppermute | solution.py:398
  33.6 1.3 %collective-permute-start.7 = (bf16[8,768,128]{2,1,0:T(8,128)(2,1)S(1)}, bf16[8,768,128]{2,1,0:T(8,128)(2,1)S(1)}, u32[]{:S(2)}, u32[]{:S(2)}) collective-permute-start(bf16[8,768,128]{2,1,0:T(8,128)(2,1)S(1)} %get-tuple-element.42.pack.refs_2_.refs_5_), channel_id=1, source_target_pairs={{2,0},{1,3},{6,4},{5,7},{10,8},{9,11},{14,12},{13,15},{18,16},{17,... | collective-permute-start | bytes 4718600 | tf_op jit(solution)/shard_map/ppermute | solution.py:398
  35.6 1.0 %tree_merge.5.refs_0_ = f32[208,128]{1,0:T(8,128)S(1)} custom-call(f32[208,128]{1,0:T(8,128)S(1)} %tree_merge.4.refs_0_, f32[208,128]{1,0:T(8,128)S(1)} %collective-permute-done.2.refs_1_, s32[255,128]{1,0:T(8,128)S(1)} %copy-done.1), custom_call_target="tpu_custom_call" | custom-call | flops 67108864 | bytes 212992 | tf_op jit(solution)/shard_map/tree_merge/pallas_call | solution.py:251
  36.6 2.4 %collective-permute-start.6 = (f32[208,128]{1,0:T(8,128)S(1)}, f32[208,128]{1,0:T(8,128)S(1)}, u32[]{:S(2)}, u32[]{:S(2)}) collective-permute-start(f32[208,128]{1,0:T(8,128)S(1)} %tree_merge.5.refs_0_), channel_id=1, source_target_pairs={{0,4},{1,5},{2,6},{3,7},{4,0},{5,1},{6,2},{7,3},{8,12},{9,13},{10,... | collective-permute-start | bytes 319496 | tf_op jit(solution)/shard_map/ppermute | solution.py:407
  39.1 12.3 %near_early.1 = (f32[8,512,128]{2,1,0:T(8,128)S(1)}, f32[8,512,128]{2,1,0:T(8,128)S(1)}) custom-call(s32[8,12]{1,0:T(8,128)S(1)} %copy-done.4, s32[8,12]{1,0:T(8,128)S(1)} %collective-permute-done.refs_0_.refs_1_, bf16[8,512,128]{2,1,0:T(8,128)(2,1)S(1)} %get-tuple-element.31.rows.refs_2_.refs_1_, ...), custom_call_target="tpu_custom_call" | custom-call | flops 1000 | bytes 1000 | tf_op jit(solution)/shard_map/near_early/pallas_call | solution.py:365
  51.4 4.4 %collective-permute-done.7.refs_3_ = bf16[8,768,128]{2,1,0:T(8,128)(2,1)S(1)} collective-permute-done((bf16[8,768,128]{2,1,0:T(8,128)(2,1)S(1)}, bf16[8,768,128]{2,1,0:T(8,128)(2,1)S(1)}, u32[]{:S(2)}, u32[]{:S(2)}) %collective-permute-start.7) | collective-permute-done | bytes 1572896 | tf_op jit(solution)/shard_map/ppermute | solution.py:398
  55.9 4.5 %near_beside.1 = f32[8,512,128]{2,1,0:T(8,128)S(1)} custom-call(s32[8,12]{1,0:T(8,128)S(1)} %collective-permute-done.refs_0_.refs_1_, bf16[8,512,128]{2,1,0:T(8,128)(2,1)S(1)} %collective-permute-done.5.refs_1_.refs_3_, f32[8,512,128]{2,1,0:T(8,128)S(1)} %get-tuple-element.47.refs_2_, bf16[8,768,128]{2,1,0:T(8,128)(2,1)S(1)} %collective-permute-done.7.refs_3_, ...), custom_call_target="tpu_custom_call" | custom-call | flops 1000 | bytes 1000 | tf_op jit(solution)/shard_map/near_beside/pallas_call | solution.py:365
  60.5 1.0 %tree_merge.6.refs_0_ = f32[208,128]{1,0:T(8,128)S(1)} custom-call(f32[208,128]{1,0:T(8,128)S(1)} %tree_merge.5.refs_0_, f32[208,128]{1,0:T(8,128)S(1)} %collective-permute-done.6.refs_1_, s32[255,128]{1,0:T(8,128)S(1)} %copy-done.1), custom_call_target="tpu_custom_call" | custom-call | flops 67108864 | bytes 212992 | tf_op jit(solution)/shard_map/tree_merge/pallas_call | solution.py:251
  61.5 5.7 %collective-permute-start.10 = (f32[208,128]{1,0:T(8,128)S(1)}, f32[208,128]{1,0:T(8,128)S(1)}, u32[]{:S(2)}, u32[]{:S(2)}) collective-permute-start(f32[208,128]{1,0:T(8,128)S(1)} %tree_merge.6.refs_0_), channel_id=1, source_target_pairs={{0,16},{1,17},{2,18},{3,19},{4,20},{5,21},{6,22},{7,23},{8,24},{9,... | collective-permute-start | bytes 319496 | tf_op jit(solution)/shard_map/ppermute | solution.py:407
  68.6 3.1 %near_last.1 = f32[8,512,128]{2,1,0:T(8,128)S(1)} custom-call(s32[8,12]{1,0:T(8,128)S(1)} %copy-done.4, bf16[8,512,128]{2,1,0:T(8,128)(2,1)S(1)} %get-tuple-element.31.rows.refs_2_.refs_1_, f32[8,512,128]{2,1,0:T(8,128)S(1)} %get-tuple-element.52.refs_2_, bf16[8,768,128]{2,1,0:T(8,128)(2,1)S(1)} %collective-permute-done.7.refs_3_, ...), custom_call_target="tpu_custom_call" | custom-call | flops 1000 | bytes 1000 | tf_op jit(solution)/shard_map/near_last/pallas_call | solution.py:365
  71.7 3.9 %collective-permute-done.10.refs_2_ = f32[208,128]{1,0:T(8,128)S(1)} collective-permute-done((f32[208,128]{1,0:T(8,128)S(1)}, f32[208,128]{1,0:T(8,128)S(1)}, u32[]{:S(2)}, u32[]{:S(2)}) %collective-permute-start.10) | collective-permute-done | bytes 106528 | tf_op jit(solution)/shard_map/ppermute | solution.py:407
  75.6 1.1 %collective-permute-done.9.refs_1_ = f32[208,128]{1,0:T(8,128)S(1)} collective-permute-done((f32[208,128]{1,0:T(8,128)S(1)}, f32[208,128]{1,0:T(8,128)S(1)}, u32[]{:S(2)}, u32[]{:S(2)}) %collective-permute-start.9) | collective-permute-done | bytes 106528 | tf_op jit(solution)/shard_map/ppermute | solution.py:407
  76.6 2.9 %tree_merge.7 = f32[4,128]{1,0:T(4,128)} custom-call(f32[208,128]{1,0:T(8,128)S(1)} %tree_merge.6.refs_0_, f32[208,128]{1,0:T(8,128)S(1)} %collective-permute-done.9.refs_1_, f32[208,128]{1,0:T(8,128)S(1)} %collective-permute-done.10.refs_2_, f32[208,128]{1,0:T(8,128)S(1)} %collective-permute-done.11.refs_3_, s32[255,128]{1,0:T(8,128)S(1)} %copy-done.1), custom_call_target="tpu_custom_call" | custom-call | flops 134217728 | bytes 425984 | tf_op jit(solution)/shard_map/tree_merge/pallas_call | solution.py:251
  79.6 1.6 %add_multiply_fusion = f32[8,512,128]{2,1,0:T(8,128)} fusion(f32[8,512,128]{2,1,0:T(8,128)S(1)} %near_last.1, f32[8,512,128]{2,1,0:T(8,128)S(1)} %collective-permute-done.12), kind=kLoop, calls=%fused_computation | loop fusion | flops 1048576 | bytes 6291456 | tf_op jit(solution)/shard_map/mul | solution.py:468
  (27 shorter events, 6.3 us)
Async XLA Ops:
  0.6 1.2 %copy-start.2 = (bf16[4096,128]{1,0:T(8,128)(2,1)S(1)}, bf16[4096,128]{1,0:T(8,128)(2,1)}, u32[]{:S(2)}) copy-start(bf16[4096,128]{1,0:T(8,128)(2,1)} %probes.1) | copy-start | bytes 3145732
  1.9 1.0 %copy-start.3 = (bf16[4096,64]{0,1:T(8,128)(2,1)S(1)}, bf16[4096,64]{0,1:T(8,128)(2,1)}, u32[]{:S(2)}) copy-start(bf16[4096,64]{0,1:T(8,128)(2,1)} %param.7) | copy-start | bytes 1572868
  2.9 0.7 copy-start.5
  6.3 25.1 %collective-permute-start.3 = (bf16[8,768,128]{2,1,0:T(8,128)(2,1)S(1)}, bf16[8,768,128]{2,1,0:T(8,128)(2,1)S(1)}, u32[]{:S(2)}, u32[]{:S(2)}) collective-permute-start(bf16[8,768,128]{2,1,0:T(8,128)(2,1)S(1)} %get-tuple-element.42.pack.refs_2_.refs_5_), channel_id=1, source_target_pairs={{3,1},{0,2},{7,5},{4,6},{11,9},{8,10},{15,13},{12,14},{19,17},{16,... | collective-permute-start | bytes 4718600 | tf_op jit(solution)/shard_map/ppermute | solution.py:398
  11.2 22.3 %collective-permute-start.4 = (bf16[8,768,128]{2,1,0:T(8,128)(2,1)S(1)}, bf16[8,768,128]{2,1,0:T(8,128)(2,1)S(1)}, u32[]{:S(2)}, u32[]{:S(2)}) collective-permute-start(bf16[8,768,128]{2,1,0:T(8,128)(2,1)S(1)} %get-tuple-element.42.pack.refs_2_.refs_5_), channel_id=1, source_target_pairs={{3,7},{7,11},{4,0},{11,15},{8,4},{15,19},{12,8},{19,23},{16,12},{2... | collective-permute-start | bytes 4718600 | tf_op jit(solution)/shard_map/ppermute | solution.py:398
  12.5 13.3 %collective-permute-start.5 = (bf16[8,512,128]{2,1,0:T(8,128)(2,1)S(1)}, bf16[8,512,128]{2,1,0:T(8,128)(2,1)S(1)}, u32[]{:S(2)}, u32[]{:S(2)}) collective-permute-start(bf16[8,512,128]{2,1,0:T(8,128)(2,1)S(1)} %get-tuple-element.31.rows.refs_2_.refs_1_), channel_id=1, source_target_pairs={{0,1},{1,0},{2,3},{3,2},{4,5},{5,4},{6,7},{7,6},{8,9},{9,8},{10,11... | collective-permute-start | bytes 3145736 | tf_op jit(solution)/shard_map/ppermute | solution.py:407
  12.6 9.1 %collective-permute-start = (s32[8,12]{1,0:T(8,128)}, s32[8,12]{1,0:T(8,128)S(1)}, u32[]{:S(2)}, u32[]{:S(2)}) collective-permute-start(s32[8,12]{1,0:T(8,128)} %refs_0_.3), channel_id=1, source_target_pairs={{0,1},{1,0},{2,3},{3,2},{4,5},{5,4},{6,7},{7,6},{8,9},{9,8},{10,11... | collective-permute-start | bytes 1160 | tf_op jit(solution)/shard_map/ppermute | solution.py:407
  13.1 0.9 %copy-start = (s32[255,128]{1,0:T(8,128)S(1)}, s32[255,128]{1,0:T(8,128)}, u32[]{:S(2)}) copy-start(s32[255,128]{1,0:T(8,128)} %refs_4_.1) | copy-start | bytes 391684
  14.0 0.7 copy-start.6
  21.7 1.4 %collective-permute-start.1 = (f32[208,128]{1,0:T(8,128)S(1)}, f32[208,128]{1,0:T(8,128)S(1)}, u32[]{:S(2)}, u32[]{:S(2)}) collective-permute-start(f32[208,128]{1,0:T(8,128)S(1)} %local_tree.1.refs_0_), channel_id=1, source_target_pairs={{0,1},{1,0},{2,3},{3,2},{4,5},{5,4},{6,7},{7,6},{8,9},{9,8},{10,11... | collective-permute-start | bytes 319496 | tf_op jit(solution)/shard_map/ppermute | solution.py:407
  24.1 11.5 %copy-start.1 = (s32[255,128]{1,0:T(8,128)S(1)}, s32[255,128]{1,0:T(8,128)}, u32[]{:S(2)}) copy-start(s32[255,128]{1,0:T(8,128)} %refs_4_.1) | copy-start | bytes 391684
  24.1 15.0 %copy-start.4 = (s32[8,12]{1,0:T(8,128)S(1)}, s32[8,12]{1,0:T(8,128)}, u32[]{:S(2)}) copy-start(s32[8,12]{1,0:T(8,128)} %refs_0_.3) | copy-start | bytes 1156
  24.1 7.2 %collective-permute-start.2 = (f32[208,128]{1,0:T(8,128)S(1)}, f32[208,128]{1,0:T(8,128)S(1)}, u32[]{:S(2)}, u32[]{:S(2)}) collective-permute-start(f32[208,128]{1,0:T(8,128)S(1)} %tree_merge.4.refs_0_), channel_id=1, source_target_pairs={{0,2},{1,3},{2,0},{3,1},{4,6},{5,7},{6,4},{7,5},{8,10},{9,11},{10,... | collective-permute-start | bytes 319496 | tf_op jit(solution)/shard_map/ppermute | solution.py:407
  33.6 22.3 %collective-permute-start.7 = (bf16[8,768,128]{2,1,0:T(8,128)(2,1)S(1)}, bf16[8,768,128]{2,1,0:T(8,128)(2,1)S(1)}, u32[]{:S(2)}, u32[]{:S(2)}) collective-permute-start(bf16[8,768,128]{2,1,0:T(8,128)(2,1)S(1)} %get-tuple-element.42.pack.refs_2_.refs_5_), channel_id=1, source_target_pairs={{2,0},{1,3},{6,4},{5,7},{10,8},{9,11},{14,12},{13,15},{18,16},{17,... | collective-permute-start | bytes 4718600 | tf_op jit(solution)/shard_map/ppermute | solution.py:398
  34.8 21.0 %collective-permute-start.8 = (bf16[8,768,128]{2,1,0:T(8,128)(2,1)S(1)}, bf16[8,768,128]{2,1,0:T(8,128)(2,1)S(1)}, u32[]{:S(2)}, u32[]{:S(2)}) collective-permute-start(bf16[8,768,128]{2,1,0:T(8,128)(2,1)S(1)} %collective-permute-done.3.refs_7_), channel_id=1, source_target_pairs={{1,5},{5,9},{6,2},{9,13},{10,6},{13,17},{14,10},{17,21},{18,14},{2... | collective-permute-start | bytes 4718600 | tf_op jit(solution)/shard_map/ppermute | solution.py:398
  36.6 14.8 %collective-permute-start.6 = (f32[208,128]{1,0:T(8,128)S(1)}, f32[208,128]{1,0:T(8,128)S(1)}, u32[]{:S(2)}, u32[]{:S(2)}) collective-permute-start(f32[208,128]{1,0:T(8,128)S(1)} %tree_merge.5.refs_0_), channel_id=1, source_target_pairs={{0,4},{1,5},{2,6},{3,7},{4,0},{5,1},{6,2},{7,3},{8,12},{9,13},{10,... | collective-permute-start | bytes 319496 | tf_op jit(solution)/shard_map/ppermute | solution.py:407
  60.4 19.2 %collective-permute-start.12 = (f32[8,512,128]{2,1,0:T(8,128)S(1)}, f32[8,512,128]{2,1,0:T(8,128)S(1)}, u32[]{:S(2)}, u32[]{:S(2)}) collective-permute-start(f32[8,512,128]{2,1,0:T(8,128)S(1)} %near_beside.1), channel_id=1, source_target_pairs={{0,1},{1,0},{2,3},{3,2},{4,5},{5,4},{6,7},{7,6},{8,9},{9,8},{10,11... | collective-permute-start | bytes 6291464 | tf_op jit(solution)/shard_map/ppermute | solution.py:407
  61.5 14.1 %collective-permute-start.10 = (f32[208,128]{1,0:T(8,128)S(1)}, f32[208,128]{1,0:T(8,128)S(1)}, u32[]{:S(2)}, u32[]{:S(2)}) collective-permute-start(f32[208,128]{1,0:T(8,128)S(1)} %tree_merge.6.refs_0_), channel_id=1, source_target_pairs={{0,16},{1,17},{2,18},{3,19},{4,20},{5,21},{6,22},{7,23},{8,24},{9,... | collective-permute-start | bytes 319496 | tf_op jit(solution)/shard_map/ppermute | solution.py:407
  67.1 8.4 %collective-permute-start.11 = (f32[208,128]{1,0:T(8,128)S(1)}, f32[208,128]{1,0:T(8,128)S(1)}, u32[]{:S(2)}, u32[]{:S(2)}) collective-permute-start(f32[208,128]{1,0:T(8,128)S(1)} %tree_merge.6.refs_0_), channel_id=1, source_target_pairs={{0,24},{1,25},{2,26},{3,27},{4,28},{5,29},{6,30},{7,31},{8,16},{9,... | collective-permute-start | bytes 319496 | tf_op jit(solution)/shard_map/ppermute | solution.py:407
  68.1 8.5 %collective-permute-start.9 = (f32[208,128]{1,0:T(8,128)S(1)}, f32[208,128]{1,0:T(8,128)S(1)}, u32[]{:S(2)}, u32[]{:S(2)}) collective-permute-start(f32[208,128]{1,0:T(8,128)S(1)} %tree_merge.6.refs_0_), channel_id=1, source_target_pairs={{0,8},{1,9},{2,10},{3,11},{4,12},{5,13},{6,14},{7,15},{8,0},{9,1},... | collective-permute-start | bytes 319496 | tf_op jit(solution)/shard_map/ppermute | solution.py:407

commit v7 on v6

--- a/solution.py
+++ b/solution.py
@@ -268,7 +268,7 @@
     )(*parts, merge_sets)
 
 
-def near_kernel(*refs, flips, has_acc, sets, tasks, dim):
+def near_kernel(*refs, flips, row_counts, has_acc, sets, tasks, dim):
     refs = list(refs)
 
     def take(number):
@@ -276,11 +276,11 @@
         del refs[:number]
         return taken
 
-    lists, rows = take(len(flips)), take(len(flips))
+    lists, rows = take(len(flips)), [take(number) for number in row_counts]
     accs = [take(1)[0] if has else None for has in has_acc]
     buffers = [take(max(which) + 1) for _, which in sets]
     outs, (pair_list,) = take(len(flips)), refs
-    blocks, leaf = rows[0].shape[:2]
+    blocks, leaf = rows[0][0].shape[:2]
     near = lists[0].shape[1]
     window = blocks * lax.axis_size("sub")
     sub = lax.axis_index("sub")
@@ -319,7 +319,7 @@
 
     half = leaf // 2
 
-    def add_all(buffer, t, pairs):
+    def add_all(buffer, targets, t, pairs):
         j = tasks[t][1]
 
         def add_pair(i):
@@ -330,7 +330,7 @@
             probes = buffer[local, :leaf, :]
             total = None
             for c in range(0, leaf, half):
-                weights = jnp.exp(dot(rows[j][g], form[:, c : c + half])).astype(BF16)
+                weights = jnp.exp(dot(targets[g], form[:, c : c + half])).astype(BF16)
                 term = dot(weights, probes[c : c + half])
                 total = term if total is None else total + term
             return g, total
@@ -347,18 +347,27 @@
             g, total = add_pair(pairs - 1)
             outs[j][g] += total
 
-    for t, (number, _) in enumerate(tasks):
+    for t, (number, j) in enumerate(tasks):
         held = place(sets[number][1])
+        edge = (sub == 0) | (sub == lax.axis_size("sub") - 1)
         for k, buffer in enumerate(buffers[number]):
-            pairs = found[t] if len(buffers[number]) == 1 else jnp.where(held == k, found[t], 0)
-            add_all(buffer, t, pairs)
+            for r, targets in enumerate(rows[j]):
+                pairs = found[t]
+                if len(buffers[number]) > 1:
+                    if len(rows[j]) > 1 and r != k:
+                        continue
+                    pairs = jnp.where(held == k, pairs, 0)
+                elif len(rows[j]) > 1:
+                    pairs = jnp.where(edge == (r == 0), pairs, 0)
+                add_all(buffer, targets, t, pairs)
 
 
 def near_call(groups, sources, tasks, dim, name):
     flips, lists, rows, accs = zip(*groups)
-    blocks, leaf = rows[0].shape[:2]
+    rows = [r if isinstance(r, tuple) else (r,) for r in rows]
+    blocks, leaf = rows[0][0].shape[:2]
     held = [acc for acc in accs if acc is not None]
-    args = [*lists, *rows, *held, *(b for _, _, buffers in sources for b in buffers)]
+    args = [*lists, *(r for pair in rows for r in pair), *held, *(b for _, _, buffers in sources for b in buffers)]
     smem = pl.BlockSpec(memory_space=pltpu.SMEM)
     vmem = pl.BlockSpec(memory_space=pltpu.VMEM)
     near = lists[0].shape[1]
@@ -366,6 +375,7 @@
         functools.partial(
             near_kernel,
             flips=flips,
+            row_counts=tuple(len(pair) for pair in rows),
             has_acc=tuple(acc is not None for acc in accs),
             sets=tuple((bases, which) for bases, which, _ in sources),
             tasks=tasks,
@@ -418,7 +428,9 @@
     pack, rows = order_call(points.T, order.reshape(blocks, 1, leaf), probes, blocks)
     outer_across = send(pack, [(3, 0, 1), (0, 0, 2)])
     outer_next = send(pack, [(3, 1, 3), (0, -1, 0)])
-    beside_rows = exchange(rows, 0, 1)[1]
+    inward, outward = [(1, 0, 0), (2, 0, 3)], [(0, 0, 1), (3, 0, 2)]
+    beside_pack = send(pack, inward)
+    edge_rows = send(rows, inward)
     beside_lists = exchange(near_lists, 0, 1)[1]
 
     node = local_tree_call(pack, rows, leaf_sets, merge_sets, dim)
@@ -431,23 +443,22 @@
     own_pack, node = tie(pack, node)
     parts = exchange(node, 1, 1)
     own_set = (own_base, single, [own_pack])
-    (beside,) = near_call(
-        [(1, beside_lists, beside_rows, None)], [own_set], ((0, 0),), dim, "near_own"
+    (own,) = near_call([(0, near_lists, rows, None)], [own_set], ((0, 0),), dim, "near_own")
+
+    *parts, outer_across, outer_next, beside_pack, edge_rows, late_rows, own = tie(
+        *parts, outer_across, outer_next, beside_pack, edge_rows, rows, own
     )
-
-    *parts, outer_across, outer_next, own_pack, beside = tie(
-        *parts, outer_across, outer_next, own_pack, beside
-    )
-    inner_across = send(own_pack, [(2, 0, 0), (1, 0, 3)])
     forwarded = send(outer_across, [(1, 1, 1), (2, -1, 2)])
+    inner_across = send(beside_pack, [(0, 0, 3), (3, 0, 0)])
+    beside_rows = (edge_rows, send(late_rows, outward))
     node = level(parts, 1)
     own_pack, node = tie(own_pack, node)
     parts = exchange(node, 2, 1)
     own_set = (own_base, single, [own_pack])
     early_set = (early_base, by_edge, [outer_next, outer_across])
     own, beside = near_call(
-        [(0, near_lists, rows, None), (1, beside_lists, beside_rows, beside)],
-        [own_set, early_set], ((0, 0), (1, 0), (1, 1)), dim, "near_early",
+        [(0, near_lists, rows, own), (1, beside_lists, beside_rows, None)],
+        [own_set, early_set], ((1, 0), (0, 1), (1, 1)), dim, "near_early",
     )
 
     *parts, inner_across, forwarded, beside = tie(*parts, inner_across, forwarded, beside)

time: 81.8 us -> 85.3 us (1.043)
  waiting for transfers between devices: 16 us -> 6.12 us
  starting transfers between devices: 20.4 us -> 29.5 us
  Pallas kernels: 37.8 us -> 41.5 us
    ppermute x4 -> x7, starting transfers between devices: 8.31 us -> 13.7 us  [send(): return lax.ppermute(x, axes, pairs)]
    ppermute x9 -> x8, waiting for transfers between devices: 9.39 us -> 4.01 us  [exchange(): lax.ppermute(x, axes, [(i, i ^ d << shift) for i in range(count)])]
    ppermute x4 -> x7, waiting for transfers between devices: 6.62 us -> 2.11 us  [send(): return lax.ppermute(x, axes, pairs)]
    ppermute x9 -> x8, starting transfers between devices: 12.1 us -> 15.8 us  [exchange(): lax.ppermute(x, axes, [(i, i ^ d << shift) for i in range(count)])]
    pallas_call x4, Pallas kernels: 22.3 us -> 26 us  [near_call(): pl.pallas_call(functools.partial(near_kernel, flips=flips, row_counts=tup...]
  transfers between devices with their start and end apart: 13 -> 15, of which waited for: 6 -> 3; matrix products, arithmetic and copies ran while one was open for 0% -> 0% of each run, Pallas kernels for 38% -> 42%
where the time goes in v7:
time: 85.3 us; the launch traced here: 84.2 us
  Pallas kernels  41.5 us (49%)
  starting transfers between devices  29.5 us (35%)
  waiting for transfers between devices  6.12 us (7%)
  local copies, waits for them, and re-layouts  4.58 us (5%)
  other arithmetic  1.56 us (2%)
  between operations  0.89 us (1%)
    pallas_call x4, Pallas kernels, near_call(): pl.pallas_call(functools.partial(near_kernel, flips=flips, row_counts=tup...  26 us
    ppermute x8, starting transfers between devices, exchange(): lax.ppermute(x, axes, [(i, i ^ d << shift) for i in range(count)])  15.8 us
    ppermute x7, starting transfers between devices, send(): return lax.ppermute(x, axes, pairs)  13.7 us
    pallas_call x1, Pallas kernels, local_tree_call(): pl.pallas_call(functools.partial(local_tree_kernel, dim=dim), in_specs=[p...  7.02 us
    pallas_call x4, Pallas kernels, merge_call(): pl.pallas_call(functools.partial(merge_kernel, dim=dim, blocks=blocks, sh...  5.87 us
    unnamed x14, local copies, waits for them, and re-layouts  4.58 us
    ppermute x8, waiting for transfers between devices, exchange(): lax.ppermute(x, axes, [(i, i ^ d << shift) for i in range(count)])  4.01 us
    pallas_call x1, Pallas kernels, order_call(): pl.pallas_call(order_kernel, grid=(blocks // many,), in_specs=[pl.BlockSp...  2.64 us
  transfers between devices with their start and end apart: 15, of which 3 were waited for; matrix products, arithmetic and copies ran while one was open for 0% of the time, Pallas kernels for 42%

profile of v7, /device:TPU:0, one launch (start us, length us, event | category | flops | bytes accessed | tf_op | source)
XLA Modules:
  0.0 84.2 jit_solution(13741814777160222936)
XLA Ops:
  0.6 1.2 %copy-done.2 = bf16[4096,128]{1,0:T(8,128)(2,1)S(1)} copy-done((bf16[4096,128]{1,0:T(8,128)(2,1)S(1)}, bf16[4096,128]{1,0:T(8,128)(2,1)}, u32[]{:S(2)}) %copy-start.2) | copy-done | bytes 1048600
  1.9 1.0 %copy-done.3 = bf16[4096,64]{0,1:T(8,128)(2,1)S(1)} copy-done((bf16[4096,64]{0,1:T(8,128)(2,1)S(1)}, bf16[4096,64]{0,1:T(8,128)(2,1)}, u32[]{:S(2)}) %copy-start.3) | copy-done | bytes 524312
  3.6 2.6 %tree_order.1 = (bf16[8,768,128]{2,1,0:T(8,128)(2,1)S(1)}, bf16[8,512,128]{2,1,0:T(8,128)(2,1)S(1)}) custom-call(bf16[64,4096]{1,0:T(8,128)(2,1)S(1)} %bitcast.4, s32[8,1,512]{2,1,0:T(1,128)S(1)} %bitcast.5, bf16[4096,128]{1,0:T(8,128)(2,1)S(1)} %copy-done.2), custom_call_target="tpu_custom_call" | custom-call | flops 268435456 | bytes 5242880 | tf_op jit(solution)/shard_map/tree_order/pallas_call | solution.py:94
  6.3 5.0 %collective-permute-start.3 = (bf16[8,768,128]{2,1,0:T(8,128)(2,1)S(1)}, bf16[8,768,128]{2,1,0:T(8,128)(2,1)S(1)}, u32[]{:S(2)}, u32[]{:S(2)}) collective-permute-start(bf16[8,768,128]{2,1,0:T(8,128)(2,1)S(1)} %get-tuple-element.46.pack.refs_2_.refs_6_), channel_id=1, source_target_pairs={{3,1},{0,2},{7,5},{4,6},{11,9},{8,10},{15,13},{12,14},{19,17},{16,... | collective-permute-start | bytes 4718600 | tf_op jit(solution)/shard_map/ppermute | solution.py:408
  11.2 1.3 %collective-permute-start.4 = (bf16[8,768,128]{2,1,0:T(8,128)(2,1)S(1)}, bf16[8,768,128]{2,1,0:T(8,128)(2,1)S(1)}, u32[]{:S(2)}, u32[]{:S(2)}) collective-permute-start(bf16[8,768,128]{2,1,0:T(8,128)(2,1)S(1)} %get-tuple-element.46.pack.refs_2_.refs_6_), channel_id=1, source_target_pairs={{3,7},{7,11},{4,0},{11,15},{8,4},{15,19},{12,8},{19,23},{16,12},{2... | collective-permute-start | bytes 4718600 | tf_op jit(solution)/shard_map/ppermute | solution.py:408
  12.5 1.3 %collective-permute-start.5 = (bf16[8,768,128]{2,1,0:T(8,128)(2,1)S(1)}, bf16[8,768,128]{2,1,0:T(8,128)(2,1)S(1)}, u32[]{:S(2)}, u32[]{:S(2)}) collective-permute-start(bf16[8,768,128]{2,1,0:T(8,128)(2,1)S(1)} %get-tuple-element.46.pack.refs_2_.refs_6_), channel_id=1, source_target_pairs={{1,0},{2,3},{5,4},{6,7},{9,8},{10,11},{13,12},{14,15},{17,16},{18,... | collective-permute-start | bytes 4718600 | tf_op jit(solution)/shard_map/ppermute | solution.py:408
  13.8 1.3 %collective-permute-start.6 = (bf16[8,512,128]{2,1,0:T(8,128)(2,1)S(1)}, bf16[8,512,128]{2,1,0:T(8,128)(2,1)S(1)}, u32[]{:S(2)}, u32[]{:S(2)}) collective-permute-start(bf16[8,512,128]{2,1,0:T(8,128)(2,1)S(1)} %get-tuple-element.44.rows.refs_1_.refs_2_), channel_id=1, source_target_pairs={{1,0},{2,3},{5,4},{6,7},{9,8},{10,11},{13,12},{14,15},{17,16},{18,... | collective-permute-start | bytes 3145736 | tf_op jit(solution)/shard_map/ppermute | solution.py:408
  15.1 1.4 %collective-permute-start = (s32[8,12]{1,0:T(8,128)}, s32[8,12]{1,0:T(8,128)S(1)}, u32[]{:S(2)}, u32[]{:S(2)}) collective-permute-start(s32[8,12]{1,0:T(8,128)} %refs_0_.5), channel_id=1, source_target_pairs={{0,1},{1,0},{2,3},{3,2},{4,5},{5,4},{6,7},{7,6},{8,9},{9,8},{10,11... | collective-permute-start | bytes 1160 | tf_op jit(solution)/shard_map/ppermute | solution.py:417
  18.1 7.0 %local_tree.1.refs_0_ = f32[208,128]{1,0:T(8,128)S(1)} custom-call(bf16[8,768,128]{2,1,0:T(8,128)(2,1)S(1)} %get-tuple-element.46.pack.refs_2_.refs_6_, bf16[8,512,128]{2,1,0:T(8,128)(2,1)S(1)} %get-tuple-element.44.rows.refs_1_.refs_2_, s32[8,128]{1,0:T(8,128)S(1)} %copy-done.6, s32[255,128]{1,0:T(8,128)S(1)} %copy-done), custom_call_target="tpu_custom_call" | custom-call | flops 536870912 | bytes 3145728 | tf_op jit(solution)/shard_map/local_tree/pallas_call | solution.py:177
  25.2 1.3 %collective-permute-done.1.refs_1_ = f32[208,128]{1,0:T(8,128)S(1)} collective-permute-done((f32[208,128]{1,0:T(8,128)S(1)}, f32[208,128]{1,0:T(8,128)S(1)}, u32[]{:S(2)}, u32[]{:S(2)}) %collective-permute-start.1) | collective-permute-done | bytes 106528 | tf_op jit(solution)/shard_map/ppermute | solution.py:417
  27.5 1.7 %collective-permute-start.2 = (f32[208,128]{1,0:T(8,128)S(1)}, f32[208,128]{1,0:T(8,128)S(1)}, u32[]{:S(2)}, u32[]{:S(2)}) collective-permute-start(f32[208,128]{1,0:T(8,128)S(1)} %tree_merge.4.refs_0_), channel_id=1, source_target_pairs={{0,2},{1,3},{2,0},{3,1},{4,6},{5,7},{6,4},{7,5},{8,10},{9,11},{10,... | collective-permute-start | bytes 319496 | tf_op jit(solution)/shard_map/ppermute | solution.py:417
  29.2 6.6 %near_own.1.refs_5_ = f32[8,512,128]{2,1,0:T(8,128)S(1)} custom-call(s32[8,12]{1,0:T(8,128)S(1)} %copy-done.4, bf16[8,512,128]{2,1,0:T(8,128)(2,1)S(1)} %get-tuple-element.44.rows.refs_1_.refs_2_, bf16[8,768,128]{2,1,0:T(8,128)(2,1)S(1)} %get-tuple-element.46.pack.refs_2_.refs_6_), custom_call_target="tpu_custom_call" | custom-call | flops 1000 | bytes 1000 | tf_op jit(solution)/shard_map/near_own/pallas_call | solution.py:374
  35.9 2.2 %collective-permute-start.8 = (bf16[8,768,128]{2,1,0:T(8,128)(2,1)S(1)}, bf16[8,768,128]{2,1,0:T(8,128)(2,1)S(1)}, u32[]{:S(2)}, u32[]{:S(2)}) collective-permute-start(bf16[8,768,128]{2,1,0:T(8,128)(2,1)S(1)} %collective-permute-done.5), channel_id=1, source_target_pairs={{0,3},{3,0},{4,7},{7,4},{8,11},{11,8},{12,15},{15,12},{16,19},{19,... | collective-permute-start | bytes 4718600 | tf_op jit(solution)/shard_map/ppermute | solution.py:408
  38.8 2.0 %collective-permute-start.10 = (bf16[8,512,128]{2,1,0:T(8,128)(2,1)S(1)}, bf16[8,512,128]{2,1,0:T(8,128)(2,1)S(1)}, u32[]{:S(2)}, u32[]{:S(2)}) collective-permute-start(bf16[8,512,128]{2,1,0:T(8,128)(2,1)S(1)} %get-tuple-element.44.rows.refs_1_.refs_2_), channel_id=1, source_target_pairs={{0,1},{3,2},{4,5},{7,6},{8,9},{11,10},{12,13},{15,14},{16,17},{19,... | collective-permute-start | bytes 3145736 | tf_op jit(solution)/shard_map/ppermute | solution.py:408
  41.8 3.4 %collective-permute-start.7 = (f32[208,128]{1,0:T(8,128)S(1)}, f32[208,128]{1,0:T(8,128)S(1)}, u32[]{:S(2)}, u32[]{:S(2)}) collective-permute-start(f32[208,128]{1,0:T(8,128)S(1)} %tree_merge.5.refs_0_), channel_id=1, source_target_pairs={{0,4},{1,5},{2,6},{3,7},{4,0},{5,1},{6,2},{7,3},{8,12},{9,13},{10,... | collective-permute-start | bytes 319496 | tf_op jit(solution)/shard_map/ppermute | solution.py:417
  45.2 10.3 %near_early.1 = (f32[8,512,128]{2,1,0:T(8,128)S(1)}, f32[8,512,128]{2,1,0:T(8,128)S(1)}) custom-call(s32[8,12]{1,0:T(8,128)S(1)} %copy-done.4, s32[8,12]{1,0:T(8,128)S(1)} %collective-permute-done.refs_1_.refs_0_, bf16[8,512,128]{2,1,0:T(8,128)(2,1)S(1)} %get-tuple-element.44.rows.refs_1_.refs_2_, ...), custom_call_target="tpu_custom_call" | custom-call | flops 1000 | bytes 1000 | tf_op jit(solution)/shard_map/near_early/pallas_call | solution.py:374
  55.5 2.1 %collective-permute-done.8.refs_4_.refs_3_ = bf16[8,768,128]{2,1,0:T(8,128)(2,1)S(1)} collective-permute-done((bf16[8,768,128]{2,1,0:T(8,128)(2,1)S(1)}, bf16[8,768,128]{2,1,0:T(8,128)(2,1)S(1)}, u32[]{:S(2)}, u32[]{:S(2)}) %collective-permute-start.8) | collective-permute-done | bytes 1572896 | tf_op jit(solution)/shard_map/ppermute | solution.py:408
  57.6 3.8 %near_beside.1 = f32[8,512,128]{2,1,0:T(8,128)S(1)} custom-call(s32[8,12]{1,0:T(8,128)S(1)} %collective-permute-done.refs_1_.refs_0_, bf16[8,512,128]{2,1,0:T(8,128)(2,1)S(1)} %collective-permute-done.6.refs_3_.refs_1_, bf16[8,512,128]{2,1,0:T(8,128)(2,1)S(1)} %collective-permute-done.10.refs_4_.refs_2_, f32[8,512,128]{2,1,0:T(8,128)S(1)} %get-tuple-element.51.refs_3_, ...), custom_call_target="tpu_custom_call" | custom-call | flops 1000 | bytes 1000 | tf_op jit(solution)/shard_map/near_beside/pallas_call | solution.py:374
  62.5 6.3 %collective-permute-start.11 = (f32[208,128]{1,0:T(8,128)S(1)}, f32[208,128]{1,0:T(8,128)S(1)}, u32[]{:S(2)}, u32[]{:S(2)}) collective-permute-start(f32[208,128]{1,0:T(8,128)S(1)} %tree_merge.6.refs_0_), channel_id=1, source_target_pairs={{0,8},{1,9},{2,10},{3,11},{4,12},{5,13},{6,14},{7,15},{8,0},{9,1},... | collective-permute-start | bytes 319496 | tf_op jit(solution)/shard_map/ppermute | solution.py:417
  68.8 2.3 %collective-permute-start.12 = (f32[208,128]{1,0:T(8,128)S(1)}, f32[208,128]{1,0:T(8,128)S(1)}, u32[]{:S(2)}, u32[]{:S(2)}) collective-permute-start(f32[208,128]{1,0:T(8,128)S(1)} %tree_merge.6.refs_0_), channel_id=1, source_target_pairs={{0,16},{1,17},{2,18},{3,19},{4,20},{5,21},{6,22},{7,23},{8,24},{9,... | collective-permute-start | bytes 319496 | tf_op jit(solution)/shard_map/ppermute | solution.py:417
  71.7 5.3 %near_last.1 = f32[8,512,128]{2,1,0:T(8,128)S(1)} custom-call(s32[8,12]{1,0:T(8,128)S(1)} %copy-done.4, bf16[8,512,128]{2,1,0:T(8,128)(2,1)S(1)} %get-tuple-element.44.rows.refs_1_.refs_2_, f32[8,512,128]{2,1,0:T(8,128)S(1)} %get-tuple-element.56.refs_2_, bf16[8,768,128]{2,1,0:T(8,128)(2,1)S(1)} %collective-permute-done.8.refs_4_.refs_3_, ...), custom_call_target="tpu_custom_call" | custom-call | flops 1000 | bytes 1000 | tf_op jit(solution)/shard_map/near_last/pallas_call | solution.py:374
  77.0 2.7 %collective-permute-done.13.refs_3_ = f32[208,128]{1,0:T(8,128)S(1)} collective-permute-done((f32[208,128]{1,0:T(8,128)S(1)}, f32[208,128]{1,0:T(8,128)S(1)}, u32[]{:S(2)}, u32[]{:S(2)}) %collective-permute-start.13) | collective-permute-done | bytes 106528 | tf_op jit(solution)/shard_map/ppermute | solution.py:417
  79.7 2.9 %tree_merge.7 = f32[4,128]{1,0:T(4,128)} custom-call(f32[208,128]{1,0:T(8,128)S(1)} %tree_merge.6.refs_0_, f32[208,128]{1,0:T(8,128)S(1)} %collective-permute-done.11.refs_1_, f32[208,128]{1,0:T(8,128)S(1)} %collective-permute-done.12.refs_2_, f32[208,128]{1,0:T(8,128)S(1)} %collective-permute-done.13.refs_3_, s32[255,128]{1,0:T(8,128)S(1)} %copy-done.1), custom_call_target="tpu_custom_call" | custom-call | flops 134217728 | bytes 425984 | tf_op jit(solution)/shard_map/tree_merge/pallas_call | solution.py:251
  82.6 1.6 %add_multiply_fusion = f32[8,512,128]{2,1,0:T(8,128)} fusion(f32[8,512,128]{2,1,0:T(8,128)S(1)} %near_last.1, f32[8,512,128]{2,1,0:T(8,128)S(1)} %collective-permute-done.14), kind=kLoop, calls=%fused_computation | loop fusion | flops 1048576 | bytes 6291456 | tf_op jit(solution)/shard_map/mul | solution.py:479
  (31 shorter events, 6.8 us)
Async XLA Ops:
  0.6 1.2 %copy-start.2 = (bf16[4096,128]{1,0:T(8,128)(2,1)S(1)}, bf16[4096,128]{1,0:T(8,128)(2,1)}, u32[]{:S(2)}) copy-start(bf16[4096,128]{1,0:T(8,128)(2,1)} %probes.1) | copy-start | bytes 3145732
  1.9 1.0 %copy-start.3 = (bf16[4096,64]{0,1:T(8,128)(2,1)S(1)}, bf16[4096,64]{0,1:T(8,128)(2,1)}, u32[]{:S(2)}) copy-start(bf16[4096,64]{0,1:T(8,128)(2,1)} %param.7) | copy-start | bytes 1572868
  2.9 0.7 copy-start.5
  3.6 25.6 %copy-start.4 = (s32[8,12]{1,0:T(8,128)S(1)}, s32[8,12]{1,0:T(8,128)}, u32[]{:S(2)}) copy-start(s32[8,12]{1,0:T(8,128)} %refs_0_.5) | copy-start | bytes 1156
  6.3 29.6 %collective-permute-start.3 = (bf16[8,768,128]{2,1,0:T(8,128)(2,1)S(1)}, bf16[8,768,128]{2,1,0:T(8,128)(2,1)S(1)}, u32[]{:S(2)}, u32[]{:S(2)}) collective-permute-start(bf16[8,768,128]{2,1,0:T(8,128)(2,1)S(1)} %get-tuple-element.46.pack.refs_2_.refs_6_), channel_id=1, source_target_pairs={{3,1},{0,2},{7,5},{4,6},{11,9},{8,10},{15,13},{12,14},{19,17},{16,... | collective-permute-start | bytes 4718600 | tf_op jit(solution)/shard_map/ppermute | solution.py:408
  11.2 24.6 %collective-permute-start.4 = (bf16[8,768,128]{2,1,0:T(8,128)(2,1)S(1)}, bf16[8,768,128]{2,1,0:T(8,128)(2,1)S(1)}, u32[]{:S(2)}, u32[]{:S(2)}) collective-permute-start(bf16[8,768,128]{2,1,0:T(8,128)(2,1)S(1)} %get-tuple-element.46.pack.refs_2_.refs_6_), channel_id=1, source_target_pairs={{3,7},{7,11},{4,0},{11,15},{8,4},{15,19},{12,8},{19,23},{16,12},{2... | collective-permute-start | bytes 4718600 | tf_op jit(solution)/shard_map/ppermute | solution.py:408
  12.5 23.3 %collective-permute-start.5 = (bf16[8,768,128]{2,1,0:T(8,128)(2,1)S(1)}, bf16[8,768,128]{2,1,0:T(8,128)(2,1)S(1)}, u32[]{:S(2)}, u32[]{:S(2)}) collective-permute-start(bf16[8,768,128]{2,1,0:T(8,128)(2,1)S(1)} %get-tuple-element.46.pack.refs_2_.refs_6_), channel_id=1, source_target_pairs={{1,0},{2,3},{5,4},{6,7},{9,8},{10,11},{13,12},{14,15},{17,16},{18,... | collective-permute-start | bytes 4718600 | tf_op jit(solution)/shard_map/ppermute | solution.py:408
  13.8 22.0 %collective-permute-start.6 = (bf16[8,512,128]{2,1,0:T(8,128)(2,1)S(1)}, bf16[8,512,128]{2,1,0:T(8,128)(2,1)S(1)}, u32[]{:S(2)}, u32[]{:S(2)}) collective-permute-start(bf16[8,512,128]{2,1,0:T(8,128)(2,1)S(1)} %get-tuple-element.44.rows.refs_1_.refs_2_), channel_id=1, source_target_pairs={{1,0},{2,3},{5,4},{6,7},{9,8},{10,11},{13,12},{14,15},{17,16},{18,... | collective-permute-start | bytes 3145736 | tf_op jit(solution)/shard_map/ppermute | solution.py:408
  15.1 10.0 %collective-permute-start = (s32[8,12]{1,0:T(8,128)}, s32[8,12]{1,0:T(8,128)S(1)}, u32[]{:S(2)}, u32[]{:S(2)}) collective-permute-start(s32[8,12]{1,0:T(8,128)} %refs_0_.5), channel_id=1, source_target_pairs={{0,1},{1,0},{2,3},{3,2},{4,5},{5,4},{6,7},{7,6},{8,9},{9,8},{10,11... | collective-permute-start | bytes 1160 | tf_op jit(solution)/shard_map/ppermute | solution.py:417
  16.5 0.9 %copy-start = (s32[255,128]{1,0:T(8,128)S(1)}, s32[255,128]{1,0:T(8,128)}, u32[]{:S(2)}) copy-start(s32[255,128]{1,0:T(8,128)} %refs_4_.1) | copy-start | bytes 391684
  17.4 0.7 copy-start.6
  25.1 1.4 %collective-permute-start.1 = (f32[208,128]{1,0:T(8,128)S(1)}, f32[208,128]{1,0:T(8,128)S(1)}, u32[]{:S(2)}, u32[]{:S(2)}) collective-permute-start(f32[208,128]{1,0:T(8,128)S(1)} %local_tree.1.refs_0_), channel_id=1, source_target_pairs={{0,1},{1,0},{2,3},{3,2},{4,5},{5,4},{6,7},{7,6},{8,9},{9,8},{10,11... | collective-permute-start | bytes 319496 | tf_op jit(solution)/shard_map/ppermute | solution.py:417
  27.5 13.3 %copy-start.1 = (s32[255,128]{1,0:T(8,128)S(1)}, s32[255,128]{1,0:T(8,128)}, u32[]{:S(2)}) copy-start(s32[255,128]{1,0:T(8,128)} %refs_4_.1) | copy-start | bytes 391684
  27.5 8.3 %collective-permute-start.2 = (f32[208,128]{1,0:T(8,128)S(1)}, f32[208,128]{1,0:T(8,128)S(1)}, u32[]{:S(2)}, u32[]{:S(2)}) collective-permute-start(f32[208,128]{1,0:T(8,128)S(1)} %tree_merge.4.refs_0_), channel_id=1, source_target_pairs={{0,2},{1,3},{2,0},{3,1},{4,6},{5,7},{6,4},{7,5},{8,10},{9,11},{10,... | collective-permute-start | bytes 319496 | tf_op jit(solution)/shard_map/ppermute | solution.py:417
  35.9 21.7 %collective-permute-start.8 = (bf16[8,768,128]{2,1,0:T(8,128)(2,1)S(1)}, bf16[8,768,128]{2,1,0:T(8,128)(2,1)S(1)}, u32[]{:S(2)}, u32[]{:S(2)}) collective-permute-start(bf16[8,768,128]{2,1,0:T(8,128)(2,1)S(1)} %collective-permute-done.5), channel_id=1, source_target_pairs={{0,3},{3,0},{4,7},{7,4},{8,11},{11,8},{12,15},{15,12},{16,19},{19,... | collective-permute-start | bytes 4718600 | tf_op jit(solution)/shard_map/ppermute | solution.py:408
  38.0 19.6 %collective-permute-start.9 = (bf16[8,768,128]{2,1,0:T(8,128)(2,1)S(1)}, bf16[8,768,128]{2,1,0:T(8,128)(2,1)S(1)}, u32[]{:S(2)}, u32[]{:S(2)}) collective-permute-start(bf16[8,768,128]{2,1,0:T(8,128)(2,1)S(1)} %collective-permute-done.3.refs_8_), channel_id=1, source_target_pairs={{1,5},{5,9},{6,2},{9,13},{10,6},{13,17},{14,10},{17,21},{18,14},{2... | collective-permute-start | bytes 4718600 | tf_op jit(solution)/shard_map/ppermute | solution.py:408
  38.8 6.4 %collective-permute-start.10 = (bf16[8,512,128]{2,1,0:T(8,128)(2,1)S(1)}, bf16[8,512,128]{2,1,0:T(8,128)(2,1)S(1)}, u32[]{:S(2)}, u32[]{:S(2)}) collective-permute-start(bf16[8,512,128]{2,1,0:T(8,128)(2,1)S(1)} %get-tuple-element.44.rows.refs_1_.refs_2_), channel_id=1, source_target_pairs={{0,1},{3,2},{4,5},{7,6},{8,9},{11,10},{12,13},{15,14},{16,17},{19,... | collective-permute-start | bytes 3145736 | tf_op jit(solution)/shard_map/ppermute | solution.py:408
  41.8 13.7 %collective-permute-start.7 = (f32[208,128]{1,0:T(8,128)S(1)}, f32[208,128]{1,0:T(8,128)S(1)}, u32[]{:S(2)}, u32[]{:S(2)}) collective-permute-start(f32[208,128]{1,0:T(8,128)S(1)} %tree_merge.5.refs_0_), channel_id=1, source_target_pairs={{0,4},{1,5},{2,6},{3,7},{4,0},{5,1},{6,2},{7,3},{8,12},{9,13},{10,... | collective-permute-start | bytes 319496 | tf_op jit(solution)/shard_map/ppermute | solution.py:417
  61.4 21.2 %collective-permute-start.14 = (f32[8,512,128]{2,1,0:T(8,128)S(1)}, f32[8,512,128]{2,1,0:T(8,128)S(1)}, u32[]{:S(2)}, u32[]{:S(2)}) collective-permute-start(f32[8,512,128]{2,1,0:T(8,128)S(1)} %near_beside.1), channel_id=1, source_target_pairs={{0,1},{1,0},{2,3},{3,2},{4,5},{5,4},{6,7},{7,6},{8,9},{9,8},{10,11... | collective-permute-start | bytes 6291464 | tf_op jit(solution)/shard_map/ppermute | solution.py:417
  62.5 14.5 %collective-permute-start.11 = (f32[208,128]{1,0:T(8,128)S(1)}, f32[208,128]{1,0:T(8,128)S(1)}, u32[]{:S(2)}, u32[]{:S(2)}) collective-permute-start(f32[208,128]{1,0:T(8,128)S(1)} %tree_merge.6.refs_0_), channel_id=1, source_target_pairs={{0,8},{1,9},{2,10},{3,11},{4,12},{5,13},{6,14},{7,15},{8,0},{9,1},... | collective-permute-start | bytes 319496 | tf_op jit(solution)/shard_map/ppermute | solution.py:417
  68.8 8.2 %collective-permute-start.12 = (f32[208,128]{1,0:T(8,128)S(1)}, f32[208,128]{1,0:T(8,128)S(1)}, u32[]{:S(2)}, u32[]{:S(2)}) collective-permute-start(f32[208,128]{1,0:T(8,128)S(1)} %tree_merge.6.refs_0_), channel_id=1, source_target_pairs={{0,16},{1,17},{2,18},{3,19},{4,20},{5,21},{6,22},{7,23},{8,24},{9,... | collective-permute-start | bytes 319496 | tf_op jit(solution)/shard_map/ppermute | solution.py:417
  71.1 8.6 %collective-permute-start.13 = (f32[208,128]{1,0:T(8,128)S(1)}, f32[208,128]{1,0:T(8,128)S(1)}, u32[]{:S(2)}, u32[]{:S(2)}) collective-permute-start(f32[208,128]{1,0:T(8,128)S(1)} %tree_merge.6.refs_0_), channel_id=1, source_target_pairs={{0,24},{1,25},{2,26},{3,27},{4,28},{5,29},{6,30},{7,31},{8,16},{9,... | collective-permute-start | bytes 319496 | tf_op jit(solution)/shard_map/ppermute | solution.py:417

commit v8 on v6

--- a/solution.py
+++ b/solution.py
@@ -236,7 +236,7 @@
         out[...] = samples[0]
     else:
         column = lax.broadcasted_iota(jnp.int32, (piece, skel), 1)
-        row = lax.broadcasted_iota(jnp.int32, (piece, skel), 0) + rank * piece
+        row = lax.broadcasted_iota(jnp.int32, (piece, skel), 0) + lax.shift_right_logical(rank, 1) * piece
         take = jnp.where(column == row, 1.0, 0.0).astype(BF16)
         hi, lo = split(samples[0])
         low = (samples[0] - hi.astype(F32) - lo.astype(F32)).astype(BF16)
@@ -429,20 +429,39 @@
 
     node = level(exchange(node, 0, 1), 0)
     own_pack, node = tie(pack, node)
-    parts = exchange(node, 1, 1)
+    other = send(node, [(1, 0, 2), (2, 0, 1)])
+
+    def among_inner(x, shift, stage):
+        parts = [x]
+        for d in range(1, 1 << stage):
+            step = d << shift - sub_bits
+            pairs = [
+                (place * sub_count + inner, (place ^ step) * sub_count + inner)
+                for place in range(leaf_count)
+                for inner in (1, 2)
+            ]
+            parts.append(lax.ppermute(x, axes, pairs))
+        return parts
+
     own_set = (own_base, single, [own_pack])
     (beside,) = near_call(
         [(1, beside_lists, beside_rows, None)], [own_set], ((0, 0),), dim, "near_own"
     )
 
+    other, beside = tie(other, beside)
+    node = level([node, other], 1)
+    shift, stage = sub_bits, 1
+    parts = among_inner(node, shift, stage)
     *parts, outer_across, outer_next, own_pack, beside = tie(
         *parts, outer_across, outer_next, own_pack, beside
     )
+    forwarded = send(outer_across, [(1, 1, 1), (2, -1, 2)])
     inner_across = send(own_pack, [(2, 0, 0), (1, 0, 3)])
-    forwarded = send(outer_across, [(1, 1, 1), (2, -1, 2)])
-    node = level(parts, 1)
+    while shift + stage < bits:
+        node = level(parts, shift)
+        shift, stage = shift + stage, min(2, bits - shift - stage)
+        parts = among_inner(node, shift, stage)
     own_pack, node = tie(own_pack, node)
-    parts = exchange(node, 2, 1)
     own_set = (own_base, single, [own_pack])
     early_set = (early_base, by_edge, [outer_next, outer_across])
     own, beside = near_call(
@@ -457,21 +476,19 @@
     )
     given = exchange(beside, 0, 1)[1]
     *parts, beside = tie(*parts, beside)
-    shift, stage = 2, 1
-    while shift + stage < bits:
-        node = level(parts, shift)
-        shift, stage = shift + stage, min(2, bits - shift - stage)
-        parts = exchange(node, shift, stage)
+    piece = skel // count
+    root_rows = level(parts, shift, 2 * piece)
+    shared_rows = send(root_rows, [(1, 0, 0), (2, 0, 3)])
+    own, root_rows = tie(own, root_rows)
     (own,) = near_call([(0, near_lists, rows, own)], [late_set], ((0, 0),), dim, "near_last")
-    *parts, own = tie(*parts, own)
-    node = level(parts, shift, skel // count)
     near = (own + given) * (leaf ** -0.5)
-    if skel // count:
-        root = node.reshape(-1)
-    else:
-        size = skel * LANES // count
-        rank = lax.axis_index("leaf") * sub_count + lax.axis_index("sub")
-        root = lax.dynamic_slice_in_dim(node.reshape(-1), rank * size, size, 0)
+    sub_place = lax.axis_index("sub")
+    edge = (sub_place == 0) | (sub_place == sub_count - 1)
+    rank = lax.axis_index("leaf") * sub_count + sub_place
+    size = skel * LANES // count
+    root_rows = jnp.where(edge, shared_rows, root_rows).reshape(-1)
+    start = (rank % 2 if piece else rank) * size
+    root = lax.dynamic_slice_in_dim(root_rows, start, size, 0)
     return near.reshape(npts, LANES), root
 
 

time: 81.8 us -> 89.7 us (1.097)
  the two profiles are of different devices: /device:TPU:0 before, /device:TPU:4 now
where the time goes in v8:
time: 89.7 us; the launch traced here: 88.1 us
  Pallas kernels  39.6 us (44%)
  starting transfers between devices  28.5 us (32%)
  local copies, waits for them, and re-layouts  8.24 us (9%)
  waiting for transfers between devices  7.72 us (9%)
  other arithmetic  3.22 us (4%)
  between operations  0.91 us (1%)
    pallas_call x4, Pallas kernels, near_call(): pl.pallas_call(functools.partial(near_kernel, flips=flips, has_acc=tuple(...  24.7 us
    ppermute x4, starting transfers between devices, among_inner(): parts.append(lax.ppermute(x, axes, pairs))  15.3 us
    ppermute x6, starting transfers between devices, send(): return lax.ppermute(x, axes, pairs)  9.3 us
    unnamed x22, local copies, waits for them, and re-layouts  7.58 us
    pallas_call x1, Pallas kernels, local_tree_call(): pl.pallas_call(functools.partial(local_tree_kernel, dim=dim), in_specs=[p...  7 us
    ppermute x4, waiting for transfers between devices, among_inner(): parts.append(lax.ppermute(x, axes, pairs))  6.05 us
    pallas_call x4, Pallas kernels, merge_call(): pl.pallas_call(functools.partial(merge_kernel, dim=dim, blocks=blocks, sh...  5.29 us
    ppermute x4, starting transfers between devices, exchange(): lax.ppermute(x, axes, [(i, i ^ d << shift) for i in range(count)])  3.86 us
  transfers between devices with their start and end apart: 14, of which 4 were waited for; matrix products, arithmetic and copies ran while one was open for 1% of the time, Pallas kernels for 36%

profile of v8, /device:TPU:4, one launch (start us, length us, event | category | flops | bytes accessed | tf_op | source)
XLA Modules:
  0.0 88.1 jit_solution(14579284044188684193)
XLA Ops:
  0.6 1.2 %copy-done.6 = bf16[4096,128]{1,0:T(8,128)(2,1)S(1)} copy-done((bf16[4096,128]{1,0:T(8,128)(2,1)S(1)}, bf16[4096,128]{1,0:T(8,128)(2,1)}, u32[]{:S(2)}) %copy-start.6) | copy-done | bytes 1048600
  1.9 1.0 %copy-done.7 = bf16[4096,64]{0,1:T(8,128)(2,1)S(1)} copy-done((bf16[4096,64]{0,1:T(8,128)(2,1)S(1)}, bf16[4096,64]{0,1:T(8,128)(2,1)}, u32[]{:S(2)}) %copy-start.7) | copy-done | bytes 524312
  3.6 2.6 %tree_order.1 = (bf16[8,768,128]{2,1,0:T(8,128)(2,1)S(1)}, bf16[8,512,128]{2,1,0:T(8,128)(2,1)S(1)}) custom-call(bf16[64,4096]{1,0:T(8,128)(2,1)S(1)} %bitcast.5, s32[8,1,512]{2,1,0:T(1,128)S(1)} %bitcast.6, bf16[4096,128]{1,0:T(8,128)(2,1)S(1)} %copy-done.6), custom_call_target="tpu_custom_call" | custom-call | flops 268435456 | bytes 5242880 | tf_op jit(solution)/shard_map/tree_order/pallas_call | solution.py:94
  6.3 1.3 %collective-permute-start.5 = (bf16[8,768,128]{2,1,0:T(8,128)(2,1)S(1)}, bf16[8,768,128]{2,1,0:T(8,128)(2,1)S(1)}, u32[]{:S(2)}, u32[]{:S(2)}) collective-permute-start(bf16[8,768,128]{2,1,0:T(8,128)(2,1)S(1)} %get-tuple-element.44.pack.refs_2_.refs_5_), channel_id=1, source_target_pairs={{3,1},{0,2},{7,5},{4,6},{11,9},{8,10},{15,13},{12,14},{19,17},{16,... | collective-permute-start | bytes 4718600 | tf_op jit(solution)/shard_map/ppermute | solution.py:398
  8.3 3.3 %collective-permute-start.1 = (bf16[8,512,128]{2,1,0:T(8,128)(2,1)S(1)}, bf16[8,512,128]{2,1,0:T(8,128)(2,1)S(1)}, u32[]{:S(2)}, u32[]{:S(2)}) collective-permute-start(bf16[8,512,128]{2,1,0:T(8,128)(2,1)S(1)} %get-tuple-element.32.rows.refs_2_.refs_1_), channel_id=1, source_target_pairs={{0,1},{1,0},{2,3},{3,2},{4,5},{5,4},{6,7},{7,6},{8,9},{9,8},{10,11... | collective-permute-start | bytes 3145736 | tf_op jit(solution)/shard_map/ppermute | solution.py:407
  13.3 7.0 %local_tree.1.refs_0_ = f32[208,128]{1,0:T(8,128)S(1)} custom-call(bf16[8,768,128]{2,1,0:T(8,128)(2,1)S(1)} %get-tuple-element.44.pack.refs_2_.refs_5_, bf16[8,512,128]{2,1,0:T(8,128)(2,1)S(1)} %get-tuple-element.32.rows.refs_2_.refs_1_, s32[8,128]{1,0:T(8,128)S(1)} %copy-done.10, s32[255,128]{1,0:T(8,128)S(1)} %copy-done.2), custom_call_target="tpu_custom_call" | custom-call | flops 536870912 | bytes 3145728 | tf_op jit(solution)/shard_map/local_tree/pallas_call | solution.py:177
  22.7 2.2 %collective-permute-start.3 = (f32[208,128]{1,0:T(8,128)S(1)}, f32[208,128]{1,0:T(8,128)S(1)}, u32[]{:S(2)}, u32[]{:S(2)}) collective-permute-start(f32[208,128]{1,0:T(8,128)S(1)} %tree_merge.4.refs_0_), channel_id=1, source_target_pairs={{1,2},{2,1},{5,6},{6,5},{9,10},{10,9},{13,14},{14,13},{17,18},{18,... | collective-permute-start | bytes 319496 | tf_op jit(solution)/shard_map/ppermute | solution.py:398
  25.0 4.0 %near_own.1.refs_4_ = f32[8,512,128]{2,1,0:T(8,128)S(1)} custom-call(s32[8,12]{1,0:T(8,128)S(1)} %collective-permute-done.refs_0_.refs_1_, bf16[8,512,128]{2,1,0:T(8,128)(2,1)S(1)} %collective-permute-done.1.refs_1_.refs_3_, bf16[8,768,128]{2,1,0:T(8,128)(2,1)S(1)} %get-tuple-element.44.pack.refs_2_.refs_5_), custom_call_target="tpu_custom_call" | custom-call | flops 1000 | bytes 1000 | tf_op jit(solution)/shard_map/near_own/pallas_call | solution.py:365
  30.7 3.4 %collective-permute-start.4 = (f32[208,128]{1,0:T(8,128)S(1)}, f32[208,128]{1,0:T(8,128)S(1)}, u32[]{:S(2)}, u32[]{:S(2)}) collective-permute-start(f32[208,128]{1,0:T(8,128)S(1)} %tree_merge.5.refs_0_), channel_id=1, source_target_pairs={{1,5},{2,6},{5,1},{6,2},{9,13},{10,14},{13,9},{14,10},{17,21},{18,... | collective-permute-start | bytes 319496 | tf_op jit(solution)/shard_map/ppermute | solution.py:443
  34.1 3.2 %collective-permute-done.4.refs_1_ = f32[208,128]{1,0:T(8,128)S(1)} collective-permute-done((f32[208,128]{1,0:T(8,128)S(1)}, f32[208,128]{1,0:T(8,128)S(1)}, u32[]{:S(2)}, u32[]{:S(2)}) %collective-permute-start.4) | collective-permute-done | bytes 106528 | tf_op jit(solution)/shard_map/ppermute | solution.py:443
  37.3 1.4 %collective-permute-start.10 = (bf16[8,768,128]{2,1,0:T(8,128)(2,1)S(1)}, bf16[8,768,128]{2,1,0:T(8,128)(2,1)S(1)}, u32[]{:S(2)}, u32[]{:S(2)}) collective-permute-start(bf16[8,768,128]{2,1,0:T(8,128)(2,1)S(1)} %get-tuple-element.44.pack.refs_2_.refs_5_), channel_id=1, source_target_pairs={{2,0},{1,3},{6,4},{5,7},{10,8},{9,11},{14,12},{13,15},{18,16},{17,... | collective-permute-start | bytes 4718600 | tf_op jit(solution)/shard_map/ppermute | solution.py:398
  38.7 1.3 %collective-permute-start.11 = (bf16[8,768,128]{2,1,0:T(8,128)(2,1)S(1)}, bf16[8,768,128]{2,1,0:T(8,128)(2,1)S(1)}, u32[]{:S(2)}, u32[]{:S(2)}) collective-permute-start(bf16[8,768,128]{2,1,0:T(8,128)(2,1)S(1)} %collective-permute-done.5.refs_7_), channel_id=1, source_target_pairs={{1,5},{5,9},{6,2},{9,13},{10,6},{13,17},{14,10},{17,21},{18,14},{2... | collective-permute-start | bytes 4718600 | tf_op jit(solution)/shard_map/ppermute | solution.py:398
  41.0 5.5 %collective-permute-start.7 = (f32[208,128]{1,0:T(8,128)S(1)}, f32[208,128]{1,0:T(8,128)S(1)}, u32[]{:S(2)}, u32[]{:S(2)}) collective-permute-start(f32[208,128]{1,0:T(8,128)S(1)} %tree_merge.6.refs_0_), channel_id=1, source_target_pairs={{1,9},{2,10},{5,13},{6,14},{9,1},{10,2},{13,5},{14,6},{17,25},{18,... | collective-permute-start | bytes 319496 | tf_op jit(solution)/shard_map/ppermute | solution.py:443
  46.5 4.5 %collective-permute-start.8 = (f32[208,128]{1,0:T(8,128)S(1)}, f32[208,128]{1,0:T(8,128)S(1)}, u32[]{:S(2)}, u32[]{:S(2)}) collective-permute-start(f32[208,128]{1,0:T(8,128)S(1)} %tree_merge.6.refs_0_), channel_id=1, source_target_pairs={{1,17},{2,18},{5,21},{6,22},{9,25},{10,26},{13,29},{14,30},{17,1},... | collective-permute-start | bytes 319496 | tf_op jit(solution)/shard_map/ppermute | solution.py:443
  51.0 1.9 %collective-permute-start.9 = (f32[208,128]{1,0:T(8,128)S(1)}, f32[208,128]{1,0:T(8,128)S(1)}, u32[]{:S(2)}, u32[]{:S(2)}) collective-permute-start(f32[208,128]{1,0:T(8,128)S(1)} %tree_merge.6.refs_0_), channel_id=1, source_target_pairs={{1,25},{2,26},{5,29},{6,30},{9,17},{10,18},{13,21},{14,22},{17,9},... | collective-permute-start | bytes 319496 | tf_op jit(solution)/shard_map/ppermute | solution.py:443
  52.9 11.7 %near_early.1 = (f32[8,512,128]{2,1,0:T(8,128)S(1)}, f32[8,512,128]{2,1,0:T(8,128)S(1)}) custom-call(s32[8,12]{1,0:T(8,128)S(1)} %copy-done.8, s32[8,12]{1,0:T(8,128)S(1)} %collective-permute-done.refs_0_.refs_1_, bf16[8,512,128]{2,1,0:T(8,128)(2,1)S(1)} %get-tuple-element.32.rows.refs_2_.refs_1_, ...), custom_call_target="tpu_custom_call" | custom-call | flops 1000 | bytes 1000 | tf_op jit(solution)/shard_map/near_early/pallas_call | solution.py:365
  64.6 2.9 %collective-permute-done.9.refs_3_ = f32[208,128]{1,0:T(8,128)S(1)} collective-permute-done((f32[208,128]{1,0:T(8,128)S(1)}, f32[208,128]{1,0:T(8,128)S(1)}, u32[]{:S(2)}, u32[]{:S(2)}) %collective-permute-start.9) | collective-permute-done | bytes 106528 | tf_op jit(solution)/shard_map/ppermute | solution.py:443
  67.5 5.1 %near_beside.1 = f32[8,512,128]{2,1,0:T(8,128)} custom-call(s32[8,12]{1,0:T(8,128)S(1)} %collective-permute-done.refs_0_.refs_1_, bf16[8,512,128]{2,1,0:T(8,128)(2,1)S(1)} %collective-permute-done.1.refs_1_.refs_3_, f32[8,512,128]{2,1,0:T(8,128)S(1)} %get-tuple-element.53.refs_2_, bf16[8,768,128]{2,1,0:T(8,128)(2,1)S(1)} %collective-permute-done.10.refs_3_, ...), custom_call_target="tpu_custom_call" | custom-call | flops 1000 | bytes 1000 | tf_op jit(solution)/shard_map/near_beside/pallas_call | solution.py:365
  72.6 2.4 %tree_merge.7 = f32[8,128]{1,0:T(8,128)S(1)} custom-call(f32[208,128]{1,0:T(8,128)S(1)} %tree_merge.6.refs_0_, f32[208,128]{1,0:T(8,128)S(1)} %collective-permute-done.7.refs_1_, f32[208,128]{1,0:T(8,128)S(1)} %collective-permute-done.8.refs_2_, f32[208,128]{1,0:T(8,128)S(1)} %collective-permute-done.9.refs_3_, s32[255,128]{1,0:T(8,128)S(1)} %copy-done.3), custom_call_target="tpu_custom_call" | custom-call | flops 134217728 | bytes 425984 | tf_op jit(solution)/shard_map/tree_merge/pallas_call | solution.py:251
  75.0 2.4 %collective-permute-start.13 = (f32[8,128]{1,0:T(8,128)S(1)}, f32[8,128]{1,0:T(8,128)S(1)}, u32[]{:S(2)}, u32[]{:S(2)}) collective-permute-start(f32[8,128]{1,0:T(8,128)S(1)} %tree_merge.7), channel_id=1, source_target_pairs={{1,0},{2,3},{5,4},{6,7},{9,8},{10,11},{13,12},{14,15},{17,16},{18,... | collective-permute-start | bytes 12296 | tf_op jit(solution)/shard_map/ppermute | solution.py:398
  77.4 1.4 %copy-done.1 = bf16[8,768,128]{2,1,0:T(8,128)(2,1)S(1)} copy-done((bf16[8,768,128]{2,1,0:T(8,128)(2,1)S(1)}, bf16[8,768,128]{2,1,0:T(8,128)(2,1)}, u32[]{:S(2)}) %copy-start.1) | copy-done | bytes 1572888
  78.8 1.6 %copy-done.5 = f32[8,512,128]{2,1,0:T(8,128)S(1)} copy-done((f32[8,512,128]{2,1,0:T(8,128)S(1)}, f32[8,512,128]{2,1,0:T(8,128)}, u32[]{:S(2)}) %copy-start.5) | copy-done | bytes 2097176
  80.4 3.8 %near_last.1 = f32[8,512,128]{2,1,0:T(8,128)S(1)} custom-call(s32[8,12]{1,0:T(8,128)S(1)} %copy-done.8, bf16[8,512,128]{2,1,0:T(8,128)(2,1)S(1)} %get-tuple-element.32.rows.refs_2_.refs_1_, f32[8,512,128]{2,1,0:T(8,128)S(1)} %copy-done.5, bf16[8,768,128]{2,1,0:T(8,128)(2,1)S(1)} %collective-permute-done.10.refs_3_, bf16[8,768,128]{2,1,0:T(8,128)(2,1)S(1)} %copy-done.1), custom_call_target="tpu_custom_call" | custom-call | flops 1000 | bytes 1000 | tf_op jit(solution)/shard_map/near_last/pallas_call | solution.py:365
  84.9 3.2 %add_multiply_fusion = f32[8,512,128]{2,1,0:T(8,128)} fusion(f32[8,512,128]{2,1,0:T(8,128)S(1)} %near_last.1, f32[8,512,128]{2,1,0:T(8,128)} %collective-permute-done.12), kind=kLoop, calls=%fused_computation | loop fusion | flops 1048576 | bytes 6291456 | tf_op jit(solution)/shard_map/mul | solution.py:484
  (39 shorter events, 8.9 us)
Async XLA Ops:
  0.6 1.2 %copy-start.6 = (bf16[4096,128]{1,0:T(8,128)(2,1)S(1)}, bf16[4096,128]{1,0:T(8,128)(2,1)}, u32[]{:S(2)}) copy-start(bf16[4096,128]{1,0:T(8,128)(2,1)} %probes.1) | copy-start | bytes 3145732
  1.9 1.0 %copy-start.7 = (bf16[4096,64]{0,1:T(8,128)(2,1)S(1)}, bf16[4096,64]{0,1:T(8,128)(2,1)}, u32[]{:S(2)}) copy-start(bf16[4096,64]{0,1:T(8,128)(2,1)} %param.7) | copy-start | bytes 1572868
  2.9 0.7 copy-start.9
  6.3 31.0 %collective-permute-start.5 = (bf16[8,768,128]{2,1,0:T(8,128)(2,1)S(1)}, bf16[8,768,128]{2,1,0:T(8,128)(2,1)S(1)}, u32[]{:S(2)}, u32[]{:S(2)}) collective-permute-start(bf16[8,768,128]{2,1,0:T(8,128)(2,1)S(1)} %get-tuple-element.44.pack.refs_2_.refs_5_), channel_id=1, source_target_pairs={{3,1},{0,2},{7,5},{4,6},{11,9},{8,10},{15,13},{12,14},{19,17},{16,... | collective-permute-start | bytes 4718600 | tf_op jit(solution)/shard_map/ppermute | solution.py:398
  7.6 29.7 %collective-permute-start.6 = (bf16[8,768,128]{2,1,0:T(8,128)(2,1)S(1)}, bf16[8,768,128]{2,1,0:T(8,128)(2,1)S(1)}, u32[]{:S(2)}, u32[]{:S(2)}) collective-permute-start(bf16[8,768,128]{2,1,0:T(8,128)(2,1)S(1)} %get-tuple-element.44.pack.refs_2_.refs_5_), channel_id=1, source_target_pairs={{3,7},{7,11},{4,0},{11,15},{8,4},{15,19},{12,8},{19,23},{16,12},{2... | collective-permute-start | bytes 4718600 | tf_op jit(solution)/shard_map/ppermute | solution.py:398
  8.3 16.6 %collective-permute-start.1 = (bf16[8,512,128]{2,1,0:T(8,128)(2,1)S(1)}, bf16[8,512,128]{2,1,0:T(8,128)(2,1)S(1)}, u32[]{:S(2)}, u32[]{:S(2)}) collective-permute-start(bf16[8,512,128]{2,1,0:T(8,128)(2,1)S(1)} %get-tuple-element.32.rows.refs_2_.refs_1_), channel_id=1, source_target_pairs={{0,1},{1,0},{2,3},{3,2},{4,5},{5,4},{6,7},{7,6},{8,9},{9,8},{10,11... | collective-permute-start | bytes 3145736 | tf_op jit(solution)/shard_map/ppermute | solution.py:407
  11.6 8.7 %collective-permute-start = (s32[8,12]{1,0:T(8,128)}, s32[8,12]{1,0:T(8,128)S(1)}, u32[]{:S(2)}, u32[]{:S(2)}) collective-permute-start(s32[8,12]{1,0:T(8,128)} %refs_0_.3), channel_id=1, source_target_pairs={{0,1},{1,0},{2,3},{3,2},{4,5},{5,4},{6,7},{7,6},{8,9},{9,8},{10,11... | collective-permute-start | bytes 1160 | tf_op jit(solution)/shard_map/ppermute | solution.py:407
  11.7 0.9 %copy-start.2 = (s32[255,128]{1,0:T(8,128)S(1)}, s32[255,128]{1,0:T(8,128)}, u32[]{:S(2)}) copy-start(s32[255,128]{1,0:T(8,128)} %refs_4_.1) | copy-start | bytes 391684
  20.3 1.4 %collective-permute-start.2 = (f32[208,128]{1,0:T(8,128)S(1)}, f32[208,128]{1,0:T(8,128)S(1)}, u32[]{:S(2)}, u32[]{:S(2)}) collective-permute-start(f32[208,128]{1,0:T(8,128)S(1)} %local_tree.1.refs_0_), channel_id=1, source_target_pairs={{0,1},{1,0},{2,3},{3,2},{4,5},{5,4},{6,7},{7,6},{8,9},{9,8},{10,11... | collective-permute-start | bytes 319496 | tf_op jit(solution)/shard_map/ppermute | solution.py:407
  22.7 7.0 %copy-start.3 = (s32[255,128]{1,0:T(8,128)S(1)}, s32[255,128]{1,0:T(8,128)}, u32[]{:S(2)}) copy-start(s32[255,128]{1,0:T(8,128)} %refs_4_.1) | copy-start | bytes 391684
  22.7 30.2 %copy-start.8 = (s32[8,12]{1,0:T(8,128)S(1)}, s32[8,12]{1,0:T(8,128)}, u32[]{:S(2)}) copy-start(s32[8,12]{1,0:T(8,128)} %refs_0_.3) | copy-start | bytes 1156
  22.7 7.0 %collective-permute-start.3 = (f32[208,128]{1,0:T(8,128)S(1)}, f32[208,128]{1,0:T(8,128)S(1)}, u32[]{:S(2)}, u32[]{:S(2)}) collective-permute-start(f32[208,128]{1,0:T(8,128)S(1)} %tree_merge.4.refs_0_), channel_id=1, source_target_pairs={{1,2},{2,1},{5,6},{6,5},{9,10},{10,9},{13,14},{14,13},{17,18},{18,... | collective-permute-start | bytes 319496 | tf_op jit(solution)/shard_map/ppermute | solution.py:398
  30.7 6.6 %collective-permute-start.4 = (f32[208,128]{1,0:T(8,128)S(1)}, f32[208,128]{1,0:T(8,128)S(1)}, u32[]{:S(2)}, u32[]{:S(2)}) collective-permute-start(f32[208,128]{1,0:T(8,128)S(1)} %tree_merge.5.refs_0_), channel_id=1, source_target_pairs={{1,5},{2,6},{5,1},{6,2},{9,13},{10,14},{13,9},{14,10},{17,21},{18,... | collective-permute-start | bytes 319496 | tf_op jit(solution)/shard_map/ppermute | solution.py:443
  37.3 30.2 %collective-permute-start.10 = (bf16[8,768,128]{2,1,0:T(8,128)(2,1)S(1)}, bf16[8,768,128]{2,1,0:T(8,128)(2,1)S(1)}, u32[]{:S(2)}, u32[]{:S(2)}) collective-permute-start(bf16[8,768,128]{2,1,0:T(8,128)(2,1)S(1)} %get-tuple-element.44.pack.refs_2_.refs_5_), channel_id=1, source_target_pairs={{2,0},{1,3},{6,4},{5,7},{10,8},{9,11},{14,12},{13,15},{18,16},{17,... | collective-permute-start | bytes 4718600 | tf_op jit(solution)/shard_map/ppermute | solution.py:398
  38.7 28.8 %collective-permute-start.11 = (bf16[8,768,128]{2,1,0:T(8,128)(2,1)S(1)}, bf16[8,768,128]{2,1,0:T(8,128)(2,1)S(1)}, u32[]{:S(2)}, u32[]{:S(2)}) collective-permute-start(bf16[8,768,128]{2,1,0:T(8,128)(2,1)S(1)} %collective-permute-done.5.refs_7_), channel_id=1, source_target_pairs={{1,5},{5,9},{6,2},{9,13},{10,6},{13,17},{14,10},{17,21},{18,14},{2... | collective-permute-start | bytes 4718600 | tf_op jit(solution)/shard_map/ppermute | solution.py:398
  41.0 23.6 %collective-permute-start.7 = (f32[208,128]{1,0:T(8,128)S(1)}, f32[208,128]{1,0:T(8,128)S(1)}, u32[]{:S(2)}, u32[]{:S(2)}) collective-permute-start(f32[208,128]{1,0:T(8,128)S(1)} %tree_merge.6.refs_0_), channel_id=1, source_target_pairs={{1,9},{2,10},{5,13},{6,14},{9,1},{10,2},{13,5},{14,6},{17,25},{18,... | collective-permute-start | bytes 319496 | tf_op jit(solution)/shard_map/ppermute | solution.py:443
  46.5 18.2 %collective-permute-start.8 = (f32[208,128]{1,0:T(8,128)S(1)}, f32[208,128]{1,0:T(8,128)S(1)}, u32[]{:S(2)}, u32[]{:S(2)}) collective-permute-start(f32[208,128]{1,0:T(8,128)S(1)} %tree_merge.6.refs_0_), channel_id=1, source_target_pairs={{1,17},{2,18},{5,21},{6,22},{9,25},{10,26},{13,29},{14,30},{17,1},... | collective-permute-start | bytes 319496 | tf_op jit(solution)/shard_map/ppermute | solution.py:443
  51.0 16.5 %collective-permute-start.9 = (f32[208,128]{1,0:T(8,128)S(1)}, f32[208,128]{1,0:T(8,128)S(1)}, u32[]{:S(2)}, u32[]{:S(2)}) collective-permute-start(f32[208,128]{1,0:T(8,128)S(1)} %tree_merge.6.refs_0_), channel_id=1, source_target_pairs={{1,25},{2,26},{5,29},{6,30},{9,17},{10,18},{13,21},{14,22},{17,9},... | collective-permute-start | bytes 319496 | tf_op jit(solution)/shard_map/ppermute | solution.py:443
  64.6 8.0 %copy-start.4 = (f32[8,512,128]{2,1,0:T(8,128)}, f32[8,512,128]{2,1,0:T(8,128)S(1)}, u32[]{:S(2)}) copy-start(f32[8,512,128]{2,1,0:T(8,128)S(1)} %get-tuple-element.60.refs_2_) | copy-start | bytes 6291460
  67.5 5.1 %copy-start = (bf16[8,768,128]{2,1,0:T(8,128)(2,1)}, bf16[8,768,128]{2,1,0:T(8,128)(2,1)S(1)}, u32[]{:S(2)}) copy-start(bf16[8,768,128]{2,1,0:T(8,128)(2,1)S(1)} %collective-permute-done.11.refs_4_) | copy-start | bytes 4718596
  72.6 12.3 %collective-permute-start.12 = (f32[8,512,128]{2,1,0:T(8,128)}, f32[8,512,128]{2,1,0:T(8,128)}, u32[]{:S(2)}, u32[]{:S(2)}) collective-permute-start(f32[8,512,128]{2,1,0:T(8,128)} %near_beside.1), channel_id=1, source_target_pairs={{0,1},{1,0},{2,3},{3,2},{4,5},{5,4},{6,7},{7,6},{8,9},{9,8},{10,11... | collective-permute-start | bytes 6291464 | tf_op jit(solution)/shard_map/ppermute | solution.py:407
  75.0 9.2 %collective-permute-start.13 = (f32[8,128]{1,0:T(8,128)S(1)}, f32[8,128]{1,0:T(8,128)S(1)}, u32[]{:S(2)}, u32[]{:S(2)}) collective-permute-start(f32[8,128]{1,0:T(8,128)S(1)} %tree_merge.7), channel_id=1, source_target_pairs={{1,0},{2,3},{5,4},{6,7},{9,8},{10,11},{13,12},{14,15},{17,16},{18,... | collective-permute-start | bytes 12296 | tf_op jit(solution)/shard_map/ppermute | solution.py:398
  77.4 1.4 %copy-start.1 = (bf16[8,768,128]{2,1,0:T(8,128)(2,1)S(1)}, bf16[8,768,128]{2,1,0:T(8,128)(2,1)}, u32[]{:S(2)}) copy-start(bf16[8,768,128]{2,1,0:T(8,128)(2,1)} %copy-done) | copy-start | bytes 4718596
  78.8 1.6 %copy-start.5 = (f32[8,512,128]{2,1,0:T(8,128)S(1)}, f32[8,512,128]{2,1,0:T(8,128)}, u32[]{:S(2)}) copy-start(f32[8,512,128]{2,1,0:T(8,128)} %copy-done.4) | copy-start | bytes 6291460
  (1 other events, 0.7 us)

commit v9 on v6

--- a/solution.py
+++ b/solution.py
@@ -451,17 +451,17 @@
     )
 
     *parts, inner_across, forwarded, beside = tie(*parts, inner_across, forwarded, beside)
-    late_set = (late_base, by_edge, [inner_across, forwarded])
-    (beside,) = near_call(
-        [(1, beside_lists, beside_rows, beside)], [late_set], ((0, 0),), dim, "near_beside"
-    )
-    given = exchange(beside, 0, 1)[1]
-    *parts, beside = tie(*parts, beside)
     shift, stage = 2, 1
     while shift + stage < bits:
         node = level(parts, shift)
         shift, stage = shift + stage, min(2, bits - shift - stage)
         parts = exchange(node, shift, stage)
+    *parts, beside = tie(*parts, beside)
+    late_set = (late_base, by_edge, [inner_across, forwarded])
+    (beside,) = near_call(
+        [(1, beside_lists, beside_rows, beside)], [late_set], ((0, 0),), dim, "near_beside"
+    )
+    given = exchange(beside, 0, 1)[1]
     (own,) = near_call([(0, near_lists, rows, own)], [late_set], ((0, 0),), dim, "near_last")
     *parts, own = tie(*parts, own)
     node = level(parts, shift, skel // count)

time: 81.8 us -> 86.6 us (1.059)
  Pallas kernels: 37.8 us -> 41.5 us
  waiting for transfers between devices: 16 us -> 17.3 us
    pallas_call x4, Pallas kernels: 22.3 us -> 26 us  [near_call(): pl.pallas_call(functools.partial(near_kernel, flips=flips, has_acc=tuple(...]
    ppermute x9, waiting for transfers between devices: 9.39 us -> 11.2 us  [exchange(): lax.ppermute(x, axes, [(i, i ^ d << shift) for i in range(count)])]
where the time goes in v9:
time: 86.6 us; the launch traced here: 86.7 us
  Pallas kernels  41.5 us (48%)
  starting transfers between devices  20.9 us (24%)
  waiting for transfers between devices  17.3 us (20%)
  local copies, waits for them, and re-layouts  4.58 us (5%)
  other arithmetic  1.56 us (2%)
    pallas_call x4, Pallas kernels, near_call(): pl.pallas_call(functools.partial(near_kernel, flips=flips, has_acc=tuple(...  26 us
    ppermute x9, starting transfers between devices, exchange(): lax.ppermute(x, axes, [(i, i ^ d << shift) for i in range(count)])  12.6 us
    ppermute x9, waiting for transfers between devices, exchange(): lax.ppermute(x, axes, [(i, i ^ d << shift) for i in range(count)])  11.2 us
    ppermute x4, starting transfers between devices, send(): return lax.ppermute(x, axes, pairs)  8.31 us
    pallas_call x1, Pallas kernels, local_tree_call(): pl.pallas_call(functools.partial(local_tree_kernel, dim=dim), in_specs=[p...  7.01 us
    ppermute x4, waiting for transfers between devices, send(): return lax.ppermute(x, axes, pairs)  6.07 us
    pallas_call x4, Pallas kernels, merge_call(): pl.pallas_call(functools.partial(merge_kernel, dim=dim, blocks=blocks, sh...  5.87 us
    unnamed x14, local copies, waits for them, and re-layouts  4.58 us
  transfers between devices with their start and end apart: 13, of which 6 were waited for; matrix products, arithmetic and copies ran while one was open for 0% of the time, Pallas kernels for 38%

profile of v9, /device:TPU:0, one launch (start us, length us, event | category | flops | bytes accessed | tf_op | source)
XLA Modules:
  0.0 86.7 jit_solution(12548548127961372004)
XLA Ops:
  0.6 1.2 %copy-done.2 = bf16[4096,128]{1,0:T(8,128)(2,1)S(1)} copy-done((bf16[4096,128]{1,0:T(8,128)(2,1)S(1)}, bf16[4096,128]{1,0:T(8,128)(2,1)}, u32[]{:S(2)}) %copy-start.2) | copy-done | bytes 1048600
  1.9 1.0 %copy-done.3 = bf16[4096,64]{0,1:T(8,128)(2,1)S(1)} copy-done((bf16[4096,64]{0,1:T(8,128)(2,1)S(1)}, bf16[4096,64]{0,1:T(8,128)(2,1)}, u32[]{:S(2)}) %copy-start.3) | copy-done | bytes 524312
  3.6 2.6 %tree_order.1 = (bf16[8,768,128]{2,1,0:T(8,128)(2,1)S(1)}, bf16[8,512,128]{2,1,0:T(8,128)(2,1)S(1)}) custom-call(bf16[64,4096]{1,0:T(8,128)(2,1)S(1)} %bitcast.4, s32[8,1,512]{2,1,0:T(1,128)S(1)} %bitcast.5, bf16[4096,128]{1,0:T(8,128)(2,1)S(1)} %copy-done.2), custom_call_target="tpu_custom_call" | custom-call | flops 268435456 | bytes 5242880 | tf_op jit(solution)/shard_map/tree_order/pallas_call | solution.py:94
  6.3 5.0 %collective-permute-start.3 = (bf16[8,768,128]{2,1,0:T(8,128)(2,1)S(1)}, bf16[8,768,128]{2,1,0:T(8,128)(2,1)S(1)}, u32[]{:S(2)}, u32[]{:S(2)}) collective-permute-start(bf16[8,768,128]{2,1,0:T(8,128)(2,1)S(1)} %get-tuple-element.45.pack.refs_2_.refs_5_), channel_id=1, source_target_pairs={{3,1},{0,2},{7,5},{4,6},{11,9},{8,10},{15,13},{12,14},{19,17},{16,... | collective-permute-start | bytes 4718600 | tf_op jit(solution)/shard_map/ppermute | solution.py:398
  11.2 1.3 %collective-permute-start.4 = (bf16[8,768,128]{2,1,0:T(8,128)(2,1)S(1)}, bf16[8,768,128]{2,1,0:T(8,128)(2,1)S(1)}, u32[]{:S(2)}, u32[]{:S(2)}) collective-permute-start(bf16[8,768,128]{2,1,0:T(8,128)(2,1)S(1)} %get-tuple-element.45.pack.refs_2_.refs_5_), channel_id=1, source_target_pairs={{3,7},{7,11},{4,0},{11,15},{8,4},{15,19},{12,8},{19,23},{16,12},{2... | collective-permute-start | bytes 4718600 | tf_op jit(solution)/shard_map/ppermute | solution.py:398
  14.7 7.0 %local_tree.1.refs_0_ = f32[208,128]{1,0:T(8,128)S(1)} custom-call(bf16[8,768,128]{2,1,0:T(8,128)(2,1)S(1)} %get-tuple-element.45.pack.refs_2_.refs_5_, bf16[8,512,128]{2,1,0:T(8,128)(2,1)S(1)} %get-tuple-element.34.rows.refs_2_.refs_1_, s32[8,128]{1,0:T(8,128)S(1)} %copy-done.6, s32[255,128]{1,0:T(8,128)S(1)} %copy-done), custom_call_target="tpu_custom_call" | custom-call | flops 536870912 | bytes 3145728 | tf_op jit(solution)/shard_map/local_tree/pallas_call | solution.py:177
  21.9 1.2 %collective-permute-done.1.refs_1_ = f32[208,128]{1,0:T(8,128)S(1)} collective-permute-done((f32[208,128]{1,0:T(8,128)S(1)}, f32[208,128]{1,0:T(8,128)S(1)}, u32[]{:S(2)}, u32[]{:S(2)}) %collective-permute-start.1) | collective-permute-done | bytes 106528 | tf_op jit(solution)/shard_map/ppermute | solution.py:407
  24.1 1.7 %collective-permute-start.2 = (f32[208,128]{1,0:T(8,128)S(1)}, f32[208,128]{1,0:T(8,128)S(1)}, u32[]{:S(2)}, u32[]{:S(2)}) collective-permute-start(f32[208,128]{1,0:T(8,128)S(1)} %tree_merge.4.refs_0_), channel_id=1, source_target_pairs={{0,2},{1,3},{2,0},{3,1},{4,6},{5,7},{6,4},{7,5},{8,10},{9,11},{10,... | collective-permute-start | bytes 319496 | tf_op jit(solution)/shard_map/ppermute | solution.py:407
  25.8 3.3 %near_own.1.refs_4_ = f32[8,512,128]{2,1,0:T(8,128)S(1)} custom-call(s32[8,12]{1,0:T(8,128)S(1)} %collective-permute-done.refs_0_.refs_1_, bf16[8,512,128]{2,1,0:T(8,128)(2,1)S(1)} %collective-permute-done.5.refs_1_.refs_3_, bf16[8,768,128]{2,1,0:T(8,128)(2,1)S(1)} %get-tuple-element.45.pack.refs_2_.refs_5_), custom_call_target="tpu_custom_call" | custom-call | flops 1000 | bytes 1000 | tf_op jit(solution)/shard_map/near_own/pallas_call | solution.py:365
  29.2 2.2 %collective-permute-done.2.refs_1_ = f32[208,128]{1,0:T(8,128)S(1)} collective-permute-done((f32[208,128]{1,0:T(8,128)S(1)}, f32[208,128]{1,0:T(8,128)S(1)}, u32[]{:S(2)}, u32[]{:S(2)}) %collective-permute-start.2) | collective-permute-done | bytes 106528 | tf_op jit(solution)/shard_map/ppermute | solution.py:407
  31.4 2.2 %collective-permute-done.4.refs_6_ = bf16[8,768,128]{2,1,0:T(8,128)(2,1)S(1)} collective-permute-done((bf16[8,768,128]{2,1,0:T(8,128)(2,1)S(1)}, bf16[8,768,128]{2,1,0:T(8,128)(2,1)S(1)}, u32[]{:S(2)}, u32[]{:S(2)}) %collective-permute-start.4) | collective-permute-done | bytes 1572896 | tf_op jit(solution)/shard_map/ppermute | solution.py:398
  33.6 1.3 %collective-permute-start.7 = (bf16[8,768,128]{2,1,0:T(8,128)(2,1)S(1)}, bf16[8,768,128]{2,1,0:T(8,128)(2,1)S(1)}, u32[]{:S(2)}, u32[]{:S(2)}) collective-permute-start(bf16[8,768,128]{2,1,0:T(8,128)(2,1)S(1)} %get-tuple-element.45.pack.refs_2_.refs_5_), channel_id=1, source_target_pairs={{2,0},{1,3},{6,4},{5,7},{10,8},{9,11},{14,12},{13,15},{18,16},{17,... | collective-permute-start | bytes 4718600 | tf_op jit(solution)/shard_map/ppermute | solution.py:398
  35.6 1.0 %tree_merge.5.refs_0_ = f32[208,128]{1,0:T(8,128)S(1)} custom-call(f32[208,128]{1,0:T(8,128)S(1)} %tree_merge.4.refs_0_, f32[208,128]{1,0:T(8,128)S(1)} %collective-permute-done.2.refs_1_, s32[255,128]{1,0:T(8,128)S(1)} %copy-done.1), custom_call_target="tpu_custom_call" | custom-call | flops 67108864 | bytes 212992 | tf_op jit(solution)/shard_map/tree_merge/pallas_call | solution.py:251
  36.6 2.5 %collective-permute-start.6 = (f32[208,128]{1,0:T(8,128)S(1)}, f32[208,128]{1,0:T(8,128)S(1)}, u32[]{:S(2)}, u32[]{:S(2)}) collective-permute-start(f32[208,128]{1,0:T(8,128)S(1)} %tree_merge.5.refs_0_), channel_id=1, source_target_pairs={{0,4},{1,5},{2,6},{3,7},{4,0},{5,1},{6,2},{7,3},{8,12},{9,13},{10,... | collective-permute-start | bytes 319496 | tf_op jit(solution)/shard_map/ppermute | solution.py:407
  39.1 12.9 %near_early.1 = (f32[8,512,128]{2,1,0:T(8,128)S(1)}, f32[8,512,128]{2,1,0:T(8,128)S(1)}) custom-call(s32[8,12]{1,0:T(8,128)S(1)} %copy-done.4, s32[8,12]{1,0:T(8,128)S(1)} %collective-permute-done.refs_0_.refs_1_, bf16[8,512,128]{2,1,0:T(8,128)(2,1)S(1)} %get-tuple-element.34.rows.refs_2_.refs_1_, ...), custom_call_target="tpu_custom_call" | custom-call | flops 1000 | bytes 1000 | tf_op jit(solution)/shard_map/near_early/pallas_call | solution.py:365
  52.0 3.9 %collective-permute-done.7.refs_3_ = bf16[8,768,128]{2,1,0:T(8,128)(2,1)S(1)} collective-permute-done((bf16[8,768,128]{2,1,0:T(8,128)(2,1)S(1)}, bf16[8,768,128]{2,1,0:T(8,128)(2,1)S(1)}, u32[]{:S(2)}, u32[]{:S(2)}) %collective-permute-start.7) | collective-permute-done | bytes 1572896 | tf_op jit(solution)/shard_map/ppermute | solution.py:398
  55.9 1.0 %tree_merge.6.refs_0_ = f32[208,128]{1,0:T(8,128)S(1)} custom-call(f32[208,128]{1,0:T(8,128)S(1)} %tree_merge.5.refs_0_, f32[208,128]{1,0:T(8,128)S(1)} %collective-permute-done.6.refs_1_, s32[255,128]{1,0:T(8,128)S(1)} %copy-done.1), custom_call_target="tpu_custom_call" | custom-call | flops 67108864 | bytes 212992 | tf_op jit(solution)/shard_map/tree_merge/pallas_call | solution.py:251
  56.8 6.3 %collective-permute-start.10 = (f32[208,128]{1,0:T(8,128)S(1)}, f32[208,128]{1,0:T(8,128)S(1)}, u32[]{:S(2)}, u32[]{:S(2)}) collective-permute-start(f32[208,128]{1,0:T(8,128)S(1)} %tree_merge.6.refs_0_), channel_id=1, source_target_pairs={{0,16},{1,17},{2,18},{3,19},{4,20},{5,21},{6,22},{7,23},{8,24},{9,... | collective-permute-start | bytes 319496 | tf_op jit(solution)/shard_map/ppermute | solution.py:407
  63.2 1.3 %collective-permute-start.11 = (f32[208,128]{1,0:T(8,128)S(1)}, f32[208,128]{1,0:T(8,128)S(1)}, u32[]{:S(2)}, u32[]{:S(2)}) collective-permute-start(f32[208,128]{1,0:T(8,128)S(1)} %tree_merge.6.refs_0_), channel_id=1, source_target_pairs={{0,24},{1,25},{2,26},{3,27},{4,28},{5,29},{6,30},{7,31},{8,16},{9,... | collective-permute-start | bytes 319496 | tf_op jit(solution)/shard_map/ppermute | solution.py:407
  64.5 7.0 %collective-permute-done.10.refs_2_ = f32[208,128]{1,0:T(8,128)S(1)} collective-permute-done((f32[208,128]{1,0:T(8,128)S(1)}, f32[208,128]{1,0:T(8,128)S(1)}, u32[]{:S(2)}, u32[]{:S(2)}) %collective-permute-start.10) | collective-permute-done | bytes 106528 | tf_op jit(solution)/shard_map/ppermute | solution.py:407
  72.3 5.2 %near_beside.1 = f32[8,512,128]{2,1,0:T(8,128)S(1)} custom-call(s32[8,12]{1,0:T(8,128)S(1)} %collective-permute-done.refs_0_.refs_1_, bf16[8,512,128]{2,1,0:T(8,128)(2,1)S(1)} %collective-permute-done.5.refs_1_.refs_3_, f32[8,512,128]{2,1,0:T(8,128)S(1)} %get-tuple-element.59.refs_2_, bf16[8,768,128]{2,1,0:T(8,128)(2,1)S(1)} %collective-permute-done.7.refs_3_, ...), custom_call_target="tpu_custom_call" | custom-call | flops 1000 | bytes 1000 | tf_op jit(solution)/shard_map/near_beside/pallas_call | solution.py:365
  77.7 4.5 %near_last.1 = f32[8,512,128]{2,1,0:T(8,128)S(1)} custom-call(s32[8,12]{1,0:T(8,128)S(1)} %copy-done.4, bf16[8,512,128]{2,1,0:T(8,128)(2,1)S(1)} %get-tuple-element.34.rows.refs_2_.refs_1_, f32[8,512,128]{2,1,0:T(8,128)S(1)} %get-tuple-element.55.refs_2_, bf16[8,768,128]{2,1,0:T(8,128)(2,1)S(1)} %collective-permute-done.7.refs_3_, ...), custom_call_target="tpu_custom_call" | custom-call | flops 1000 | bytes 1000 | tf_op jit(solution)/shard_map/near_last/pallas_call | solution.py:365
  82.2 3.0 %tree_merge.7 = f32[4,128]{1,0:T(4,128)} custom-call(f32[208,128]{1,0:T(8,128)S(1)} %tree_merge.6.refs_0_, f32[208,128]{1,0:T(8,128)S(1)} %collective-permute-done.9.refs_1_, f32[208,128]{1,0:T(8,128)S(1)} %collective-permute-done.10.refs_2_, f32[208,128]{1,0:T(8,128)S(1)} %collective-permute-done.11.refs_3_, s32[255,128]{1,0:T(8,128)S(1)} %copy-done.1), custom_call_target="tpu_custom_call" | custom-call | flops 134217728 | bytes 425984 | tf_op jit(solution)/shard_map/tree_merge/pallas_call | solution.py:251
  85.2 1.6 %add_multiply_fusion = f32[8,512,128]{2,1,0:T(8,128)} fusion(f32[8,512,128]{2,1,0:T(8,128)S(1)} %near_last.1, f32[8,512,128]{2,1,0:T(8,128)S(1)} %collective-permute-done.12), kind=kLoop, calls=%fused_computation | loop fusion | flops 1048576 | bytes 6291456 | tf_op jit(solution)/shard_map/mul | solution.py:468
  (27 shorter events, 5.7 us)
Async XLA Ops:
  0.6 1.2 %copy-start.2 = (bf16[4096,128]{1,0:T(8,128)(2,1)S(1)}, bf16[4096,128]{1,0:T(8,128)(2,1)}, u32[]{:S(2)}) copy-start(bf16[4096,128]{1,0:T(8,128)(2,1)} %probes.1) | copy-start | bytes 3145732
  1.9 1.0 %copy-start.3 = (bf16[4096,64]{0,1:T(8,128)(2,1)S(1)}, bf16[4096,64]{0,1:T(8,128)(2,1)}, u32[]{:S(2)}) copy-start(bf16[4096,64]{0,1:T(8,128)(2,1)} %param.7) | copy-start | bytes 1572868
  2.9 0.7 copy-start.5
  6.3 25.1 %collective-permute-start.3 = (bf16[8,768,128]{2,1,0:T(8,128)(2,1)S(1)}, bf16[8,768,128]{2,1,0:T(8,128)(2,1)S(1)}, u32[]{:S(2)}, u32[]{:S(2)}) collective-permute-start(bf16[8,768,128]{2,1,0:T(8,128)(2,1)S(1)} %get-tuple-element.45.pack.refs_2_.refs_5_), channel_id=1, source_target_pairs={{3,1},{0,2},{7,5},{4,6},{11,9},{8,10},{15,13},{12,14},{19,17},{16,... | collective-permute-start | bytes 4718600 | tf_op jit(solution)/shard_map/ppermute | solution.py:398
  11.2 22.3 %collective-permute-start.4 = (bf16[8,768,128]{2,1,0:T(8,128)(2,1)S(1)}, bf16[8,768,128]{2,1,0:T(8,128)(2,1)S(1)}, u32[]{:S(2)}, u32[]{:S(2)}) collective-permute-start(bf16[8,768,128]{2,1,0:T(8,128)(2,1)S(1)} %get-tuple-element.45.pack.refs_2_.refs_5_), channel_id=1, source_target_pairs={{3,7},{7,11},{4,0},{11,15},{8,4},{15,19},{12,8},{19,23},{16,12},{2... | collective-permute-start | bytes 4718600 | tf_op jit(solution)/shard_map/ppermute | solution.py:398
  12.5 13.3 %collective-permute-start.5 = (bf16[8,512,128]{2,1,0:T(8,128)(2,1)S(1)}, bf16[8,512,128]{2,1,0:T(8,128)(2,1)S(1)}, u32[]{:S(2)}, u32[]{:S(2)}) collective-permute-start(bf16[8,512,128]{2,1,0:T(8,128)(2,1)S(1)} %get-tuple-element.34.rows.refs_2_.refs_1_), channel_id=1, source_target_pairs={{0,1},{1,0},{2,3},{3,2},{4,5},{5,4},{6,7},{7,6},{8,9},{9,8},{10,11... | collective-permute-start | bytes 3145736 | tf_op jit(solution)/shard_map/ppermute | solution.py:407
  12.6 9.1 %collective-permute-start = (s32[8,12]{1,0:T(8,128)}, s32[8,12]{1,0:T(8,128)S(1)}, u32[]{:S(2)}, u32[]{:S(2)}) collective-permute-start(s32[8,12]{1,0:T(8,128)} %refs_0_.3), channel_id=1, source_target_pairs={{0,1},{1,0},{2,3},{3,2},{4,5},{5,4},{6,7},{7,6},{8,9},{9,8},{10,11... | collective-permute-start | bytes 1160 | tf_op jit(solution)/shard_map/ppermute | solution.py:407
  13.1 0.9 %copy-start = (s32[255,128]{1,0:T(8,128)S(1)}, s32[255,128]{1,0:T(8,128)}, u32[]{:S(2)}) copy-start(s32[255,128]{1,0:T(8,128)} %refs_4_.1) | copy-start | bytes 391684
  14.0 0.7 copy-start.6
  21.7 1.4 %collective-permute-start.1 = (f32[208,128]{1,0:T(8,128)S(1)}, f32[208,128]{1,0:T(8,128)S(1)}, u32[]{:S(2)}, u32[]{:S(2)}) collective-permute-start(f32[208,128]{1,0:T(8,128)S(1)} %local_tree.1.refs_0_), channel_id=1, source_target_pairs={{0,1},{1,0},{2,3},{3,2},{4,5},{5,4},{6,7},{7,6},{8,9},{9,8},{10,11... | collective-permute-start | bytes 319496 | tf_op jit(solution)/shard_map/ppermute | solution.py:407
  24.1 11.5 %copy-start.1 = (s32[255,128]{1,0:T(8,128)S(1)}, s32[255,128]{1,0:T(8,128)}, u32[]{:S(2)}) copy-start(s32[255,128]{1,0:T(8,128)} %refs_4_.1) | copy-start | bytes 391684
  24.1 15.0 %copy-start.4 = (s32[8,12]{1,0:T(8,128)S(1)}, s32[8,12]{1,0:T(8,128)}, u32[]{:S(2)}) copy-start(s32[8,12]{1,0:T(8,128)} %refs_0_.3) | copy-start | bytes 1156
  24.1 7.2 %collective-permute-start.2 = (f32[208,128]{1,0:T(8,128)S(1)}, f32[208,128]{1,0:T(8,128)S(1)}, u32[]{:S(2)}, u32[]{:S(2)}) collective-permute-start(f32[208,128]{1,0:T(8,128)S(1)} %tree_merge.4.refs_0_), channel_id=1, source_target_pairs={{0,2},{1,3},{2,0},{3,1},{4,6},{5,7},{6,4},{7,5},{8,10},{9,11},{10,... | collective-permute-start | bytes 319496 | tf_op jit(solution)/shard_map/ppermute | solution.py:407
  33.6 22.3 %collective-permute-start.7 = (bf16[8,768,128]{2,1,0:T(8,128)(2,1)S(1)}, bf16[8,768,128]{2,1,0:T(8,128)(2,1)S(1)}, u32[]{:S(2)}, u32[]{:S(2)}) collective-permute-start(bf16[8,768,128]{2,1,0:T(8,128)(2,1)S(1)} %get-tuple-element.45.pack.refs_2_.refs_5_), channel_id=1, source_target_pairs={{2,0},{1,3},{6,4},{5,7},{10,8},{9,11},{14,12},{13,15},{18,16},{17,... | collective-permute-start | bytes 4718600 | tf_op jit(solution)/shard_map/ppermute | solution.py:398
  34.8 21.0 %collective-permute-start.8 = (bf16[8,768,128]{2,1,0:T(8,128)(2,1)S(1)}, bf16[8,768,128]{2,1,0:T(8,128)(2,1)S(1)}, u32[]{:S(2)}, u32[]{:S(2)}) collective-permute-start(bf16[8,768,128]{2,1,0:T(8,128)(2,1)S(1)} %collective-permute-done.3.refs_7_), channel_id=1, source_target_pairs={{1,5},{5,9},{6,2},{9,13},{10,6},{13,17},{14,10},{17,21},{18,14},{2... | collective-permute-start | bytes 4718600 | tf_op jit(solution)/shard_map/ppermute | solution.py:398
  36.6 15.4 %collective-permute-start.6 = (f32[208,128]{1,0:T(8,128)S(1)}, f32[208,128]{1,0:T(8,128)S(1)}, u32[]{:S(2)}, u32[]{:S(2)}) collective-permute-start(f32[208,128]{1,0:T(8,128)S(1)} %tree_merge.5.refs_0_), channel_id=1, source_target_pairs={{0,4},{1,5},{2,6},{3,7},{4,0},{5,1},{6,2},{7,3},{8,12},{9,13},{10,... | collective-permute-start | bytes 319496 | tf_op jit(solution)/shard_map/ppermute | solution.py:407
  56.8 14.7 %collective-permute-start.10 = (f32[208,128]{1,0:T(8,128)S(1)}, f32[208,128]{1,0:T(8,128)S(1)}, u32[]{:S(2)}, u32[]{:S(2)}) collective-permute-start(f32[208,128]{1,0:T(8,128)S(1)} %tree_merge.6.refs_0_), channel_id=1, source_target_pairs={{0,16},{1,17},{2,18},{3,19},{4,20},{5,21},{6,22},{7,23},{8,24},{9,... | collective-permute-start | bytes 319496 | tf_op jit(solution)/shard_map/ppermute | solution.py:407
  63.2 8.4 %collective-permute-start.11 = (f32[208,128]{1,0:T(8,128)S(1)}, f32[208,128]{1,0:T(8,128)S(1)}, u32[]{:S(2)}, u32[]{:S(2)}) collective-permute-start(f32[208,128]{1,0:T(8,128)S(1)} %tree_merge.6.refs_0_), channel_id=1, source_target_pairs={{0,24},{1,25},{2,26},{3,27},{4,28},{5,29},{6,30},{7,31},{8,16},{9,... | collective-permute-start | bytes 319496 | tf_op jit(solution)/shard_map/ppermute | solution.py:407
  64.5 7.8 %collective-permute-start.9 = (f32[208,128]{1,0:T(8,128)S(1)}, f32[208,128]{1,0:T(8,128)S(1)}, u32[]{:S(2)}, u32[]{:S(2)}) collective-permute-start(f32[208,128]{1,0:T(8,128)S(1)} %tree_merge.6.refs_0_), channel_id=1, source_target_pairs={{0,8},{1,9},{2,10},{3,11},{4,12},{5,13},{6,14},{7,15},{8,0},{9,1},... | collective-permute-start | bytes 319496 | tf_op jit(solution)/shard_map/ppermute | solution.py:407
  77.6 7.6 %collective-permute-start.12 = (f32[8,512,128]{2,1,0:T(8,128)S(1)}, f32[8,512,128]{2,1,0:T(8,128)S(1)}, u32[]{:S(2)}, u32[]{:S(2)}) collective-permute-start(f32[8,512,128]{2,1,0:T(8,128)S(1)} %near_beside.1), channel_id=1, source_target_pairs={{0,1},{1,0},{2,3},{3,2},{4,5},{5,4},{6,7},{7,6},{8,9},{9,8},{10,11... | collective-permute-start | bytes 6291464 | tf_op jit(solution)/shard_map/ppermute | solution.py:407

commit v10 on v7

--- a/solution.py
+++ b/solution.py
@@ -268,7 +268,7 @@
     )(*parts, merge_sets)
 
 
-def near_kernel(*refs, flips, row_counts, has_acc, sets, tasks, dim):
+def near_kernel(*refs, flips, row_counts, has_acc, sets, tasks, span, dim):
     refs = list(refs)
 
     def take(number):
@@ -300,7 +300,7 @@
         target_first = lax.axis_index("leaf") * window + (sub ^ flip) * blocks
 
         def list_block(g, counts, j=j, mine=mine, firsts=firsts, target_first=target_first):
-            for s in range(near):
+            for s in range(*span):
                 source = lists[j][g, s]
                 used = (source != target_first + g) if s else True
                 after = []
@@ -362,7 +362,7 @@
                 add_all(buffer, targets, t, pairs)
 
 
-def near_call(groups, sources, tasks, dim, name):
+def near_call(groups, sources, tasks, dim, name, self_tiles=False):
     flips, lists, rows, accs = zip(*groups)
     rows = [r if isinstance(r, tuple) else (r,) for r in rows]
     blocks, leaf = rows[0][0].shape[:2]
@@ -379,6 +379,7 @@
             has_acc=tuple(acc is not None for acc in accs),
             sets=tuple((bases, which) for bases, which, _ in sources),
             tasks=tasks,
+            span=(0, 1) if self_tiles else (1, near),
             dim=dim,
         ),
         in_specs=[smem] * len(lists) + [vmem] * (len(args) - len(lists)),
@@ -443,7 +444,9 @@
     own_pack, node = tie(pack, node)
     parts = exchange(node, 1, 1)
     own_set = (own_base, single, [own_pack])
-    (own,) = near_call([(0, near_lists, rows, None)], [own_set], ((0, 0),), dim, "near_own")
+    (own,) = near_call(
+        [(0, near_lists, rows, None)], [own_set], ((0, 0),), dim, "near_own", self_tiles=True
+    )
 
     *parts, outer_across, outer_next, beside_pack, edge_rows, late_rows, own = tie(
         *parts, outer_across, outer_next, beside_pack, edge_rows, rows, own
@@ -458,7 +461,7 @@
     early_set = (early_base, by_edge, [outer_next, outer_across])
     own, beside = near_call(
         [(0, near_lists, rows, own), (1, beside_lists, beside_rows, None)],
-        [own_set, early_set], ((1, 0), (0, 1), (1, 1)), dim, "near_early",
+        [own_set, early_set], ((0, 0), (1, 0), (0, 1), (1, 1)), dim, "near_early",
     )
 
     *parts, inner_across, forwarded, beside = tie(*parts, inner_across, forwarded, beside)

time: 85.3 us -> 82.2 us (0.964)
  starting transfers between devices: 29.5 us -> 26.7 us
  Pallas kernels: 41.5 us -> 40.2 us
  waiting for transfers between devices: 6.12 us -> 7.4 us
    ppermute x8, starting transfers between devices: 15.8 us -> 12.5 us  [exchange(): lax.ppermute(x, axes, [(i, i ^ d << shift) for i in range(count)])]
    ppermute x8, waiting for transfers between devices: 4.01 us -> 6.78 us  [exchange(): lax.ppermute(x, axes, [(i, i ^ d << shift) for i in range(count)])]
    ppermute x7, waiting for transfers between devices: 2.11 us -> 0.63 us  [send(): return lax.ppermute(x, axes, pairs)]
    pallas_call x4, Pallas kernels: 26 us -> 24.7 us  [near_call(): pl.pallas_call(functools.partial(near_kernel, flips=flips, row_counts=tup...]
  transfers between devices with their start and end apart: 15 -> 15, of which waited for: 3 -> 3; matrix products, arithmetic and copies ran while one was open for 0% -> 0% of each run, Pallas kernels for 42% -> 40%
where the time goes in v10:
time: 82.2 us; the launch traced here: 81.4 us
  Pallas kernels  40.2 us (49%)
  starting transfers between devices  26.7 us (32%)
  waiting for transfers between devices  7.4 us (9%)
  local copies, waits for them, and re-layouts  4.58 us (6%)
  other arithmetic  1.56 us (2%)
  between operations  0.88 us (1%)
    pallas_call x4, Pallas kernels, near_call(): pl.pallas_call(functools.partial(near_kernel, flips=flips, row_counts=tup...  24.7 us
    ppermute x7, starting transfers between devices, send(): return lax.ppermute(x, axes, pairs)  14.3 us
    ppermute x8, starting transfers between devices, exchange(): lax.ppermute(x, axes, [(i, i ^ d << shift) for i in range(count)])  12.5 us
    pallas_call x1, Pallas kernels, local_tree_call(): pl.pallas_call(functools.partial(local_tree_kernel, dim=dim), in_specs=[p...  7.02 us
    ppermute x8, waiting for transfers between devices, exchange(): lax.ppermute(x, axes, [(i, i ^ d << shift) for i in range(count)])  6.78 us
    pallas_call x4, Pallas kernels, merge_call(): pl.pallas_call(functools.partial(merge_kernel, dim=dim, blocks=blocks, sh...  5.87 us
    unnamed x14, local copies, waits for them, and re-layouts  4.58 us
    pallas_call x1, Pallas kernels, order_call(): pl.pallas_call(order_kernel, grid=(blocks // many,), in_specs=[pl.BlockSp...  2.64 us
  transfers between devices with their start and end apart: 15, of which 3 were waited for; matrix products, arithmetic and copies ran while one was open for 0% of the time, Pallas kernels for 40%

profile of v10, /device:TPU:0, one launch (start us, length us, event | category | flops | bytes accessed | tf_op | source)
XLA Modules:
  0.0 81.4 jit_solution(18335877848809596893)
XLA Ops:
  0.6 1.2 %copy-done.2 = bf16[4096,128]{1,0:T(8,128)(2,1)S(1)} copy-done((bf16[4096,128]{1,0:T(8,128)(2,1)S(1)}, bf16[4096,128]{1,0:T(8,128)(2,1)}, u32[]{:S(2)}) %copy-start.2) | copy-done | bytes 1048600
  1.9 1.0 %copy-done.3 = bf16[4096,64]{0,1:T(8,128)(2,1)S(1)} copy-done((bf16[4096,64]{0,1:T(8,128)(2,1)S(1)}, bf16[4096,64]{0,1:T(8,128)(2,1)}, u32[]{:S(2)}) %copy-start.3) | copy-done | bytes 524312
  3.6 2.6 %tree_order.1 = (bf16[8,768,128]{2,1,0:T(8,128)(2,1)S(1)}, bf16[8,512,128]{2,1,0:T(8,128)(2,1)S(1)}) custom-call(bf16[64,4096]{1,0:T(8,128)(2,1)S(1)} %bitcast.4, s32[8,1,512]{2,1,0:T(1,128)S(1)} %bitcast.5, bf16[4096,128]{1,0:T(8,128)(2,1)S(1)} %copy-done.2), custom_call_target="tpu_custom_call" | custom-call | flops 268435456 | bytes 5242880 | tf_op jit(solution)/shard_map/tree_order/pallas_call | solution.py:94
  6.3 5.0 %collective-permute-start.3 = (bf16[8,768,128]{2,1,0:T(8,128)(2,1)S(1)}, bf16[8,768,128]{2,1,0:T(8,128)(2,1)S(1)}, u32[]{:S(2)}, u32[]{:S(2)}) collective-permute-start(bf16[8,768,128]{2,1,0:T(8,128)(2,1)S(1)} %get-tuple-element.46.pack.refs_2_.refs_6_), channel_id=1, source_target_pairs={{3,1},{0,2},{7,5},{4,6},{11,9},{8,10},{15,13},{12,14},{19,17},{16,... | collective-permute-start | bytes 4718600 | tf_op jit(solution)/shard_map/ppermute | solution.py:409
  11.2 1.3 %collective-permute-start.4 = (bf16[8,768,128]{2,1,0:T(8,128)(2,1)S(1)}, bf16[8,768,128]{2,1,0:T(8,128)(2,1)S(1)}, u32[]{:S(2)}, u32[]{:S(2)}) collective-permute-start(bf16[8,768,128]{2,1,0:T(8,128)(2,1)S(1)} %get-tuple-element.46.pack.refs_2_.refs_6_), channel_id=1, source_target_pairs={{3,7},{7,11},{4,0},{11,15},{8,4},{15,19},{12,8},{19,23},{16,12},{2... | collective-permute-start | bytes 4718600 | tf_op jit(solution)/shard_map/ppermute | solution.py:409
  12.5 1.3 %collective-permute-start.5 = (bf16[8,768,128]{2,1,0:T(8,128)(2,1)S(1)}, bf16[8,768,128]{2,1,0:T(8,128)(2,1)S(1)}, u32[]{:S(2)}, u32[]{:S(2)}) collective-permute-start(bf16[8,768,128]{2,1,0:T(8,128)(2,1)S(1)} %get-tuple-element.46.pack.refs_2_.refs_6_), channel_id=1, source_target_pairs={{1,0},{2,3},{5,4},{6,7},{9,8},{10,11},{13,12},{14,15},{17,16},{18,... | collective-permute-start | bytes 4718600 | tf_op jit(solution)/shard_map/ppermute | solution.py:409
  13.8 1.3 %collective-permute-start.6 = (bf16[8,512,128]{2,1,0:T(8,128)(2,1)S(1)}, bf16[8,512,128]{2,1,0:T(8,128)(2,1)S(1)}, u32[]{:S(2)}, u32[]{:S(2)}) collective-permute-start(bf16[8,512,128]{2,1,0:T(8,128)(2,1)S(1)} %get-tuple-element.44.rows.refs_1_.refs_2_), channel_id=1, source_target_pairs={{1,0},{2,3},{5,4},{6,7},{9,8},{10,11},{13,12},{14,15},{17,16},{18,... | collective-permute-start | bytes 3145736 | tf_op jit(solution)/shard_map/ppermute | solution.py:409
  15.1 1.4 %collective-permute-start = (s32[8,12]{1,0:T(8,128)}, s32[8,12]{1,0:T(8,128)S(1)}, u32[]{:S(2)}, u32[]{:S(2)}) collective-permute-start(s32[8,12]{1,0:T(8,128)} %refs_0_.5), channel_id=1, source_target_pairs={{0,1},{1,0},{2,3},{3,2},{4,5},{5,4},{6,7},{7,6},{8,9},{9,8},{10,11... | collective-permute-start | bytes 1160 | tf_op jit(solution)/shard_map/ppermute | solution.py:418
  18.1 7.0 %local_tree.1.refs_0_ = f32[208,128]{1,0:T(8,128)S(1)} custom-call(bf16[8,768,128]{2,1,0:T(8,128)(2,1)S(1)} %get-tuple-element.46.pack.refs_2_.refs_6_, bf16[8,512,128]{2,1,0:T(8,128)(2,1)S(1)} %get-tuple-element.44.rows.refs_1_.refs_2_, s32[8,128]{1,0:T(8,128)S(1)} %copy-done.6, s32[255,128]{1,0:T(8,128)S(1)} %copy-done), custom_call_target="tpu_custom_call" | custom-call | flops 536870912 | bytes 3145728 | tf_op jit(solution)/shard_map/local_tree/pallas_call | solution.py:177
  25.2 1.3 %collective-permute-done.1.refs_1_ = f32[208,128]{1,0:T(8,128)S(1)} collective-permute-done((f32[208,128]{1,0:T(8,128)S(1)}, f32[208,128]{1,0:T(8,128)S(1)}, u32[]{:S(2)}, u32[]{:S(2)}) %collective-permute-start.1) | collective-permute-done | bytes 106528 | tf_op jit(solution)/shard_map/ppermute | solution.py:418
  27.5 1.7 %collective-permute-start.2 = (f32[208,128]{1,0:T(8,128)S(1)}, f32[208,128]{1,0:T(8,128)S(1)}, u32[]{:S(2)}, u32[]{:S(2)}) collective-permute-start(f32[208,128]{1,0:T(8,128)S(1)} %tree_merge.4.refs_0_), channel_id=1, source_target_pairs={{0,2},{1,3},{2,0},{3,1},{4,6},{5,7},{6,4},{7,5},{8,10},{9,11},{10,... | collective-permute-start | bytes 319496 | tf_op jit(solution)/shard_map/ppermute | solution.py:418
  29.2 3.7 %near_own.1.refs_5_ = f32[8,512,128]{2,1,0:T(8,128)S(1)} custom-call(s32[8,12]{1,0:T(8,128)S(1)} %copy-done.4, bf16[8,512,128]{2,1,0:T(8,128)(2,1)S(1)} %get-tuple-element.44.rows.refs_1_.refs_2_, bf16[8,768,128]{2,1,0:T(8,128)(2,1)S(1)} %get-tuple-element.46.pack.refs_2_.refs_6_), custom_call_target="tpu_custom_call" | custom-call | flops 1000 | bytes 1000 | tf_op jit(solution)/shard_map/near_own/pallas_call | solution.py:374
  33.6 1.9 %collective-permute-start.8 = (bf16[8,768,128]{2,1,0:T(8,128)(2,1)S(1)}, bf16[8,768,128]{2,1,0:T(8,128)(2,1)S(1)}, u32[]{:S(2)}, u32[]{:S(2)}) collective-permute-start(bf16[8,768,128]{2,1,0:T(8,128)(2,1)S(1)} %collective-permute-done.5), channel_id=1, source_target_pairs={{0,3},{3,0},{4,7},{7,4},{8,11},{11,8},{12,15},{15,12},{16,19},{19,... | collective-permute-start | bytes 4718600 | tf_op jit(solution)/shard_map/ppermute | solution.py:409
  36.3 2.8 %collective-permute-start.10 = (bf16[8,512,128]{2,1,0:T(8,128)(2,1)S(1)}, bf16[8,512,128]{2,1,0:T(8,128)(2,1)S(1)}, u32[]{:S(2)}, u32[]{:S(2)}) collective-permute-start(bf16[8,512,128]{2,1,0:T(8,128)(2,1)S(1)} %get-tuple-element.44.rows.refs_1_.refs_2_), channel_id=1, source_target_pairs={{0,1},{3,2},{4,5},{7,6},{8,9},{11,10},{12,13},{15,14},{16,17},{19,... | collective-permute-start | bytes 3145736 | tf_op jit(solution)/shard_map/ppermute | solution.py:409
  40.0 2.4 %collective-permute-start.7 = (f32[208,128]{1,0:T(8,128)S(1)}, f32[208,128]{1,0:T(8,128)S(1)}, u32[]{:S(2)}, u32[]{:S(2)}) collective-permute-start(f32[208,128]{1,0:T(8,128)S(1)} %tree_merge.5.refs_0_), channel_id=1, source_target_pairs={{0,4},{1,5},{2,6},{3,7},{4,0},{5,1},{6,2},{7,3},{8,12},{9,13},{10,... | collective-permute-start | bytes 319496 | tf_op jit(solution)/shard_map/ppermute | solution.py:418
  42.4 12.9 %near_early.1 = (f32[8,512,128]{2,1,0:T(8,128)S(1)}, f32[8,512,128]{2,1,0:T(8,128)S(1)}) custom-call(s32[8,12]{1,0:T(8,128)S(1)} %copy-done.4, s32[8,12]{1,0:T(8,128)S(1)} %collective-permute-done.refs_1_.refs_0_, bf16[8,512,128]{2,1,0:T(8,128)(2,1)S(1)} %get-tuple-element.44.rows.refs_1_.refs_2_, ...), custom_call_target="tpu_custom_call" | custom-call | flops 1000 | bytes 1000 | tf_op jit(solution)/shard_map/near_early/pallas_call | solution.py:374
  55.4 4.8 %near_beside.1 = f32[8,512,128]{2,1,0:T(8,128)S(1)} custom-call(s32[8,12]{1,0:T(8,128)S(1)} %collective-permute-done.refs_1_.refs_0_, bf16[8,512,128]{2,1,0:T(8,128)(2,1)S(1)} %collective-permute-done.6.refs_3_.refs_1_, bf16[8,512,128]{2,1,0:T(8,128)(2,1)S(1)} %collective-permute-done.10.refs_4_.refs_2_, f32[8,512,128]{2,1,0:T(8,128)S(1)} %get-tuple-element.51.refs_3_, ...), custom_call_target="tpu_custom_call" | custom-call | flops 1000 | bytes 1000 | tf_op jit(solution)/shard_map/near_beside/pallas_call | solution.py:374
  60.2 1.0 %tree_merge.6.refs_0_ = f32[208,128]{1,0:T(8,128)S(1)} custom-call(f32[208,128]{1,0:T(8,128)S(1)} %tree_merge.5.refs_0_, f32[208,128]{1,0:T(8,128)S(1)} %collective-permute-done.7.refs_1_, s32[255,128]{1,0:T(8,128)S(1)} %copy-done.1), custom_call_target="tpu_custom_call" | custom-call | flops 67108864 | bytes 212992 | tf_op jit(solution)/shard_map/tree_merge/pallas_call | solution.py:251
  61.2 4.5 %collective-permute-start.11 = (f32[208,128]{1,0:T(8,128)S(1)}, f32[208,128]{1,0:T(8,128)S(1)}, u32[]{:S(2)}, u32[]{:S(2)}) collective-permute-start(f32[208,128]{1,0:T(8,128)S(1)} %tree_merge.6.refs_0_), channel_id=1, source_target_pairs={{0,8},{1,9},{2,10},{3,11},{4,12},{5,13},{6,14},{7,15},{8,0},{9,1},... | collective-permute-start | bytes 319496 | tf_op jit(solution)/shard_map/ppermute | solution.py:418
  65.7 1.9 %collective-permute-start.12 = (f32[208,128]{1,0:T(8,128)S(1)}, f32[208,128]{1,0:T(8,128)S(1)}, u32[]{:S(2)}, u32[]{:S(2)}) collective-permute-start(f32[208,128]{1,0:T(8,128)S(1)} %tree_merge.6.refs_0_), channel_id=1, source_target_pairs={{0,16},{1,17},{2,18},{3,19},{4,20},{5,21},{6,22},{7,23},{8,24},{9,... | collective-permute-start | bytes 319496 | tf_op jit(solution)/shard_map/ppermute | solution.py:418
  68.1 3.3 %near_last.1 = f32[8,512,128]{2,1,0:T(8,128)S(1)} custom-call(s32[8,12]{1,0:T(8,128)S(1)} %copy-done.4, bf16[8,512,128]{2,1,0:T(8,128)(2,1)S(1)} %get-tuple-element.44.rows.refs_1_.refs_2_, f32[8,512,128]{2,1,0:T(8,128)S(1)} %get-tuple-element.56.refs_2_, bf16[8,768,128]{2,1,0:T(8,128)(2,1)S(1)} %collective-permute-done.8.refs_4_.refs_3_, ...), custom_call_target="tpu_custom_call" | custom-call | flops 1000 | bytes 1000 | tf_op jit(solution)/shard_map/near_last/pallas_call | solution.py:374
  71.4 5.5 %collective-permute-done.12.refs_2_ = f32[208,128]{1,0:T(8,128)S(1)} collective-permute-done((f32[208,128]{1,0:T(8,128)S(1)}, f32[208,128]{1,0:T(8,128)S(1)}, u32[]{:S(2)}, u32[]{:S(2)}) %collective-permute-start.12) | collective-permute-done | bytes 106528 | tf_op jit(solution)/shard_map/ppermute | solution.py:418
  76.9 2.9 %tree_merge.7 = f32[4,128]{1,0:T(4,128)} custom-call(f32[208,128]{1,0:T(8,128)S(1)} %tree_merge.6.refs_0_, f32[208,128]{1,0:T(8,128)S(1)} %collective-permute-done.11.refs_1_, f32[208,128]{1,0:T(8,128)S(1)} %collective-permute-done.12.refs_2_, f32[208,128]{1,0:T(8,128)S(1)} %collective-permute-done.13.refs_3_, s32[255,128]{1,0:T(8,128)S(1)} %copy-done.1), custom_call_target="tpu_custom_call" | custom-call | flops 134217728 | bytes 425984 | tf_op jit(solution)/shard_map/tree_merge/pallas_call | solution.py:251
  79.8 1.6 %add_multiply_fusion = f32[8,512,128]{2,1,0:T(8,128)} fusion(f32[8,512,128]{2,1,0:T(8,128)S(1)} %near_last.1, f32[8,512,128]{2,1,0:T(8,128)S(1)} %collective-permute-done.14), kind=kLoop, calls=%fused_computation | loop fusion | flops 1048576 | bytes 6291456 | tf_op jit(solution)/shard_map/mul | solution.py:482
  (31 shorter events, 6.4 us)
Async XLA Ops:
  0.6 1.2 %copy-start.2 = (bf16[4096,128]{1,0:T(8,128)(2,1)S(1)}, bf16[4096,128]{1,0:T(8,128)(2,1)}, u32[]{:S(2)}) copy-start(bf16[4096,128]{1,0:T(8,128)(2,1)} %probes.1) | copy-start | bytes 3145732
  1.9 1.0 %copy-start.3 = (bf16[4096,64]{0,1:T(8,128)(2,1)S(1)}, bf16[4096,64]{0,1:T(8,128)(2,1)}, u32[]{:S(2)}) copy-start(bf16[4096,64]{0,1:T(8,128)(2,1)} %param.7) | copy-start | bytes 1572868
  2.9 0.7 copy-start.5
  3.6 25.6 %copy-start.4 = (s32[8,12]{1,0:T(8,128)S(1)}, s32[8,12]{1,0:T(8,128)}, u32[]{:S(2)}) copy-start(s32[8,12]{1,0:T(8,128)} %refs_0_.5) | copy-start | bytes 1156
  6.3 26.7 %collective-permute-start.3 = (bf16[8,768,128]{2,1,0:T(8,128)(2,1)S(1)}, bf16[8,768,128]{2,1,0:T(8,128)(2,1)S(1)}, u32[]{:S(2)}, u32[]{:S(2)}) collective-permute-start(bf16[8,768,128]{2,1,0:T(8,128)(2,1)S(1)} %get-tuple-element.46.pack.refs_2_.refs_6_), channel_id=1, source_target_pairs={{3,1},{0,2},{7,5},{4,6},{11,9},{8,10},{15,13},{12,14},{19,17},{16,... | collective-permute-start | bytes 4718600 | tf_op jit(solution)/shard_map/ppermute | solution.py:409
  11.2 22.3 %collective-permute-start.4 = (bf16[8,768,128]{2,1,0:T(8,128)(2,1)S(1)}, bf16[8,768,128]{2,1,0:T(8,128)(2,1)S(1)}, u32[]{:S(2)}, u32[]{:S(2)}) collective-permute-start(bf16[8,768,128]{2,1,0:T(8,128)(2,1)S(1)} %get-tuple-element.46.pack.refs_2_.refs_6_), channel_id=1, source_target_pairs={{3,7},{7,11},{4,0},{11,15},{8,4},{15,19},{12,8},{19,23},{16,12},{2... | collective-permute-start | bytes 4718600 | tf_op jit(solution)/shard_map/ppermute | solution.py:409
  12.5 21.0 %collective-permute-start.5 = (bf16[8,768,128]{2,1,0:T(8,128)(2,1)S(1)}, bf16[8,768,128]{2,1,0:T(8,128)(2,1)S(1)}, u32[]{:S(2)}, u32[]{:S(2)}) collective-permute-start(bf16[8,768,128]{2,1,0:T(8,128)(2,1)S(1)} %get-tuple-element.46.pack.refs_2_.refs_6_), channel_id=1, source_target_pairs={{1,0},{2,3},{5,4},{6,7},{9,8},{10,11},{13,12},{14,15},{17,16},{18,... | collective-permute-start | bytes 4718600 | tf_op jit(solution)/shard_map/ppermute | solution.py:409
  13.8 19.1 %collective-permute-start.6 = (bf16[8,512,128]{2,1,0:T(8,128)(2,1)S(1)}, bf16[8,512,128]{2,1,0:T(8,128)(2,1)S(1)}, u32[]{:S(2)}, u32[]{:S(2)}) collective-permute-start(bf16[8,512,128]{2,1,0:T(8,128)(2,1)S(1)} %get-tuple-element.44.rows.refs_1_.refs_2_), channel_id=1, source_target_pairs={{1,0},{2,3},{5,4},{6,7},{9,8},{10,11},{13,12},{14,15},{17,16},{18,... | collective-permute-start | bytes 3145736 | tf_op jit(solution)/shard_map/ppermute | solution.py:409
  15.1 10.0 %collective-permute-start = (s32[8,12]{1,0:T(8,128)}, s32[8,12]{1,0:T(8,128)S(1)}, u32[]{:S(2)}, u32[]{:S(2)}) collective-permute-start(s32[8,12]{1,0:T(8,128)} %refs_0_.5), channel_id=1, source_target_pairs={{0,1},{1,0},{2,3},{3,2},{4,5},{5,4},{6,7},{7,6},{8,9},{9,8},{10,11... | collective-permute-start | bytes 1160 | tf_op jit(solution)/shard_map/ppermute | solution.py:418
  16.5 0.9 %copy-start = (s32[255,128]{1,0:T(8,128)S(1)}, s32[255,128]{1,0:T(8,128)}, u32[]{:S(2)}) copy-start(s32[255,128]{1,0:T(8,128)} %refs_4_.1) | copy-start | bytes 391684
  17.4 0.7 copy-start.6
  25.1 1.4 %collective-permute-start.1 = (f32[208,128]{1,0:T(8,128)S(1)}, f32[208,128]{1,0:T(8,128)S(1)}, u32[]{:S(2)}, u32[]{:S(2)}) collective-permute-start(f32[208,128]{1,0:T(8,128)S(1)} %local_tree.1.refs_0_), channel_id=1, source_target_pairs={{0,1},{1,0},{2,3},{3,2},{4,5},{5,4},{6,7},{7,6},{8,9},{9,8},{10,11... | collective-permute-start | bytes 319496 | tf_op jit(solution)/shard_map/ppermute | solution.py:418
  27.5 11.6 %copy-start.1 = (s32[255,128]{1,0:T(8,128)S(1)}, s32[255,128]{1,0:T(8,128)}, u32[]{:S(2)}) copy-start(s32[255,128]{1,0:T(8,128)} %refs_4_.1) | copy-start | bytes 391684
  27.5 5.4 %collective-permute-start.2 = (f32[208,128]{1,0:T(8,128)S(1)}, f32[208,128]{1,0:T(8,128)S(1)}, u32[]{:S(2)}, u32[]{:S(2)}) collective-permute-start(f32[208,128]{1,0:T(8,128)S(1)} %tree_merge.4.refs_0_), channel_id=1, source_target_pairs={{0,2},{1,3},{2,0},{3,1},{4,6},{5,7},{6,4},{7,5},{8,10},{9,11},{10,... | collective-permute-start | bytes 319496 | tf_op jit(solution)/shard_map/ppermute | solution.py:418
  33.6 21.8 %collective-permute-start.8 = (bf16[8,768,128]{2,1,0:T(8,128)(2,1)S(1)}, bf16[8,768,128]{2,1,0:T(8,128)(2,1)S(1)}, u32[]{:S(2)}, u32[]{:S(2)}) collective-permute-start(bf16[8,768,128]{2,1,0:T(8,128)(2,1)S(1)} %collective-permute-done.5), channel_id=1, source_target_pairs={{0,3},{3,0},{4,7},{7,4},{8,11},{11,8},{12,15},{15,12},{16,19},{19,... | collective-permute-start | bytes 4718600 | tf_op jit(solution)/shard_map/ppermute | solution.py:409
  35.5 19.9 %collective-permute-start.9 = (bf16[8,768,128]{2,1,0:T(8,128)(2,1)S(1)}, bf16[8,768,128]{2,1,0:T(8,128)(2,1)S(1)}, u32[]{:S(2)}, u32[]{:S(2)}) collective-permute-start(bf16[8,768,128]{2,1,0:T(8,128)(2,1)S(1)} %collective-permute-done.3.refs_8_), channel_id=1, source_target_pairs={{1,5},{5,9},{6,2},{9,13},{10,6},{13,17},{14,10},{17,21},{18,14},{2... | collective-permute-start | bytes 4718600 | tf_op jit(solution)/shard_map/ppermute | solution.py:409
  36.3 6.1 %collective-permute-start.10 = (bf16[8,512,128]{2,1,0:T(8,128)(2,1)S(1)}, bf16[8,512,128]{2,1,0:T(8,128)(2,1)S(1)}, u32[]{:S(2)}, u32[]{:S(2)}) collective-permute-start(bf16[8,512,128]{2,1,0:T(8,128)(2,1)S(1)} %get-tuple-element.44.rows.refs_1_.refs_2_), channel_id=1, source_target_pairs={{0,1},{3,2},{4,5},{7,6},{8,9},{11,10},{12,13},{15,14},{16,17},{19,... | collective-permute-start | bytes 3145736 | tf_op jit(solution)/shard_map/ppermute | solution.py:409
  40.0 15.3 %collective-permute-start.7 = (f32[208,128]{1,0:T(8,128)S(1)}, f32[208,128]{1,0:T(8,128)S(1)}, u32[]{:S(2)}, u32[]{:S(2)}) collective-permute-start(f32[208,128]{1,0:T(8,128)S(1)} %tree_merge.5.refs_0_), channel_id=1, source_target_pairs={{0,4},{1,5},{2,6},{3,7},{4,0},{5,1},{6,2},{7,3},{8,12},{9,13},{10,... | collective-permute-start | bytes 319496 | tf_op jit(solution)/shard_map/ppermute | solution.py:418
  60.1 19.7 %collective-permute-start.14 = (f32[8,512,128]{2,1,0:T(8,128)S(1)}, f32[8,512,128]{2,1,0:T(8,128)S(1)}, u32[]{:S(2)}, u32[]{:S(2)}) collective-permute-start(f32[8,512,128]{2,1,0:T(8,128)S(1)} %near_beside.1), channel_id=1, source_target_pairs={{0,1},{1,0},{2,3},{3,2},{4,5},{5,4},{6,7},{7,6},{8,9},{9,8},{10,11... | collective-permute-start | bytes 6291464 | tf_op jit(solution)/shard_map/ppermute | solution.py:418
  61.2 10.2 %collective-permute-start.11 = (f32[208,128]{1,0:T(8,128)S(1)}, f32[208,128]{1,0:T(8,128)S(1)}, u32[]{:S(2)}, u32[]{:S(2)}) collective-permute-start(f32[208,128]{1,0:T(8,128)S(1)} %tree_merge.6.refs_0_), channel_id=1, source_target_pairs={{0,8},{1,9},{2,10},{3,11},{4,12},{5,13},{6,14},{7,15},{8,0},{9,1},... | collective-permute-start | bytes 319496 | tf_op jit(solution)/shard_map/ppermute | solution.py:418
  65.7 11.2 %collective-permute-start.12 = (f32[208,128]{1,0:T(8,128)S(1)}, f32[208,128]{1,0:T(8,128)S(1)}, u32[]{:S(2)}, u32[]{:S(2)}) collective-permute-start(f32[208,128]{1,0:T(8,128)S(1)} %tree_merge.6.refs_0_), channel_id=1, source_target_pairs={{0,16},{1,17},{2,18},{3,19},{4,20},{5,21},{6,22},{7,23},{8,24},{9,... | collective-permute-start | bytes 319496 | tf_op jit(solution)/shard_map/ppermute | solution.py:418
  67.5 9.4 %collective-permute-start.13 = (f32[208,128]{1,0:T(8,128)S(1)}, f32[208,128]{1,0:T(8,128)S(1)}, u32[]{:S(2)}, u32[]{:S(2)}) collective-permute-start(f32[208,128]{1,0:T(8,128)S(1)} %tree_merge.6.refs_0_), channel_id=1, source_target_pairs={{0,24},{1,25},{2,26},{3,27},{4,28},{5,29},{6,30},{7,31},{8,16},{9,... | collective-permute-start | bytes 319496 | tf_op jit(solution)/shard_map/ppermute | solution.py:418

commit v11 on v7

--- a/solution.py
+++ b/solution.py
@@ -268,7 +268,7 @@
     )(*parts, merge_sets)
 
 
-def near_kernel(*refs, flips, row_counts, has_acc, sets, tasks, dim):
+def near_kernel(*refs, flips, row_counts, has_acc, sets, tasks, span, dim):
     refs = list(refs)
 
     def take(number):
@@ -300,7 +300,7 @@
         target_first = lax.axis_index("leaf") * window + (sub ^ flip) * blocks
 
         def list_block(g, counts, j=j, mine=mine, firsts=firsts, target_first=target_first):
-            for s in range(near):
+            for s in range(*span):
                 source = lists[j][g, s]
                 used = (source != target_first + g) if s else True
                 after = []
@@ -379,6 +379,7 @@
             has_acc=tuple(acc is not None for acc in accs),
             sets=tuple((bases, which) for bases, which, _ in sources),
             tasks=tasks,
+            span=(0, near),
             dim=dim,
         ),
         in_specs=[smem] * len(lists) + [vmem] * (len(args) - len(lists)),
@@ -428,13 +429,9 @@
     pack, rows = order_call(points.T, order.reshape(blocks, 1, leaf), probes, blocks)
     outer_across = send(pack, [(3, 0, 1), (0, 0, 2)])
     outer_next = send(pack, [(3, 1, 3), (0, -1, 0)])
-    inward, outward = [(1, 0, 0), (2, 0, 3)], [(0, 0, 1), (3, 0, 2)]
-    beside_pack = send(pack, inward)
-    edge_rows = send(rows, inward)
-    beside_lists = exchange(near_lists, 0, 1)[1]
+    beside_pack = send(pack, [(1, 0, 0), (2, 0, 3)])
 
     node = local_tree_call(pack, rows, leaf_sets, merge_sets, dim)
-    node, beside_lists = tie(node, beside_lists)
 
     def level(parts, bit, piece=None):
         return merge_call(parts, merge_sets, dim, blocks, bit, piece)
@@ -442,23 +439,25 @@
     node = level(exchange(node, 0, 1), 0)
     own_pack, node = tie(pack, node)
     parts = exchange(node, 1, 1)
-    own_set = (own_base, single, [own_pack])
-    (own,) = near_call([(0, near_lists, rows, None)], [own_set], ((0, 0),), dim, "near_own")
-
-    *parts, outer_across, outer_next, beside_pack, edge_rows, late_rows, own = tie(
-        *parts, outer_across, outer_next, beside_pack, edge_rows, rows, own
+    *parts, outer_across, outer_next, beside_pack, late_rows, late_lists = tie(
+        *parts, outer_across, outer_next, beside_pack, rows, near_lists
     )
     forwarded = send(outer_across, [(1, 1, 1), (2, -1, 2)])
     inner_across = send(beside_pack, [(0, 0, 3), (3, 0, 0)])
-    beside_rows = (edge_rows, send(late_rows, outward))
+    beside_rows = exchange(late_rows, 0, 1)[1]
+    beside_lists = exchange(late_lists, 0, 1)[1]
     node = level(parts, 1)
     own_pack, node = tie(own_pack, node)
     parts = exchange(node, 2, 1)
     own_set = (own_base, single, [own_pack])
     early_set = (early_base, by_edge, [outer_next, outer_across])
-    own, beside = near_call(
-        [(0, near_lists, rows, own), (1, beside_lists, beside_rows, None)],
-        [own_set, early_set], ((1, 0), (0, 1), (1, 1)), dim, "near_early",
+    (own,) = near_call(
+        [(0, near_lists, rows, None)], [own_set, early_set], ((0, 0), (1, 0)), dim, "near_own"
+    )
+    beside_rows, beside_lists, own = tie(beside_rows, beside_lists, own)
+    (beside,) = near_call(
+        [(1, beside_lists, beside_rows, None)],
+        [own_set, early_set], ((0, 0), (1, 0)), dim, "near_early",
     )
 
     *parts, inner_across, forwarded, beside = tie(*parts, inner_across, forwarded, beside)

time: 85.3 us -> 80 us (0.938); the launches traced: 84.2 us -> 79.8 us
  waiting for transfers between devices: 6.12 us -> 14.2 us
  starting transfers between devices: 29.5 us -> 21.5 us
  Pallas kernels: 41.5 us -> 37.2 us
    ppermute x8 -> x9, waiting for transfers between devices: 4.01 us -> 10 us  [exchange(): lax.ppermute(x, axes, [(i, i ^ d << shift) for i in range(count)])]
    ppermute x8 -> x9, starting transfers between devices: 15.8 us -> 11.2 us  [exchange(): lax.ppermute(x, axes, [(i, i ^ d << shift) for i in range(count)])]
    pallas_call x4, Pallas kernels: 26 us -> 21.7 us  [near_call(): pl.pallas_call(functools.partial(near_kernel, flips=flips, row_counts=tup...]
    ppermute x7 -> x5, starting transfers between devices: 13.7 us -> 10.2 us  [send(): return lax.ppermute(x, axes, pairs)]
    ppermute x7 -> x5, waiting for transfers between devices: 2.11 us -> 4.19 us  [send(): return lax.ppermute(x, axes, pairs)]
  transfers between devices with their start and end apart: 15 -> 14, of which waited for: 3 -> 5; matrix products, arithmetic and copies ran while one was open for 0% -> 0% of each run, Pallas kernels for 42% -> 38%
where the time goes in v11:
time: 80 us; the launch traced here: 79.8 us
  Pallas kernels  37.2 us (47%)
  starting transfers between devices  21.5 us (27%)
  waiting for transfers between devices  14.2 us (18%)
  local copies, waits for them, and re-layouts  4.57 us (6%)
  other arithmetic  1.56 us (2%)
  between operations  0.86 us (1%)
    pallas_call x4, Pallas kernels, near_call(): pl.pallas_call(functools.partial(near_kernel, flips=flips, row_counts=tup...  21.7 us
    ppermute x9, starting transfers between devices, exchange(): lax.ppermute(x, axes, [(i, i ^ d << shift) for i in range(count)])  11.2 us
    ppermute x5, starting transfers between devices, send(): return lax.ppermute(x, axes, pairs)  10.2 us
    ppermute x9, waiting for transfers between devices, exchange(): lax.ppermute(x, axes, [(i, i ^ d << shift) for i in range(count)])  10 us
    pallas_call x1, Pallas kernels, local_tree_call(): pl.pallas_call(functools.partial(local_tree_kernel, dim=dim), in_specs=[p...  7.01 us
    pallas_call x4, Pallas kernels, merge_call(): pl.pallas_call(functools.partial(merge_kernel, dim=dim, blocks=blocks, sh...  5.87 us
    unnamed x14, local copies, waits for them, and re-layouts  4.57 us
    ppermute x5, waiting for transfers between devices, send(): return lax.ppermute(x, axes, pairs)  4.19 us
  transfers between devices with their start and end apart: 14, of which 5 were waited for; matrix products, arithmetic and copies ran while one was open for 0% of the time, Pallas kernels for 38%

profile of v11, /device:TPU:0, one launch (start us, length us, event | category | flops | bytes accessed | tf_op | source)
XLA Modules:
  0.0 79.8 jit_solution(9479622466258642867)
XLA Ops:
  0.6 1.2 %copy-done.2 = bf16[4096,128]{1,0:T(8,128)(2,1)S(1)} copy-done((bf16[4096,128]{1,0:T(8,128)(2,1)S(1)}, bf16[4096,128]{1,0:T(8,128)(2,1)}, u32[]{:S(2)}) %copy-start.2) | copy-done | bytes 1048600
  1.9 1.0 %copy-done.3 = bf16[4096,64]{0,1:T(8,128)(2,1)S(1)} copy-done((bf16[4096,64]{0,1:T(8,128)(2,1)S(1)}, bf16[4096,64]{0,1:T(8,128)(2,1)}, u32[]{:S(2)}) %copy-start.3) | copy-done | bytes 524312
  3.6 2.6 %tree_order.1 = (bf16[8,768,128]{2,1,0:T(8,128)(2,1)S(1)}, bf16[8,512,128]{2,1,0:T(8,128)(2,1)S(1)}) custom-call(bf16[64,4096]{1,0:T(8,128)(2,1)S(1)} %bitcast.4, s32[8,1,512]{2,1,0:T(1,128)S(1)} %bitcast.5, bf16[4096,128]{1,0:T(8,128)(2,1)S(1)} %copy-done.2), custom_call_target="tpu_custom_call" | custom-call | flops 268435456 | bytes 5242880 | tf_op jit(solution)/shard_map/tree_order/pallas_call | solution.py:94
  6.3 5.0 %collective-permute-start.2 = (bf16[8,768,128]{2,1,0:T(8,128)(2,1)S(1)}, bf16[8,768,128]{2,1,0:T(8,128)(2,1)S(1)}, u32[]{:S(2)}, u32[]{:S(2)}) collective-permute-start(bf16[8,768,128]{2,1,0:T(8,128)(2,1)S(1)} %get-tuple-element.41.pack.refs_2_), channel_id=1, source_target_pairs={{3,1},{0,2},{7,5},{4,6},{11,9},{8,10},{15,13},{12,14},{19,17},{16,... | collective-permute-start | bytes 4718600 | tf_op jit(solution)/shard_map/ppermute | solution.py:409
  11.2 1.3 %collective-permute-start.3 = (bf16[8,768,128]{2,1,0:T(8,128)(2,1)S(1)}, bf16[8,768,128]{2,1,0:T(8,128)(2,1)S(1)}, u32[]{:S(2)}, u32[]{:S(2)}) collective-permute-start(bf16[8,768,128]{2,1,0:T(8,128)(2,1)S(1)} %get-tuple-element.41.pack.refs_2_), channel_id=1, source_target_pairs={{3,7},{7,11},{4,0},{11,15},{8,4},{15,19},{12,8},{19,23},{16,12},{2... | collective-permute-start | bytes 4718600 | tf_op jit(solution)/shard_map/ppermute | solution.py:409
  12.6 1.3 %collective-permute-start.4 = (bf16[8,768,128]{2,1,0:T(8,128)(2,1)S(1)}, bf16[8,768,128]{2,1,0:T(8,128)(2,1)S(1)}, u32[]{:S(2)}, u32[]{:S(2)}) collective-permute-start(bf16[8,768,128]{2,1,0:T(8,128)(2,1)S(1)} %get-tuple-element.41.pack.refs_2_), channel_id=1, source_target_pairs={{1,0},{2,3},{5,4},{6,7},{9,8},{10,11},{13,12},{14,15},{17,16},{18,... | collective-permute-start | bytes 4718600 | tf_op jit(solution)/shard_map/ppermute | solution.py:409
  15.4 7.0 %local_tree.1.refs_0_ = f32[208,128]{1,0:T(8,128)S(1)} custom-call(bf16[8,768,128]{2,1,0:T(8,128)(2,1)S(1)} %get-tuple-element.41.pack.refs_2_, bf16[8,512,128]{2,1,0:T(8,128)(2,1)S(1)} %get-tuple-element.39.rows.refs_1_, s32[8,128]{1,0:T(8,128)S(1)} %copy-done.6, s32[255,128]{1,0:T(8,128)S(1)} %copy-done), custom_call_target="tpu_custom_call" | custom-call | flops 536870912 | bytes 3145728 | tf_op jit(solution)/shard_map/local_tree/pallas_call | solution.py:177
  22.5 1.3 %collective-permute-start = (f32[208,128]{1,0:T(8,128)S(1)}, f32[208,128]{1,0:T(8,128)S(1)}, u32[]{:S(2)}, u32[]{:S(2)}) collective-permute-start(f32[208,128]{1,0:T(8,128)S(1)} %local_tree.1.refs_0_), channel_id=1, source_target_pairs={{0,1},{1,0},{2,3},{3,2},{4,5},{5,4},{6,7},{7,6},{8,9},{9,8},{10,11... | collective-permute-start | bytes 319496 | tf_op jit(solution)/shard_map/ppermute | solution.py:418
  25.7 1.9 %collective-permute-start.1 = (f32[208,128]{1,0:T(8,128)S(1)}, f32[208,128]{1,0:T(8,128)S(1)}, u32[]{:S(2)}, u32[]{:S(2)}) collective-permute-start(f32[208,128]{1,0:T(8,128)S(1)} %tree_merge.4.refs_0_), channel_id=1, source_target_pairs={{0,2},{1,3},{2,0},{3,1},{4,6},{5,7},{6,4},{7,5},{8,10},{9,11},{10,... | collective-permute-start | bytes 319496 | tf_op jit(solution)/shard_map/ppermute | solution.py:418
  27.6 3.8 %collective-permute-done.1.refs_1_ = f32[208,128]{1,0:T(8,128)S(1)} collective-permute-done((f32[208,128]{1,0:T(8,128)S(1)}, f32[208,128]{1,0:T(8,128)S(1)}, u32[]{:S(2)}, u32[]{:S(2)}) %collective-permute-start.1) | collective-permute-done | bytes 106528 | tf_op jit(solution)/shard_map/ppermute | solution.py:418
  31.4 2.2 %collective-permute-done.3.refs_3_ = bf16[8,768,128]{2,1,0:T(8,128)(2,1)S(1)} collective-permute-done((bf16[8,768,128]{2,1,0:T(8,128)(2,1)S(1)}, bf16[8,768,128]{2,1,0:T(8,128)(2,1)S(1)}, u32[]{:S(2)}, u32[]{:S(2)}) %collective-permute-start.3) | collective-permute-done | bytes 1572896 | tf_op jit(solution)/shard_map/ppermute | solution.py:409
  34.3 1.9 %collective-permute-start.6 = (bf16[8,768,128]{2,1,0:T(8,128)(2,1)S(1)}, bf16[8,768,128]{2,1,0:T(8,128)(2,1)S(1)}, u32[]{:S(2)}, u32[]{:S(2)}) collective-permute-start(bf16[8,768,128]{2,1,0:T(8,128)(2,1)S(1)} %collective-permute-done.4), channel_id=1, source_target_pairs={{0,3},{3,0},{4,7},{7,4},{8,11},{11,8},{12,15},{15,12},{16,19},{19,... | collective-permute-start | bytes 4718600 | tf_op jit(solution)/shard_map/ppermute | solution.py:409
  37.3 2.5 %collective-permute-start.5 = (f32[208,128]{1,0:T(8,128)S(1)}, f32[208,128]{1,0:T(8,128)S(1)}, u32[]{:S(2)}, u32[]{:S(2)}) collective-permute-start(f32[208,128]{1,0:T(8,128)S(1)} %tree_merge.5.refs_0_), channel_id=1, source_target_pairs={{0,4},{1,5},{2,6},{3,7},{4,0},{5,1},{6,2},{7,3},{8,12},{9,13},{10,... | collective-permute-start | bytes 319496 | tf_op jit(solution)/shard_map/ppermute | solution.py:418
  40.0 8.7 %near_own.1.refs_2_ = f32[8,512,128]{2,1,0:T(8,128)S(1)} custom-call(s32[8,12]{1,0:T(8,128)S(1)} %copy-done.4, bf16[8,512,128]{2,1,0:T(8,128)(2,1)S(1)} %get-tuple-element.39.rows.refs_1_, bf16[8,768,128]{2,1,0:T(8,128)(2,1)S(1)} %get-tuple-element.41.pack.refs_2_, bf16[8,768,128]{2,1,0:T(8,128)(2,1)S(1)} %collective-permute-done.3.refs_3_, ...), custom_call_target="tpu_custom_call" | custom-call | flops 1000 | bytes 1000 | tf_op jit(solution)/shard_map/near_own/pallas_call | solution.py:374
  48.7 5.3 %near_early.1.refs_2_ = f32[8,512,128]{2,1,0:T(8,128)S(1)} custom-call(s32[8,12]{1,0:T(8,128)S(1)} %collective-permute-done.9.refs_0_, bf16[8,512,128]{2,1,0:T(8,128)(2,1)S(1)} %collective-permute-done.8.refs_1_, bf16[8,768,128]{2,1,0:T(8,128)(2,1)S(1)} %get-tuple-element.41.pack.refs_2_, bf16[8,768,128]{2,1,0:T(8,128)(2,1)S(1)} %collective-permute-done.3.refs_3_, ...), custom_call_target="tpu_custom_call" | custom-call | flops 1000 | bytes 1000 | tf_op jit(solution)/shard_map/near_early/pallas_call | solution.py:374
  54.1 2.0 %collective-permute-done.6.refs_3_ = bf16[8,768,128]{2,1,0:T(8,128)(2,1)S(1)} collective-permute-done((bf16[8,768,128]{2,1,0:T(8,128)(2,1)S(1)}, bf16[8,768,128]{2,1,0:T(8,128)(2,1)S(1)}, u32[]{:S(2)}, u32[]{:S(2)}) %collective-permute-start.6) | collective-permute-done | bytes 1572896 | tf_op jit(solution)/shard_map/ppermute | solution.py:409
  56.1 4.5 %near_beside.1 = f32[8,512,128]{2,1,0:T(8,128)S(1)} custom-call(s32[8,12]{1,0:T(8,128)S(1)} %collective-permute-done.9.refs_0_, bf16[8,512,128]{2,1,0:T(8,128)(2,1)S(1)} %collective-permute-done.8.refs_1_, f32[8,512,128]{2,1,0:T(8,128)S(1)} %near_early.1.refs_2_, bf16[8,768,128]{2,1,0:T(8,128)(2,1)S(1)} %collective-permute-done.6.refs_3_, ...), custom_call_target="tpu_custom_call" | custom-call | flops 1000 | bytes 1000 | tf_op jit(solution)/shard_map/near_beside/pallas_call | solution.py:374
  60.7 1.0 %tree_merge.6.refs_0_ = f32[208,128]{1,0:T(8,128)S(1)} custom-call(f32[208,128]{1,0:T(8,128)S(1)} %tree_merge.5.refs_0_, f32[208,128]{1,0:T(8,128)S(1)} %collective-permute-done.5.refs_1_, s32[255,128]{1,0:T(8,128)S(1)} %copy-done.1), custom_call_target="tpu_custom_call" | custom-call | flops 67108864 | bytes 212992 | tf_op jit(solution)/shard_map/tree_merge/pallas_call | solution.py:251
  61.7 1.9 %collective-permute-start.10 = (f32[208,128]{1,0:T(8,128)S(1)}, f32[208,128]{1,0:T(8,128)S(1)}, u32[]{:S(2)}, u32[]{:S(2)}) collective-permute-start(f32[208,128]{1,0:T(8,128)S(1)} %tree_merge.6.refs_0_), channel_id=1, source_target_pairs={{0,8},{1,9},{2,10},{3,11},{4,12},{5,13},{6,14},{7,15},{8,0},{9,1},... | collective-permute-start | bytes 319496 | tf_op jit(solution)/shard_map/ppermute | solution.py:418
  63.6 3.3 %collective-permute-start.11 = (f32[208,128]{1,0:T(8,128)S(1)}, f32[208,128]{1,0:T(8,128)S(1)}, u32[]{:S(2)}, u32[]{:S(2)}) collective-permute-start(f32[208,128]{1,0:T(8,128)S(1)} %tree_merge.6.refs_0_), channel_id=1, source_target_pairs={{0,16},{1,17},{2,18},{3,19},{4,20},{5,21},{6,22},{7,23},{8,24},{9,... | collective-permute-start | bytes 319496 | tf_op jit(solution)/shard_map/ppermute | solution.py:418
  66.9 3.1 %near_last.1 = f32[8,512,128]{2,1,0:T(8,128)S(1)} custom-call(s32[8,12]{1,0:T(8,128)S(1)} %copy-done.4, bf16[8,512,128]{2,1,0:T(8,128)(2,1)S(1)} %get-tuple-element.39.rows.refs_1_, f32[8,512,128]{2,1,0:T(8,128)S(1)} %near_own.1.refs_2_, bf16[8,768,128]{2,1,0:T(8,128)(2,1)S(1)} %collective-permute-done.6.refs_3_, ...), custom_call_target="tpu_custom_call" | custom-call | flops 1000 | bytes 1000 | tf_op jit(solution)/shard_map/near_last/pallas_call | solution.py:374
  70.0 5.3 %collective-permute-done.11.refs_2_ = f32[208,128]{1,0:T(8,128)S(1)} collective-permute-done((f32[208,128]{1,0:T(8,128)S(1)}, f32[208,128]{1,0:T(8,128)S(1)}, u32[]{:S(2)}, u32[]{:S(2)}) %collective-permute-start.11) | collective-permute-done | bytes 106528 | tf_op jit(solution)/shard_map/ppermute | solution.py:418
  75.3 2.9 %tree_merge.7 = f32[4,128]{1,0:T(4,128)} custom-call(f32[208,128]{1,0:T(8,128)S(1)} %tree_merge.6.refs_0_, f32[208,128]{1,0:T(8,128)S(1)} %collective-permute-done.10.refs_1_, f32[208,128]{1,0:T(8,128)S(1)} %collective-permute-done.11.refs_2_, f32[208,128]{1,0:T(8,128)S(1)} %collective-permute-done.12.refs_3_, s32[255,128]{1,0:T(8,128)S(1)} %copy-done.1), custom_call_target="tpu_custom_call" | custom-call | flops 134217728 | bytes 425984 | tf_op jit(solution)/shard_map/tree_merge/pallas_call | solution.py:251
  78.3 1.6 %add_multiply_fusion = f32[8,512,128]{2,1,0:T(8,128)} fusion(f32[8,512,128]{2,1,0:T(8,128)S(1)} %near_last.1, f32[8,512,128]{2,1,0:T(8,128)S(1)} %collective-permute-done.13), kind=kLoop, calls=%fused_computation | loop fusion | flops 1048576 | bytes 6291456 | tf_op jit(solution)/shard_map/mul | solution.py:478
  (29 shorter events, 6.3 us)
Async XLA Ops:
  0.6 1.2 %copy-start.2 = (bf16[4096,128]{1,0:T(8,128)(2,1)S(1)}, bf16[4096,128]{1,0:T(8,128)(2,1)}, u32[]{:S(2)}) copy-start(bf16[4096,128]{1,0:T(8,128)(2,1)} %probes.1) | copy-start | bytes 3145732
  1.9 1.0 %copy-start.3 = (bf16[4096,64]{0,1:T(8,128)(2,1)S(1)}, bf16[4096,64]{0,1:T(8,128)(2,1)}, u32[]{:S(2)}) copy-start(bf16[4096,64]{0,1:T(8,128)(2,1)} %param.7) | copy-start | bytes 1572868
  2.9 0.7 copy-start.5
  3.6 36.2 %copy-start.4 = (s32[8,12]{1,0:T(8,128)S(1)}, s32[8,12]{1,0:T(8,128)}, u32[]{:S(2)}) copy-start(s32[8,12]{1,0:T(8,128)} %refs_0_.3) | copy-start | bytes 1156
  6.3 25.1 %collective-permute-start.2 = (bf16[8,768,128]{2,1,0:T(8,128)(2,1)S(1)}, bf16[8,768,128]{2,1,0:T(8,128)(2,1)S(1)}, u32[]{:S(2)}, u32[]{:S(2)}) collective-permute-start(bf16[8,768,128]{2,1,0:T(8,128)(2,1)S(1)} %get-tuple-element.41.pack.refs_2_), channel_id=1, source_target_pairs={{3,1},{0,2},{7,5},{4,6},{11,9},{8,10},{15,13},{12,14},{19,17},{16,... | collective-permute-start | bytes 4718600 | tf_op jit(solution)/shard_map/ppermute | solution.py:409
  11.2 22.3 %collective-permute-start.3 = (bf16[8,768,128]{2,1,0:T(8,128)(2,1)S(1)}, bf16[8,768,128]{2,1,0:T(8,128)(2,1)S(1)}, u32[]{:S(2)}, u32[]{:S(2)}) collective-permute-start(bf16[8,768,128]{2,1,0:T(8,128)(2,1)S(1)} %get-tuple-element.41.pack.refs_2_), channel_id=1, source_target_pairs={{3,7},{7,11},{4,0},{11,15},{8,4},{15,19},{12,8},{19,23},{16,12},{2... | collective-permute-start | bytes 4718600 | tf_op jit(solution)/shard_map/ppermute | solution.py:409
  12.6 21.0 %collective-permute-start.4 = (bf16[8,768,128]{2,1,0:T(8,128)(2,1)S(1)}, bf16[8,768,128]{2,1,0:T(8,128)(2,1)S(1)}, u32[]{:S(2)}, u32[]{:S(2)}) collective-permute-start(bf16[8,768,128]{2,1,0:T(8,128)(2,1)S(1)} %get-tuple-element.41.pack.refs_2_), channel_id=1, source_target_pairs={{1,0},{2,3},{5,4},{6,7},{9,8},{10,11},{13,12},{14,15},{17,16},{18,... | collective-permute-start | bytes 4718600 | tf_op jit(solution)/shard_map/ppermute | solution.py:409
  13.8 0.9 %copy-start = (s32[255,128]{1,0:T(8,128)S(1)}, s32[255,128]{1,0:T(8,128)}, u32[]{:S(2)}) copy-start(s32[255,128]{1,0:T(8,128)} %refs_4_.1) | copy-start | bytes 391684
  14.8 0.7 copy-start.6
  22.5 2.3 %collective-permute-start = (f32[208,128]{1,0:T(8,128)S(1)}, f32[208,128]{1,0:T(8,128)S(1)}, u32[]{:S(2)}, u32[]{:S(2)}) collective-permute-start(f32[208,128]{1,0:T(8,128)S(1)} %local_tree.1.refs_0_), channel_id=1, source_target_pairs={{0,1},{1,0},{2,3},{3,2},{4,5},{5,4},{6,7},{7,6},{8,9},{9,8},{10,11... | collective-permute-start | bytes 319496 | tf_op jit(solution)/shard_map/ppermute | solution.py:418
  25.7 5.7 %collective-permute-start.1 = (f32[208,128]{1,0:T(8,128)S(1)}, f32[208,128]{1,0:T(8,128)S(1)}, u32[]{:S(2)}, u32[]{:S(2)}) collective-permute-start(f32[208,128]{1,0:T(8,128)S(1)} %tree_merge.4.refs_0_), channel_id=1, source_target_pairs={{0,2},{1,3},{2,0},{3,1},{4,6},{5,7},{6,4},{7,5},{8,10},{9,11},{10,... | collective-permute-start | bytes 319496 | tf_op jit(solution)/shard_map/ppermute | solution.py:418
  33.6 20.5 %collective-permute-start.7 = (bf16[8,768,128]{2,1,0:T(8,128)(2,1)S(1)}, bf16[8,768,128]{2,1,0:T(8,128)(2,1)S(1)}, u32[]{:S(2)}, u32[]{:S(2)}) collective-permute-start(bf16[8,768,128]{2,1,0:T(8,128)(2,1)S(1)} %collective-permute-done.2.refs_4_), channel_id=1, source_target_pairs={{1,5},{5,9},{6,2},{9,13},{10,6},{13,17},{14,10},{17,21},{18,14},{2... | collective-permute-start | bytes 4718600 | tf_op jit(solution)/shard_map/ppermute | solution.py:409
  34.3 21.7 %collective-permute-start.6 = (bf16[8,768,128]{2,1,0:T(8,128)(2,1)S(1)}, bf16[8,768,128]{2,1,0:T(8,128)(2,1)S(1)}, u32[]{:S(2)}, u32[]{:S(2)}) collective-permute-start(bf16[8,768,128]{2,1,0:T(8,128)(2,1)S(1)} %collective-permute-done.4), channel_id=1, source_target_pairs={{0,3},{3,0},{4,7},{7,4},{8,11},{11,8},{12,15},{15,12},{16,19},{19,... | collective-permute-start | bytes 4718600 | tf_op jit(solution)/shard_map/ppermute | solution.py:409
  36.3 12.5 %collective-permute-start.8 = (bf16[8,512,128]{2,1,0:T(8,128)(2,1)S(1)}, bf16[8,512,128]{2,1,0:T(8,128)(2,1)S(1)}, u32[]{:S(2)}, u32[]{:S(2)}) collective-permute-start(bf16[8,512,128]{2,1,0:T(8,128)(2,1)S(1)} %get-tuple-element.39.rows.refs_1_), channel_id=1, source_target_pairs={{0,1},{1,0},{2,3},{3,2},{4,5},{5,4},{6,7},{7,6},{8,9},{9,8},{10,11... | collective-permute-start | bytes 3145736 | tf_op jit(solution)/shard_map/ppermute | solution.py:418
  37.3 16.7 %collective-permute-start.5 = (f32[208,128]{1,0:T(8,128)S(1)}, f32[208,128]{1,0:T(8,128)S(1)}, u32[]{:S(2)}, u32[]{:S(2)}) collective-permute-start(f32[208,128]{1,0:T(8,128)S(1)} %tree_merge.5.refs_0_), channel_id=1, source_target_pairs={{0,4},{1,5},{2,6},{3,7},{4,0},{5,1},{6,2},{7,3},{8,12},{9,13},{10,... | collective-permute-start | bytes 319496 | tf_op jit(solution)/shard_map/ppermute | solution.py:418
  39.8 8.9 %collective-permute-start.9 = (s32[8,12]{1,0:T(8,128)S(1)}, s32[8,12]{1,0:T(8,128)S(1)}, u32[]{:S(2)}, u32[]{:S(2)}) collective-permute-start(s32[8,12]{1,0:T(8,128)S(1)} %copy-done.4), channel_id=1, source_target_pairs={{0,1},{1,0},{2,3},{3,2},{4,5},{5,4},{6,7},{7,6},{8,9},{9,8},{10,11... | collective-permute-start | bytes 1160 | tf_op jit(solution)/shard_map/ppermute | solution.py:418
  54.1 6.6 %copy-start.1 = (s32[255,128]{1,0:T(8,128)S(1)}, s32[255,128]{1,0:T(8,128)}, u32[]{:S(2)}) copy-start(s32[255,128]{1,0:T(8,128)} %refs_4_.1) | copy-start | bytes 391684
  60.6 17.7 %collective-permute-start.13 = (f32[8,512,128]{2,1,0:T(8,128)S(1)}, f32[8,512,128]{2,1,0:T(8,128)S(1)}, u32[]{:S(2)}, u32[]{:S(2)}) collective-permute-start(f32[8,512,128]{2,1,0:T(8,128)S(1)} %near_beside.1), channel_id=1, source_target_pairs={{0,1},{1,0},{2,3},{3,2},{4,5},{5,4},{6,7},{7,6},{8,9},{9,8},{10,11... | collective-permute-start | bytes 6291464 | tf_op jit(solution)/shard_map/ppermute | solution.py:418
  61.7 8.3 %collective-permute-start.10 = (f32[208,128]{1,0:T(8,128)S(1)}, f32[208,128]{1,0:T(8,128)S(1)}, u32[]{:S(2)}, u32[]{:S(2)}) collective-permute-start(f32[208,128]{1,0:T(8,128)S(1)} %tree_merge.6.refs_0_), channel_id=1, source_target_pairs={{0,8},{1,9},{2,10},{3,11},{4,12},{5,13},{6,14},{7,15},{8,0},{9,1},... | collective-permute-start | bytes 319496 | tf_op jit(solution)/shard_map/ppermute | solution.py:418
  63.6 11.7 %collective-permute-start.11 = (f32[208,128]{1,0:T(8,128)S(1)}, f32[208,128]{1,0:T(8,128)S(1)}, u32[]{:S(2)}, u32[]{:S(2)}) collective-permute-start(f32[208,128]{1,0:T(8,128)S(1)} %tree_merge.6.refs_0_), channel_id=1, source_target_pairs={{0,16},{1,17},{2,18},{3,19},{4,20},{5,21},{6,22},{7,23},{8,24},{9,... | collective-permute-start | bytes 319496 | tf_op jit(solution)/shard_map/ppermute | solution.py:418
  66.9 8.4 %collective-permute-start.12 = (f32[208,128]{1,0:T(8,128)S(1)}, f32[208,128]{1,0:T(8,128)S(1)}, u32[]{:S(2)}, u32[]{:S(2)}) collective-permute-start(f32[208,128]{1,0:T(8,128)S(1)} %tree_merge.6.refs_0_), channel_id=1, source_target_pairs={{0,24},{1,25},{2,26},{3,27},{4,28},{5,29},{6,30},{7,31},{8,16},{9,... | collective-permute-start | bytes 319496 | tf_op jit(solution)/shard_map/ppermute | solution.py:418

commit v12 on v11

--- a/solution.py
+++ b/solution.py
@@ -460,21 +460,26 @@
         [own_set, early_set], ((0, 0), (1, 0)), dim, "near_early",
     )
 
-    *parts, inner_across, forwarded, beside = tie(*parts, inner_across, forwarded, beside)
+    *parts, inner_across, forwarded, beside, own = tie(
+        *parts, inner_across, forwarded, beside, own
+    )
     late_set = (late_base, by_edge, [inner_across, forwarded])
+    bit = 2
+    while bit < bits - 2:
+        node = level(parts, bit)
+        bit += 1
+        parts = exchange(node, bit, 1)
+    (own,) = near_call([(0, near_lists, rows, own)], [late_set], ((0, 0),), dim, "near_last")
+    *parts, own = tie(*parts, own)
+    node = level(parts, bit)
+    bit += 1
+    beside, node = tie(beside, node)
     (beside,) = near_call(
         [(1, beside_lists, beside_rows, beside)], [late_set], ((0, 0),), dim, "near_beside"
     )
     given = exchange(beside, 0, 1)[1]
-    *parts, beside = tie(*parts, beside)
-    shift, stage = 2, 1
-    while shift + stage < bits:
-        node = level(parts, shift)
-        shift, stage = shift + stage, min(2, bits - shift - stage)
-        parts = exchange(node, shift, stage)
-    (own,) = near_call([(0, near_lists, rows, own)], [late_set], ((0, 0),), dim, "near_last")
-    *parts, own = tie(*parts, own)
-    node = level(parts, shift, skel // count)
+    node, beside = tie(node, beside)
+    node = level(exchange(node, bit, 1), bit, skel // count)
     near = (own + given) * (leaf ** -0.5)
     if skel // count:
         root = node.reshape(-1)

time: 80 us -> 80.6 us (level)
  starting transfers between devices: 21.5 us -> 23.4 us
  waiting for transfers between devices: 14.2 us -> 12.3 us
    ppermute x5, waiting for transfers between devices: 4.19 us -> 2.22 us  [send(): return lax.ppermute(x, axes, pairs)]
    ppermute x9 -> x8, starting transfers between devices: 11.2 us -> 13.2 us  [exchange(): lax.ppermute(x, axes, [(i, i ^ d << shift) for i in range(count)])]
    pallas_call x4 -> x5, Pallas kernels: 5.87 us -> 5.58 us  [merge_call(): pl.pallas_call(functools.partial(merge_kernel, dim=dim, blocks=blocks, sh...]
    ppermute x9 -> x8, waiting for transfers between devices: 10 us -> 10.1 us  [exchange(): lax.ppermute(x, axes, [(i, i ^ d << shift) for i in range(count)])]
  transfers between devices with their start and end apart: 14 -> 13, of which waited for: 5 -> 4; matrix products, arithmetic and copies ran while one was open for 0% -> 0% of each run, Pallas kernels for 38% -> 39%
where the time goes in v12:
time: 80.6 us; the launch traced here: 80.2 us
  Pallas kernels  37.5 us (47%)
  starting transfers between devices  23.4 us (29%)
  waiting for transfers between devices  12.3 us (15%)
  local copies, waits for them, and re-layouts  4.57 us (6%)
  other arithmetic  1.56 us (2%)
  between operations  0.86 us (1%)
    pallas_call x4, Pallas kernels, near_call(): pl.pallas_call(functools.partial(near_kernel, flips=flips, row_counts=tup...  22.3 us
    ppermute x8, starting transfers between devices, exchange(): lax.ppermute(x, axes, [(i, i ^ d << shift) for i in range(count)])  13.2 us
    ppermute x5, starting transfers between devices, send(): return lax.ppermute(x, axes, pairs)  10.2 us
    ppermute x8, waiting for transfers between devices, exchange(): lax.ppermute(x, axes, [(i, i ^ d << shift) for i in range(count)])  10.1 us
    pallas_call x1, Pallas kernels, local_tree_call(): pl.pallas_call(functools.partial(local_tree_kernel, dim=dim), in_specs=[p...  7.01 us
    pallas_call x5, Pallas kernels, merge_call(): pl.pallas_call(functools.partial(merge_kernel, dim=dim, blocks=blocks, sh...  5.58 us
    unnamed x14, local copies, waits for them, and re-layouts  4.57 us
    pallas_call x1, Pallas kernels, order_call(): pl.pallas_call(order_kernel, grid=(blocks // many,), in_specs=[pl.BlockSp...  2.64 us
  transfers between devices with their start and end apart: 13, of which 4 were waited for; matrix products, arithmetic and copies ran while one was open for 0% of the time, Pallas kernels for 39%

profile of v12, /device:TPU:0, one launch (start us, length us, event | category | flops | bytes accessed | tf_op | source)
XLA Modules:
  0.0 80.2 jit_solution(2836974920526186453)
XLA Ops:
  0.6 1.2 %copy-done.2 = bf16[4096,128]{1,0:T(8,128)(2,1)S(1)} copy-done((bf16[4096,128]{1,0:T(8,128)(2,1)S(1)}, bf16[4096,128]{1,0:T(8,128)(2,1)}, u32[]{:S(2)}) %copy-start.2) | copy-done | bytes 1048600
  1.9 1.0 %copy-done.3 = bf16[4096,64]{0,1:T(8,128)(2,1)S(1)} copy-done((bf16[4096,64]{0,1:T(8,128)(2,1)S(1)}, bf16[4096,64]{0,1:T(8,128)(2,1)}, u32[]{:S(2)}) %copy-start.3) | copy-done | bytes 524312
  3.6 2.6 %tree_order.1 = (bf16[8,768,128]{2,1,0:T(8,128)(2,1)S(1)}, bf16[8,512,128]{2,1,0:T(8,128)(2,1)S(1)}) custom-call(bf16[64,4096]{1,0:T(8,128)(2,1)S(1)} %bitcast.4, s32[8,1,512]{2,1,0:T(1,128)S(1)} %bitcast.5, bf16[4096,128]{1,0:T(8,128)(2,1)S(1)} %copy-done.2), custom_call_target="tpu_custom_call" | custom-call | flops 268435456 | bytes 5242880 | tf_op jit(solution)/shard_map/tree_order/pallas_call | solution.py:94
  6.3 5.0 %collective-permute-start.2 = (bf16[8,768,128]{2,1,0:T(8,128)(2,1)S(1)}, bf16[8,768,128]{2,1,0:T(8,128)(2,1)S(1)}, u32[]{:S(2)}, u32[]{:S(2)}) collective-permute-start(bf16[8,768,128]{2,1,0:T(8,128)(2,1)S(1)} %get-tuple-element.41.pack.refs_2_), channel_id=1, source_target_pairs={{3,1},{0,2},{7,5},{4,6},{11,9},{8,10},{15,13},{12,14},{19,17},{16,... | collective-permute-start | bytes 4718600 | tf_op jit(solution)/shard_map/ppermute | solution.py:409
  11.2 1.3 %collective-permute-start.3 = (bf16[8,768,128]{2,1,0:T(8,128)(2,1)S(1)}, bf16[8,768,128]{2,1,0:T(8,128)(2,1)S(1)}, u32[]{:S(2)}, u32[]{:S(2)}) collective-permute-start(bf16[8,768,128]{2,1,0:T(8,128)(2,1)S(1)} %get-tuple-element.41.pack.refs_2_), channel_id=1, source_target_pairs={{3,7},{7,11},{4,0},{11,15},{8,4},{15,19},{12,8},{19,23},{16,12},{2... | collective-permute-start | bytes 4718600 | tf_op jit(solution)/shard_map/ppermute | solution.py:409
  12.6 1.3 %collective-permute-start.4 = (bf16[8,768,128]{2,1,0:T(8,128)(2,1)S(1)}, bf16[8,768,128]{2,1,0:T(8,128)(2,1)S(1)}, u32[]{:S(2)}, u32[]{:S(2)}) collective-permute-start(bf16[8,768,128]{2,1,0:T(8,128)(2,1)S(1)} %get-tuple-element.41.pack.refs_2_), channel_id=1, source_target_pairs={{1,0},{2,3},{5,4},{6,7},{9,8},{10,11},{13,12},{14,15},{17,16},{18,... | collective-permute-start | bytes 4718600 | tf_op jit(solution)/shard_map/ppermute | solution.py:409
  15.4 7.0 %local_tree.1.refs_0_ = f32[208,128]{1,0:T(8,128)S(1)} custom-call(bf16[8,768,128]{2,1,0:T(8,128)(2,1)S(1)} %get-tuple-element.41.pack.refs_2_, bf16[8,512,128]{2,1,0:T(8,128)(2,1)S(1)} %get-tuple-element.39.rows.refs_1_, s32[8,128]{1,0:T(8,128)S(1)} %copy-done.6, s32[255,128]{1,0:T(8,128)S(1)} %copy-done), custom_call_target="tpu_custom_call" | custom-call | flops 536870912 | bytes 3145728 | tf_op jit(solution)/shard_map/local_tree/pallas_call | solution.py:177
  22.5 1.3 %collective-permute-start = (f32[208,128]{1,0:T(8,128)S(1)}, f32[208,128]{1,0:T(8,128)S(1)}, u32[]{:S(2)}, u32[]{:S(2)}) collective-permute-start(f32[208,128]{1,0:T(8,128)S(1)} %local_tree.1.refs_0_), channel_id=1, source_target_pairs={{0,1},{1,0},{2,3},{3,2},{4,5},{5,4},{6,7},{7,6},{8,9},{9,8},{10,11... | collective-permute-start | bytes 319496 | tf_op jit(solution)/shard_map/ppermute | solution.py:418
  25.7 1.9 %collective-permute-start.1 = (f32[208,128]{1,0:T(8,128)S(1)}, f32[208,128]{1,0:T(8,128)S(1)}, u32[]{:S(2)}, u32[]{:S(2)}) collective-permute-start(f32[208,128]{1,0:T(8,128)S(1)} %tree_merge.5.refs_0_), channel_id=1, source_target_pairs={{0,2},{1,3},{2,0},{3,1},{4,6},{5,7},{6,4},{7,5},{8,10},{9,11},{10,... | collective-permute-start | bytes 319496 | tf_op jit(solution)/shard_map/ppermute | solution.py:418
  27.6 3.8 %collective-permute-done.1.refs_1_ = f32[208,128]{1,0:T(8,128)S(1)} collective-permute-done((f32[208,128]{1,0:T(8,128)S(1)}, f32[208,128]{1,0:T(8,128)S(1)}, u32[]{:S(2)}, u32[]{:S(2)}) %collective-permute-start.1) | collective-permute-done | bytes 106528 | tf_op jit(solution)/shard_map/ppermute | solution.py:418
  31.4 2.2 %collective-permute-done.3.refs_3_ = bf16[8,768,128]{2,1,0:T(8,128)(2,1)S(1)} collective-permute-done((bf16[8,768,128]{2,1,0:T(8,128)(2,1)S(1)}, bf16[8,768,128]{2,1,0:T(8,128)(2,1)S(1)}, u32[]{:S(2)}, u32[]{:S(2)}) %collective-permute-start.3) | collective-permute-done | bytes 1572896 | tf_op jit(solution)/shard_map/ppermute | solution.py:409
  34.3 1.9 %collective-permute-start.6 = (bf16[8,768,128]{2,1,0:T(8,128)(2,1)S(1)}, bf16[8,768,128]{2,1,0:T(8,128)(2,1)S(1)}, u32[]{:S(2)}, u32[]{:S(2)}) collective-permute-start(bf16[8,768,128]{2,1,0:T(8,128)(2,1)S(1)} %collective-permute-done.4), channel_id=1, source_target_pairs={{0,3},{3,0},{4,7},{7,4},{8,11},{11,8},{12,15},{15,12},{16,19},{19,... | collective-permute-start | bytes 4718600 | tf_op jit(solution)/shard_map/ppermute | solution.py:409
  36.3 1.0 %tree_merge.6.refs_0_ = f32[208,128]{1,0:T(8,128)S(1)} custom-call(f32[208,128]{1,0:T(8,128)S(1)} %tree_merge.5.refs_0_, f32[208,128]{1,0:T(8,128)S(1)} %collective-permute-done.1.refs_1_, s32[255,128]{1,0:T(8,128)S(1)} %copy-done), custom_call_target="tpu_custom_call" | custom-call | flops 67108864 | bytes 212992 | tf_op jit(solution)/shard_map/tree_merge/pallas_call | solution.py:251
  37.3 2.5 %collective-permute-start.5 = (f32[208,128]{1,0:T(8,128)S(1)}, f32[208,128]{1,0:T(8,128)S(1)}, u32[]{:S(2)}, u32[]{:S(2)}) collective-permute-start(f32[208,128]{1,0:T(8,128)S(1)} %tree_merge.6.refs_0_), channel_id=1, source_target_pairs={{0,4},{1,5},{2,6},{3,7},{4,0},{5,1},{6,2},{7,3},{8,12},{9,13},{10,... | collective-permute-start | bytes 319496 | tf_op jit(solution)/shard_map/ppermute | solution.py:418
  40.0 11.8 %near_own.1.refs_2_ = f32[8,512,128]{2,1,0:T(8,128)S(1)} custom-call(s32[8,12]{1,0:T(8,128)S(1)} %copy-done.4, bf16[8,512,128]{2,1,0:T(8,128)(2,1)S(1)} %get-tuple-element.39.rows.refs_1_, bf16[8,768,128]{2,1,0:T(8,128)(2,1)S(1)} %get-tuple-element.41.pack.refs_2_, bf16[8,768,128]{2,1,0:T(8,128)(2,1)S(1)} %collective-permute-done.3.refs_3_, ...), custom_call_target="tpu_custom_call" | custom-call | flops 1000 | bytes 1000 | tf_op jit(solution)/shard_map/near_own/pallas_call | solution.py:374
  51.8 5.5 %near_early.1.refs_2_ = f32[8,512,128]{2,1,0:T(8,128)S(1)} custom-call(s32[8,12]{1,0:T(8,128)S(1)} %collective-permute-done.9.refs_0_, bf16[8,512,128]{2,1,0:T(8,128)(2,1)S(1)} %collective-permute-done.8.refs_1_, bf16[8,768,128]{2,1,0:T(8,128)(2,1)S(1)} %get-tuple-element.41.pack.refs_2_, bf16[8,768,128]{2,1,0:T(8,128)(2,1)S(1)} %collective-permute-done.3.refs_3_, ...), custom_call_target="tpu_custom_call" | custom-call | flops 1000 | bytes 1000 | tf_op jit(solution)/shard_map/near_early/pallas_call | solution.py:374
  57.3 1.0 %tree_merge.7.refs_0_ = f32[208,128]{1,0:T(8,128)S(1)} custom-call(f32[208,128]{1,0:T(8,128)S(1)} %tree_merge.6.refs_0_, f32[208,128]{1,0:T(8,128)S(1)} %collective-permute-done.5.refs_1_, s32[255,128]{1,0:T(8,128)S(1)} %copy-done.1), custom_call_target="tpu_custom_call" | custom-call | flops 67108864 | bytes 212992 | tf_op jit(solution)/shard_map/tree_merge/pallas_call | solution.py:251
  58.3 1.4 %collective-permute-start.10 = (f32[208,128]{1,0:T(8,128)S(1)}, f32[208,128]{1,0:T(8,128)S(1)}, u32[]{:S(2)}, u32[]{:S(2)}) collective-permute-start(f32[208,128]{1,0:T(8,128)S(1)} %tree_merge.7.refs_0_), channel_id=1, source_target_pairs={{0,8},{1,9},{2,10},{3,11},{4,12},{5,13},{6,14},{7,15},{8,0},{9,1},... | collective-permute-start | bytes 319496 | tf_op jit(solution)/shard_map/ppermute | solution.py:418
  59.7 3.4 %near_last.1 = f32[8,512,128]{2,1,0:T(8,128)S(1)} custom-call(s32[8,12]{1,0:T(8,128)S(1)} %copy-done.4, bf16[8,512,128]{2,1,0:T(8,128)(2,1)S(1)} %get-tuple-element.39.rows.refs_1_, f32[8,512,128]{2,1,0:T(8,128)S(1)} %near_own.1.refs_2_, bf16[8,768,128]{2,1,0:T(8,128)(2,1)S(1)} %collective-permute-done.6.refs_3_, ...), custom_call_target="tpu_custom_call" | custom-call | flops 1000 | bytes 1000 | tf_op jit(solution)/shard_map/near_last/pallas_call | solution.py:374
  64.1 1.6 %near_beside.1 = f32[8,512,128]{2,1,0:T(8,128)S(1)} custom-call(s32[8,12]{1,0:T(8,128)S(1)} %collective-permute-done.9.refs_0_, bf16[8,512,128]{2,1,0:T(8,128)(2,1)S(1)} %collective-permute-done.8.refs_1_, f32[8,512,128]{2,1,0:T(8,128)S(1)} %near_early.1.refs_2_, bf16[8,768,128]{2,1,0:T(8,128)(2,1)S(1)} %collective-permute-done.6.refs_3_, ...), custom_call_target="tpu_custom_call" | custom-call | flops 1000 | bytes 1000 | tf_op jit(solution)/shard_map/near_beside/pallas_call | solution.py:374
  65.8 5.8 %collective-permute-start.12 = (f32[208,128]{1,0:T(8,128)S(1)}, f32[208,128]{1,0:T(8,128)S(1)}, u32[]{:S(2)}, u32[]{:S(2)}) collective-permute-start(f32[208,128]{1,0:T(8,128)S(1)} %tree_merge.8.refs_0_), channel_id=1, source_target_pairs={{0,16},{1,17},{2,18},{3,19},{4,20},{5,21},{6,22},{7,23},{8,24},{9,... | collective-permute-start | bytes 319496 | tf_op jit(solution)/shard_map/ppermute | solution.py:418
  71.6 5.4 %collective-permute-done.12.refs_1_ = f32[208,128]{1,0:T(8,128)S(1)} collective-permute-done((f32[208,128]{1,0:T(8,128)S(1)}, f32[208,128]{1,0:T(8,128)S(1)}, u32[]{:S(2)}, u32[]{:S(2)}) %collective-permute-start.12) | collective-permute-done | bytes 106528 | tf_op jit(solution)/shard_map/ppermute | solution.py:418
  77.0 1.7 %tree_merge.9 = f32[4,128]{1,0:T(4,128)} custom-call(f32[208,128]{1,0:T(8,128)S(1)} %tree_merge.8.refs_0_, f32[208,128]{1,0:T(8,128)S(1)} %collective-permute-done.12.refs_1_, s32[255,128]{1,0:T(8,128)S(1)} %copy-done.1), custom_call_target="tpu_custom_call" | custom-call | flops 67108864 | bytes 212992 | tf_op jit(solution)/shard_map/tree_merge/pallas_call | solution.py:251
  78.7 1.6 %add_multiply_fusion = f32[8,512,128]{2,1,0:T(8,128)} fusion(f32[8,512,128]{2,1,0:T(8,128)S(1)} %near_last.1, f32[8,512,128]{2,1,0:T(8,128)S(1)} %collective-permute-done.11), kind=kLoop, calls=%fused_computation | loop fusion | flops 1048576 | bytes 6291456 | tf_op jit(solution)/shard_map/mul | solution.py:483
  (28 shorter events, 6.3 us)
Async XLA Ops:
  0.6 1.2 %copy-start.2 = (bf16[4096,128]{1,0:T(8,128)(2,1)S(1)}, bf16[4096,128]{1,0:T(8,128)(2,1)}, u32[]{:S(2)}) copy-start(bf16[4096,128]{1,0:T(8,128)(2,1)} %probes.1) | copy-start | bytes 3145732
  1.9 1.0 %copy-start.3 = (bf16[4096,64]{0,1:T(8,128)(2,1)S(1)}, bf16[4096,64]{0,1:T(8,128)(2,1)}, u32[]{:S(2)}) copy-start(bf16[4096,64]{0,1:T(8,128)(2,1)} %param.7) | copy-start | bytes 1572868
  2.9 0.7 copy-start.5
  3.6 36.2 %copy-start.4 = (s32[8,12]{1,0:T(8,128)S(1)}, s32[8,12]{1,0:T(8,128)}, u32[]{:S(2)}) copy-start(s32[8,12]{1,0:T(8,128)} %refs_0_.3) | copy-start | bytes 1156
  6.3 25.1 %collective-permute-start.2 = (bf16[8,768,128]{2,1,0:T(8,128)(2,1)S(1)}, bf16[8,768,128]{2,1,0:T(8,128)(2,1)S(1)}, u32[]{:S(2)}, u32[]{:S(2)}) collective-permute-start(bf16[8,768,128]{2,1,0:T(8,128)(2,1)S(1)} %get-tuple-element.41.pack.refs_2_), channel_id=1, source_target_pairs={{3,1},{0,2},{7,5},{4,6},{11,9},{8,10},{15,13},{12,14},{19,17},{16,... | collective-permute-start | bytes 4718600 | tf_op jit(solution)/shard_map/ppermute | solution.py:409
  11.2 22.3 %collective-permute-start.3 = (bf16[8,768,128]{2,1,0:T(8,128)(2,1)S(1)}, bf16[8,768,128]{2,1,0:T(8,128)(2,1)S(1)}, u32[]{:S(2)}, u32[]{:S(2)}) collective-permute-start(bf16[8,768,128]{2,1,0:T(8,128)(2,1)S(1)} %get-tuple-element.41.pack.refs_2_), channel_id=1, source_target_pairs={{3,7},{7,11},{4,0},{11,15},{8,4},{15,19},{12,8},{19,23},{16,12},{2... | collective-permute-start | bytes 4718600 | tf_op jit(solution)/shard_map/ppermute | solution.py:409
  12.6 21.0 %collective-permute-start.4 = (bf16[8,768,128]{2,1,0:T(8,128)(2,1)S(1)}, bf16[8,768,128]{2,1,0:T(8,128)(2,1)S(1)}, u32[]{:S(2)}, u32[]{:S(2)}) collective-permute-start(bf16[8,768,128]{2,1,0:T(8,128)(2,1)S(1)} %get-tuple-element.41.pack.refs_2_), channel_id=1, source_target_pairs={{1,0},{2,3},{5,4},{6,7},{9,8},{10,11},{13,12},{14,15},{17,16},{18,... | collective-permute-start | bytes 4718600 | tf_op jit(solution)/shard_map/ppermute | solution.py:409
  13.8 0.9 %copy-start = (s32[255,128]{1,0:T(8,128)S(1)}, s32[255,128]{1,0:T(8,128)}, u32[]{:S(2)}) copy-start(s32[255,128]{1,0:T(8,128)} %refs_2_.9) | copy-start | bytes 391684
  14.8 0.7 copy-start.6
  22.5 2.3 %collective-permute-start = (f32[208,128]{1,0:T(8,128)S(1)}, f32[208,128]{1,0:T(8,128)S(1)}, u32[]{:S(2)}, u32[]{:S(2)}) collective-permute-start(f32[208,128]{1,0:T(8,128)S(1)} %local_tree.1.refs_0_), channel_id=1, source_target_pairs={{0,1},{1,0},{2,3},{3,2},{4,5},{5,4},{6,7},{7,6},{8,9},{9,8},{10,11... | collective-permute-start | bytes 319496 | tf_op jit(solution)/shard_map/ppermute | solution.py:418
  25.7 5.7 %collective-permute-start.1 = (f32[208,128]{1,0:T(8,128)S(1)}, f32[208,128]{1,0:T(8,128)S(1)}, u32[]{:S(2)}, u32[]{:S(2)}) collective-permute-start(f32[208,128]{1,0:T(8,128)S(1)} %tree_merge.5.refs_0_), channel_id=1, source_target_pairs={{0,2},{1,3},{2,0},{3,1},{4,6},{5,7},{6,4},{7,5},{8,10},{9,11},{10,... | collective-permute-start | bytes 319496 | tf_op jit(solution)/shard_map/ppermute | solution.py:418
  33.6 23.7 %collective-permute-start.7 = (bf16[8,768,128]{2,1,0:T(8,128)(2,1)S(1)}, bf16[8,768,128]{2,1,0:T(8,128)(2,1)S(1)}, u32[]{:S(2)}, u32[]{:S(2)}) collective-permute-start(bf16[8,768,128]{2,1,0:T(8,128)(2,1)S(1)} %collective-permute-done.2.refs_4_), channel_id=1, source_target_pairs={{1,5},{5,9},{6,2},{9,13},{10,6},{13,17},{14,10},{17,21},{18,14},{2... | collective-permute-start | bytes 4718600 | tf_op jit(solution)/shard_map/ppermute | solution.py:409
  34.3 23.0 %collective-permute-start.6 = (bf16[8,768,128]{2,1,0:T(8,128)(2,1)S(1)}, bf16[8,768,128]{2,1,0:T(8,128)(2,1)S(1)}, u32[]{:S(2)}, u32[]{:S(2)}) collective-permute-start(bf16[8,768,128]{2,1,0:T(8,128)(2,1)S(1)} %collective-permute-done.4), channel_id=1, source_target_pairs={{0,3},{3,0},{4,7},{7,4},{8,11},{11,8},{12,15},{15,12},{16,19},{19,... | collective-permute-start | bytes 4718600 | tf_op jit(solution)/shard_map/ppermute | solution.py:409
  36.3 15.5 %collective-permute-start.8 = (bf16[8,512,128]{2,1,0:T(8,128)(2,1)S(1)}, bf16[8,512,128]{2,1,0:T(8,128)(2,1)S(1)}, u32[]{:S(2)}, u32[]{:S(2)}) collective-permute-start(bf16[8,512,128]{2,1,0:T(8,128)(2,1)S(1)} %get-tuple-element.39.rows.refs_1_), channel_id=1, source_target_pairs={{0,1},{1,0},{2,3},{3,2},{4,5},{5,4},{6,7},{7,6},{8,9},{9,8},{10,11... | collective-permute-start | bytes 3145736 | tf_op jit(solution)/shard_map/ppermute | solution.py:418
  37.3 20.0 %collective-permute-start.5 = (f32[208,128]{1,0:T(8,128)S(1)}, f32[208,128]{1,0:T(8,128)S(1)}, u32[]{:S(2)}, u32[]{:S(2)}) collective-permute-start(f32[208,128]{1,0:T(8,128)S(1)} %tree_merge.6.refs_0_), channel_id=1, source_target_pairs={{0,4},{1,5},{2,6},{3,7},{4,0},{5,1},{6,2},{7,3},{8,12},{9,13},{10,... | collective-permute-start | bytes 319496 | tf_op jit(solution)/shard_map/ppermute | solution.py:418
  39.8 12.0 %collective-permute-start.9 = (s32[8,12]{1,0:T(8,128)S(1)}, s32[8,12]{1,0:T(8,128)S(1)}, u32[]{:S(2)}, u32[]{:S(2)}) collective-permute-start(s32[8,12]{1,0:T(8,128)S(1)} %copy-done.4), channel_id=1, source_target_pairs={{0,1},{1,0},{2,3},{3,2},{4,5},{5,4},{6,7},{7,6},{8,9},{9,8},{10,11... | collective-permute-start | bytes 1160 | tf_op jit(solution)/shard_map/ppermute | solution.py:418
  51.7 5.6 %copy-start.1 = (s32[255,128]{1,0:T(8,128)S(1)}, s32[255,128]{1,0:T(8,128)}, u32[]{:S(2)}) copy-start(s32[255,128]{1,0:T(8,128)} %refs_2_.9) | copy-start | bytes 391684
  58.3 4.8 %collective-permute-start.10 = (f32[208,128]{1,0:T(8,128)S(1)}, f32[208,128]{1,0:T(8,128)S(1)}, u32[]{:S(2)}, u32[]{:S(2)}) collective-permute-start(f32[208,128]{1,0:T(8,128)S(1)} %tree_merge.7.refs_0_), channel_id=1, source_target_pairs={{0,8},{1,9},{2,10},{3,11},{4,12},{5,13},{6,14},{7,15},{8,0},{9,1},... | collective-permute-start | bytes 319496 | tf_op jit(solution)/shard_map/ppermute | solution.py:418
  65.7 12.9 %collective-permute-start.11 = (f32[8,512,128]{2,1,0:T(8,128)S(1)}, f32[8,512,128]{2,1,0:T(8,128)S(1)}, u32[]{:S(2)}, u32[]{:S(2)}) collective-permute-start(f32[8,512,128]{2,1,0:T(8,128)S(1)} %near_beside.1), channel_id=1, source_target_pairs={{0,1},{1,0},{2,3},{3,2},{4,5},{5,4},{6,7},{7,6},{8,9},{9,8},{10,11... | collective-permute-start | bytes 6291464 | tf_op jit(solution)/shard_map/ppermute | solution.py:418
  65.8 11.2 %collective-permute-start.12 = (f32[208,128]{1,0:T(8,128)S(1)}, f32[208,128]{1,0:T(8,128)S(1)}, u32[]{:S(2)}, u32[]{:S(2)}) collective-permute-start(f32[208,128]{1,0:T(8,128)S(1)} %tree_merge.8.refs_0_), channel_id=1, source_target_pairs={{0,16},{1,17},{2,18},{3,19},{4,20},{5,21},{6,22},{7,23},{8,24},{9,... | collective-permute-start | bytes 319496 | tf_op jit(solution)/shard_map/ppermute | solution.py:418

commit v13 on v12

--- a/solution.py
+++ b/solution.py
@@ -473,13 +473,13 @@
     *parts, own = tie(*parts, own)
     node = level(parts, bit)
     bit += 1
-    beside, node = tie(beside, node)
+    beside, *parts = tie(beside, *exchange(node, bit, 1))
     (beside,) = near_call(
         [(1, beside_lists, beside_rows, beside)], [late_set], ((0, 0),), dim, "near_beside"
     )
     given = exchange(beside, 0, 1)[1]
-    node, beside = tie(node, beside)
-    node = level(exchange(node, bit, 1), bit, skel // count)
+    *parts, beside = tie(*parts, beside)
+    node = level(parts, bit, skel // count)
     near = (own + given) * (leaf ** -0.5)
     if skel // count:
         root = node.reshape(-1)

time: 80.6 us -> 82.9 us (1.029); the launches traced: 80.2 us -> 81.5 us
  starting transfers between devices: 23.4 us -> 19.4 us
  waiting for transfers between devices: 12.3 us -> 15.5 us
  Pallas kernels: 37.5 us -> 39.5 us
    ppermute x8, starting transfers between devices: 13.2 us -> 9.12 us  [exchange(): lax.ppermute(x, axes, [(i, i ^ d << shift) for i in range(count)])]
    ppermute x8, waiting for transfers between devices: 10.1 us -> 13 us  [exchange(): lax.ppermute(x, axes, [(i, i ^ d << shift) for i in range(count)])]
    pallas_call x4, Pallas kernels: 22.3 us -> 24.3 us  [near_call(): pl.pallas_call(functools.partial(near_kernel, flips=flips, row_counts=tup...]
  transfers between devices with their start and end apart: 13 -> 13, of which waited for: 4 -> 6; matrix products, arithmetic and copies ran while one was open for 0% -> 0% of each run, Pallas kernels for 39% -> 39%
where the time goes in v13:
time: 82.9 us; the launch traced here: 81.5 us
  Pallas kernels  39.5 us (48%)
  starting transfers between devices  19.4 us (23%)
  waiting for transfers between devices  15.5 us (19%)
  local copies, waits for them, and re-layouts  4.57 us (6%)
  other arithmetic  1.66 us (2%)
  between operations  0.85 us (1%)
    pallas_call x4, Pallas kernels, near_call(): pl.pallas_call(functools.partial(near_kernel, flips=flips, row_counts=tup...  24.3 us
    ppermute x8, waiting for transfers between devices, exchange(): lax.ppermute(x, axes, [(i, i ^ d << shift) for i in range(count)])  13 us
    ppermute x5, starting transfers between devices, send(): return lax.ppermute(x, axes, pairs)  10.2 us
    ppermute x8, starting transfers between devices, exchange(): lax.ppermute(x, axes, [(i, i ^ d << shift) for i in range(count)])  9.12 us
    pallas_call x1, Pallas kernels, local_tree_call(): pl.pallas_call(functools.partial(local_tree_kernel, dim=dim), in_specs=[p...  7.01 us
    pallas_call x5, Pallas kernels, merge_call(): pl.pallas_call(functools.partial(merge_kernel, dim=dim, blocks=blocks, sh...  5.61 us
    unnamed x14, local copies, waits for them, and re-layouts  4.57 us
    pallas_call x1, Pallas kernels, order_call(): pl.pallas_call(order_kernel, grid=(blocks // many,), in_specs=[pl.BlockSp...  2.64 us
  transfers between devices with their start and end apart: 13, of which 6 were waited for; matrix products, arithmetic and copies ran while one was open for 0% of the time, Pallas kernels for 39%

profile of v13, /device:TPU:0, one launch (start us, length us, event | category | flops | bytes accessed | tf_op | source)
XLA Modules:
  0.0 81.5 jit_solution(14898956227854024986)
XLA Ops:
  0.6 1.2 %copy-done.2 = bf16[4096,128]{1,0:T(8,128)(2,1)S(1)} copy-done((bf16[4096,128]{1,0:T(8,128)(2,1)S(1)}, bf16[4096,128]{1,0:T(8,128)(2,1)}, u32[]{:S(2)}) %copy-start.2) | copy-done | bytes 1048600
  1.9 1.0 %copy-done.3 = bf16[4096,64]{0,1:T(8,128)(2,1)S(1)} copy-done((bf16[4096,64]{0,1:T(8,128)(2,1)S(1)}, bf16[4096,64]{0,1:T(8,128)(2,1)}, u32[]{:S(2)}) %copy-start.3) | copy-done | bytes 524312
  3.6 2.6 %tree_order.1 = (bf16[8,768,128]{2,1,0:T(8,128)(2,1)S(1)}, bf16[8,512,128]{2,1,0:T(8,128)(2,1)S(1)}) custom-call(bf16[64,4096]{1,0:T(8,128)(2,1)S(1)} %bitcast.4, s32[8,1,512]{2,1,0:T(1,128)S(1)} %bitcast.5, bf16[4096,128]{1,0:T(8,128)(2,1)S(1)} %copy-done.2), custom_call_target="tpu_custom_call" | custom-call | flops 268435456 | bytes 5242880 | tf_op jit(solution)/shard_map/tree_order/pallas_call | solution.py:94
  6.3 5.0 %collective-permute-start.2 = (bf16[8,768,128]{2,1,0:T(8,128)(2,1)S(1)}, bf16[8,768,128]{2,1,0:T(8,128)(2,1)S(1)}, u32[]{:S(2)}, u32[]{:S(2)}) collective-permute-start(bf16[8,768,128]{2,1,0:T(8,128)(2,1)S(1)} %get-tuple-element.43.pack.refs_2_), channel_id=1, source_target_pairs={{3,1},{0,2},{7,5},{4,6},{11,9},{8,10},{15,13},{12,14},{19,17},{16,... | collective-permute-start | bytes 4718600 | tf_op jit(solution)/shard_map/ppermute | solution.py:409
  11.2 1.3 %collective-permute-start.3 = (bf16[8,768,128]{2,1,0:T(8,128)(2,1)S(1)}, bf16[8,768,128]{2,1,0:T(8,128)(2,1)S(1)}, u32[]{:S(2)}, u32[]{:S(2)}) collective-permute-start(bf16[8,768,128]{2,1,0:T(8,128)(2,1)S(1)} %get-tuple-element.43.pack.refs_2_), channel_id=1, source_target_pairs={{3,7},{7,11},{4,0},{11,15},{8,4},{15,19},{12,8},{19,23},{16,12},{2... | collective-permute-start | bytes 4718600 | tf_op jit(solution)/shard_map/ppermute | solution.py:409
  12.6 1.3 %collective-permute-start.4 = (bf16[8,768,128]{2,1,0:T(8,128)(2,1)S(1)}, bf16[8,768,128]{2,1,0:T(8,128)(2,1)S(1)}, u32[]{:S(2)}, u32[]{:S(2)}) collective-permute-start(bf16[8,768,128]{2,1,0:T(8,128)(2,1)S(1)} %get-tuple-element.43.pack.refs_2_), channel_id=1, source_target_pairs={{1,0},{2,3},{5,4},{6,7},{9,8},{10,11},{13,12},{14,15},{17,16},{18,... | collective-permute-start | bytes 4718600 | tf_op jit(solution)/shard_map/ppermute | solution.py:409
  15.4 7.0 %local_tree.1.refs_0_ = f32[208,128]{1,0:T(8,128)S(1)} custom-call(bf16[8,768,128]{2,1,0:T(8,128)(2,1)S(1)} %get-tuple-element.43.pack.refs_2_, bf16[8,512,128]{2,1,0:T(8,128)(2,1)S(1)} %get-tuple-element.41.rows.refs_1_, s32[8,128]{1,0:T(8,128)S(1)} %copy-done.6, s32[255,128]{1,0:T(8,128)S(1)} %copy-done), custom_call_target="tpu_custom_call" | custom-call | flops 536870912 | bytes 3145728 | tf_op jit(solution)/shard_map/local_tree/pallas_call | solution.py:177
  22.5 1.3 %collective-permute-start = (f32[208,128]{1,0:T(8,128)S(1)}, f32[208,128]{1,0:T(8,128)S(1)}, u32[]{:S(2)}, u32[]{:S(2)}) collective-permute-start(f32[208,128]{1,0:T(8,128)S(1)} %local_tree.1.refs_0_), channel_id=1, source_target_pairs={{0,1},{1,0},{2,3},{3,2},{4,5},{5,4},{6,7},{7,6},{8,9},{9,8},{10,11... | collective-permute-start | bytes 319496 | tf_op jit(solution)/shard_map/ppermute | solution.py:418
  25.7 1.9 %collective-permute-start.1 = (f32[208,128]{1,0:T(8,128)S(1)}, f32[208,128]{1,0:T(8,128)S(1)}, u32[]{:S(2)}, u32[]{:S(2)}) collective-permute-start(f32[208,128]{1,0:T(8,128)S(1)} %tree_merge.5.refs_0_), channel_id=1, source_target_pairs={{0,2},{1,3},{2,0},{3,1},{4,6},{5,7},{6,4},{7,5},{8,10},{9,11},{10,... | collective-permute-start | bytes 319496 | tf_op jit(solution)/shard_map/ppermute | solution.py:418
  27.6 3.8 %collective-permute-done.1.refs_1_ = f32[208,128]{1,0:T(8,128)S(1)} collective-permute-done((f32[208,128]{1,0:T(8,128)S(1)}, f32[208,128]{1,0:T(8,128)S(1)}, u32[]{:S(2)}, u32[]{:S(2)}) %collective-permute-start.1) | collective-permute-done | bytes 106528 | tf_op jit(solution)/shard_map/ppermute | solution.py:418
  31.4 2.2 %collective-permute-done.3.refs_3_ = bf16[8,768,128]{2,1,0:T(8,128)(2,1)S(1)} collective-permute-done((bf16[8,768,128]{2,1,0:T(8,128)(2,1)S(1)}, bf16[8,768,128]{2,1,0:T(8,128)(2,1)S(1)}, u32[]{:S(2)}, u32[]{:S(2)}) %collective-permute-start.3) | collective-permute-done | bytes 1572896 | tf_op jit(solution)/shard_map/ppermute | solution.py:409
  34.3 1.9 %collective-permute-start.6 = (bf16[8,768,128]{2,1,0:T(8,128)(2,1)S(1)}, bf16[8,768,128]{2,1,0:T(8,128)(2,1)S(1)}, u32[]{:S(2)}, u32[]{:S(2)}) collective-permute-start(bf16[8,768,128]{2,1,0:T(8,128)(2,1)S(1)} %collective-permute-done.4), channel_id=1, source_target_pairs={{0,3},{3,0},{4,7},{7,4},{8,11},{11,8},{12,15},{15,12},{16,19},{19,... | collective-permute-start | bytes 4718600 | tf_op jit(solution)/shard_map/ppermute | solution.py:409
  36.3 1.0 %tree_merge.6.refs_0_ = f32[208,128]{1,0:T(8,128)S(1)} custom-call(f32[208,128]{1,0:T(8,128)S(1)} %tree_merge.5.refs_0_, f32[208,128]{1,0:T(8,128)S(1)} %collective-permute-done.1.refs_1_, s32[255,128]{1,0:T(8,128)S(1)} %copy-done), custom_call_target="tpu_custom_call" | custom-call | flops 67108864 | bytes 212992 | tf_op jit(solution)/shard_map/tree_merge/pallas_call | solution.py:251
  37.3 2.5 %collective-permute-start.5 = (f32[208,128]{1,0:T(8,128)S(1)}, f32[208,128]{1,0:T(8,128)S(1)}, u32[]{:S(2)}, u32[]{:S(2)}) collective-permute-start(f32[208,128]{1,0:T(8,128)S(1)} %tree_merge.6.refs_0_), channel_id=1, source_target_pairs={{0,4},{1,5},{2,6},{3,7},{4,0},{5,1},{6,2},{7,3},{8,12},{9,13},{10,... | collective-permute-start | bytes 319496 | tf_op jit(solution)/shard_map/ppermute | solution.py:418
  40.0 9.9 %near_own.1.refs_2_ = f32[8,512,128]{2,1,0:T(8,128)S(1)} custom-call(s32[8,12]{1,0:T(8,128)S(1)} %copy-done.4, bf16[8,512,128]{2,1,0:T(8,128)(2,1)S(1)} %get-tuple-element.41.rows.refs_1_, bf16[8,768,128]{2,1,0:T(8,128)(2,1)S(1)} %get-tuple-element.43.pack.refs_2_, bf16[8,768,128]{2,1,0:T(8,128)(2,1)S(1)} %collective-permute-done.3.refs_3_, ...), custom_call_target="tpu_custom_call" | custom-call | flops 1000 | bytes 1000 | tf_op jit(solution)/shard_map/near_own/pallas_call | solution.py:374
  49.9 5.8 %near_early.1.refs_2_ = f32[8,512,128]{2,1,0:T(8,128)S(1)} custom-call(s32[8,12]{1,0:T(8,128)S(1)} %collective-permute-done.9.refs_0_, bf16[8,512,128]{2,1,0:T(8,128)(2,1)S(1)} %collective-permute-done.8.refs_1_, bf16[8,768,128]{2,1,0:T(8,128)(2,1)S(1)} %get-tuple-element.43.pack.refs_2_, bf16[8,768,128]{2,1,0:T(8,128)(2,1)S(1)} %collective-permute-done.3.refs_3_, ...), custom_call_target="tpu_custom_call" | custom-call | flops 1000 | bytes 1000 | tf_op jit(solution)/shard_map/near_early/pallas_call | solution.py:374
  57.0 2.7 %collective-permute-start.10 = (f32[208,128]{1,0:T(8,128)S(1)}, f32[208,128]{1,0:T(8,128)S(1)}, u32[]{:S(2)}, u32[]{:S(2)}) collective-permute-start(f32[208,128]{1,0:T(8,128)S(1)} %tree_merge.7.refs_0_), channel_id=1, source_target_pairs={{0,8},{1,9},{2,10},{3,11},{4,12},{5,13},{6,14},{7,15},{8,0},{9,1},... | collective-permute-start | bytes 319496 | tf_op jit(solution)/shard_map/ppermute | solution.py:418
  59.7 5.5 %near_last.1 = f32[8,512,128]{2,1,0:T(8,128)S(1)} custom-call(s32[8,12]{1,0:T(8,128)S(1)} %copy-done.4, bf16[8,512,128]{2,1,0:T(8,128)(2,1)S(1)} %get-tuple-element.41.rows.refs_1_, f32[8,512,128]{2,1,0:T(8,128)S(1)} %near_own.1.refs_2_, bf16[8,768,128]{2,1,0:T(8,128)(2,1)S(1)} %collective-permute-done.6.refs_3_, ...), custom_call_target="tpu_custom_call" | custom-call | flops 1000 | bytes 1000 | tf_op jit(solution)/shard_map/near_last/pallas_call | solution.py:374
  65.2 1.0 %tree_merge.8.refs_0_ = f32[208,128]{1,0:T(8,128)S(1)} custom-call(f32[208,128]{1,0:T(8,128)S(1)} %tree_merge.7.refs_0_, f32[208,128]{1,0:T(8,128)S(1)} %collective-permute-done.10.refs_1_, s32[255,128]{1,0:T(8,128)S(1)} %copy-done.1), custom_call_target="tpu_custom_call" | custom-call | flops 67108864 | bytes 212992 | tf_op jit(solution)/shard_map/tree_merge/pallas_call | solution.py:251
  66.7 5.8 %collective-permute-done.11.refs_1_ = f32[208,128]{1,0:T(8,128)S(1)} collective-permute-done((f32[208,128]{1,0:T(8,128)S(1)}, f32[208,128]{1,0:T(8,128)S(1)}, u32[]{:S(2)}, u32[]{:S(2)}) %collective-permute-start.11) | collective-permute-done | bytes 106528 | tf_op jit(solution)/shard_map/ppermute | solution.py:418
  72.5 3.1 %near_beside.1 = f32[8,512,128]{2,1,0:T(8,128)S(1)} custom-call(s32[8,12]{1,0:T(8,128)S(1)} %collective-permute-done.9.refs_0_, bf16[8,512,128]{2,1,0:T(8,128)(2,1)S(1)} %collective-permute-done.8.refs_1_, f32[8,512,128]{2,1,0:T(8,128)S(1)} %near_early.1.refs_2_, bf16[8,768,128]{2,1,0:T(8,128)(2,1)S(1)} %collective-permute-done.6.refs_3_, ...), custom_call_target="tpu_custom_call" | custom-call | flops 1000 | bytes 1000 | tf_op jit(solution)/shard_map/near_beside/pallas_call | solution.py:374
  75.7 1.7 %tree_merge.9 = f32[4,128]{1,0:T(4,128)} custom-call(f32[208,128]{1,0:T(8,128)S(1)} %tree_merge.8.refs_0_, f32[208,128]{1,0:T(8,128)S(1)} %collective-permute-done.11.refs_1_, s32[255,128]{1,0:T(8,128)S(1)} %copy-done.1), custom_call_target="tpu_custom_call" | custom-call | flops 67108864 | bytes 212992 | tf_op jit(solution)/shard_map/tree_merge/pallas_call | solution.py:251
  77.4 2.4 %collective-permute-done.12 = f32[8,512,128]{2,1,0:T(8,128)S(1)} collective-permute-done((f32[8,512,128]{2,1,0:T(8,128)S(1)}, f32[8,512,128]{2,1,0:T(8,128)S(1)}, u32[]{:S(2)}, u32[]{:S(2)}) %collective-permute-start.12) | collective-permute-done | bytes 2097184 | tf_op jit(solution)/shard_map/ppermute | solution.py:418
  79.8 1.7 %add_multiply_fusion = f32[8,512,128]{2,1,0:T(8,128)} fusion(f32[8,512,128]{2,1,0:T(8,128)S(1)} %near_last.1, f32[8,512,128]{2,1,0:T(8,128)S(1)} %collective-permute-done.12), kind=kLoop, calls=%fused_computation | loop fusion | flops 1048576 | bytes 6291456 | tf_op jit(solution)/shard_map/mul | solution.py:483
  (28 shorter events, 7.1 us)
Async XLA Ops:
  0.6 1.2 %copy-start.2 = (bf16[4096,128]{1,0:T(8,128)(2,1)S(1)}, bf16[4096,128]{1,0:T(8,128)(2,1)}, u32[]{:S(2)}) copy-start(bf16[4096,128]{1,0:T(8,128)(2,1)} %probes.1) | copy-start | bytes 3145732
  1.9 1.0 %copy-start.3 = (bf16[4096,64]{0,1:T(8,128)(2,1)S(1)}, bf16[4096,64]{0,1:T(8,128)(2,1)}, u32[]{:S(2)}) copy-start(bf16[4096,64]{0,1:T(8,128)(2,1)} %param.7) | copy-start | bytes 1572868
  2.9 0.7 copy-start.5
  3.6 36.2 %copy-start.4 = (s32[8,12]{1,0:T(8,128)S(1)}, s32[8,12]{1,0:T(8,128)}, u32[]{:S(2)}) copy-start(s32[8,12]{1,0:T(8,128)} %refs_0_.3) | copy-start | bytes 1156
  6.3 25.1 %collective-permute-start.2 = (bf16[8,768,128]{2,1,0:T(8,128)(2,1)S(1)}, bf16[8,768,128]{2,1,0:T(8,128)(2,1)S(1)}, u32[]{:S(2)}, u32[]{:S(2)}) collective-permute-start(bf16[8,768,128]{2,1,0:T(8,128)(2,1)S(1)} %get-tuple-element.43.pack.refs_2_), channel_id=1, source_target_pairs={{3,1},{0,2},{7,5},{4,6},{11,9},{8,10},{15,13},{12,14},{19,17},{16,... | collective-permute-start | bytes 4718600 | tf_op jit(solution)/shard_map/ppermute | solution.py:409
  11.2 22.3 %collective-permute-start.3 = (bf16[8,768,128]{2,1,0:T(8,128)(2,1)S(1)}, bf16[8,768,128]{2,1,0:T(8,128)(2,1)S(1)}, u32[]{:S(2)}, u32[]{:S(2)}) collective-permute-start(bf16[8,768,128]{2,1,0:T(8,128)(2,1)S(1)} %get-tuple-element.43.pack.refs_2_), channel_id=1, source_target_pairs={{3,7},{7,11},{4,0},{11,15},{8,4},{15,19},{12,8},{19,23},{16,12},{2... | collective-permute-start | bytes 4718600 | tf_op jit(solution)/shard_map/ppermute | solution.py:409
  12.6 21.0 %collective-permute-start.4 = (bf16[8,768,128]{2,1,0:T(8,128)(2,1)S(1)}, bf16[8,768,128]{2,1,0:T(8,128)(2,1)S(1)}, u32[]{:S(2)}, u32[]{:S(2)}) collective-permute-start(bf16[8,768,128]{2,1,0:T(8,128)(2,1)S(1)} %get-tuple-element.43.pack.refs_2_), channel_id=1, source_target_pairs={{1,0},{2,3},{5,4},{6,7},{9,8},{10,11},{13,12},{14,15},{17,16},{18,... | collective-permute-start | bytes 4718600 | tf_op jit(solution)/shard_map/ppermute | solution.py:409
  13.8 0.9 %copy-start = (s32[255,128]{1,0:T(8,128)S(1)}, s32[255,128]{1,0:T(8,128)}, u32[]{:S(2)}) copy-start(s32[255,128]{1,0:T(8,128)} %refs_2_.9) | copy-start | bytes 391684
  14.8 0.7 copy-start.6
  22.5 2.3 %collective-permute-start = (f32[208,128]{1,0:T(8,128)S(1)}, f32[208,128]{1,0:T(8,128)S(1)}, u32[]{:S(2)}, u32[]{:S(2)}) collective-permute-start(f32[208,128]{1,0:T(8,128)S(1)} %local_tree.1.refs_0_), channel_id=1, source_target_pairs={{0,1},{1,0},{2,3},{3,2},{4,5},{5,4},{6,7},{7,6},{8,9},{9,8},{10,11... | collective-permute-start | bytes 319496 | tf_op jit(solution)/shard_map/ppermute | solution.py:418
  25.7 5.7 %collective-permute-start.1 = (f32[208,128]{1,0:T(8,128)S(1)}, f32[208,128]{1,0:T(8,128)S(1)}, u32[]{:S(2)}, u32[]{:S(2)}) collective-permute-start(f32[208,128]{1,0:T(8,128)S(1)} %tree_merge.5.refs_0_), channel_id=1, source_target_pairs={{0,2},{1,3},{2,0},{3,1},{4,6},{5,7},{6,4},{7,5},{8,10},{9,11},{10,... | collective-permute-start | bytes 319496 | tf_op jit(solution)/shard_map/ppermute | solution.py:418
  33.6 22.1 %collective-permute-start.7 = (bf16[8,768,128]{2,1,0:T(8,128)(2,1)S(1)}, bf16[8,768,128]{2,1,0:T(8,128)(2,1)S(1)}, u32[]{:S(2)}, u32[]{:S(2)}) collective-permute-start(bf16[8,768,128]{2,1,0:T(8,128)(2,1)S(1)} %collective-permute-done.2.refs_4_), channel_id=1, source_target_pairs={{1,5},{5,9},{6,2},{9,13},{10,6},{13,17},{14,10},{17,21},{18,14},{2... | collective-permute-start | bytes 4718600 | tf_op jit(solution)/shard_map/ppermute | solution.py:409
  34.3 21.7 %collective-permute-start.6 = (bf16[8,768,128]{2,1,0:T(8,128)(2,1)S(1)}, bf16[8,768,128]{2,1,0:T(8,128)(2,1)S(1)}, u32[]{:S(2)}, u32[]{:S(2)}) collective-permute-start(bf16[8,768,128]{2,1,0:T(8,128)(2,1)S(1)} %collective-permute-done.4), channel_id=1, source_target_pairs={{0,3},{3,0},{4,7},{7,4},{8,11},{11,8},{12,15},{15,12},{16,19},{19,... | collective-permute-start | bytes 4718600 | tf_op jit(solution)/shard_map/ppermute | solution.py:409
  36.3 13.6 %collective-permute-start.8 = (bf16[8,512,128]{2,1,0:T(8,128)(2,1)S(1)}, bf16[8,512,128]{2,1,0:T(8,128)(2,1)S(1)}, u32[]{:S(2)}, u32[]{:S(2)}) collective-permute-start(bf16[8,512,128]{2,1,0:T(8,128)(2,1)S(1)} %get-tuple-element.41.rows.refs_1_), channel_id=1, source_target_pairs={{0,1},{1,0},{2,3},{3,2},{4,5},{5,4},{6,7},{7,6},{8,9},{9,8},{10,11... | collective-permute-start | bytes 3145736 | tf_op jit(solution)/shard_map/ppermute | solution.py:418
  37.3 18.4 %collective-permute-start.5 = (f32[208,128]{1,0:T(8,128)S(1)}, f32[208,128]{1,0:T(8,128)S(1)}, u32[]{:S(2)}, u32[]{:S(2)}) collective-permute-start(f32[208,128]{1,0:T(8,128)S(1)} %tree_merge.6.refs_0_), channel_id=1, source_target_pairs={{0,4},{1,5},{2,6},{3,7},{4,0},{5,1},{6,2},{7,3},{8,12},{9,13},{10,... | collective-permute-start | bytes 319496 | tf_op jit(solution)/shard_map/ppermute | solution.py:418
  39.8 10.1 %collective-permute-start.9 = (s32[8,12]{1,0:T(8,128)S(1)}, s32[8,12]{1,0:T(8,128)S(1)}, u32[]{:S(2)}, u32[]{:S(2)}) collective-permute-start(s32[8,12]{1,0:T(8,128)S(1)} %copy-done.4), channel_id=1, source_target_pairs={{0,1},{1,0},{2,3},{3,2},{4,5},{5,4},{6,7},{7,6},{8,9},{9,8},{10,11... | collective-permute-start | bytes 1160 | tf_op jit(solution)/shard_map/ppermute | solution.py:418
  49.9 6.2 %copy-start.1 = (s32[255,128]{1,0:T(8,128)S(1)}, s32[255,128]{1,0:T(8,128)}, u32[]{:S(2)}) copy-start(s32[255,128]{1,0:T(8,128)} %refs_2_.9) | copy-start | bytes 391684
  57.0 8.2 %collective-permute-start.10 = (f32[208,128]{1,0:T(8,128)S(1)}, f32[208,128]{1,0:T(8,128)S(1)}, u32[]{:S(2)}, u32[]{:S(2)}) collective-permute-start(f32[208,128]{1,0:T(8,128)S(1)} %tree_merge.7.refs_0_), channel_id=1, source_target_pairs={{0,8},{1,9},{2,10},{3,11},{4,12},{5,13},{6,14},{7,15},{8,0},{9,1},... | collective-permute-start | bytes 319496 | tf_op jit(solution)/shard_map/ppermute | solution.py:418
  66.2 6.3 %collective-permute-start.11 = (f32[208,128]{1,0:T(8,128)S(1)}, f32[208,128]{1,0:T(8,128)S(1)}, u32[]{:S(2)}, u32[]{:S(2)}) collective-permute-start(f32[208,128]{1,0:T(8,128)S(1)} %tree_merge.8.refs_0_), channel_id=1, source_target_pairs={{0,16},{1,17},{2,18},{3,19},{4,20},{5,21},{6,22},{7,23},{8,24},{9,... | collective-permute-start | bytes 319496 | tf_op jit(solution)/shard_map/ppermute | solution.py:418
  75.6 4.2 %collective-permute-start.12 = (f32[8,512,128]{2,1,0:T(8,128)S(1)}, f32[8,512,128]{2,1,0:T(8,128)S(1)}, u32[]{:S(2)}, u32[]{:S(2)}) collective-permute-start(f32[8,512,128]{2,1,0:T(8,128)S(1)} %near_beside.1), channel_id=1, source_target_pairs={{0,1},{1,0},{2,3},{3,2},{4,5},{5,4},{6,7},{7,6},{8,9},{9,8},{10,11... | collective-permute-start | bytes 6291464 | tf_op jit(solution)/shard_map/ppermute | solution.py:418

commit v14 on v13

--- a/solution.py
+++ b/solution.py
@@ -473,12 +473,13 @@
     *parts, own = tie(*parts, own)
     node = level(parts, bit)
     bit += 1
-    beside, *parts = tie(beside, *exchange(node, bit, 1))
+    beside, node = tie(beside, node)
+    parts = exchange(node, bit, 1)
     (beside,) = near_call(
         [(1, beside_lists, beside_rows, beside)], [late_set], ((0, 0),), dim, "near_beside"
     )
+    *parts, beside = tie(*parts, beside)
     given = exchange(beside, 0, 1)[1]
-    *parts, beside = tie(*parts, beside)
     node = level(parts, bit, skel // count)
     near = (own + given) * (leaf ** -0.5)
     if skel // count:

time: 82.9 us -> 78.6 us (0.948); the launches traced: 81.5 us -> 78.3 us
  waiting for transfers between devices: 15.5 us -> 11.8 us
  Pallas kernels: 39.5 us -> 41 us
  starting transfers between devices: 19.4 us -> 18.5 us
    ppermute x8, waiting for transfers between devices: 13 us -> 9.54 us  [exchange(): lax.ppermute(x, axes, [(i, i ^ d << shift) for i in range(count)])]
    pallas_call x4, Pallas kernels: 24.3 us -> 25.7 us  [near_call(): pl.pallas_call(functools.partial(near_kernel, flips=flips, row_counts=tup...]
    ppermute x8, starting transfers between devices: 9.12 us -> 8.23 us  [exchange(): lax.ppermute(x, axes, [(i, i ^ d << shift) for i in range(count)])]
  transfers between devices with their start and end apart: 13 -> 13, of which waited for: 6 -> 5; matrix products, arithmetic and copies ran while one was open for 0% -> 0% of each run, Pallas kernels for 39% -> 46%
where the time goes in v14:
time: 78.6 us; the launch traced here: 78.3 us
  Pallas kernels  41 us (52%)
  starting transfers between devices  18.5 us (24%)
  waiting for transfers between devices  11.8 us (15%)
  local copies, waits for them, and re-layouts  4.57 us (6%)
  other arithmetic  1.66 us (2%)
  between operations  0.86 us (1%)
    pallas_call x4, Pallas kernels, near_call(): pl.pallas_call(functools.partial(near_kernel, flips=flips, row_counts=tup...  25.7 us
    ppermute x5, starting transfers between devices, send(): return lax.ppermute(x, axes, pairs)  10.2 us
    ppermute x8, waiting for transfers between devices, exchange(): lax.ppermute(x, axes, [(i, i ^ d << shift) for i in range(count)])  9.54 us
    ppermute x8, starting transfers between devices, exchange(): lax.ppermute(x, axes, [(i, i ^ d << shift) for i in range(count)])  8.23 us
    pallas_call x1, Pallas kernels, local_tree_call(): pl.pallas_call(functools.partial(local_tree_kernel, dim=dim), in_specs=[p...  7.01 us
    pallas_call x5, Pallas kernels, merge_call(): pl.pallas_call(functools.partial(merge_kernel, dim=dim, blocks=blocks, sh...  5.62 us
    unnamed x14, local copies, waits for them, and re-layouts  4.57 us
    pallas_call x1, Pallas kernels, order_call(): pl.pallas_call(order_kernel, grid=(blocks // many,), in_specs=[pl.BlockSp...  2.64 us
  transfers between devices with their start and end apart: 13, of which 5 were waited for; matrix products, arithmetic and copies ran while one was open for 0% of the time, Pallas kernels for 46%

profile of v14, /device:TPU:0, one launch (start us, length us, event | category | flops | bytes accessed | tf_op | source)
XLA Modules:
  0.0 78.3 jit_solution(10349660214332578209)
XLA Ops:
  0.6 1.2 %copy-done.2 = bf16[4096,128]{1,0:T(8,128)(2,1)S(1)} copy-done((bf16[4096,128]{1,0:T(8,128)(2,1)S(1)}, bf16[4096,128]{1,0:T(8,128)(2,1)}, u32[]{:S(2)}) %copy-start.2) | copy-done | bytes 1048600
  1.9 1.0 %copy-done.3 = bf16[4096,64]{0,1:T(8,128)(2,1)S(1)} copy-done((bf16[4096,64]{0,1:T(8,128)(2,1)S(1)}, bf16[4096,64]{0,1:T(8,128)(2,1)}, u32[]{:S(2)}) %copy-start.3) | copy-done | bytes 524312
  3.6 2.6 %tree_order.1 = (bf16[8,768,128]{2,1,0:T(8,128)(2,1)S(1)}, bf16[8,512,128]{2,1,0:T(8,128)(2,1)S(1)}) custom-call(bf16[64,4096]{1,0:T(8,128)(2,1)S(1)} %bitcast.4, s32[8,1,512]{2,1,0:T(1,128)S(1)} %bitcast.5, bf16[4096,128]{1,0:T(8,128)(2,1)S(1)} %copy-done.2), custom_call_target="tpu_custom_call" | custom-call | flops 268435456 | bytes 5242880 | tf_op jit(solution)/shard_map/tree_order/pallas_call | solution.py:94
  6.3 5.0 %collective-permute-start.2 = (bf16[8,768,128]{2,1,0:T(8,128)(2,1)S(1)}, bf16[8,768,128]{2,1,0:T(8,128)(2,1)S(1)}, u32[]{:S(2)}, u32[]{:S(2)}) collective-permute-start(bf16[8,768,128]{2,1,0:T(8,128)(2,1)S(1)} %get-tuple-element.43.pack.refs_2_), channel_id=1, source_target_pairs={{3,1},{0,2},{7,5},{4,6},{11,9},{8,10},{15,13},{12,14},{19,17},{16,... | collective-permute-start | bytes 4718600 | tf_op jit(solution)/shard_map/ppermute | solution.py:409
  11.2 1.3 %collective-permute-start.3 = (bf16[8,768,128]{2,1,0:T(8,128)(2,1)S(1)}, bf16[8,768,128]{2,1,0:T(8,128)(2,1)S(1)}, u32[]{:S(2)}, u32[]{:S(2)}) collective-permute-start(bf16[8,768,128]{2,1,0:T(8,128)(2,1)S(1)} %get-tuple-element.43.pack.refs_2_), channel_id=1, source_target_pairs={{3,7},{7,11},{4,0},{11,15},{8,4},{15,19},{12,8},{19,23},{16,12},{2... | collective-permute-start | bytes 4718600 | tf_op jit(solution)/shard_map/ppermute | solution.py:409
  12.6 1.3 %collective-permute-start.4 = (bf16[8,768,128]{2,1,0:T(8,128)(2,1)S(1)}, bf16[8,768,128]{2,1,0:T(8,128)(2,1)S(1)}, u32[]{:S(2)}, u32[]{:S(2)}) collective-permute-start(bf16[8,768,128]{2,1,0:T(8,128)(2,1)S(1)} %get-tuple-element.43.pack.refs_2_), channel_id=1, source_target_pairs={{1,0},{2,3},{5,4},{6,7},{9,8},{10,11},{13,12},{14,15},{17,16},{18,... | collective-permute-start | bytes 4718600 | tf_op jit(solution)/shard_map/ppermute | solution.py:409
  15.4 7.0 %local_tree.1.refs_0_ = f32[208,128]{1,0:T(8,128)S(1)} custom-call(bf16[8,768,128]{2,1,0:T(8,128)(2,1)S(1)} %get-tuple-element.43.pack.refs_2_, bf16[8,512,128]{2,1,0:T(8,128)(2,1)S(1)} %get-tuple-element.41.rows.refs_1_, s32[8,128]{1,0:T(8,128)S(1)} %copy-done.6, s32[255,128]{1,0:T(8,128)S(1)} %copy-done), custom_call_target="tpu_custom_call" | custom-call | flops 536870912 | bytes 3145728 | tf_op jit(solution)/shard_map/local_tree/pallas_call | solution.py:177
  22.5 1.3 %collective-permute-start = (f32[208,128]{1,0:T(8,128)S(1)}, f32[208,128]{1,0:T(8,128)S(1)}, u32[]{:S(2)}, u32[]{:S(2)}) collective-permute-start(f32[208,128]{1,0:T(8,128)S(1)} %local_tree.1.refs_0_), channel_id=1, source_target_pairs={{0,1},{1,0},{2,3},{3,2},{4,5},{5,4},{6,7},{7,6},{8,9},{9,8},{10,11... | collective-permute-start | bytes 319496 | tf_op jit(solution)/shard_map/ppermute | solution.py:418
  25.7 1.9 %collective-permute-start.1 = (f32[208,128]{1,0:T(8,128)S(1)}, f32[208,128]{1,0:T(8,128)S(1)}, u32[]{:S(2)}, u32[]{:S(2)}) collective-permute-start(f32[208,128]{1,0:T(8,128)S(1)} %tree_merge.5.refs_0_), channel_id=1, source_target_pairs={{0,2},{1,3},{2,0},{3,1},{4,6},{5,7},{6,4},{7,5},{8,10},{9,11},{10,... | collective-permute-start | bytes 319496 | tf_op jit(solution)/shard_map/ppermute | solution.py:418
  27.6 3.8 %collective-permute-done.1.refs_1_ = f32[208,128]{1,0:T(8,128)S(1)} collective-permute-done((f32[208,128]{1,0:T(8,128)S(1)}, f32[208,128]{1,0:T(8,128)S(1)}, u32[]{:S(2)}, u32[]{:S(2)}) %collective-permute-start.1) | collective-permute-done | bytes 106528 | tf_op jit(solution)/shard_map/ppermute | solution.py:418
  31.4 2.2 %collective-permute-done.3.refs_3_ = bf16[8,768,128]{2,1,0:T(8,128)(2,1)S(1)} collective-permute-done((bf16[8,768,128]{2,1,0:T(8,128)(2,1)S(1)}, bf16[8,768,128]{2,1,0:T(8,128)(2,1)S(1)}, u32[]{:S(2)}, u32[]{:S(2)}) %collective-permute-start.3) | collective-permute-done | bytes 1572896 | tf_op jit(solution)/shard_map/ppermute | solution.py:409
  34.3 1.9 %collective-permute-start.6 = (bf16[8,768,128]{2,1,0:T(8,128)(2,1)S(1)}, bf16[8,768,128]{2,1,0:T(8,128)(2,1)S(1)}, u32[]{:S(2)}, u32[]{:S(2)}) collective-permute-start(bf16[8,768,128]{2,1,0:T(8,128)(2,1)S(1)} %collective-permute-done.4), channel_id=1, source_target_pairs={{0,3},{3,0},{4,7},{7,4},{8,11},{11,8},{12,15},{15,12},{16,19},{19,... | collective-permute-start | bytes 4718600 | tf_op jit(solution)/shard_map/ppermute | solution.py:409
  37.3 2.5 %collective-permute-start.5 = (f32[208,128]{1,0:T(8,128)S(1)}, f32[208,128]{1,0:T(8,128)S(1)}, u32[]{:S(2)}, u32[]{:S(2)}) collective-permute-start(f32[208,128]{1,0:T(8,128)S(1)} %tree_merge.6.refs_0_), channel_id=1, source_target_pairs={{0,4},{1,5},{2,6},{3,7},{4,0},{5,1},{6,2},{7,3},{8,12},{9,13},{10,... | collective-permute-start | bytes 319496 | tf_op jit(solution)/shard_map/ppermute | solution.py:418
  40.0 12.0 %near_own.1.refs_2_ = f32[8,512,128]{2,1,0:T(8,128)S(1)} custom-call(s32[8,12]{1,0:T(8,128)S(1)} %copy-done.4, bf16[8,512,128]{2,1,0:T(8,128)(2,1)S(1)} %get-tuple-element.41.rows.refs_1_, bf16[8,768,128]{2,1,0:T(8,128)(2,1)S(1)} %get-tuple-element.43.pack.refs_2_, bf16[8,768,128]{2,1,0:T(8,128)(2,1)S(1)} %collective-permute-done.3.refs_3_, ...), custom_call_target="tpu_custom_call" | custom-call | flops 1000 | bytes 1000 | tf_op jit(solution)/shard_map/near_own/pallas_call | solution.py:374
  52.0 6.5 %near_early.1.refs_2_ = f32[8,512,128]{2,1,0:T(8,128)S(1)} custom-call(s32[8,12]{1,0:T(8,128)S(1)} %collective-permute-done.9.refs_0_, bf16[8,512,128]{2,1,0:T(8,128)(2,1)S(1)} %collective-permute-done.8.refs_1_, bf16[8,768,128]{2,1,0:T(8,128)(2,1)S(1)} %get-tuple-element.43.pack.refs_2_, bf16[8,768,128]{2,1,0:T(8,128)(2,1)S(1)} %collective-permute-done.3.refs_3_, ...), custom_call_target="tpu_custom_call" | custom-call | flops 1000 | bytes 1000 | tf_op jit(solution)/shard_map/near_early/pallas_call | solution.py:374
  58.6 1.0 %tree_merge.7.refs_0_ = f32[208,128]{1,0:T(8,128)S(1)} custom-call(f32[208,128]{1,0:T(8,128)S(1)} %tree_merge.6.refs_0_, f32[208,128]{1,0:T(8,128)S(1)} %collective-permute-done.5.refs_1_, s32[255,128]{1,0:T(8,128)S(1)} %copy-done.1), custom_call_target="tpu_custom_call" | custom-call | flops 67108864 | bytes 212992 | tf_op jit(solution)/shard_map/tree_merge/pallas_call | solution.py:251
  59.6 1.2 %collective-permute-start.10 = (f32[208,128]{1,0:T(8,128)S(1)}, f32[208,128]{1,0:T(8,128)S(1)}, u32[]{:S(2)}, u32[]{:S(2)}) collective-permute-start(f32[208,128]{1,0:T(8,128)S(1)} %tree_merge.7.refs_0_), channel_id=1, source_target_pairs={{0,8},{1,9},{2,10},{3,11},{4,12},{5,13},{6,14},{7,15},{8,0},{9,1},... | collective-permute-start | bytes 319496 | tf_op jit(solution)/shard_map/ppermute | solution.py:418
  60.8 3.8 %near_last.1 = f32[8,512,128]{2,1,0:T(8,128)S(1)} custom-call(s32[8,12]{1,0:T(8,128)S(1)} %copy-done.4, bf16[8,512,128]{2,1,0:T(8,128)(2,1)S(1)} %get-tuple-element.41.rows.refs_1_, f32[8,512,128]{2,1,0:T(8,128)S(1)} %near_own.1.refs_2_, bf16[8,768,128]{2,1,0:T(8,128)(2,1)S(1)} %collective-permute-done.6.refs_3_, ...), custom_call_target="tpu_custom_call" | custom-call | flops 1000 | bytes 1000 | tf_op jit(solution)/shard_map/near_last/pallas_call | solution.py:374
  65.6 1.1 %collective-permute-start.11 = (f32[208,128]{1,0:T(8,128)S(1)}, f32[208,128]{1,0:T(8,128)S(1)}, u32[]{:S(2)}, u32[]{:S(2)}) collective-permute-start(f32[208,128]{1,0:T(8,128)S(1)} %tree_merge.8.refs_0_), channel_id=1, source_target_pairs={{0,16},{1,17},{2,18},{3,19},{4,20},{5,21},{6,22},{7,23},{8,24},{9,... | collective-permute-start | bytes 319496 | tf_op jit(solution)/shard_map/ppermute | solution.py:418
  66.7 3.4 %near_beside.1 = f32[8,512,128]{2,1,0:T(8,128)S(1)} custom-call(s32[8,12]{1,0:T(8,128)S(1)} %collective-permute-done.9.refs_0_, bf16[8,512,128]{2,1,0:T(8,128)(2,1)S(1)} %collective-permute-done.8.refs_1_, f32[8,512,128]{2,1,0:T(8,128)S(1)} %near_early.1.refs_2_, bf16[8,768,128]{2,1,0:T(8,128)(2,1)S(1)} %collective-permute-done.6.refs_3_, ...), custom_call_target="tpu_custom_call" | custom-call | flops 1000 | bytes 1000 | tf_op jit(solution)/shard_map/near_beside/pallas_call | solution.py:374
  70.1 2.3 %collective-permute-done.11.refs_1_ = f32[208,128]{1,0:T(8,128)S(1)} collective-permute-done((f32[208,128]{1,0:T(8,128)S(1)}, f32[208,128]{1,0:T(8,128)S(1)}, u32[]{:S(2)}, u32[]{:S(2)}) %collective-permute-start.11) | collective-permute-done | bytes 106528 | tf_op jit(solution)/shard_map/ppermute | solution.py:418
  72.4 1.7 %tree_merge.9 = f32[4,128]{1,0:T(4,128)} custom-call(f32[208,128]{1,0:T(8,128)S(1)} %tree_merge.8.refs_0_, f32[208,128]{1,0:T(8,128)S(1)} %collective-permute-done.11.refs_1_, s32[255,128]{1,0:T(8,128)S(1)} %copy-done.1), custom_call_target="tpu_custom_call" | custom-call | flops 67108864 | bytes 212992 | tf_op jit(solution)/shard_map/tree_merge/pallas_call | solution.py:251
  74.1 2.5 %collective-permute-done.12 = f32[8,512,128]{2,1,0:T(8,128)S(1)} collective-permute-done((f32[8,512,128]{2,1,0:T(8,128)S(1)}, f32[8,512,128]{2,1,0:T(8,128)S(1)}, u32[]{:S(2)}, u32[]{:S(2)}) %collective-permute-start.12) | collective-permute-done | bytes 2097184 | tf_op jit(solution)/shard_map/ppermute | solution.py:418
  76.6 1.7 %add_multiply_fusion = f32[8,512,128]{2,1,0:T(8,128)} fusion(f32[8,512,128]{2,1,0:T(8,128)S(1)} %near_last.1, f32[8,512,128]{2,1,0:T(8,128)S(1)} %collective-permute-done.12), kind=kLoop, calls=%fused_computation | loop fusion | flops 1048576 | bytes 6291456 | tf_op jit(solution)/shard_map/mul | solution.py:484
  (28 shorter events, 7.2 us)
Async XLA Ops:
  0.6 1.2 %copy-start.2 = (bf16[4096,128]{1,0:T(8,128)(2,1)S(1)}, bf16[4096,128]{1,0:T(8,128)(2,1)}, u32[]{:S(2)}) copy-start(bf16[4096,128]{1,0:T(8,128)(2,1)} %probes.1) | copy-start | bytes 3145732
  1.9 1.0 %copy-start.3 = (bf16[4096,64]{0,1:T(8,128)(2,1)S(1)}, bf16[4096,64]{0,1:T(8,128)(2,1)}, u32[]{:S(2)}) copy-start(bf16[4096,64]{0,1:T(8,128)(2,1)} %param.7) | copy-start | bytes 1572868
  2.9 0.7 copy-start.5
  3.6 36.2 %copy-start.4 = (s32[8,12]{1,0:T(8,128)S(1)}, s32[8,12]{1,0:T(8,128)}, u32[]{:S(2)}) copy-start(s32[8,12]{1,0:T(8,128)} %refs_0_.3) | copy-start | bytes 1156
  6.3 25.1 %collective-permute-start.2 = (bf16[8,768,128]{2,1,0:T(8,128)(2,1)S(1)}, bf16[8,768,128]{2,1,0:T(8,128)(2,1)S(1)}, u32[]{:S(2)}, u32[]{:S(2)}) collective-permute-start(bf16[8,768,128]{2,1,0:T(8,128)(2,1)S(1)} %get-tuple-element.43.pack.refs_2_), channel_id=1, source_target_pairs={{3,1},{0,2},{7,5},{4,6},{11,9},{8,10},{15,13},{12,14},{19,17},{16,... | collective-permute-start | bytes 4718600 | tf_op jit(solution)/shard_map/ppermute | solution.py:409
  11.2 22.3 %collective-permute-start.3 = (bf16[8,768,128]{2,1,0:T(8,128)(2,1)S(1)}, bf16[8,768,128]{2,1,0:T(8,128)(2,1)S(1)}, u32[]{:S(2)}, u32[]{:S(2)}) collective-permute-start(bf16[8,768,128]{2,1,0:T(8,128)(2,1)S(1)} %get-tuple-element.43.pack.refs_2_), channel_id=1, source_target_pairs={{3,7},{7,11},{4,0},{11,15},{8,4},{15,19},{12,8},{19,23},{16,12},{2... | collective-permute-start | bytes 4718600 | tf_op jit(solution)/shard_map/ppermute | solution.py:409
  12.6 21.0 %collective-permute-start.4 = (bf16[8,768,128]{2,1,0:T(8,128)(2,1)S(1)}, bf16[8,768,128]{2,1,0:T(8,128)(2,1)S(1)}, u32[]{:S(2)}, u32[]{:S(2)}) collective-permute-start(bf16[8,768,128]{2,1,0:T(8,128)(2,1)S(1)} %get-tuple-element.43.pack.refs_2_), channel_id=1, source_target_pairs={{1,0},{2,3},{5,4},{6,7},{9,8},{10,11},{13,12},{14,15},{17,16},{18,... | collective-permute-start | bytes 4718600 | tf_op jit(solution)/shard_map/ppermute | solution.py:409
  13.8 0.9 %copy-start = (s32[255,128]{1,0:T(8,128)S(1)}, s32[255,128]{1,0:T(8,128)}, u32[]{:S(2)}) copy-start(s32[255,128]{1,0:T(8,128)} %refs_2_.9) | copy-start | bytes 391684
  14.8 0.7 copy-start.6
  22.5 2.3 %collective-permute-start = (f32[208,128]{1,0:T(8,128)S(1)}, f32[208,128]{1,0:T(8,128)S(1)}, u32[]{:S(2)}, u32[]{:S(2)}) collective-permute-start(f32[208,128]{1,0:T(8,128)S(1)} %local_tree.1.refs_0_), channel_id=1, source_target_pairs={{0,1},{1,0},{2,3},{3,2},{4,5},{5,4},{6,7},{7,6},{8,9},{9,8},{10,11... | collective-permute-start | bytes 319496 | tf_op jit(solution)/shard_map/ppermute | solution.py:418
  25.7 5.7 %collective-permute-start.1 = (f32[208,128]{1,0:T(8,128)S(1)}, f32[208,128]{1,0:T(8,128)S(1)}, u32[]{:S(2)}, u32[]{:S(2)}) collective-permute-start(f32[208,128]{1,0:T(8,128)S(1)} %tree_merge.5.refs_0_), channel_id=1, source_target_pairs={{0,2},{1,3},{2,0},{3,1},{4,6},{5,7},{6,4},{7,5},{8,10},{9,11},{10,... | collective-permute-start | bytes 319496 | tf_op jit(solution)/shard_map/ppermute | solution.py:418
  33.6 25.0 %collective-permute-start.7 = (bf16[8,768,128]{2,1,0:T(8,128)(2,1)S(1)}, bf16[8,768,128]{2,1,0:T(8,128)(2,1)S(1)}, u32[]{:S(2)}, u32[]{:S(2)}) collective-permute-start(bf16[8,768,128]{2,1,0:T(8,128)(2,1)S(1)} %collective-permute-done.2.refs_4_), channel_id=1, source_target_pairs={{1,5},{5,9},{6,2},{9,13},{10,6},{13,17},{14,10},{17,21},{18,14},{2... | collective-permute-start | bytes 4718600 | tf_op jit(solution)/shard_map/ppermute | solution.py:409
  34.3 24.3 %collective-permute-start.6 = (bf16[8,768,128]{2,1,0:T(8,128)(2,1)S(1)}, bf16[8,768,128]{2,1,0:T(8,128)(2,1)S(1)}, u32[]{:S(2)}, u32[]{:S(2)}) collective-permute-start(bf16[8,768,128]{2,1,0:T(8,128)(2,1)S(1)} %collective-permute-done.4), channel_id=1, source_target_pairs={{0,3},{3,0},{4,7},{7,4},{8,11},{11,8},{12,15},{15,12},{16,19},{19,... | collective-permute-start | bytes 4718600 | tf_op jit(solution)/shard_map/ppermute | solution.py:409
  36.3 15.8 %collective-permute-start.8 = (bf16[8,512,128]{2,1,0:T(8,128)(2,1)S(1)}, bf16[8,512,128]{2,1,0:T(8,128)(2,1)S(1)}, u32[]{:S(2)}, u32[]{:S(2)}) collective-permute-start(bf16[8,512,128]{2,1,0:T(8,128)(2,1)S(1)} %get-tuple-element.41.rows.refs_1_), channel_id=1, source_target_pairs={{0,1},{1,0},{2,3},{3,2},{4,5},{5,4},{6,7},{7,6},{8,9},{9,8},{10,11... | collective-permute-start | bytes 3145736 | tf_op jit(solution)/shard_map/ppermute | solution.py:418
  37.3 21.2 %collective-permute-start.5 = (f32[208,128]{1,0:T(8,128)S(1)}, f32[208,128]{1,0:T(8,128)S(1)}, u32[]{:S(2)}, u32[]{:S(2)}) collective-permute-start(f32[208,128]{1,0:T(8,128)S(1)} %tree_merge.6.refs_0_), channel_id=1, source_target_pairs={{0,4},{1,5},{2,6},{3,7},{4,0},{5,1},{6,2},{7,3},{8,12},{9,13},{10,... | collective-permute-start | bytes 319496 | tf_op jit(solution)/shard_map/ppermute | solution.py:418
  39.8 12.2 %collective-permute-start.9 = (s32[8,12]{1,0:T(8,128)S(1)}, s32[8,12]{1,0:T(8,128)S(1)}, u32[]{:S(2)}, u32[]{:S(2)}) collective-permute-start(s32[8,12]{1,0:T(8,128)S(1)} %copy-done.4), channel_id=1, source_target_pairs={{0,1},{1,0},{2,3},{3,2},{4,5},{5,4},{6,7},{7,6},{8,9},{9,8},{10,11... | collective-permute-start | bytes 1160 | tf_op jit(solution)/shard_map/ppermute | solution.py:418
  52.0 6.6 %copy-start.1 = (s32[255,128]{1,0:T(8,128)S(1)}, s32[255,128]{1,0:T(8,128)}, u32[]{:S(2)}) copy-start(s32[255,128]{1,0:T(8,128)} %refs_2_.9) | copy-start | bytes 391684
  59.6 5.0 %collective-permute-start.10 = (f32[208,128]{1,0:T(8,128)S(1)}, f32[208,128]{1,0:T(8,128)S(1)}, u32[]{:S(2)}, u32[]{:S(2)}) collective-permute-start(f32[208,128]{1,0:T(8,128)S(1)} %tree_merge.7.refs_0_), channel_id=1, source_target_pairs={{0,8},{1,9},{2,10},{3,11},{4,12},{5,13},{6,14},{7,15},{8,0},{9,1},... | collective-permute-start | bytes 319496 | tf_op jit(solution)/shard_map/ppermute | solution.py:418
  65.6 6.8 %collective-permute-start.11 = (f32[208,128]{1,0:T(8,128)S(1)}, f32[208,128]{1,0:T(8,128)S(1)}, u32[]{:S(2)}, u32[]{:S(2)}) collective-permute-start(f32[208,128]{1,0:T(8,128)S(1)} %tree_merge.8.refs_0_), channel_id=1, source_target_pairs={{0,16},{1,17},{2,18},{3,19},{4,20},{5,21},{6,22},{7,23},{8,24},{9,... | collective-permute-start | bytes 319496 | tf_op jit(solution)/shard_map/ppermute | solution.py:418
  72.4 4.2 %collective-permute-start.12 = (f32[8,512,128]{2,1,0:T(8,128)S(1)}, f32[8,512,128]{2,1,0:T(8,128)S(1)}, u32[]{:S(2)}, u32[]{:S(2)}) collective-permute-start(f32[8,512,128]{2,1,0:T(8,128)S(1)} %near_beside.1), channel_id=1, source_target_pairs={{0,1},{1,0},{2,3},{3,2},{4,5},{5,4},{6,7},{7,6},{8,9},{9,8},{10,11... | collective-permute-start | bytes 6291464 | tf_op jit(solution)/shard_map/ppermute | solution.py:418

commit v15 on v14

--- a/solution.py
+++ b/solution.py
@@ -335,17 +335,18 @@
                 total = term if total is None else total + term
             return g, total
 
-        def add_pairs(i, carry):
-            for g, total in [add_pair(2 * i), add_pair(2 * i + 1)]:
+        def add_four(i, carry):
+            for g, total in [add_pair(4 * i + k) for k in range(4)]:
                 outs[j][g] += total
             return carry
 
-        lax.fori_loop(0, pairs // 2, add_pairs, 0)
-
-        @pl.when(pairs % 2 == 1)
-        def _():
-            g, total = add_pair(pairs - 1)
+        def add_one(i, carry):
+            g, total = add_pair(i)
             outs[j][g] += total
+            return carry
+
+        lax.fori_loop(0, pairs // 4, add_four, 0)
+        lax.fori_loop(pairs // 4 * 4, pairs, add_one, 0)
 
     for t, (number, j) in enumerate(tasks):
         held = place(sets[number][1])

time: 78.6 us -> 78.7 us (level)
  Pallas kernels: 41 us -> 36 us
  waiting for transfers between devices: 11.8 us -> 14.7 us
  starting transfers between devices: 18.5 us -> 21 us
    pallas_call x4, Pallas kernels: 25.7 us -> 20.8 us  [near_call(): pl.pallas_call(functools.partial(near_kernel, flips=flips, row_counts=tup...]
    ppermute x5, waiting for transfers between devices: 2.22 us -> 5.63 us  [send(): return lax.ppermute(x, axes, pairs)]
    ppermute x8, starting transfers between devices: 8.23 us -> 10.8 us  [exchange(): lax.ppermute(x, axes, [(i, i ^ d << shift) for i in range(count)])]
  transfers between devices with their start and end apart: 13 -> 13, of which waited for: 5 -> 6; matrix products, arithmetic and copies ran while one was open for 0% -> 0% of each run, Pallas kernels for 46% -> 40%
where the time goes in v15:
time: 78.7 us; the launch traced here: 78.8 us
  Pallas kernels  36 us (46%)
  starting transfers between devices  21 us (27%)
  waiting for transfers between devices  14.7 us (19%)
  local copies, waits for them, and re-layouts  4.57 us (6%)
  other arithmetic  1.66 us (2%)
  between operations  0.84 us (1%)
    pallas_call x4, Pallas kernels, near_call(): pl.pallas_call(functools.partial(near_kernel, flips=flips, row_counts=tup...  20.8 us
    ppermute x8, starting transfers between devices, exchange(): lax.ppermute(x, axes, [(i, i ^ d << shift) for i in range(count)])  10.8 us
    ppermute x5, starting transfers between devices, send(): return lax.ppermute(x, axes, pairs)  10.2 us
    ppermute x8, waiting for transfers between devices, exchange(): lax.ppermute(x, axes, [(i, i ^ d << shift) for i in range(count)])  9.11 us
    pallas_call x1, Pallas kernels, local_tree_call(): pl.pallas_call(functools.partial(local_tree_kernel, dim=dim), in_specs=[p...  7.01 us
    ppermute x5, waiting for transfers between devices, send(): return lax.ppermute(x, axes, pairs)  5.63 us
    pallas_call x5, Pallas kernels, merge_call(): pl.pallas_call(functools.partial(merge_kernel, dim=dim, blocks=blocks, sh...  5.6 us
    unnamed x14, local copies, waits for them, and re-layouts  4.57 us
  transfers between devices with their start and end apart: 13, of which 6 were waited for; matrix products, arithmetic and copies ran while one was open for 0% of the time, Pallas kernels for 40%

profile of v15, /device:TPU:0, one launch (start us, length us, event | category | flops | bytes accessed | tf_op | source)
XLA Modules:
  0.0 78.8 jit_solution(7253196522586355982)
XLA Ops:
  0.6 1.2 %copy-done.2 = bf16[4096,128]{1,0:T(8,128)(2,1)S(1)} copy-done((bf16[4096,128]{1,0:T(8,128)(2,1)S(1)}, bf16[4096,128]{1,0:T(8,128)(2,1)}, u32[]{:S(2)}) %copy-start.2) | copy-done | bytes 1048600
  1.9 1.0 %copy-done.3 = bf16[4096,64]{0,1:T(8,128)(2,1)S(1)} copy-done((bf16[4096,64]{0,1:T(8,128)(2,1)S(1)}, bf16[4096,64]{0,1:T(8,128)(2,1)}, u32[]{:S(2)}) %copy-start.3) | copy-done | bytes 524312
  3.6 2.6 %tree_order.1 = (bf16[8,768,128]{2,1,0:T(8,128)(2,1)S(1)}, bf16[8,512,128]{2,1,0:T(8,128)(2,1)S(1)}) custom-call(bf16[64,4096]{1,0:T(8,128)(2,1)S(1)} %bitcast.4, s32[8,1,512]{2,1,0:T(1,128)S(1)} %bitcast.5, bf16[4096,128]{1,0:T(8,128)(2,1)S(1)} %copy-done.2), custom_call_target="tpu_custom_call" | custom-call | flops 268435456 | bytes 5242880 | tf_op jit(solution)/shard_map/tree_order/pallas_call | solution.py:94
  6.3 5.0 %collective-permute-start.2 = (bf16[8,768,128]{2,1,0:T(8,128)(2,1)S(1)}, bf16[8,768,128]{2,1,0:T(8,128)(2,1)S(1)}, u32[]{:S(2)}, u32[]{:S(2)}) collective-permute-start(bf16[8,768,128]{2,1,0:T(8,128)(2,1)S(1)} %get-tuple-element.43.pack.refs_2_), channel_id=1, source_target_pairs={{3,1},{0,2},{7,5},{4,6},{11,9},{8,10},{15,13},{12,14},{19,17},{16,... | collective-permute-start | bytes 4718600 | tf_op jit(solution)/shard_map/ppermute | solution.py:410
  11.2 1.3 %collective-permute-start.3 = (bf16[8,768,128]{2,1,0:T(8,128)(2,1)S(1)}, bf16[8,768,128]{2,1,0:T(8,128)(2,1)S(1)}, u32[]{:S(2)}, u32[]{:S(2)}) collective-permute-start(bf16[8,768,128]{2,1,0:T(8,128)(2,1)S(1)} %get-tuple-element.43.pack.refs_2_), channel_id=1, source_target_pairs={{3,7},{7,11},{4,0},{11,15},{8,4},{15,19},{12,8},{19,23},{16,12},{2... | collective-permute-start | bytes 4718600 | tf_op jit(solution)/shard_map/ppermute | solution.py:410
  12.6 1.3 %collective-permute-start.4 = (bf16[8,768,128]{2,1,0:T(8,128)(2,1)S(1)}, bf16[8,768,128]{2,1,0:T(8,128)(2,1)S(1)}, u32[]{:S(2)}, u32[]{:S(2)}) collective-permute-start(bf16[8,768,128]{2,1,0:T(8,128)(2,1)S(1)} %get-tuple-element.43.pack.refs_2_), channel_id=1, source_target_pairs={{1,0},{2,3},{5,4},{6,7},{9,8},{10,11},{13,12},{14,15},{17,16},{18,... | collective-permute-start | bytes 4718600 | tf_op jit(solution)/shard_map/ppermute | solution.py:410
  15.4 7.0 %local_tree.1.refs_0_ = f32[208,128]{1,0:T(8,128)S(1)} custom-call(bf16[8,768,128]{2,1,0:T(8,128)(2,1)S(1)} %get-tuple-element.43.pack.refs_2_, bf16[8,512,128]{2,1,0:T(8,128)(2,1)S(1)} %get-tuple-element.41.rows.refs_1_, s32[8,128]{1,0:T(8,128)S(1)} %copy-done.6, s32[255,128]{1,0:T(8,128)S(1)} %copy-done), custom_call_target="tpu_custom_call" | custom-call | flops 536870912 | bytes 3145728 | tf_op jit(solution)/shard_map/local_tree/pallas_call | solution.py:177
  22.5 1.3 %collective-permute-start = (f32[208,128]{1,0:T(8,128)S(1)}, f32[208,128]{1,0:T(8,128)S(1)}, u32[]{:S(2)}, u32[]{:S(2)}) collective-permute-start(f32[208,128]{1,0:T(8,128)S(1)} %local_tree.1.refs_0_), channel_id=1, source_target_pairs={{0,1},{1,0},{2,3},{3,2},{4,5},{5,4},{6,7},{7,6},{8,9},{9,8},{10,11... | collective-permute-start | bytes 319496 | tf_op jit(solution)/shard_map/ppermute | solution.py:419
  25.7 1.9 %collective-permute-start.1 = (f32[208,128]{1,0:T(8,128)S(1)}, f32[208,128]{1,0:T(8,128)S(1)}, u32[]{:S(2)}, u32[]{:S(2)}) collective-permute-start(f32[208,128]{1,0:T(8,128)S(1)} %tree_merge.5.refs_0_), channel_id=1, source_target_pairs={{0,2},{1,3},{2,0},{3,1},{4,6},{5,7},{6,4},{7,5},{8,10},{9,11},{10,... | collective-permute-start | bytes 319496 | tf_op jit(solution)/shard_map/ppermute | solution.py:419
  27.6 3.8 %collective-permute-done.1.refs_1_ = f32[208,128]{1,0:T(8,128)S(1)} collective-permute-done((f32[208,128]{1,0:T(8,128)S(1)}, f32[208,128]{1,0:T(8,128)S(1)}, u32[]{:S(2)}, u32[]{:S(2)}) %collective-permute-start.1) | collective-permute-done | bytes 106528 | tf_op jit(solution)/shard_map/ppermute | solution.py:419
  31.4 2.2 %collective-permute-done.3.refs_3_ = bf16[8,768,128]{2,1,0:T(8,128)(2,1)S(1)} collective-permute-done((bf16[8,768,128]{2,1,0:T(8,128)(2,1)S(1)}, bf16[8,768,128]{2,1,0:T(8,128)(2,1)S(1)}, u32[]{:S(2)}, u32[]{:S(2)}) %collective-permute-start.3) | collective-permute-done | bytes 1572896 | tf_op jit(solution)/shard_map/ppermute | solution.py:410
  34.3 1.9 %collective-permute-start.6 = (bf16[8,768,128]{2,1,0:T(8,128)(2,1)S(1)}, bf16[8,768,128]{2,1,0:T(8,128)(2,1)S(1)}, u32[]{:S(2)}, u32[]{:S(2)}) collective-permute-start(bf16[8,768,128]{2,1,0:T(8,128)(2,1)S(1)} %collective-permute-done.4), channel_id=1, source_target_pairs={{0,3},{3,0},{4,7},{7,4},{8,11},{11,8},{12,15},{15,12},{16,19},{19,... | collective-permute-start | bytes 4718600 | tf_op jit(solution)/shard_map/ppermute | solution.py:410
  37.3 2.5 %collective-permute-start.5 = (f32[208,128]{1,0:T(8,128)S(1)}, f32[208,128]{1,0:T(8,128)S(1)}, u32[]{:S(2)}, u32[]{:S(2)}) collective-permute-start(f32[208,128]{1,0:T(8,128)S(1)} %tree_merge.6.refs_0_), channel_id=1, source_target_pairs={{0,4},{1,5},{2,6},{3,7},{4,0},{5,1},{6,2},{7,3},{8,12},{9,13},{10,... | collective-permute-start | bytes 319496 | tf_op jit(solution)/shard_map/ppermute | solution.py:419
  40.0 8.1 %near_own.1.refs_2_ = f32[8,512,128]{2,1,0:T(8,128)S(1)} custom-call(s32[8,12]{1,0:T(8,128)S(1)} %copy-done.4, bf16[8,512,128]{2,1,0:T(8,128)(2,1)S(1)} %get-tuple-element.41.rows.refs_1_, bf16[8,768,128]{2,1,0:T(8,128)(2,1)S(1)} %get-tuple-element.43.pack.refs_2_, bf16[8,768,128]{2,1,0:T(8,128)(2,1)S(1)} %collective-permute-done.3.refs_3_, ...), custom_call_target="tpu_custom_call" | custom-call | flops 1000 | bytes 1000 | tf_op jit(solution)/shard_map/near_own/pallas_call | solution.py:375
  48.1 4.5 %near_early.1.refs_2_ = f32[8,512,128]{2,1,0:T(8,128)S(1)} custom-call(s32[8,12]{1,0:T(8,128)S(1)} %collective-permute-done.9.refs_0_, bf16[8,512,128]{2,1,0:T(8,128)(2,1)S(1)} %collective-permute-done.8.refs_1_, bf16[8,768,128]{2,1,0:T(8,128)(2,1)S(1)} %get-tuple-element.43.pack.refs_2_, bf16[8,768,128]{2,1,0:T(8,128)(2,1)S(1)} %collective-permute-done.3.refs_3_, ...), custom_call_target="tpu_custom_call" | custom-call | flops 1000 | bytes 1000 | tf_op jit(solution)/shard_map/near_early/pallas_call | solution.py:375
  52.6 3.4 %collective-permute-done.6.refs_3_ = bf16[8,768,128]{2,1,0:T(8,128)(2,1)S(1)} collective-permute-done((bf16[8,768,128]{2,1,0:T(8,128)(2,1)S(1)}, bf16[8,768,128]{2,1,0:T(8,128)(2,1)S(1)}, u32[]{:S(2)}, u32[]{:S(2)}) %collective-permute-start.6) | collective-permute-done | bytes 1572896 | tf_op jit(solution)/shard_map/ppermute | solution.py:410
  57.0 2.7 %collective-permute-start.10 = (f32[208,128]{1,0:T(8,128)S(1)}, f32[208,128]{1,0:T(8,128)S(1)}, u32[]{:S(2)}, u32[]{:S(2)}) collective-permute-start(f32[208,128]{1,0:T(8,128)S(1)} %tree_merge.7.refs_0_), channel_id=1, source_target_pairs={{0,8},{1,9},{2,10},{3,11},{4,12},{5,13},{6,14},{7,15},{8,0},{9,1},... | collective-permute-start | bytes 319496 | tf_op jit(solution)/shard_map/ppermute | solution.py:419
  59.7 5.0 %near_last.1 = f32[8,512,128]{2,1,0:T(8,128)S(1)} custom-call(s32[8,12]{1,0:T(8,128)S(1)} %copy-done.4, bf16[8,512,128]{2,1,0:T(8,128)(2,1)S(1)} %get-tuple-element.41.rows.refs_1_, f32[8,512,128]{2,1,0:T(8,128)S(1)} %near_own.1.refs_2_, bf16[8,768,128]{2,1,0:T(8,128)(2,1)S(1)} %collective-permute-done.6.refs_3_, ...), custom_call_target="tpu_custom_call" | custom-call | flops 1000 | bytes 1000 | tf_op jit(solution)/shard_map/near_last/pallas_call | solution.py:375
  65.8 2.2 %collective-permute-start.11 = (f32[208,128]{1,0:T(8,128)S(1)}, f32[208,128]{1,0:T(8,128)S(1)}, u32[]{:S(2)}, u32[]{:S(2)}) collective-permute-start(f32[208,128]{1,0:T(8,128)S(1)} %tree_merge.8.refs_0_), channel_id=1, source_target_pairs={{0,16},{1,17},{2,18},{3,19},{4,20},{5,21},{6,22},{7,23},{8,24},{9,... | collective-permute-start | bytes 319496 | tf_op jit(solution)/shard_map/ppermute | solution.py:419
  68.0 3.1 %near_beside.1 = f32[8,512,128]{2,1,0:T(8,128)S(1)} custom-call(s32[8,12]{1,0:T(8,128)S(1)} %collective-permute-done.9.refs_0_, bf16[8,512,128]{2,1,0:T(8,128)(2,1)S(1)} %collective-permute-done.8.refs_1_, f32[8,512,128]{2,1,0:T(8,128)S(1)} %near_early.1.refs_2_, bf16[8,768,128]{2,1,0:T(8,128)(2,1)S(1)} %collective-permute-done.6.refs_3_, ...), custom_call_target="tpu_custom_call" | custom-call | flops 1000 | bytes 1000 | tf_op jit(solution)/shard_map/near_beside/pallas_call | solution.py:375
  71.1 1.9 %collective-permute-done.11.refs_1_ = f32[208,128]{1,0:T(8,128)S(1)} collective-permute-done((f32[208,128]{1,0:T(8,128)S(1)}, f32[208,128]{1,0:T(8,128)S(1)}, u32[]{:S(2)}, u32[]{:S(2)}) %collective-permute-start.11) | collective-permute-done | bytes 106528 | tf_op jit(solution)/shard_map/ppermute | solution.py:419
  73.0 1.7 %tree_merge.9 = f32[4,128]{1,0:T(4,128)} custom-call(f32[208,128]{1,0:T(8,128)S(1)} %tree_merge.8.refs_0_, f32[208,128]{1,0:T(8,128)S(1)} %collective-permute-done.11.refs_1_, s32[255,128]{1,0:T(8,128)S(1)} %copy-done.1), custom_call_target="tpu_custom_call" | custom-call | flops 67108864 | bytes 212992 | tf_op jit(solution)/shard_map/tree_merge/pallas_call | solution.py:251
  74.7 2.5 %collective-permute-done.12 = f32[8,512,128]{2,1,0:T(8,128)S(1)} collective-permute-done((f32[8,512,128]{2,1,0:T(8,128)S(1)}, f32[8,512,128]{2,1,0:T(8,128)S(1)}, u32[]{:S(2)}, u32[]{:S(2)}) %collective-permute-start.12) | collective-permute-done | bytes 2097184 | tf_op jit(solution)/shard_map/ppermute | solution.py:419
  77.2 1.7 %add_multiply_fusion = f32[8,512,128]{2,1,0:T(8,128)} fusion(f32[8,512,128]{2,1,0:T(8,128)S(1)} %near_last.1, f32[8,512,128]{2,1,0:T(8,128)S(1)} %collective-permute-done.12), kind=kLoop, calls=%fused_computation | loop fusion | flops 1048576 | bytes 6291456 | tf_op jit(solution)/shard_map/mul | solution.py:485
  (28 shorter events, 8.2 us)
Async XLA Ops:
  0.6 1.2 %copy-start.2 = (bf16[4096,128]{1,0:T(8,128)(2,1)S(1)}, bf16[4096,128]{1,0:T(8,128)(2,1)}, u32[]{:S(2)}) copy-start(bf16[4096,128]{1,0:T(8,128)(2,1)} %probes.1) | copy-start | bytes 3145732
  1.9 1.0 %copy-start.3 = (bf16[4096,64]{0,1:T(8,128)(2,1)S(1)}, bf16[4096,64]{0,1:T(8,128)(2,1)}, u32[]{:S(2)}) copy-start(bf16[4096,64]{0,1:T(8,128)(2,1)} %param.7) | copy-start | bytes 1572868
  2.9 0.7 copy-start.5
  3.6 36.2 %copy-start.4 = (s32[8,12]{1,0:T(8,128)S(1)}, s32[8,12]{1,0:T(8,128)}, u32[]{:S(2)}) copy-start(s32[8,12]{1,0:T(8,128)} %refs_0_.3) | copy-start | bytes 1156
  6.3 25.1 %collective-permute-start.2 = (bf16[8,768,128]{2,1,0:T(8,128)(2,1)S(1)}, bf16[8,768,128]{2,1,0:T(8,128)(2,1)S(1)}, u32[]{:S(2)}, u32[]{:S(2)}) collective-permute-start(bf16[8,768,128]{2,1,0:T(8,128)(2,1)S(1)} %get-tuple-element.43.pack.refs_2_), channel_id=1, source_target_pairs={{3,1},{0,2},{7,5},{4,6},{11,9},{8,10},{15,13},{12,14},{19,17},{16,... | collective-permute-start | bytes 4718600 | tf_op jit(solution)/shard_map/ppermute | solution.py:410
  11.2 22.3 %collective-permute-start.3 = (bf16[8,768,128]{2,1,0:T(8,128)(2,1)S(1)}, bf16[8,768,128]{2,1,0:T(8,128)(2,1)S(1)}, u32[]{:S(2)}, u32[]{:S(2)}) collective-permute-start(bf16[8,768,128]{2,1,0:T(8,128)(2,1)S(1)} %get-tuple-element.43.pack.refs_2_), channel_id=1, source_target_pairs={{3,7},{7,11},{4,0},{11,15},{8,4},{15,19},{12,8},{19,23},{16,12},{2... | collective-permute-start | bytes 4718600 | tf_op jit(solution)/shard_map/ppermute | solution.py:410
  12.6 21.0 %collective-permute-start.4 = (bf16[8,768,128]{2,1,0:T(8,128)(2,1)S(1)}, bf16[8,768,128]{2,1,0:T(8,128)(2,1)S(1)}, u32[]{:S(2)}, u32[]{:S(2)}) collective-permute-start(bf16[8,768,128]{2,1,0:T(8,128)(2,1)S(1)} %get-tuple-element.43.pack.refs_2_), channel_id=1, source_target_pairs={{1,0},{2,3},{5,4},{6,7},{9,8},{10,11},{13,12},{14,15},{17,16},{18,... | collective-permute-start | bytes 4718600 | tf_op jit(solution)/shard_map/ppermute | solution.py:410
  13.8 0.9 %copy-start = (s32[255,128]{1,0:T(8,128)S(1)}, s32[255,128]{1,0:T(8,128)}, u32[]{:S(2)}) copy-start(s32[255,128]{1,0:T(8,128)} %refs_2_.9) | copy-start | bytes 391684
  14.8 0.7 copy-start.6
  22.5 2.3 %collective-permute-start = (f32[208,128]{1,0:T(8,128)S(1)}, f32[208,128]{1,0:T(8,128)S(1)}, u32[]{:S(2)}, u32[]{:S(2)}) collective-permute-start(f32[208,128]{1,0:T(8,128)S(1)} %local_tree.1.refs_0_), channel_id=1, source_target_pairs={{0,1},{1,0},{2,3},{3,2},{4,5},{5,4},{6,7},{7,6},{8,9},{9,8},{10,11... | collective-permute-start | bytes 319496 | tf_op jit(solution)/shard_map/ppermute | solution.py:419
  25.7 5.7 %collective-permute-start.1 = (f32[208,128]{1,0:T(8,128)S(1)}, f32[208,128]{1,0:T(8,128)S(1)}, u32[]{:S(2)}, u32[]{:S(2)}) collective-permute-start(f32[208,128]{1,0:T(8,128)S(1)} %tree_merge.5.refs_0_), channel_id=1, source_target_pairs={{0,2},{1,3},{2,0},{3,1},{4,6},{5,7},{6,4},{7,5},{8,10},{9,11},{10,... | collective-permute-start | bytes 319496 | tf_op jit(solution)/shard_map/ppermute | solution.py:419
  33.6 19.1 %collective-permute-start.7 = (bf16[8,768,128]{2,1,0:T(8,128)(2,1)S(1)}, bf16[8,768,128]{2,1,0:T(8,128)(2,1)S(1)}, u32[]{:S(2)}, u32[]{:S(2)}) collective-permute-start(bf16[8,768,128]{2,1,0:T(8,128)(2,1)S(1)} %collective-permute-done.2.refs_4_), channel_id=1, source_target_pairs={{1,5},{5,9},{6,2},{9,13},{10,6},{13,17},{14,10},{17,21},{18,14},{2... | collective-permute-start | bytes 4718600 | tf_op jit(solution)/shard_map/ppermute | solution.py:410
  34.3 21.7 %collective-permute-start.6 = (bf16[8,768,128]{2,1,0:T(8,128)(2,1)S(1)}, bf16[8,768,128]{2,1,0:T(8,128)(2,1)S(1)}, u32[]{:S(2)}, u32[]{:S(2)}) collective-permute-start(bf16[8,768,128]{2,1,0:T(8,128)(2,1)S(1)} %collective-permute-done.4), channel_id=1, source_target_pairs={{0,3},{3,0},{4,7},{7,4},{8,11},{11,8},{12,15},{15,12},{16,19},{19,... | collective-permute-start | bytes 4718600 | tf_op jit(solution)/shard_map/ppermute | solution.py:410
  36.3 11.8 %collective-permute-start.8 = (bf16[8,512,128]{2,1,0:T(8,128)(2,1)S(1)}, bf16[8,512,128]{2,1,0:T(8,128)(2,1)S(1)}, u32[]{:S(2)}, u32[]{:S(2)}) collective-permute-start(bf16[8,512,128]{2,1,0:T(8,128)(2,1)S(1)} %get-tuple-element.41.rows.refs_1_), channel_id=1, source_target_pairs={{0,1},{1,0},{2,3},{3,2},{4,5},{5,4},{6,7},{7,6},{8,9},{9,8},{10,11... | collective-permute-start | bytes 3145736 | tf_op jit(solution)/shard_map/ppermute | solution.py:419
  37.3 15.3 %collective-permute-start.5 = (f32[208,128]{1,0:T(8,128)S(1)}, f32[208,128]{1,0:T(8,128)S(1)}, u32[]{:S(2)}, u32[]{:S(2)}) collective-permute-start(f32[208,128]{1,0:T(8,128)S(1)} %tree_merge.6.refs_0_), channel_id=1, source_target_pairs={{0,4},{1,5},{2,6},{3,7},{4,0},{5,1},{6,2},{7,3},{8,12},{9,13},{10,... | collective-permute-start | bytes 319496 | tf_op jit(solution)/shard_map/ppermute | solution.py:419
  39.8 8.3 %collective-permute-start.9 = (s32[8,12]{1,0:T(8,128)S(1)}, s32[8,12]{1,0:T(8,128)S(1)}, u32[]{:S(2)}, u32[]{:S(2)}) collective-permute-start(s32[8,12]{1,0:T(8,128)S(1)} %copy-done.4), channel_id=1, source_target_pairs={{0,1},{1,0},{2,3},{3,2},{4,5},{5,4},{6,7},{7,6},{8,9},{9,8},{10,11... | collective-permute-start | bytes 1160 | tf_op jit(solution)/shard_map/ppermute | solution.py:419
  48.1 8.0 %copy-start.1 = (s32[255,128]{1,0:T(8,128)S(1)}, s32[255,128]{1,0:T(8,128)}, u32[]{:S(2)}) copy-start(s32[255,128]{1,0:T(8,128)} %refs_2_.9) | copy-start | bytes 391684
  57.0 7.7 %collective-permute-start.10 = (f32[208,128]{1,0:T(8,128)S(1)}, f32[208,128]{1,0:T(8,128)S(1)}, u32[]{:S(2)}, u32[]{:S(2)}) collective-permute-start(f32[208,128]{1,0:T(8,128)S(1)} %tree_merge.7.refs_0_), channel_id=1, source_target_pairs={{0,8},{1,9},{2,10},{3,11},{4,12},{5,13},{6,14},{7,15},{8,0},{9,1},... | collective-permute-start | bytes 319496 | tf_op jit(solution)/shard_map/ppermute | solution.py:419
  65.8 7.3 %collective-permute-start.11 = (f32[208,128]{1,0:T(8,128)S(1)}, f32[208,128]{1,0:T(8,128)S(1)}, u32[]{:S(2)}, u32[]{:S(2)}) collective-permute-start(f32[208,128]{1,0:T(8,128)S(1)} %tree_merge.8.refs_0_), channel_id=1, source_target_pairs={{0,16},{1,17},{2,18},{3,19},{4,20},{5,21},{6,22},{7,23},{8,24},{9,... | collective-permute-start | bytes 319496 | tf_op jit(solution)/shard_map/ppermute | solution.py:419
  73.0 4.2 %collective-permute-start.12 = (f32[8,512,128]{2,1,0:T(8,128)S(1)}, f32[8,512,128]{2,1,0:T(8,128)S(1)}, u32[]{:S(2)}, u32[]{:S(2)}) collective-permute-start(f32[8,512,128]{2,1,0:T(8,128)S(1)} %near_beside.1), channel_id=1, source_target_pairs={{0,1},{1,0},{2,3},{3,2},{4,5},{5,4},{6,7},{7,6},{8,9},{9,8},{10,11... | collective-permute-start | bytes 6291464 | tf_op jit(solution)/shard_map/ppermute | solution.py:419
